TPU v7x, 32 devices: a whole 2x2x4 slice. The times are simulated.
32 devices in a mesh: particle: 4 (over z), tile: 8 (over y, x, core).
Axes of the slice: x: 2, y: 2, z: 4, core: 2. Of those that a mesh axis runs over, the one named last changes fastest.
Arguments:
- biomass: float32 [16, 32768], P('particle', 'tile'), as said below
- water: float32 [16, 32768], P('particle', 'tile'), may hold values from -5 to 5
- flow_blocks: bfloat16 [256, 3, 128, 128], P('tile'), may hold values from -0.15625 to 0.15625
- neighbours: int32 [256, 3], P('tile'), may hold values from 0 to 255, as said below
- rain: float32 [4, 16, 32768], P(None, 'particle', 'tile'), may hold values from -4 to 4
- growth_rate: float32 [32768], P('tile'), may hold values from 0.05 to 0.5
- observations: float32 [2, 32768], P(None, 'tile'), may hold values from -5 to 5
- obs_precision: float32 [32768], P('tile'), as said below
- ancestors: int32 [2, 16], replicated, may hold values from 0 to 15
Outputs:
- means: float32 [2, 2, 32768], P(None, None, 'tile')
- biomass_out: float32 [16, 32768], P('particle', 'tile')
- water_out: float32 [16, 32768], P('particle', 'tile')
Inputs may be any that keep to these rules, and one draw needn't show every extreme that they name: `neighbours`: row n lists block n first, then one block 1 to 4 blocks below n and one 1 to 4 blocks above n, each clipped to the grid's ends. `biomass`: every entry lies between 0.5 and 2. `obs_precision`: every entry lies between 0.3 / sqrt(32768) and 3 / sqrt(32768).
All inputs are finite; a program needn't handle non-finite values.
Results may differ from a plain program's by a relative error of at most 0.0019.
Values may be sent and summed in bfloat16 or wider, within the bound.
No kernel may reach another device: no remote copies, remote signals or barrier semaphores. Data moves between devices by JAX's collectives and lax.ppermute only.
A program may use at most 64 MiB of HBM per device.

v0:
```python
import jax
import jax.numpy as jnp
from jax import lax
from jax.sharding import PartitionSpec as P

BLK = 128
CYCLES = 2
DAYS = 2
HALO = 4


def padded(cells, sides, width):
    for axis, dim in sides:
        count = lax.axis_size(axis)
        ends = count - 1
        head = lax.slice_in_dim(cells, 0, width, axis=dim)
        tail = lax.slice_in_dim(cells, cells.shape[dim] - width, cells.shape[dim], axis=dim)
        cells = jnp.concatenate(
            [
                lax.ppermute(tail, axis, [(i, (i + 1) % count) for i in range(ends)]),
                cells,
                lax.ppermute(head, axis, [((i + 1) % count, i) for i in range(ends)]),
            ],
            axis=dim,
        )
    return cells


def body(
    biomass,
    water,
    flow_blocks,
    neighbours,
    rain,
    growth_rate,
    observations,
    obs_precision,
    ancestors,
):
    part_dev = biomass.shape[0]
    cells = biomass.shape[1]
    blocks_dev = cells // BLK
    member = lax.axis_index("particle")
    tile_pos = lax.axis_index("tile")
    local_ids = neighbours - tile_pos * blocks_dev + HALO
    bio, wat = (biomass, water)
    collected = []
    for cycle in range(CYCLES):
        misfit_local = -0.5 * jnp.sum(obs_precision * (bio - observations[cycle]) ** 2, axis=1)
        summed = lax.psum(misfit_local, "tile")
        log_weight = lax.all_gather(summed, "particle", axis=0, tiled=True)
        shifted = jnp.exp(log_weight - jnp.max(log_weight))
        weight = shifted / jnp.sum(shifted)
        my_weight = lax.dynamic_slice_in_dim(weight, member * part_dev, part_dev)
        partial_sums = jnp.stack(
            [jnp.sum(my_weight[:, None] * bio, axis=0), jnp.sum(my_weight[:, None] * wat, axis=0)]
        )
        collected.append(lax.psum(partial_sums, "particle"))
        chosen = ancestors[cycle]
        mine = lax.dynamic_slice_in_dim(chosen, member * part_dev, part_dev)
        piece = (
            lax.all_gather(bio, "particle", axis=0, tiled=True),
            lax.all_gather(wat, "particle", axis=0, tiled=True),
        )
        count = piece[0].shape[0]
        hit = jnp.arange(count, dtype=jnp.int32)[None, :] == mine[:, None]
        bio, wat = tuple(
            (jnp.sum(jnp.where(hit[:, :, None], rows[None], 0.0), axis=1) for rows in piece)
        )
        for day in range(DAYS):
            wb = wat.astype(jnp.bfloat16).reshape(part_dev, blocks_dev, BLK)
            extended = padded(wb, (("tile", 1),), HALO)
            nearby = extended[:, local_ids]
            flux = jnp.einsum(
                "pnkc,nkdc->pnd", nearby, flow_blocks, preferred_element_type=jnp.float32
            ).reshape(part_dev, cells)
            wet = wat * wat / (1.0 + wat * wat)
            new_bio = bio + growth_rate * bio * (wet - 0.4 * bio)
            new_wat = wat + flux + rain[cycle * DAYS + day] - 0.2 * bio * wet
            bio = new_bio
            wat = new_wat
    return (jnp.stack(collected), bio, wat)


def solution(mesh):
    placed = (
        P("particle", "tile"),
        P("particle", "tile"),
        P("tile", None, None, None),
        P("tile", None),
        P(None, "particle", "tile"),
        P("tile"),
        P(None, "tile"),
        P("tile"),
        P(),
    )
    return jax.shard_map(
        body,
        mesh=mesh,
        in_specs=placed,
        out_specs=(P(None, None, "tile"), P("particle", "tile"), P("particle", "tile")),
        check_vma=False,
    )
```

profile of v0, /device:TPU:0, one launch (start us, length us, event | category | flops | bytes accessed | tf_op | source)
XLA Modules:
  0.0 191.7 jit_solution(2245552599224987325)
XLA Ops:
  7.2 0.8 fusion.25
  8.2 15.8 %all-gather = f32[4,4,4096]{2,1,0:T(4,128)S(1)} all-gather(f32[1,4,4096]{2,1,0:T(4,128)} %bitcast.146), channel_id=1, replica_groups=mesh['particle'=4,'tile'=8] {'particle'}, dimensions={0}, use_global_device_ids=true | all-gather | bytes 327680 | tf_op jit(solution)/shard_map/all_gather | solution.py:62
  24.1 0.8 reshape.145
  24.8 14.9 %all-gather.1 = f32[4,4,4096]{2,1,0:T(4,128)S(1)} all-gather(f32[1,4,4096]{2,1,0:T(4,128)} %bitcast.152), channel_id=1, replica_groups=mesh['particle'=4,'tile'=8] {'particle'}, dimensions={0}, use_global_device_ids=true | all-gather | bytes 327680 | tf_op jit(solution)/shard_map/all_gather | solution.py:63
  39.7 0.8 reshape.147
  40.5 1.5 select_reduce_fusion.3
  42.0 1.3 collective-permute-start
  43.3 1.3 collective-permute-start.1
  44.6 0.7 compare_select_fusion
  45.5 0.9 fusion.24
  47.1 1.2 dynamic-slice.2
  49.1 1.3 gather_fusion
  50.4 2.9 %multiply_reduce_fusion.5 = (f32[4]{0:T(128)S(1)}, f32[4]{0:T(128)S(1)}, f32[4,4096]{1,0:T(4,128)}, f32[4,4096]{1,0:T(4,128)}, f32[32,4,128,1]{2,1,3,0:T(4,128)S(1)}) fusion(f32[4,4096]{1,0:T(4,128)} %param.9, f32[4096]{0:T(1024)S(1)} %bitcast.156, f32[4096]{0:T(1024)} %param.16, f32[4096]{0:T(1024)S(1)} %bitcast.155, f32[4,4096]{1,0:T(4,128)S(1)} %get-tuple-element.11, ...), kind=kOutput, calls=%fused_computation.50 | convolution fusion | flops 13058040 | bytes 3768352 | tf_op jit(solution)/shard_map/pnkc,nkdc->pnd/dot_general | solution.py:74
  53.4 0.9 fusion.14
  54.9 4.7 %collective-permute-start.2 = (bf16[4,4,128]{2,0,1:T(4,128)(2,1)}, bf16[4,4,128]{2,0,1:T(4,128)(2,1)S(1)}, u32[]{:S(2)}, u32[]{:S(2)}) collective-permute-start(bf16[4,4,128]{2,0,1:T(4,128)(2,1)} %get-tuple-element.27), channel_id=1, source_target_pairs={{0,1},{1,2},{2,3},{3,4},{4,5},{5,6},{6,7},{8,9},{9,10},{10,11},{11... | collective-permute-start | bytes 12296 | tf_op jit(solution)/shard_map/ppermute | solution.py:20
  59.7 1.3 collective-permute-start.3
  61.0 15.7 %all-reduce.2 = (f32[4]{0:T(128)S(1)}, f32[4]{0:T(128)S(1)}) all-reduce(f32[4]{0:T(128)S(1)} %get-tuple-element.38, f32[4]{0:T(128)S(1)} %get-tuple-element.39), channel_id=1, replica_groups=mesh['particle'=4,'tile'=8] {'tile'}, use_global_device_ids=true, to_apply=%region_10.11 | all-reduce | flops 8 | bytes 64 | tf_op jit(solution)/shard_map/psum | solution.py:50
  77.1 11.5 %all-reduce.4 = (f32[16]{0:T(128)S(1)}, f32[16]{0:T(128)S(1)}) all-reduce(f32[16]{0:T(128)S(1)} %dynamic-update-slice.1, f32[16]{0:T(128)S(1)} %dynamic-update-slice), channel_id=1, replica_groups=mesh['particle'=4,'tile'=8] {'particle'}, use_global_device_ids=true, to_apply=%add.1 | all-reduce | flops 32 | bytes 256
  88.6 0.7 reduce_max.19
  89.3 1.4 fusion.17
  90.7 1.4 broadcast_divide_fusion
  92.0 0.7 reduce_max.18
  92.7 1.4 fusion.16
  94.1 1.4 broadcast_divide_fusion.1
  95.6 0.7 multiply_reduce_fusion.4
  96.3 14.1 %all-gather.2 = f32[4,4,4096]{2,1,0:T(4,128)S(1)} all-gather(f32[1,4,4096]{2,1,0:T(4,128)} %bitcast.145), channel_id=1, replica_groups=mesh['particle'=4,'tile'=8] {'particle'}, dimensions={0}, use_global_device_ids=true | all-gather | bytes 327680 | tf_op jit(solution)/shard_map/all_gather | solution.py:62
  110.4 0.7 dynamic_slice.14
  111.1 0.8 reshape.149
  111.9 0.8 pad_maximum_fusion.2
  112.7 0.7 gather_fusion.1
  113.4 2.1 %multiply_reduce_fusion.1 = (f32[4096]{0:T(1024)S(1)}, f32[4096]{0:T(1024)S(1)}, f32[4,4096]{1,0:T(4,128)S(1)}) fusion(f32[4,4096]{1,0:T(4,128)} %get-tuple-element.21, f32[4]{0:T(128)} %dynamic_slice.14, f32[4,4096]{1,0:T(4,128)} %get-tuple-element.22, f32[4,4096]{1,0:T(4,128)S(1)} %get-tuple-element.11, f32[4,4096]{1,0:T(4,128)S(1)} %get-tuple-element.12, ...), kind=kOutput, calls=%fused_computation.44 | convolution fusion | flops 12902400 | bytes 3686416 | tf_op jit(solution)/shard_map/pnkc,nkdc->pnd/dot_general | solution.py:74
  115.5 13.8 %all-gather.3 = f32[4,4,4096]{2,1,0:T(4,128)S(1)} all-gather(f32[1,4,4096]{2,1,0:T(4,128)S(1)} %bitcast.151), channel_id=1, replica_groups=mesh['particle'=4,'tile'=8] {'particle'}, dimensions={0}, use_global_device_ids=true | all-gather | bytes 327680 | tf_op jit(solution)/shard_map/all_gather | solution.py:63
  129.3 0.8 reshape.151
  130.1 1.5 select_reduce_fusion.1
  131.6 1.3 collective-permute-start.4
  132.9 1.3 collective-permute-start.5
  134.2 1.4 maximum_bitcast_fusion
  135.6 0.9 collective-permute-done.5
  136.5 0.7 gather_fusion.2
  137.2 2.7 %multiply_add_fusion = (f32[4,4096]{1,0:T(4,128)}, f32[4,4096]{1,0:T(4,128)S(1)}, f32[32,4,128,1]{2,1,3,0:T(4,128)S(1)}) fusion(f32[4096]{0:T(1024)S(1)} %copy-done.2, f32[4,4096]{1,0:T(4,128)S(1)} %get-tuple-element.5, f32[4,4096]{1,0:T(4,128)S(1)} %get-tuple-element.6, f32[4,4,4096]{2,1,0:T(4,128)} %param.13, bf16[4,32,3,128]{3,0,2,1:T(4,128)(2,1)S(1)} %bitcast.150, ...), kind=kOutput, calls=%fused_computation.41 | convolution fusion | flops 12926976 | bytes 3653632 | tf_op jit(solution)/shard_map/pnkc,nkdc->pnd/dot_general | solution.py:74
  139.9 0.9 fusion.15
  140.8 4.3 %collective-permute-start.6 = (bf16[4,4,128]{2,0,1:T(4,128)(2,1)S(1)}, bf16[4,4,128]{2,0,1:T(4,128)(2,1)S(1)}, u32[]{:S(2)}, u32[]{:S(2)}) collective-permute-start(bf16[4,4,128]{2,0,1:T(4,128)(2,1)S(1)} %get-tuple-element.23), channel_id=1, source_target_pairs={{0,1},{1,2},{2,3},{3,4},{4,5},{5,6},{6,7},{8,9},{9,10},{10,11},{11... | collective-permute-start | bytes 12296 | tf_op jit(solution)/shard_map/ppermute | solution.py:20
  145.1 1.3 collective-permute-start.7
  147.1 1.8 collective-permute-done.7
  149.0 0.7 gather_fusion.3
  149.7 2.7 %fusion.2 = f32[4,4096]{1,0:T(4,128)} fusion(f32[4,4096]{1,0:T(4,128)S(1)} %get-tuple-element.20, bf16[4,32,3,128]{3,0,2,1:T(4,128)(2,1)S(1)} %bitcast.147, bf16[32,3,128,128]{3,2,1,0:T(8,128)(2,1)S(1)} %copy-done, f32[4,4,4096]{2,1,0:T(4,128)} %param.13, f32[4,4096]{1,0:T(4,128)S(1)} %get-tuple-element.5, f32[4,4096]{1,0:T(4,128)S(1)} %get-tuple-element.6, ...), kind=kOutput, calls=%fused_computation.7 | convolution fusion | flops 12845056 | bytes 3588096 | tf_op jit(solution)/shard_map/pnkc,nkdc->pnd/dot_general | solution.py:74
  152.4 31.0 %all-reduce.7.cloned.1.call-done = (f32[1,2,4096]{2,1,0:T(2,128)}, f32[1,2,4096]{2,1,0:T(2,128)}) async-done(((f32[1,2,4096]{2,1,0:T(2,128)}, f32[1,2,4096]{2,1,0:T(2,128)}), (f32[1,2,4096]{2,1,0:T(2,128)}, f32[1,2,4096]{2,1,0:T(2,128)})) %all-reduce.7.cloned.1.call-update) | async-done | bytes 65552 | tf_op jit(solution)/shard_map/psum | solution.py:58
  183.4 1.4 pad_maximum_fusion
  (43 shorter events, 3.1 us)
Async XLA Ops:
  7.2 43.3 %copy-start = (bf16[32,3,128,128]{3,2,1,0:T(8,128)(2,1)S(1)}, bf16[32,3,128,128]{3,2,1,0:T(8,128)(2,1)}, u32[]{:S(2)}) copy-start(bf16[32,3,128,128]{3,2,1,0:T(8,128)(2,1)} %param.11) | copy-start | bytes 9437188
  7.2 176.2 %all-reduce.7.cloned.1.call-start = ((), (), s32[]{:S(2)}) async-start(), calls=%async_computation | async-start | bytes 131072 | tf_op jit(solution)/shard_map/psum | solution.py:58
  24.8 70.7 %copy-start.1 = (f32[4,4096]{1,0:T(4,128)S(1)}, f32[4,4096]{1,0:T(4,128)}, u32[]{:S(2)}) copy-start(f32[4,4096]{1,0:T(4,128)} %param.9) | copy-start | bytes 196612
  24.8 70.7 %copy-start.3 = (f32[4,4096]{1,0:T(4,128)S(1)}, f32[4,4096]{1,0:T(4,128)}, u32[]{:S(2)}) copy-start(f32[4,4096]{1,0:T(4,128)} %param.10) | copy-start | bytes 196612
  42.0 7.0 %collective-permute-start = (bf16[4,4,128]{2,0,1:T(4,128)(2,1)S(1)}, bf16[4,4,128]{2,0,1:T(4,128)(2,1)S(1)}, u32[]{:S(2)}, u32[]{:S(2)}) collective-permute-start(bf16[4,4,128]{2,0,1:T(4,128)(2,1)S(1)} %get-tuple-element.29), channel_id=1, source_target_pairs={{0,1},{1,2},{2,3},{3,4},{4,5},{5,6},{6,7},{8,9},{9,10},{10,11},{11... | collective-permute-start | bytes 12296 | tf_op jit(solution)/shard_map/ppermute | solution.py:20
  43.3 5.7 %collective-permute-start.1 = (bf16[4,4,128]{2,0,1:T(4,128)(2,1)S(1)}, bf16[4,4,128]{2,0,1:T(4,128)(2,1)S(1)}, u32[]{:S(2)}, u32[]{:S(2)}) collective-permute-start(bf16[4,4,128]{2,0,1:T(4,128)(2,1)S(1)} %get-tuple-element.30), channel_id=1, source_target_pairs={{1,0},{2,1},{3,2},{4,3},{5,4},{6,5},{7,6},{9,8},{10,9},{11,10},{12... | collective-permute-start | bytes 12296 | tf_op jit(solution)/shard_map/ppermute | solution.py:22
  54.3 42.0 %copy-start.4 = (bf16[4,32,128]{2,0,1:T(4,128)(2,1)}, bf16[4,32,128]{2,0,1:T(4,128)(2,1)S(1)}, u32[]{:S(2)}) copy-start(bf16[4,32,128]{2,0,1:T(4,128)(2,1)S(1)} %fusion.14) | copy-start | bytes 98308
  54.9 57.0 %collective-permute-start.2 = (bf16[4,4,128]{2,0,1:T(4,128)(2,1)}, bf16[4,4,128]{2,0,1:T(4,128)(2,1)S(1)}, u32[]{:S(2)}, u32[]{:S(2)}) collective-permute-start(bf16[4,4,128]{2,0,1:T(4,128)(2,1)} %get-tuple-element.27), channel_id=1, source_target_pairs={{0,1},{1,2},{2,3},{3,4},{4,5},{5,6},{6,7},{8,9},{9,10},{10,11},{11... | collective-permute-start | bytes 12296 | tf_op jit(solution)/shard_map/ppermute | solution.py:20
  59.7 52.2 %collective-permute-start.3 = (bf16[4,4,128]{2,0,1:T(4,128)(2,1)}, bf16[4,4,128]{2,0,1:T(4,128)(2,1)}, u32[]{:S(2)}, u32[]{:S(2)}) collective-permute-start(bf16[4,4,128]{2,0,1:T(4,128)(2,1)} %get-tuple-element.28), channel_id=1, source_target_pairs={{1,0},{2,1},{3,2},{4,3},{5,4},{6,5},{7,6},{9,8},{10,9},{11,10},{12... | collective-permute-start | bytes 12296 | tf_op jit(solution)/shard_map/ppermute | solution.py:22
  111.8 22.4 %copy-start.5 = (f32[4096]{0:T(1024)S(1)}, f32[4096]{0:T(1024)}, u32[]{:S(2)}) copy-start(f32[4096]{0:T(1024)} %get-tuple-element.7) | copy-start | bytes 49156
  111.8 25.4 %copy-start.2 = (f32[4096]{0:T(1024)S(1)}, f32[4096]{0:T(1024)}, u32[]{:S(2)}) copy-start(f32[4096]{0:T(1024)} %param.14) | copy-start | bytes 49156
  131.6 4.0 %collective-permute-start.4 = (bf16[4,4,128]{2,0,1:T(4,128)(2,1)S(1)}, bf16[4,4,128]{2,0,1:T(4,128)(2,1)S(1)}, u32[]{:S(2)}, u32[]{:S(2)}) collective-permute-start(bf16[4,4,128]{2,0,1:T(4,128)(2,1)S(1)} %get-tuple-element.25), channel_id=1, source_target_pairs={{0,1},{1,2},{2,3},{3,4},{4,5},{5,6},{6,7},{8,9},{9,10},{10,11},{11... | collective-permute-start | bytes 12296 | tf_op jit(solution)/shard_map/ppermute | solution.py:20
  132.9 3.6 %collective-permute-start.5 = (bf16[4,4,128]{2,0,1:T(4,128)(2,1)S(1)}, bf16[4,4,128]{2,0,1:T(4,128)(2,1)S(1)}, u32[]{:S(2)}, u32[]{:S(2)}) collective-permute-start(bf16[4,4,128]{2,0,1:T(4,128)(2,1)S(1)} %get-tuple-element.26), channel_id=1, source_target_pairs={{1,0},{2,1},{3,2},{4,3},{5,4},{6,5},{7,6},{9,8},{10,9},{11,10},{12... | collective-permute-start | bytes 12296 | tf_op jit(solution)/shard_map/ppermute | solution.py:22
  140.8 6.3 %collective-permute-start.6 = (bf16[4,4,128]{2,0,1:T(4,128)(2,1)S(1)}, bf16[4,4,128]{2,0,1:T(4,128)(2,1)S(1)}, u32[]{:S(2)}, u32[]{:S(2)}) collective-permute-start(bf16[4,4,128]{2,0,1:T(4,128)(2,1)S(1)} %get-tuple-element.23), channel_id=1, source_target_pairs={{0,1},{1,2},{2,3},{3,4},{4,5},{5,6},{6,7},{8,9},{9,10},{10,11},{11... | collective-permute-start | bytes 12296 | tf_op jit(solution)/shard_map/ppermute | solution.py:20
  145.1 3.8 %collective-permute-start.7 = (bf16[4,4,128]{2,0,1:T(4,128)(2,1)S(1)}, bf16[4,4,128]{2,0,1:T(4,128)(2,1)S(1)}, u32[]{:S(2)}, u32[]{:S(2)}) collective-permute-start(bf16[4,4,128]{2,0,1:T(4,128)(2,1)S(1)} %get-tuple-element.24), channel_id=1, source_target_pairs={{1,0},{2,1},{3,2},{4,3},{5,4},{6,5},{7,6},{9,8},{10,9},{11,10},{12... | collective-permute-start | bytes 12296 | tf_op jit(solution)/shard_map/ppermute | solution.py:22
Sparse Core Ops, SparseCore 0:
  147.2 36.1 all-reduce.6
where the time goes:
time: 193 us; the launch traced here: 192 us
  blocking collectives  85.8 us (44%)
  waiting for transfers between devices  33.8 us (18%)
  other arithmetic  18.2 us (9%)
  starting transfers between devices  16.8 us (9%)
  between operations  15 us (8%)
  local copies, waits for them, and re-layouts  11.7 us (6%)
  matrix products  10.5 us (5%)
    psum x1, waiting for transfers between devices, body(): collected.append(lax.psum(partial_sums, 'particle'))  31 us
    all_gather x2, blocking collectives, body(): lax.all_gather(bio, 'particle', axis=0, tiled=True)  29.9 us
    all_gather x2, blocking collectives, body(): lax.all_gather(wat, 'particle', axis=0, tiled=True)  28.7 us
    psum x1, blocking collectives, body(): summed = lax.psum(misfit_local, 'tile')  15.7 us
    ppermute x4, starting transfers between devices, padded(): lax.ppermute(tail, axis, [(i, (i + 1) % count) for i in range(ends)])  11.6 us
    unnamed x1, blocking collectives  11.5 us
    dot_general x4, matrix products, body(): jnp.einsum('pnkc,nkdc->pnd', nearby, flow_blocks, preferred_element_type=...  10.5 us
    ppermute x4, starting transfers between devices, padded(): lax.ppermute(head, axis, [((i + 1) % count, i) for i in range(ends)])  5.17 us
  transfers between devices with their start and end apart: 9, of which 3 were waited for; matrix products, arithmetic and copies ran while one was open for 10% of the time, Pallas kernels for 0%

commit v1 on v0

v1 whole, which is shorter than its diff:
```python
import functools

import jax
import jax.numpy as jnp
from jax import lax
from jax.experimental import pallas as pl
from jax.experimental.pallas import tpu as pltpu
from jax.sharding import PartitionSpec as P

BLK = 128
CYCLES = 2
HALO = 4
WIDE = 2 * HALO
BOUNDS = (2.0, 5.0, 4.0, 4.0)
SCALE_STEPS = 32000.0
STEPS = 32767.0
VMEM = pl.BlockSpec(memory_space=pltpu.VMEM)
SMEM = pl.BlockSpec(memory_space=pltpu.SMEM)


def run(count, unroll, step, carry):
    if unroll:
        for n in range(count):
            carry = step(n, carry)
        return carry
    return lax.fori_loop(0, count, step, carry)


def lanes(n):
    if isinstance(n, int):
        return slice(n * BLK, (n + 1) * BLK)
    return pl.ds(pl.multiple_of(n * BLK, BLK), BLK)


def wetness(w):
    sq = w * w
    return sq / (1.0 + sq)


def dot_t(x, f):
    return lax.dot_general(x, f, (((1,), (1,)), ((), ())), preferred_element_type=jnp.float32)


def pack_kernel(bio, wat, rain, wire, held):
    part, cells = bio.shape
    nb = cells // BLK
    held[0:part, :] = bio[...]
    held[part : 2 * part, :] = wat[...]
    held[2 * part : 3 * part, :] = rain[0]
    held[3 * part : 4 * part, :] = rain[1]
    rows = 4 * part
    big = jnp.abs(held[:, 0:BLK])
    for n in range(1, nb):
        big = jnp.maximum(big, jnp.abs(held[:, lanes(n)]))
    top = jnp.max(big, axis=1, keepdims=True)
    field = lax.broadcasted_iota(jnp.int32, (rows, 1), 0) // part
    unit = jnp.where(field == 0, BOUNDS[0], jnp.where(field == 1, BOUNDS[1], BOUNDS[2])) / SCALE_STEPS
    code = jnp.floor(top / unit) + 1.0
    inv = STEPS / (code * unit)
    wire[:, lanes(nb)] = jnp.broadcast_to(code, (rows, BLK)).astype(jnp.int32).astype(jnp.int16)
    for n in range(nb):
        wire[:, lanes(n)] = jnp.round(held[:, lanes(n)] * inv).astype(jnp.int32).astype(jnp.int16)


def sides():
    pos = lax.axis_index("tile")
    return lax.rem(pos, 2) == 0


def open_kernel(members, unroll, *refs):
    pieces = refs[:members]
    anc, growth, prec, obs = refs[members : members + 4]
    wb, v0, b1, r1, bq, wq, miss, pay_a, pay_b = refs[members + 4 : members + 13]
    sel = refs[-1]
    nb = growth.shape[0]
    slots = anc.shape[1]
    rows = pieces[0].shape[0]
    part = rows // 4
    depth = members * rows * 2
    me = lax.axis_index("particle")
    line = lax.broadcasted_iota(jnp.int32, (slots, slots), 0)
    lane = lax.broadcasted_iota(jnp.int32, (slots, slots), 1)
    first = jnp.broadcast_to(anc[0:1, :], (slots, slots)).astype(jnp.float32)
    chosen = jnp.sum(jnp.where(line == lane, first, 0.0), axis=1, keepdims=True)
    own = lax.broadcasted_iota(jnp.int32, (slots, 1), 0).astype(jnp.float32)
    col = lax.broadcasted_iota(jnp.int32, (slots, depth), 1)
    piece = col // (2 * rows)
    high = (col // rows) % 2 == 0
    field = (col // part) % 4
    source = ((piece ^ me) * part + col % part).astype(jnp.float32)
    value = jnp.where(high, 256.0, 1.0)
    for g, f in enumerate((0, 1, 2, 3, 0, 1)):
        want = chosen if g < 2 else own
        hit = jnp.logical_and(field == f, source == want)
        sel[g * slots : (g + 1) * slots, :] = jnp.where(hit, value, 0.0).astype(jnp.bfloat16)

    def decode(n):
        parts = []
        for ref in pieces:
            q = ref[:, lanes(n)].astype(jnp.int32)
            parts.append((q >> 8).astype(jnp.float32).astype(jnp.bfloat16))
            parts.append((q & 255).astype(jnp.float32).astype(jnp.bfloat16))
        return jnp.dot(sel[...], jnp.concatenate(parts, axis=0), preferred_element_type=jnp.float32)

    codes = decode(nb)
    scale = [
        codes[g * slots : (g + 1) * slots] * (BOUNDS[f] / SCALE_STEPS / STEPS)
        for g, f in enumerate((0, 1, 2, 3, 0, 1))
    ]

    def step(n, acc):
        got = decode(n)
        b, w, rain0, rain1, bi, wi = (got[g * slots : (g + 1) * slots] * scale[g] for g in range(6))
        s = wetness(w)
        row = pl.ds(n, 1)
        g = growth[row, :]
        wb[n] = w.astype(jnp.bfloat16)
        v0[n] = w + rain0 - 0.2 * b * s
        b1[n] = b + g * b * (s - 0.4 * b)
        r1[n] = rain1
        bq[n] = bi
        wq[n] = wi
        off = bi - obs[0:1, lanes(n)]
        return acc + prec[row, :] * (off * off)

    miss[...] = run(nb, unroll, step, jnp.zeros((slots, BLK), jnp.float32))
    even = sides()
    for pay, right in ((pay_a, even), (pay_b, jnp.logical_not(even))):
        pay[0:WIDE] = wb[pl.ds(jnp.where(right, nb - WIDE, 0), WIDE)]
        edge = v0[pl.ds(jnp.where(right, nb - HALO, 0), HALO)]
        top = edge.astype(jnp.bfloat16)
        pay[WIDE : WIDE + HALO] = top
        pay[WIDE + HALO : WIDE + 2 * HALO] = (edge - top.astype(jnp.float32)).astype(jnp.bfloat16)


def day0_kernel(
    unroll, wb, v0, b1, r1, got_a, got_b, flow, flow_a, flow_b, ids, ids_a, ids_b, growth, prec, obs, miss,
    wb1, v1, b2, total, ext,
):
    nb = growth.shape[0]
    slots = wb.shape[1]
    pos = lax.axis_index("tile")
    count = lax.axis_size("tile")
    even = sides()
    ext[WIDE : WIDE + nb] = wb[...]
    for got, right in ((got_a, even), (got_b, jnp.logical_not(even))):
        ext[pl.ds(jnp.where(right, nb + WIDE, 0), WIDE)] = got[0:WIDE]
    other = jnp.where(even, lax.rem(pos + count - 1, count), lax.rem(pos + 1, count))
    for got, fl, idx, right, sender in (
        (got_a, flow_a, ids_a, even, pos ^ 1),
        (got_b, flow_b, ids_b, jnp.logical_not(even), other),
    ):
        shift = jnp.where(right, nb, -nb) + WIDE - sender * nb
        spot = jnp.where(right, nb + HALO, 0)
        for m in range(HALO):
            flux = sum(dot_t(ext[idx[m, k] + shift], fl[m, k]) for k in range(3))
            edge = got[WIDE + m].astype(jnp.float32) + got[WIDE + HALO + m].astype(jnp.float32)
            wb1[spot + m] = (edge + flux).astype(jnp.bfloat16)
    base = WIDE - pos * nb

    def step(n, acc):
        flux = (
            dot_t(ext[n + WIDE], flow[n, 0])
            + dot_t(ext[ids[n, 1] + base], flow[n, 1])
            + dot_t(ext[ids[n, 2] + base], flow[n, 2])
        )
        w = v0[n] + flux
        wb1[n + HALO] = w.astype(jnp.bfloat16)
        s = wetness(w)
        row = pl.ds(n, 1)
        b = b1[n]
        v1[n] = w + r1[n] - 0.2 * b * s
        b = b + growth[row, :] * b * (s - 0.4 * b)
        b2[n] = b
        off = b - obs[1:2, lanes(n)]
        return acc + prec[row, :] * (off * off)

    total[0:slots, :] = miss[...]
    total[slots : 2 * slots, :] = run(nb, unroll, step, jnp.zeros((slots, BLK), jnp.float32))


def day1_kernel(unroll, wb1, v1, b2, flow, ids, anc, rain, w2, ws, bs, v2, pay_a, pay_b):
    nb = v1.shape[0]
    part = rain.shape[1]
    pos = lax.axis_index("tile")
    me = lax.axis_index("particle")
    even = sides()
    base = HALO - pos * nb
    picks = [anc[1, me * part + i] for i in range(part)]

    def step(n, carry):
        w2[n] = v1[n] + (
            dot_t(wb1[n + HALO], flow[n, 0])
            + dot_t(wb1[ids[n, 1] + base], flow[n, 1])
            + dot_t(wb1[ids[n, 2] + base], flow[n, 2])
        )
        return carry

    run(nb, unroll, step, 0)

    def pick(n, carry):
        for i in range(part):
            ws[n, i : i + 1, :] = w2[n, pl.ds(picks[i], 1), :]
            bs[n, i : i + 1, :] = b2[n, pl.ds(picks[i], 1), :]
        w = ws[n]
        v2[n] = w + rain[0, :, lanes(n)] - 0.2 * bs[n] * wetness(w)
        return carry

    run(nb, unroll, pick, 0)
    for pay, right in ((pay_a, even), (pay_b, jnp.logical_not(even))):
        pay[0:WIDE] = ws[pl.ds(jnp.where(right, nb - WIDE, 0), WIDE)]
        pay[WIDE : WIDE + HALO] = v2[pl.ds(jnp.where(right, nb - HALO, 0), HALO)]


def close_kernel(
    unroll, ws, bs, v2, got_a, got_b, flow, flow_a, flow_b, ids, ids_a, ids_b, growth, rain,
    bio_out, wat_out, ext, ext3, w3,
):
    nb = growth.shape[0]
    pos = lax.axis_index("tile")
    count = lax.axis_size("tile")
    even = sides()
    half = jnp.bfloat16
    ext[WIDE : WIDE + nb] = ws[...]
    for got, right in ((got_a, even), (got_b, jnp.logical_not(even))):
        ext[pl.ds(jnp.where(right, nb + WIDE, 0), WIDE)] = got[0:WIDE]
    other = jnp.where(even, lax.rem(pos + count - 1, count), lax.rem(pos + 1, count))
    for got, fl, idx, right, sender in (
        (got_a, flow_a, ids_a, even, pos ^ 1),
        (got_b, flow_b, ids_b, jnp.logical_not(even), other),
    ):
        shift = jnp.where(right, nb, -nb) + WIDE - sender * nb
        spot = jnp.where(right, nb + HALO, 0)
        for m in range(HALO):
            flux = sum(dot_t(ext[idx[m, k] + shift].astype(half), fl[m, k]) for k in range(3))
            ext3[spot + m] = got[WIDE + m] + flux
    base = WIDE - pos * nb

    def step2(n, carry):
        ext3[n + HALO] = v2[n] + (
            dot_t(ext[n + WIDE].astype(half), flow[n, 0])
            + dot_t(ext[ids[n, 1] + base].astype(half), flow[n, 1])
            + dot_t(ext[ids[n, 2] + base].astype(half), flow[n, 2])
        )
        return carry

    run(nb, unroll, step2, 0)
    base3 = HALO - pos * nb

    def step3(n, carry):
        g = growth[pl.ds(n, 1), :]
        s = wetness(ws[n])
        b = bs[n]
        b = b + g * b * (s - 0.4 * b)
        w = ext3[n + HALO]
        s = wetness(w)
        flux = (
            dot_t(w.astype(half), flow[n, 0])
            + dot_t(ext3[ids[n, 1] + base3].astype(half), flow[n, 1])
            + dot_t(ext3[ids[n, 2] + base3].astype(half), flow[n, 2])
        )
        wat_out[:, lanes(n)] = w + flux + rain[1, :, lanes(n)] - 0.2 * b * s
        bio_out[:, lanes(n)] = b + g * b * (s - 0.4 * b)
        return carry

    run(nb, unroll, step3, 0)


def means_kernel(unroll, mine, theirs, bq, wq, b2, w2, means):
    nb, slots = bq.shape[:2]
    lw = -0.5 * jnp.sum(mine[...] + theirs[...], axis=1, keepdims=True)
    weights = []
    for c in range(CYCLES):
        x = lw[c * slots : (c + 1) * slots]
        e = jnp.exp(x - jnp.max(x, axis=0, keepdims=True))
        weights.append(jnp.broadcast_to(e / jnp.sum(e, axis=0, keepdims=True), (slots, BLK)))

    def step(n, carry):
        for c, pair in enumerate(((bq, wq), (b2, w2))):
            for f, ref in enumerate(pair):
                means[c, f : f + 1, lanes(n)] = jnp.sum(weights[c] * ref[n], axis=0, keepdims=True)
        return carry

    run(nb, unroll, step, 0)


def call(kernel, out, specs, scratch=(), mib=32):
    return pl.pallas_call(
        kernel,
        out_shape=tuple(jax.ShapeDtypeStruct(s, d) for s, d in out),
        in_specs=specs,
        out_specs=tuple(VMEM for _ in out),
        scratch_shapes=list(scratch),
        compiler_params=pltpu.CompilerParams(vmem_limit_bytes=mib * 2**20),
    )


def body(biomass, water, flow_blocks, neighbours, rain, growth_rate, observations, obs_precision, ancestors):
    part, cells = biomass.shape
    nb = cells // BLK
    members, tiles = lax.axis_size("particle"), lax.axis_size("tile")
    slots = members * part
    unroll = slots <= 16
    f32, bf16 = jnp.float32, jnp.bfloat16
    pos = lax.axis_index("tile")
    even = lax.rem(pos, 2) == 0
    swap_a = [(i, i ^ 1) for i in range(tiles)]
    swap_b = [(i, (i - 1) % tiles if i % 2 == 0 else (i + 1) % tiles) for i in range(tiles)]
    growth = growth_rate.reshape(nb, BLK)
    prec = obs_precision.reshape(nb, BLK)

    wire = pl.pallas_call(
        pack_kernel,
        grid=(1,),
        out_shape=jax.ShapeDtypeStruct((4 * part, cells + BLK), jnp.int16),
        in_specs=[
            pl.BlockSpec((part, cells), lambda i: (0, 0)),
            pl.BlockSpec((part, cells), lambda i: (0, 0)),
            pl.BlockSpec((2, part, cells), lambda i: (0, 0, 0)),
        ],
        out_specs=pl.BlockSpec((4 * part, cells + BLK), lambda i: (0, 0)),
        scratch_shapes=[pltpu.VMEM((4 * part, cells), f32)],
    )(biomass, water, rain)
    pieces = [wire] + [
        lax.ppermute(wire, "particle", [(i, i ^ j) for i in range(members)]) for j in range(1, members)
    ]
    start_a = jnp.where(even, nb - HALO, 0)
    start_b = jnp.where(even, 0, nb - HALO)
    flow_a = lax.ppermute(lax.dynamic_slice_in_dim(flow_blocks, start_a, HALO), "tile", swap_a)
    flow_b = lax.ppermute(lax.dynamic_slice_in_dim(flow_blocks, start_b, HALO), "tile", swap_b)
    ids_a = lax.ppermute(lax.dynamic_slice_in_dim(neighbours, start_a, HALO), "tile", swap_a)
    ids_b = lax.ppermute(lax.dynamic_slice_in_dim(neighbours, start_b, HALO), "tile", swap_b)

    field = ((nb, slots, BLK), f32)
    wb, v0, b1, r1, bq, wq, miss, pay_a, pay_b = call(
        functools.partial(open_kernel, members, unroll),
        [((nb, slots, BLK), bf16), field, field, field, field, field, ((slots, BLK), f32)]
        + [((WIDE + 2 * HALO, slots, BLK), bf16)] * 2,
        [VMEM] * (members + 4),
        [pltpu.VMEM((6 * slots, members * part * 8), bf16)],
    )(*pieces, ancestors, growth, prec, observations)
    got_a = lax.ppermute(pay_a, "tile", swap_a)
    got_b = lax.ppermute(pay_b, "tile", swap_b)
    wb1, v1, b2, total = call(
        functools.partial(day0_kernel, unroll),
        [((nb + WIDE, slots, BLK), bf16), field, field, ((2 * slots, BLK), f32)],
        [VMEM] * 9 + [SMEM] * 3 + [VMEM] * 4,
        [pltpu.VMEM((nb + 2 * WIDE, slots, BLK), bf16)],
    )(wb, v0, b1, r1, got_a, got_b, flow_blocks, flow_a, flow_b, neighbours, ids_a, ids_b, growth, prec, observations, miss)
    few = ((nb, part, BLK), f32)
    w2, ws, bs, v2, end_a, end_b = call(
        functools.partial(day1_kernel, unroll),
        [field, few, few, few] + [((WIDE + HALO, part, BLK), f32)] * 2,
        [VMEM] * 4 + [SMEM] * 2 + [VMEM],
    )(wb1, v1, b2, flow_blocks, neighbours, ancestors, rain[2:])
    last_a = lax.ppermute(end_a, "tile", swap_a)
    last_b = lax.ppermute(end_b, "tile", swap_b)
    span = 1
    theirs = lax.ppermute(total, "tile", swap_a)
    while span * 2 < tiles:
        span *= 2
        total = total + theirs
        theirs = lax.ppermute(total, "tile", [(i, i ^ span) for i in range(tiles)])
    bio_out, wat_out = call(
        functools.partial(close_kernel, unroll),
        [((part, cells), f32)] * 2,
        [VMEM] * 8 + [SMEM] * 3 + [VMEM] * 2,
        [
            pltpu.VMEM((nb + 2 * WIDE, part, BLK), f32),
            pltpu.VMEM((nb + WIDE, part, BLK), f32),
            pltpu.VMEM((8, BLK), f32),
        ],
    )(ws, bs, v2, last_a, last_b, flow_blocks, flow_a, flow_b, neighbours, ids_a, ids_b, growth, rain[2:])
    (means,) = call(
        functools.partial(means_kernel, unroll), [((CYCLES, 2, cells), f32)], [VMEM] * 6
    )(total, theirs, bq, wq, b2, w2)
    return means, bio_out, wat_out


def solution(mesh):
    placed = (
        P("particle", "tile"),
        P("particle", "tile"),
        P("tile", None, None, None),
        P("tile", None),
        P(None, "particle", "tile"),
        P("tile"),
        P(None, "tile"),
        P("tile"),
        P(),
    )
    return jax.shard_map(
        body,
        mesh=mesh,
        in_specs=placed,
        out_specs=(P(None, None, "tile"), P("particle", "tile"), P("particle", "tile")),
        check_vma=False,
    )
```

time: 193 us -> 56.5 us (0.29)
  blocking collectives: 85.8 us -> 0 us
  other arithmetic: 18.2 us -> 0.01 us
  waiting for transfers between devices: 33.8 us -> 15.9 us
  Pallas kernels: 0 us -> 14.4 us
  between operations: 15 us -> 0.73 us
  matrix products: 10.5 us -> 0 us
    all_gather x4 -> x0, blocking collectives: 58.6 us -> none  [the longest x2 29.9 us: body(): lax.all_gather(bio, 'particle', axis=0, tiled=True)]
    psum x1 -> x0, waiting for transfers between devices: 31 us -> none  [body(): collected.append(lax.psum(partial_sums, 'particle'))]
    psum x1 -> x0, blocking collectives: 15.7 us -> none  [body(): summed = lax.psum(misfit_local, 'tile')]
    pallas_call x0 -> x6, Pallas kernels: none -> 14.4 us  [the longest x1 5.41 us: body(): call(functools.partial(close_kernel, unroll), [((part, cells), f32)] * 2,...]
    ppermute x8 -> x14, waiting for transfers between devices: 2.74 us -> 15.9 us  [the longest x3 9.19 us: body(): lax.ppermute(wire, 'particle', [(i, i ^ j) for i in range(members)])]
    unnamed x1 -> x0, blocking collectives: 11.5 us -> none
    dot_general x4 -> x0, matrix products: 10.5 us -> none  [body(): jnp.einsum('pnkc,nkdc->pnd', nearby, flow_blocks, preferred_element_type=...]
    reduce_sum x5 -> x0, other arithmetic: 6.44 us -> none  [the longest x2 2.96 us: body(): jnp.sum(jnp.where(hit[:, :, None], rows[None], 0.0), axis=1)]
  transfers between devices with their start and end apart: 9 -> 14, of which waited for: 3 -> 6; matrix products, arithmetic and copies ran while one was open for 10% -> 1% of each run, Pallas kernels for 0% -> 19%
where the time goes in v1:
time: 56.5 us; the launch traced here: 55.9 us
  waiting for transfers between devices  15.9 us (28%)
  starting transfers between devices  15 us (27%)
  Pallas kernels  14.4 us (25%)
  local copies, waits for them, and re-layouts  9.81 us (17%)
  between operations  0.73 us (1%)
    ppermute x3, waiting for transfers between devices, body(): lax.ppermute(wire, 'particle', [(i, i ^ j) for i in range(members)])  9.19 us
    unnamed x23, local copies, waits for them, and re-layouts  8.62 us
    pallas_call x1, Pallas kernels, body(): call(functools.partial(close_kernel, unroll), [((part, cells), f32)] * 2,...  5.41 us
    ppermute x3, starting transfers between devices, body(): lax.ppermute(wire, 'particle', [(i, i ^ j) for i in range(members)])  4.39 us
    ppermute x1, starting transfers between devices, body(): lax.ppermute(lax.dynamic_slice_in_dim(flow_blocks, start_b, HALO), 'tile'...  3.56 us
    pallas_call x1, Pallas kernels, body(): call(functools.partial(day0_kernel, unroll), [((nb + WIDE, slots, BLK), b...  3.03 us
    ppermute x2, starting transfers between devices, body(): theirs = lax.ppermute(total, 'tile', [(i, i ^ span) for i in range(tiles)])  2.71 us
    pallas_call x1, Pallas kernels, body(): call(functools.partial(day1_kernel, unroll), [field, few, few, few] + [((...  2.66 us
  transfers between devices with their start and end apart: 14, of which 6 were waited for; matrix products, arithmetic and copies ran while one was open for 1% of the time, Pallas kernels for 19%

profile of v1, /device:TPU:0, one launch (start us, length us, event | category | flops | bytes accessed | tf_op | source)
XLA Modules:
  0.0 55.9 jit_solution(11661309379554843384)
XLA Ops:
  0.6 1.2 %constant_dynamic-slice_fusion.2 = (bf16[4,3,128,128]{3,2,1,0:T(8,128)(2,1)S(1)}, bf16[4,3,128,128]{3,2,1,0:T(8,128)(2,1)S(1)}) fusion(bf16[32,3,128,128]{3,2,1,0:T(8,128)(2,1)} %flow.5, s32[]{:T(128)S(6)} %select_n.12, s32[]{:T(128)S(6)} %select_n.11), kind=kLoop, calls=%fused_computation.2 | loop fusion | bytes 1572872 | tf_op jit(solution)/shard_map/dynamic_slice | solution.py:330
  1.8 0.5 collective-permute-start.5
  2.3 3.6 %collective-permute-start.6 = (bf16[4,3,128,128]{3,2,1,0:T(8,128)(2,1)S(1)}, bf16[4,3,128,128]{3,2,1,0:T(8,128)(2,1)S(1)}, u32[]{:S(2)}, u32[]{:S(2)}) collective-permute-start(bf16[4,3,128,128]{3,2,1,0:T(8,128)(2,1)S(1)} %get-tuple-element.45), channel_id=1, source_target_pairs={{0,7},{1,2},{2,1},{3,4},{4,3},{5,6},{6,5},{7,0},{8,15},{9,10},{10,... | collective-permute-start | bytes 1179656 | tf_op jit(solution)/shard_map/ppermute | solution.py:330
  5.9 1.8 %shard_map.112.refs_0_ = s16[16,4224]{1,0:T(8,128)(2,1)} custom-call(f32[4,4096]{1,0:T(4,128)} %bio.1, f32[4,4096]{1,0:T(4,128)} %wat.1, f32[4,4,4096]{2,1,0:T(4,128)} %rain.1), custom_call_target="tpu_custom_call" | custom-call | tf_op jit(solution)/shard_map/pallas_call | solution.py:312
  7.7 1.6 %collective-permute-start = (s16[16,4224]{1,0:T(8,128)(2,1)}, s16[16,4224]{1,0:T(8,128)(2,1)S(1)}, u32[]{:S(2)}, u32[]{:S(2)}) collective-permute-start(s16[16,4224]{1,0:T(8,128)(2,1)} %shard_map.112.refs_0_), channel_id=1, source_target_pairs={{0,8},{8,0},{16,24},{24,16},{1,9},{9,1},{17,25},{25,17},{2,10},{10... | collective-permute-start | bytes 405512 | tf_op jit(solution)/shard_map/ppermute | solution.py:325
  9.3 2.6 %collective-permute-start.1 = (s16[16,4224]{1,0:T(8,128)(2,1)}, s16[16,4224]{1,0:T(8,128)(2,1)S(1)}, u32[]{:S(2)}, u32[]{:S(2)}) collective-permute-start(s16[16,4224]{1,0:T(8,128)(2,1)} %shard_map.112.refs_0_), channel_id=1, source_target_pairs={{0,16},{8,24},{16,0},{24,8},{1,17},{9,25},{17,1},{25,9},{2,18},{10... | collective-permute-start | bytes 405512 | tf_op jit(solution)/shard_map/ppermute | solution.py:325
  11.9 0.2 collective-permute-start.2
  12.1 0.8 %copy.14.ids = s32[32,3]{1,0:T(8,128)S(1)} copy(s32[32,3]{0,1:T(4,128)} %param.12) | data formatting | bytes 768 | tf_op args[3]
  12.8 1.6 %collective-permute-done.refs_1_ = s16[16,4224]{1,0:T(8,128)(2,1)S(1)} collective-permute-done((s16[16,4224]{1,0:T(8,128)(2,1)}, s16[16,4224]{1,0:T(8,128)(2,1)S(1)}, u32[]{:S(2)}, u32[]{:S(2)}) %collective-permute-start) | collective-permute-done | bytes 135200 | tf_op jit(solution)/shard_map/ppermute | solution.py:325
  14.5 7.6 %collective-permute-done.1.refs_2_ = s16[16,4224]{1,0:T(8,128)(2,1)S(1)} collective-permute-done((s16[16,4224]{1,0:T(8,128)(2,1)}, s16[16,4224]{1,0:T(8,128)(2,1)S(1)}, u32[]{:S(2)}, u32[]{:S(2)}) %collective-permute-start.1) | collective-permute-done | bytes 135200 | tf_op jit(solution)/shard_map/ppermute | solution.py:325
  22.0 0.0 collective-permute-done.2.refs_3_
  22.0 0.9 %copy-done.2 = s16[16,4224]{1,0:T(8,128)(2,1)S(1)} copy-done((s16[16,4224]{1,0:T(8,128)(2,1)S(1)}, s16[16,4224]{1,0:T(8,128)(2,1)}, u32[]{:S(2)}) %copy-start.2) | copy-done | bytes 135192
  22.9 0.7 %copy-done.3 = f32[4096]{0:T(1024)S(1)} copy-done((f32[4096]{0:T(1024)S(1)}, f32[4096]{0:T(1024)}, u32[]{:S(2)}) %copy-start.3) | copy-done | bytes 16408
  23.7 0.8 %copy-done.5 = f32[2,4096]{1,0:T(2,128)S(1)} copy-done((f32[2,4096]{1,0:T(2,128)S(1)}, f32[2,4096]{1,0:T(2,128)}, u32[]{:S(2)}) %copy-start.5) | copy-done | bytes 32792
  24.4 0.7 %copy-done.7 = f32[4096]{0:T(1024)S(1)} copy-done((f32[4096]{0:T(1024)S(1)}, f32[4096]{0:T(1024)}, u32[]{:S(2)}) %copy-start.7) | copy-done | bytes 16408
  25.1 0.7 %copy-done.9 = s32[2,16]{1,0:T(2,128)S(1)} copy-done((s32[2,16]{1,0:T(2,128)S(1)}, s32[2,16]{1,0:T(2,128)}, u32[]{:S(2)}) %copy-start.9) | copy-done | bytes 152
  25.8 0.6 %shard_map.113 = (bf16[32,16,128]{2,1,0:T(8,128)(2,1)S(1)}, f32[32,16,128]{2,1,0:T(8,128)S(1)}, f32[32,16,128]{2,1,0:T(8,128)S(1)}, f32[32,16,128]{2,1,0:T(8,128...) custom-call(s16[16,4224]{1,0:T(8,128)(2,1)S(1)} %copy-done.2, ...), custom_call_target="tpu_custom_call" | custom-call | tf_op jit(solution)/shard_map/pallas_call | solution.py:335
  26.4 0.1 collective-permute-start.3
  26.5 1.3 %collective-permute-start.4 = (bf16[16,16,128]{2,1,0:T(8,128)(2,1)S(1)}, bf16[16,16,128]{2,1,0:T(8,128)(2,1)S(1)}, u32[]{:S(2)}, u32[]{:S(2)}) collective-permute-start(bf16[16,16,128]{2,1,0:T(8,128)(2,1)S(1)} %get-tuple-element.29), channel_id=1, source_target_pairs={{0,7},{1,2},{2,1},{3,4},{4,3},{5,6},{6,5},{7,0},{8,15},{9,10},{10,... | collective-permute-start | bytes 196616 | tf_op jit(solution)/shard_map/ppermute | solution.py:343
  27.8 0.0 collective-permute-start.7
  27.8 1.1 %collective-permute-done.7.ids_a = s32[4,3]{1,0:T(4,128)S(1)} collective-permute-done((s32[4,3]{1,0:T(4,128)S(1)}, s32[4,3]{1,0:T(4,128)S(1)}, u32[]{:S(2)}, u32[]{:S(2)}) %collective-permute-start.7) | collective-permute-done | bytes 80 | tf_op jit(solution)/shard_map/ppermute | solution.py:331
  28.9 1.4 %collective-permute-start.8 = (s32[4,3]{1,0:T(4,128)S(1)}, s32[4,3]{1,0:T(4,128)S(1)}, u32[]{:S(2)}, u32[]{:S(2)}) collective-permute-start(s32[4,3]{1,0:T(4,128)S(1)} %get-tuple-element.47), channel_id=1, source_target_pairs={{0,7},{1,2},{2,1},{3,4},{4,3},{5,6},{6,5},{7,0},{8,15},{9,10},{10,... | collective-permute-start | bytes 152 | tf_op jit(solution)/shard_map/ppermute | solution.py:332
  30.4 2.5 %collective-permute-done.8.ids_b = s32[4,3]{1,0:T(4,128)S(1)} collective-permute-done((s32[4,3]{1,0:T(4,128)S(1)}, s32[4,3]{1,0:T(4,128)S(1)}, u32[]{:S(2)}, u32[]{:S(2)}) %collective-permute-start.8) | collective-permute-done | bytes 80 | tf_op jit(solution)/shard_map/ppermute | solution.py:332
  32.8 0.0 collective-permute-done.3.got_a
  32.9 0.0 collective-permute-done.4.got_b
  32.9 0.0 collective-permute-done.5.flow_a
  32.9 0.0 collective-permute-done.6.flow_b
  32.9 0.0 copy-start
  32.9 1.9 %copy-done = bf16[32,3,128,128]{3,2,1,0:T(8,128)(2,1)S(1)} copy-done((bf16[32,3,128,128]{3,2,1,0:T(8,128)(2,1)S(1)}, bf16[32,3,128,128]{3,2,1,0:T(8,128)(2,1)}, u32[]{:S(2)}) %copy-start) | copy-done | bytes 3145752
  34.8 0.7 %copy-done.4 = f32[4096]{0:T(1024)S(1)} copy-done((f32[4096]{0:T(1024)S(1)}, f32[4096]{0:T(1024)}, u32[]{:S(2)}) %copy-start.4) | copy-done | bytes 16408
  35.5 0.8 %copy-done.6 = f32[2,4096]{1,0:T(2,128)S(1)} copy-done((f32[2,4096]{1,0:T(2,128)S(1)}, f32[2,4096]{1,0:T(2,128)}, u32[]{:S(2)}) %copy-start.6) | copy-done | bytes 32792
  36.2 0.7 %copy-done.8 = f32[4096]{0:T(1024)S(1)} copy-done((f32[4096]{0:T(1024)S(1)}, f32[4096]{0:T(1024)}, u32[]{:S(2)}) %copy-start.8) | copy-done | bytes 16408
  37.0 3.0 %shard_map.114 = (bf16[40,16,128]{2,1,0:T(8,128)(2,1)S(1)}, f32[32,16,128]{2,1,0:T(8,128)S(1)}, f32[32,16,128]{2,1,0:T(8,128)S(1)}, f32[32,128]{1,0:T(8,128)S(1)}) custom-call(bf16[32,16,128]{2,1,0:T(8,128)(2,1)S(1)} %get-tuple-element.24.wb, f32[32,16,128]{2,1,0:T(8,128)S(1)} %get-tuple-element.25.v0, f32[32,16,128]{2,1,0:T(8,128)S(1)} %get-tuple-element.26.b1, ...), custom_call_target="tpu_custom_call" | custom-call | tf_op jit(solution)/shard_map/pallas_call | solution.py:344
  40.0 0.1 collective-permute-start.9
  40.1 1.2 %collective-permute-done.9 = f32[32,128]{1,0:T(8,128)S(1)} collective-permute-done((f32[32,128]{1,0:T(8,128)S(1)}, f32[32,128]{1,0:T(8,128)S(1)}, u32[]{:S(2)}, u32[]{:S(2)}) %collective-permute-start.9) | collective-permute-done | bytes 16416 | tf_op jit(solution)/shard_map/ppermute | solution.py:359
  41.3 1.2 %collective-permute-start.10 = (f32[32,128]{1,0:T(8,128)S(1)}, f32[32,128]{1,0:T(8,128)S(1)}, u32[]{:S(2)}, u32[]{:S(2)}) collective-permute-start(f32[32,128]{1,0:T(8,128)S(1)} %add.4), channel_id=1, source_target_pairs={{0,2},{1,3},{2,0},{3,1},{4,6},{5,7},{6,4},{7,5},{8,10},{9,11},{10,... | collective-permute-start | bytes 49160 | tf_op jit(solution)/shard_map/ppermute | solution.py:363
  42.4 0.0 copy-done.10
  42.4 0.0 copy-done.1
  42.4 2.7 %shard_map.115 = (f32[32,16,128]{2,1,0:T(8,128)S(1)}, f32[32,4,128]{2,1,0:T(4,128)S(1)}, f32[32,4,128]{2,1,0:T(4,128)S(1)}, f32[32,4,128]{2,1,0:T(4,128)S(1)}, f...) custom-call(bf16[40,16,128]{2,1,0:T(8,128)(2,1)S(1)} %get-tuple-element.35.wb1, ...), custom_call_target="tpu_custom_call" | custom-call | tf_op jit(solution)/shard_map/pallas_call | solution.py:351
  45.1 0.1 collective-permute-start.12
  45.2 0.9 %collective-permute-start.13 = (f32[12,4,128]{2,1,0:T(4,128)S(1)}, f32[12,4,128]{2,1,0:T(4,128)S(1)}, u32[]{:S(2)}, u32[]{:S(2)}) collective-permute-start(f32[12,4,128]{2,1,0:T(4,128)S(1)} %get-tuple-element.42), channel_id=1, source_target_pairs={{0,7},{1,2},{2,1},{3,4},{4,3},{5,6},{6,5},{7,0},{8,15},{9,10},{10,... | collective-permute-start | bytes 73736 | tf_op jit(solution)/shard_map/ppermute | solution.py:357
  46.1 0.0 collective-permute-done.10
  46.1 1.6 %collective-permute-start.11 = (f32[32,128]{1,0:T(8,128)S(1)}, f32[32,128]{1,0:T(8,128)S(1)}, u32[]{:S(2)}, u32[]{:S(2)}) collective-permute-start(f32[32,128]{1,0:T(8,128)S(1)} %add.5.mine), channel_id=1, source_target_pairs={{0,4},{1,5},{2,6},{3,7},{4,0},{5,1},{6,2},{7,3},{8,12},{9,13},{10,... | collective-permute-start | bytes 49160 | tf_op jit(solution)/shard_map/ppermute | solution.py:363
  47.7 0.0 collective-permute-done.12.got_a
  47.7 1.9 %collective-permute-done.13.got_b = f32[12,4,128]{2,1,0:T(4,128)S(1)} collective-permute-done((f32[12,4,128]{2,1,0:T(4,128)S(1)}, f32[12,4,128]{2,1,0:T(4,128)S(1)}, u32[]{:S(2)}, u32[]{:S(2)}) %collective-permute-start.13) | collective-permute-done | bytes 24608 | tf_op jit(solution)/shard_map/ppermute | solution.py:357
  49.6 5.4 %shard_map.117 = (f32[4,4096]{1,0:T(4,128)}, f32[4,4096]{1,0:T(4,128)}) custom-call(f32[32,4,128]{2,1,0:T(4,128)S(1)} %get-tuple-element.38.ws, f32[32,4,128]{2,1,0:T(4,128)S(1)} %get-tuple-element.39.bs, f32[32,4,128]{2,1,0:T(4,128)S(1)} %get-tuple-element.40.v2, f32[12,4,128]{2,1,0:T(4,128)S(1)} %collective-permute-done.12.got_a, ...), custom_call_target="tpu_custom_call" | custom-call | tf_op jit(solution)/shard_map/pallas_call | solution.py:364
  55.0 0.0 collective-permute-done.11.theirs
  55.0 0.9 %shard_map.116 = f32[2,2,4096]{2,1,0:T(2,128)} custom-call(f32[32,128]{1,0:T(8,128)S(1)} %add.5.mine, f32[32,128]{1,0:T(8,128)S(1)} %collective-permute-done.11.theirs, f32[32,16,128]{2,1,0:T(8,128)S(1)} %get-tuple-element.32.bq, f32[32,16,128]{2,1,0:T(8,128)S(1)} %get-tuple-element.33.wq, f32[32,16,128]{2,1,0:T(8,128)S(1)} %get-tuple-element.34.b2, ...), custom_call_target="tpu_custom_call" | custom-call | tf_op jit(solution)/shard_map/pallas_call | solution.py:374
  (14 shorter events, 0.0 us)
Async XLA Ops:
  1.8 31.0 %collective-permute-start.5 = (bf16[4,3,128,128]{3,2,1,0:T(8,128)(2,1)S(1)}, bf16[4,3,128,128]{3,2,1,0:T(8,128)(2,1)S(1)}, u32[]{:S(2)}, u32[]{:S(2)}) collective-permute-start(bf16[4,3,128,128]{3,2,1,0:T(8,128)(2,1)S(1)} %get-tuple-element.46), channel_id=1, source_target_pairs={{0,1},{1,0},{2,3},{3,2},{4,5},{5,4},{6,7},{7,6},{8,9},{9,8},{10,11... | collective-permute-start | bytes 1179656 | tf_op jit(solution)/shard_map/ppermute | solution.py:329
  2.3 40.1 %copy-start.10 = (f32[4,4,4096]{2,1,0:T(4,128)S(1)}, f32[4,4,4096]{2,1,0:T(4,128)}, u32[]{:S(2)}) copy-start(f32[4,4,4096]{2,1,0:T(4,128)} %rain.1) | copy-start | bytes 786436
  2.3 30.5 %collective-permute-start.6 = (bf16[4,3,128,128]{3,2,1,0:T(8,128)(2,1)S(1)}, bf16[4,3,128,128]{3,2,1,0:T(8,128)(2,1)S(1)}, u32[]{:S(2)}, u32[]{:S(2)}) collective-permute-start(bf16[4,3,128,128]{3,2,1,0:T(8,128)(2,1)S(1)} %get-tuple-element.45), channel_id=1, source_target_pairs={{0,7},{1,2},{2,1},{3,4},{4,3},{5,6},{6,5},{7,0},{8,15},{9,10},{10,... | collective-permute-start | bytes 1179656 | tf_op jit(solution)/shard_map/ppermute | solution.py:330
  7.7 6.8 %collective-permute-start = (s16[16,4224]{1,0:T(8,128)(2,1)}, s16[16,4224]{1,0:T(8,128)(2,1)S(1)}, u32[]{:S(2)}, u32[]{:S(2)}) collective-permute-start(s16[16,4224]{1,0:T(8,128)(2,1)} %shard_map.112.refs_0_), channel_id=1, source_target_pairs={{0,8},{8,0},{16,24},{24,16},{1,9},{9,1},{17,25},{25,17},{2,10},{10... | collective-permute-start | bytes 405512 | tf_op jit(solution)/shard_map/ppermute | solution.py:325
  9.3 12.8 %collective-permute-start.1 = (s16[16,4224]{1,0:T(8,128)(2,1)}, s16[16,4224]{1,0:T(8,128)(2,1)S(1)}, u32[]{:S(2)}, u32[]{:S(2)}) collective-permute-start(s16[16,4224]{1,0:T(8,128)(2,1)} %shard_map.112.refs_0_), channel_id=1, source_target_pairs={{0,16},{8,24},{16,0},{24,8},{1,17},{9,25},{17,1},{25,9},{2,18},{10... | collective-permute-start | bytes 405512 | tf_op jit(solution)/shard_map/ppermute | solution.py:325
  11.9 10.2 %collective-permute-start.2 = (s16[16,4224]{1,0:T(8,128)(2,1)}, s16[16,4224]{1,0:T(8,128)(2,1)S(1)}, u32[]{:S(2)}, u32[]{:S(2)}) collective-permute-start(s16[16,4224]{1,0:T(8,128)(2,1)} %shard_map.112.refs_0_), channel_id=1, source_target_pairs={{0,24},{8,16},{16,8},{24,0},{1,25},{9,17},{17,9},{25,1},{2,26},{10... | collective-permute-start | bytes 405512 | tf_op jit(solution)/shard_map/ppermute | solution.py:325
  22.0 0.9 %copy-start.2 = (s16[16,4224]{1,0:T(8,128)(2,1)S(1)}, s16[16,4224]{1,0:T(8,128)(2,1)}, u32[]{:S(2)}) copy-start(s16[16,4224]{1,0:T(8,128)(2,1)} %shard_map.112.refs_0_) | copy-start | bytes 405508
  22.9 0.7 %copy-start.3 = (f32[4096]{0:T(1024)S(1)}, f32[4096]{0:T(1024)}, u32[]{:S(2)}) copy-start(f32[4096]{0:T(1024)} %param.14) | copy-start | bytes 49156
  23.7 0.8 %copy-start.5 = (f32[2,4096]{1,0:T(2,128)S(1)}, f32[2,4096]{1,0:T(2,128)}, u32[]{:S(2)}) copy-start(f32[2,4096]{1,0:T(2,128)} %obs.1) | copy-start | bytes 98308
  24.4 0.7 %copy-start.7 = (f32[4096]{0:T(1024)S(1)}, f32[4096]{0:T(1024)}, u32[]{:S(2)}) copy-start(f32[4096]{0:T(1024)} %param.16) | copy-start | bytes 49156
  25.1 0.7 %copy-start.9 = (s32[2,16]{1,0:T(2,128)S(1)}, s32[2,16]{1,0:T(2,128)}, u32[]{:S(2)}) copy-start(s32[2,16]{1,0:T(2,128)} %anc.1) | copy-start | bytes 388
  26.4 6.4 %collective-permute-start.3 = (bf16[16,16,128]{2,1,0:T(8,128)(2,1)S(1)}, bf16[16,16,128]{2,1,0:T(8,128)(2,1)S(1)}, u32[]{:S(2)}, u32[]{:S(2)}) collective-permute-start(bf16[16,16,128]{2,1,0:T(8,128)(2,1)S(1)} %get-tuple-element.28), channel_id=1, source_target_pairs={{0,1},{1,0},{2,3},{3,2},{4,5},{5,4},{6,7},{7,6},{8,9},{9,8},{10,11... | collective-permute-start | bytes 196616 | tf_op jit(solution)/shard_map/ppermute | solution.py:342
  26.5 6.3 %collective-permute-start.4 = (bf16[16,16,128]{2,1,0:T(8,128)(2,1)S(1)}, bf16[16,16,128]{2,1,0:T(8,128)(2,1)S(1)}, u32[]{:S(2)}, u32[]{:S(2)}) collective-permute-start(bf16[16,16,128]{2,1,0:T(8,128)(2,1)S(1)} %get-tuple-element.29), channel_id=1, source_target_pairs={{0,7},{1,2},{2,1},{3,4},{4,3},{5,6},{6,5},{7,0},{8,15},{9,10},{10,... | collective-permute-start | bytes 196616 | tf_op jit(solution)/shard_map/ppermute | solution.py:343
  27.8 1.2 %collective-permute-start.7 = (s32[4,3]{1,0:T(4,128)S(1)}, s32[4,3]{1,0:T(4,128)S(1)}, u32[]{:S(2)}, u32[]{:S(2)}) collective-permute-start(s32[4,3]{1,0:T(4,128)S(1)} %get-tuple-element.48), channel_id=1, source_target_pairs={{0,1},{1,0},{2,3},{3,2},{4,5},{5,4},{6,7},{7,6},{8,9},{9,8},{10,11... | collective-permute-start | bytes 152 | tf_op jit(solution)/shard_map/ppermute | solution.py:331
  28.9 3.9 %collective-permute-start.8 = (s32[4,3]{1,0:T(4,128)S(1)}, s32[4,3]{1,0:T(4,128)S(1)}, u32[]{:S(2)}, u32[]{:S(2)}) collective-permute-start(s32[4,3]{1,0:T(4,128)S(1)} %get-tuple-element.47), channel_id=1, source_target_pairs={{0,7},{1,2},{2,1},{3,4},{4,3},{5,6},{6,5},{7,0},{8,15},{9,10},{10,... | collective-permute-start | bytes 152 | tf_op jit(solution)/shard_map/ppermute | solution.py:332
  32.9 1.9 %copy-start = (bf16[32,3,128,128]{3,2,1,0:T(8,128)(2,1)S(1)}, bf16[32,3,128,128]{3,2,1,0:T(8,128)(2,1)}, u32[]{:S(2)}) copy-start(bf16[32,3,128,128]{3,2,1,0:T(8,128)(2,1)} %flow.5) | copy-start | bytes 9437188
  34.8 0.7 %copy-start.4 = (f32[4096]{0:T(1024)S(1)}, f32[4096]{0:T(1024)}, u32[]{:S(2)}) copy-start(f32[4096]{0:T(1024)} %param.14) | copy-start | bytes 49156
  35.5 0.8 %copy-start.6 = (f32[2,4096]{1,0:T(2,128)S(1)}, f32[2,4096]{1,0:T(2,128)}, u32[]{:S(2)}) copy-start(f32[2,4096]{1,0:T(2,128)} %obs.1) | copy-start | bytes 98308
  36.2 0.7 %copy-start.8 = (f32[4096]{0:T(1024)S(1)}, f32[4096]{0:T(1024)}, u32[]{:S(2)}) copy-start(f32[4096]{0:T(1024)} %param.16) | copy-start | bytes 49156
  37.0 5.5 %copy-start.1 = (bf16[32,3,128,128]{3,2,1,0:T(8,128)(2,1)S(1)}, bf16[32,3,128,128]{3,2,1,0:T(8,128)(2,1)}, u32[]{:S(2)}) copy-start(bf16[32,3,128,128]{3,2,1,0:T(8,128)(2,1)} %flow.5) | copy-start | bytes 9437188
  40.0 1.2 %collective-permute-start.9 = (f32[32,128]{1,0:T(8,128)S(1)}, f32[32,128]{1,0:T(8,128)S(1)}, u32[]{:S(2)}, u32[]{:S(2)}) collective-permute-start(f32[32,128]{1,0:T(8,128)S(1)} %get-tuple-element.31), channel_id=1, source_target_pairs={{0,1},{1,0},{2,3},{3,2},{4,5},{5,4},{6,7},{7,6},{8,9},{9,8},{10,11... | collective-permute-start | bytes 49160 | tf_op jit(solution)/shard_map/ppermute | solution.py:359
  41.3 4.9 %collective-permute-start.10 = (f32[32,128]{1,0:T(8,128)S(1)}, f32[32,128]{1,0:T(8,128)S(1)}, u32[]{:S(2)}, u32[]{:S(2)}) collective-permute-start(f32[32,128]{1,0:T(8,128)S(1)} %add.4), channel_id=1, source_target_pairs={{0,2},{1,3},{2,0},{3,1},{4,6},{5,7},{6,4},{7,5},{8,10},{9,11},{10,... | collective-permute-start | bytes 49160 | tf_op jit(solution)/shard_map/ppermute | solution.py:363
  45.1 2.6 %collective-permute-start.12 = (f32[12,4,128]{2,1,0:T(4,128)S(1)}, f32[12,4,128]{2,1,0:T(4,128)S(1)}, u32[]{:S(2)}, u32[]{:S(2)}) collective-permute-start(f32[12,4,128]{2,1,0:T(4,128)S(1)} %get-tuple-element.41), channel_id=1, source_target_pairs={{0,1},{1,0},{2,3},{3,2},{4,5},{5,4},{6,7},{7,6},{8,9},{9,8},{10,11... | collective-permute-start | bytes 73736 | tf_op jit(solution)/shard_map/ppermute | solution.py:356
  45.2 4.4 %collective-permute-start.13 = (f32[12,4,128]{2,1,0:T(4,128)S(1)}, f32[12,4,128]{2,1,0:T(4,128)S(1)}, u32[]{:S(2)}, u32[]{:S(2)}) collective-permute-start(f32[12,4,128]{2,1,0:T(4,128)S(1)} %get-tuple-element.42), channel_id=1, source_target_pairs={{0,7},{1,2},{2,1},{3,4},{4,3},{5,6},{6,5},{7,0},{8,15},{9,10},{10,... | collective-permute-start | bytes 73736 | tf_op jit(solution)/shard_map/ppermute | solution.py:357
  46.1 8.9 %collective-permute-start.11 = (f32[32,128]{1,0:T(8,128)S(1)}, f32[32,128]{1,0:T(8,128)S(1)}, u32[]{:S(2)}, u32[]{:S(2)}) collective-permute-start(f32[32,128]{1,0:T(8,128)S(1)} %add.5.mine), channel_id=1, source_target_pairs={{0,4},{1,5},{2,6},{3,7},{4,0},{5,1},{6,2},{7,3},{8,12},{9,13},{10,... | collective-permute-start | bytes 49160 | tf_op jit(solution)/shard_map/ppermute | solution.py:363

commit v2 on v1

v2 whole, which is shorter than its diff:
```python
import functools

import jax
import jax.numpy as jnp
from jax import lax
from jax.experimental import pallas as pl
from jax.experimental.pallas import tpu as pltpu
from jax.sharding import PartitionSpec as P

BLK = 128
CYCLES = 2
HALO = 4
WIDE = 2 * HALO
NBR = 3
BOUNDS = (2.0, 5.0, 4.0)
SCALE_STEPS = 32000.0
STEPS = 32767.0
VMEM = pl.BlockSpec(memory_space=pltpu.VMEM)
SMEM = pl.BlockSpec(memory_space=pltpu.SMEM)
HBM = pl.BlockSpec(memory_space=pltpu.HBM)


def run(count, unroll, step, carry):
    if unroll:
        for n in range(count):
            carry = step(n, carry)
        return carry
    return lax.fori_loop(0, count, step, carry)


def lanes(n, at=0):
    if isinstance(n, int):
        return slice(at + n * BLK, at + (n + 1) * BLK)
    return pl.ds(pl.multiple_of(at + n * BLK, BLK), BLK)


def wetness(w):
    sq = w * w
    return sq / (1.0 + sq)


def flux_of(xs, flow):
    return jnp.dot(jnp.concatenate(xs, axis=1), flow, preferred_element_type=jnp.float32)


def right_first():
    return lax.rem(lax.axis_index("tile"), 2) == 0


def pack_kernel(
    bio, wat, rain, growth, prec, obs, anc,
    wire, later, growth_out, prec_out, obs_out, anc_out, rain_out,
    fields, held, held1, factor, sems,
):
    part, cells = bio.shape
    nb = cells // BLK
    copies = [
        pltpu.make_async_copy(src, dst, sems.at[i])
        for i, (src, dst) in enumerate(
            (
                (bio, fields.at[0]),
                (wat, fields.at[1]),
                (rain.at[0], fields.at[2]),
                (rain.at[1], fields.at[3]),
                (growth, growth_out),
                (prec, prec_out),
                (obs, obs_out),
                (anc, anc_out),
                (rain.at[pl.ds(2, 2)], rain_out),
            )
        )
    ]
    for c in copies:
        c.start()
    half, quarter = cells // 2, cells // 4
    codes = []
    for f in range(4):
        copies[f].wait()
        big = jnp.abs(fields[f, :, 0:BLK])
        for n in range(1, nb):
            big = jnp.maximum(big, jnp.abs(fields[f, :, lanes(n)]))
        unit = BOUNDS[min(f, 2)] / SCALE_STEPS
        code = jnp.floor(jnp.max(big, axis=1, keepdims=True) / unit) + 1.0
        inv = jnp.broadcast_to(STEPS / (code * unit), (part, BLK))
        codes.append(jnp.broadcast_to(code, (part, BLK)))
        if f < 2:
            for h in range(2):
                row = (2 * h + f) * part
                held[row : row + part, 0:half] = fields[f, :, h * half : (h + 1) * half]
                factor[0, row : row + part, :] = inv
        else:
            ref, at = (held, half) if f == 2 else (held1, 0)
            for q in range(4):
                ref[q * part : (q + 1) * part, at : at + quarter] = fields[f, :, q * quarter : (q + 1) * quarter]
                factor[f - 1, q * part : (q + 1) * part, :] = inv
    factor[3] = jnp.zeros(factor.shape[1:], jnp.float32)
    factor[4] = jnp.zeros(factor.shape[1:], jnp.float32)
    for f in range(3):
        factor[3, f * part : (f + 1) * part, :] = codes[f]
    factor[4, 0:part, :] = codes[3]

    def coded(x):
        return jnp.round(x).astype(jnp.int32).astype(jnp.int16)

    pairs, quads = nb // 2, nb // 4
    for n in range(pairs + quads):
        wire[:, lanes(n)] = coded(held[:, lanes(n)] * factor[0 if n < pairs else 1])
    wire[:, lanes(pairs + quads)] = coded(factor[3])
    for n in range(quads):
        later[:, lanes(n)] = coded(held1[:, lanes(n)] * factor[2])
    later[:, lanes(quads)] = coded(factor[4])
    for c in copies[4:]:
        c.wait()


def flow_kernel(after, flow, ids, turned, pay_a, pay_b, raw, sems):
    nb = flow.shape[0]
    chunk = nb // 4
    copies = [
        pltpu.make_async_copy(flow.at[pl.ds(c * chunk, chunk)], raw.at[pl.ds(c * chunk, chunk)], sems.at[c])
        for c in range(4)
    ]
    for c in copies:
        c.start()
    pos = lax.axis_index("tile")
    even = right_first()
    depth = NBR * BLK
    for c in range(4):
        copies[c].wait()
        for n in range(c * chunk, (c + 1) * chunk):
            for k in range(NBR):
                turned[n, k * BLK : (k + 1) * BLK, :] = raw[n, k].T
    line = lax.broadcasted_iota(jnp.int32, (16, BLK), 0)
    for pay, right in ((pay_a, even), (pay_b, jnp.logical_not(even))):
        start = jnp.where(right, nb - HALO, 0)
        away = jnp.zeros((16, BLK), jnp.float32)
        for m in range(HALO):
            pay[m * depth : (m + 1) * depth, :] = turned[start + m]
            n = start + m + pos * nb
            for k, gap in enumerate((n - ids[start + m, 1], ids[start + m, 2] - n)):
                away = jnp.where(line == 2 * m + k, gap.astype(jnp.float32), away)
        pay[HALO * depth : HALO * depth + 16, :] = away.astype(jnp.bfloat16)


def halo_flux(ext, pay, right, nb, m):
    depth = NBR * BLK
    away = pay[HALO * depth : HALO * depth + 16, :].astype(jnp.float32)
    at = jnp.where(right, nb + WIDE + m, HALO + m)
    xs = [ext[at].astype(jnp.bfloat16)]
    for k, sign in enumerate((-1, 1)):
        gap = jnp.broadcast_to(away[2 * m + k : 2 * m + k + 1, :], ext.shape[1:])
        x = jnp.zeros(ext.shape[1:], jnp.float32)
        for d in range(HALO + 1):
            x = jnp.where(gap == d, ext[at + sign * d].astype(jnp.float32), x)
        xs.append(x.astype(jnp.bfloat16))
    return flux_of(xs, pay[m * depth : (m + 1) * depth, :])


def decode(sel, pieces, cols):
    parts = []
    for ref in pieces:
        q = ref[:, cols].astype(jnp.int32)
        parts.append((q >> 8).astype(jnp.float32).astype(jnp.bfloat16))
        parts.append((q & 255).astype(jnp.float32).astype(jnp.bfloat16))
    return jnp.dot(sel, jnp.concatenate(parts, axis=0), preferred_element_type=jnp.float32)


def open_kernel(members, unroll, *refs):
    pieces = refs[:members]
    anc, growth, prec, obs = refs[members : members + 4]
    wb, v0, b1, bq, wq, miss, quad, pay_a, pay_b = refs[members + 4 : members + 13]
    pair, scaler = refs[-2:]
    nb = growth.shape[0]
    slots = anc.shape[1]
    rows = pieces[0].shape[0]
    part = rows // 4
    depth = members * rows * 2
    me = lax.axis_index("particle")
    line = lax.broadcasted_iota(jnp.int32, (slots, slots), 0)
    lane = lax.broadcasted_iota(jnp.int32, (slots, slots), 1)
    first = jnp.broadcast_to(anc[0:1, :], (slots, slots)).astype(jnp.float32)
    chosen = jnp.sum(jnp.where(line == lane, first, 0.0), axis=1, keepdims=True)
    own = lax.broadcasted_iota(jnp.int32, (slots, 1), 0).astype(jnp.float32)
    col = lax.broadcasted_iota(jnp.int32, (slots, depth), 1)
    value = jnp.where((col // rows) % 2 == 0, 256.0, 1.0)
    group = (col % rows) // part
    source = (((col // (2 * rows)) ^ me) * part + col % part).astype(jnp.float32)

    def hits(g, want):
        return jnp.where(jnp.logical_and(group == g, source == want), value, 0.0).astype(jnp.bfloat16)

    for h in range(2):
        for i, want in enumerate((chosen, chosen, own, own)):
            at = (4 * h + i) * slots
            pair[at : at + slots, :] = hits(2 * h + i % 2, want)
    for g in range(4):
        quad[g * slots : (g + 1) * slots, :] = hits(g, own)
    for i, (g, want) in enumerate(((0, chosen), (1, chosen), (0, own), (1, own), (2, own))):
        scaler[i * slots : (i + 1) * slots, :] = hits(g, want)

    pairs, quads = nb // 2, nb // 4
    codes = decode(scaler[...], pieces, lanes(pairs + quads))
    scale = [
        codes[i * slots : (i + 1) * slots] * (BOUNDS[f] / SCALE_STEPS / STEPS) for i, f in enumerate((0, 1, 0, 1, 2))
    ]

    def step(m, acc):
        wet = decode(quad[...], pieces, lanes(m, pairs * BLK))
        for p in range(2):
            got = decode(pair[...], pieces, lanes(m + p * quads))
            for h in range(2):
                q = 2 * h + p
                n = m + q * quads
                b, w, bi, wi = (got[(4 * h + i) * slots : (4 * h + i + 1) * slots] * scale[i] for i in range(4))
                rain0 = wet[q * slots : (q + 1) * slots] * scale[4]
                s = wetness(w)
                row = pl.ds(n, 1)
                wb[n] = w.astype(jnp.bfloat16)
                v0[n] = w + rain0 - 0.2 * b * s
                b1[n] = b + growth[row, :] * b * (s - 0.4 * b)
                bq[n] = bi
                wq[n] = wi
                off = bi - obs[0:1, lanes(n)]
                acc = acc + prec[row, :] * (off * off)
        return acc

    miss[...] = run(quads, unroll, step, jnp.zeros((slots, BLK), jnp.float32))
    even = right_first()
    for pay, right in ((pay_a, even), (pay_b, jnp.logical_not(even))):
        pay[0:WIDE] = wb[pl.ds(jnp.where(right, nb - WIDE, 0), WIDE)]
        edge = v0[pl.ds(jnp.where(right, nb - HALO, 0), HALO)]
        top = edge.astype(jnp.bfloat16)
        pay[WIDE : WIDE + HALO] = top
        pay[WIDE + HALO : WIDE + 2 * HALO] = (edge - top.astype(jnp.float32)).astype(jnp.bfloat16)


def day0_kernel(
    unroll, wb, v0, b1, got_a, got_b, flow, flow_a, flow_b, ids, growth, prec, obs, miss,
    wb1, v1, b2, total, ext,
):
    nb = growth.shape[0]
    slots = wb.shape[1]
    pos = lax.axis_index("tile")
    even = right_first()
    ext[WIDE : WIDE + nb] = wb[...]
    sides = ((got_a, flow_a, even), (got_b, flow_b, jnp.logical_not(even)))
    for got, _, right in sides:
        ext[pl.ds(jnp.where(right, nb + WIDE, 0), WIDE)] = got[0:WIDE]
    base = WIDE - pos * nb

    def step(n, acc):
        w = v0[n] + flux_of((ext[n + WIDE], ext[ids[n, 1] + base], ext[ids[n, 2] + base]), flow[n])
        wb1[n + HALO] = w.astype(jnp.bfloat16)
        s = wetness(w)
        row = pl.ds(n, 1)
        b = b1[n]
        v1[n] = w - 0.2 * b * s
        b = b + growth[row, :] * b * (s - 0.4 * b)
        b2[n] = b
        off = b - obs[1:2, lanes(n)]
        return acc + prec[row, :] * (off * off)

    total[0:slots, :] = miss[...]
    total[slots : 2 * slots, :] = run(nb, unroll, step, jnp.zeros((slots, BLK), jnp.float32))
    for got, pay, right in sides:
        spot = jnp.where(right, nb + HALO, 0)
        for m in range(HALO):
            edge = got[WIDE + m].astype(jnp.float32) + got[WIDE + HALO + m].astype(jnp.float32)
            wb1[spot + m] = (edge + halo_flux(ext, pay, right, nb, m)).astype(jnp.bfloat16)


def day1_kernel(members, unroll, *refs):
    pieces = refs[:members]
    wb1, v1, b2, quad, flow, ids, anc, rain, w2, ws, bs, v2, pay_a, pay_b = refs[members:]
    nb, slots = v1.shape[:2]
    part = rain.shape[1]
    pos = lax.axis_index("tile")
    me = lax.axis_index("particle")
    even = right_first()
    base = HALO - pos * nb
    picks = [anc[1, me * part + i] for i in range(part)]
    quads = nb // 4
    scale = decode(quad[0:slots, :], pieces, lanes(quads)) * (BOUNDS[2] / SCALE_STEPS / STEPS)

    def step(m, carry):
        wet = decode(quad[...], pieces, lanes(m))
        for q in range(4):
            n = m + q * quads
            flux = flux_of((wb1[n + HALO], wb1[ids[n, 1] + base], wb1[ids[n, 2] + base]), flow[n])
            w2[n] = v1[n] + flux + wet[q * slots : (q + 1) * slots] * scale
        return carry

    run(quads, unroll, step, 0)

    def pick(n, carry):
        for i in range(part):
            ws[n, i : i + 1, :] = w2[n, pl.ds(picks[i], 1), :]
            bs[n, i : i + 1, :] = b2[n, pl.ds(picks[i], 1), :]
        w = ws[n]
        v2[n] = w + rain[0, :, lanes(n)] - 0.2 * bs[n] * wetness(w)
        return carry

    run(nb, unroll, pick, 0)
    for pay, right in ((pay_a, even), (pay_b, jnp.logical_not(even))):
        pay[0:WIDE] = ws[pl.ds(jnp.where(right, nb - WIDE, 0), WIDE)]
        pay[WIDE : WIDE + HALO] = v2[pl.ds(jnp.where(right, nb - HALO, 0), HALO)]


def close_kernel(
    unroll, ws, bs, v2, got_a, got_b, flow, flow_a, flow_b, ids, growth, rain, bio_out, wat_out, ext, ext3
):
    nb = growth.shape[0]
    pos = lax.axis_index("tile")
    even = right_first()
    half = jnp.bfloat16
    ext[WIDE : WIDE + nb] = ws[...]
    sides = ((got_a, flow_a, even), (got_b, flow_b, jnp.logical_not(even)))
    for got, _, right in sides:
        ext[pl.ds(jnp.where(right, nb + WIDE, 0), WIDE)] = got[0:WIDE]
    for got, pay, right in sides:
        spot = jnp.where(right, nb + HALO, 0)
        for m in range(HALO):
            ext3[spot + m] = got[WIDE + m] + halo_flux(ext, pay, right, nb, m)

    def near(ref, n, at):
        base = at - pos * nb
        return [ref[i].astype(half) for i in (n + at, ids[n, 1] + base, ids[n, 2] + base)]

    def step2(n, carry):
        ext3[n + HALO] = v2[n] + flux_of(near(ext, n, WIDE), flow[n])
        return carry

    run(nb, unroll, step2, 0)

    def step3(n, carry):
        g = growth[pl.ds(n, 1), :]
        b = bs[n]
        b = b + g * b * (wetness(ws[n]) - 0.4 * b)
        w = ext3[n + HALO]
        s = wetness(w)
        wat_out[:, lanes(n)] = w + flux_of(near(ext3, n, HALO), flow[n]) + rain[1, :, lanes(n)] - 0.2 * b * s
        bio_out[:, lanes(n)] = b + g * b * (s - 0.4 * b)
        return carry

    run(nb, unroll, step3, 0)


def means_kernel(unroll, count, *refs):
    bq, wq, b2, w2, means = refs[count:]
    nb, slots = bq.shape[:2]
    level = [ref[...] for ref in refs[:count]]
    while len(level) > 1:
        level = [a + b for a, b in zip(level[::2], level[1::2])]
    lw = -0.5 * jnp.sum(level[0], axis=1, keepdims=True)
    weights = []
    for c in range(CYCLES):
        x = lw[c * slots : (c + 1) * slots]
        e = jnp.exp(x - jnp.max(x, axis=0, keepdims=True))
        weights.append(jnp.broadcast_to(e / jnp.sum(e, axis=0, keepdims=True), (slots, BLK)))

    def step(n, carry):
        for c, fields in enumerate(((bq, wq), (b2, w2))):
            for f, ref in enumerate(fields):
                means[c, f : f + 1, lanes(n)] = jnp.sum(weights[c] * ref[n], axis=0, keepdims=True)
        return carry

    run(nb, unroll, step, 0)


def call(kernel, out, specs, scratch=(), mib=32):
    return pl.pallas_call(
        kernel,
        out_shape=tuple(jax.ShapeDtypeStruct(s, d) for s, d in out),
        in_specs=specs,
        out_specs=tuple(VMEM for _ in out),
        scratch_shapes=list(scratch),
        compiler_params=pltpu.CompilerParams(vmem_limit_bytes=mib * 2**20),
    )


def body(biomass, water, flow_blocks, neighbours, rain, growth_rate, observations, obs_precision, ancestors):
    part, cells = biomass.shape
    nb = cells // BLK
    members, tiles = lax.axis_size("particle"), lax.axis_size("tile")
    slots = members * part
    unroll = slots <= 16
    f32, bf16, i16 = jnp.float32, jnp.bfloat16, jnp.int16
    swap_a = [(i, i ^ 1) for i in range(tiles)]
    swap_b = [(i, (i - 1) % tiles if i % 2 == 0 else (i + 1) % tiles) for i in range(tiles)]
    pairs, quads = nb // 2, nb // 4
    rows = 4 * part

    wire, later, growth, prec, obs, anc, rain23 = call(
        pack_kernel,
        [
            ((rows, (pairs + quads + 1) * BLK), i16),
            ((rows, (quads + 1) * BLK), i16),
            ((nb, BLK), f32),
            ((nb, BLK), f32),
            (observations.shape, f32),
            (ancestors.shape, jnp.int32),
            ((2, part, cells), f32),
        ],
        [HBM] * 7,
        [
            pltpu.VMEM((4, part, cells), f32),
            pltpu.VMEM((rows, (pairs + quads) * BLK), f32),
            pltpu.VMEM((rows, quads * BLK), f32),
            pltpu.VMEM((5, rows, BLK), f32),
            pltpu.SemaphoreType.DMA((9,)),
        ],
    )(biomass, water, rain, growth_rate.reshape(nb, BLK), obs_precision.reshape(nb, BLK), observations, ancestors)

    def gathered(x):
        return [x] + [lax.ppermute(x, "particle", [(i, i ^ j) for i in range(members)]) for j in range(1, members)]

    pieces = gathered(wire)
    pieces1 = gathered(later)
    depth = NBR * BLK
    edge = ((HALO * depth + 16, BLK), bf16)
    flow, flow_a, flow_b = call(
        flow_kernel,
        [((nb, depth, BLK), bf16), edge, edge],
        [HBM, HBM, SMEM],
        [pltpu.VMEM((nb, NBR, BLK, BLK), bf16), pltpu.SemaphoreType.DMA((4,))],
    )(wire, flow_blocks, neighbours)
    flow_a = lax.ppermute(flow_a, "tile", swap_a)
    flow_b = lax.ppermute(flow_b, "tile", swap_b)

    field = ((nb, slots, BLK), f32)
    wb, v0, b1, bq, wq, miss, quad, pay_a, pay_b = call(
        functools.partial(open_kernel, members, unroll),
        [((nb, slots, BLK), bf16), field, field, field, field, ((slots, BLK), f32), ((4 * slots, members * rows * 2), bf16)]
        + [((WIDE + 2 * HALO, slots, BLK), bf16)] * 2,
        [VMEM] * (members + 4),
        [
            pltpu.VMEM((8 * slots, members * rows * 2), bf16),
            pltpu.VMEM((5 * slots, members * rows * 2), bf16),
        ],
    )(*pieces, anc, growth, prec, obs)
    got_a = lax.ppermute(pay_a, "tile", swap_a)
    got_b = lax.ppermute(pay_b, "tile", swap_b)
    wb1, v1, b2, total = call(
        functools.partial(day0_kernel, unroll),
        [((nb + WIDE, slots, BLK), bf16), field, field, ((2 * slots, BLK), f32)],
        [VMEM] * 8 + [SMEM] + [VMEM] * 4,
        [pltpu.VMEM((nb + 2 * WIDE, slots, BLK), bf16)],
    )(wb, v0, b1, got_a, got_b, flow, flow_a, flow_b, neighbours, growth, prec, obs, miss)
    few = ((nb, part, BLK), f32)
    w2, ws, bs, v2, end_a, end_b = call(
        functools.partial(day1_kernel, members, unroll),
        [field, few, few, few] + [((WIDE + HALO, part, BLK), f32)] * 2,
        [VMEM] * (members + 5) + [SMEM] * 2 + [VMEM],
    )(*pieces1, wb1, v1, b2, quad, flow, neighbours, ancestors, rain23)
    last_a = lax.ppermute(end_a, "tile", swap_a)
    last_b = lax.ppermute(end_b, "tile", swap_b)

    def shared(x, masks):
        return [x] + [lax.ppermute(x, "tile", [(i, i ^ m) for i in range(tiles)]) for m in masks]

    terms = shared(total, [1])
    span = 2
    while span < tiles:
        total = sum(terms[1:], terms[0])
        masks = [span] if span * 2 >= tiles else [span, 2 * span, 3 * span]
        terms = shared(total, masks)
        span *= 2 ** (len(masks) // 2 + 1)
    bio_out, wat_out = call(
        functools.partial(close_kernel, unroll),
        [((part, cells), f32)] * 2,
        [VMEM] * 8 + [SMEM] + [VMEM] * 2,
        [pltpu.VMEM((nb + 2 * WIDE, part, BLK), f32), pltpu.VMEM((nb + WIDE, part, BLK), f32)],
    )(ws, bs, v2, last_a, last_b, flow, flow_a, flow_b, neighbours, growth, rain23)
    (means,) = call(
        functools.partial(means_kernel, unroll, len(terms)), [((CYCLES, 2, cells), f32)], [VMEM] * (len(terms) + 4)
    )(*terms, bq, wq, b2, w2)
    return means, bio_out, wat_out


def solution(mesh):
    placed = (
        P("particle", "tile"),
        P("particle", "tile"),
        P("tile", None, None, None),
        P("tile", None),
        P(None, "particle", "tile"),
        P("tile"),
        P(None, "tile"),
        P("tile"),
        P(),
    )
    return jax.shard_map(
        body,
        mesh=mesh,
        in_specs=placed,
        out_specs=(P(None, None, "tile"), P("particle", "tile"), P("particle", "tile")),
        check_vma=False,
    )
```

time: 56.5 us -> 50.1 us (0.89)
  waiting for transfers between devices: 15.9 us -> 9.2 us
  starting transfers between devices: 15 us -> 20.5 us
  Pallas kernels: 14.4 us -> 11 us
  local copies, waits for them, and re-layouts: 9.81 us -> 8.15 us
    ppermute x10 -> x12, waiting for transfers between devices: 14 us -> 8.92 us  [the longest x6 8.9 us: gathered(): lax.ppermute(x, 'particle', [(i, i ^ j) for i in range(members)])]
    ppermute x10 -> x12, starting transfers between devices: 12.7 us -> 17.4 us  [the longest x6 9.76 us: gathered(): lax.ppermute(x, 'particle', [(i, i ^ j) for i in range(members)])]
    pallas_call x1, Pallas kernels: 5.41 us -> 2.91 us  [body(): call(functools.partial(close_kernel, unroll), [((part, cells), f32)] * 2,...]
    ppermute x1, waiting for transfers between devices: 1.92 us -> 0.01 us  [body(): last_b = lax.ppermute(end_b, 'tile', swap_b)]
    pallas_call x1, Pallas kernels: 3.03 us -> 1.64 us  [body(): call(functools.partial(day0_kernel, unroll), [((nb + WIDE, slots, BLK), b...]
    dynamic_slice x2 -> x0, local copies, waits for them, and re-layouts: 1.18 us -> none  [the longest x1 1.17 us: body(): lax.dynamic_slice_in_dim(flow_blocks, start_b, HALO)]
    pallas_call x3 -> x4, Pallas kernels: 5.36 us -> 5.89 us  [the longest x1 2.22 us: body(): call(flow_kernel, [((nb, depth, BLK), bf16), edge, edge], [HBM, HBM, SMEM...]
    unnamed x23 -> x19, local copies, waits for them, and re-layouts: 8.62 us -> 8.15 us
  transfers between devices with their start and end apart: 14 -> 16, of which waited for: 6 -> 4; matrix products, arithmetic and copies ran while one was open for 1% -> 0% of each run, Pallas kernels for 19% -> 14%
where the time goes in v2:
time: 50.1 us; the launch traced here: 49.6 us
  starting transfers between devices  20.5 us (41%)
  Pallas kernels  11 us (22%)
  waiting for transfers between devices  9.2 us (18%)
  local copies, waits for them, and re-layouts  8.15 us (16%)
  between operations  0.74 us (1%)
    ppermute x6, starting transfers between devices, gathered(): lax.ppermute(x, 'particle', [(i, i ^ j) for i in range(members)])  9.76 us
    ppermute x6, waiting for transfers between devices, gathered(): lax.ppermute(x, 'particle', [(i, i ^ j) for i in range(members)])  8.9 us
    unnamed x19, local copies, waits for them, and re-layouts  8.15 us
    ppermute x4, starting transfers between devices, shared(): lax.ppermute(x, 'tile', [(i, i ^ m) for i in range(tiles)])  3.62 us
    ppermute x1, starting transfers between devices, body(): flow_b = lax.ppermute(flow_b, 'tile', swap_b)  3.56 us
    pallas_call x1, Pallas kernels, body(): call(functools.partial(close_kernel, unroll), [((part, cells), f32)] * 2,...  2.91 us
    pallas_call x1, Pallas kernels, body(): call(flow_kernel, [((nb, depth, BLK), bf16), edge, edge], [HBM, HBM, SMEM...  2.22 us
    pallas_call x1, Pallas kernels, body(): call(functools.partial(day1_kernel, members, unroll), [field, few, few, f...  1.68 us
  transfers between devices with their start and end apart: 16, of which 4 were waited for; matrix products, arithmetic and copies ran while one was open for 0% of the time, Pallas kernels for 14%

profile of v2, /device:TPU:0, one launch (start us, length us, event | category | flops | bytes accessed | tf_op | source)
XLA Modules:
  0.0 49.6 jit_solution(11311153092830171053)
XLA Ops:
  0.6 0.8 %copy.12.ids.refs_9_ = s32[32,3]{1,0:T(8,128)S(1)} copy(s32[32,3]{0,1:T(4,128)} %param.12) | data formatting | bytes 768 | tf_op args[3]
  1.4 0.9 %copy-done.1 = f32[4,4,4096]{2,1,0:T(4,128)S(1)} copy-done((f32[4,4,4096]{2,1,0:T(4,128)S(1)}, f32[4,4,4096]{2,1,0:T(4,128)}, u32[]{:S(2)}) %copy-start.1) | copy-done | bytes 262168
  2.3 0.8 %copy-done.2 = f32[4,4096]{1,0:T(4,128)S(1)} copy-done((f32[4,4096]{1,0:T(4,128)S(1)}, f32[4,4096]{1,0:T(4,128)}, u32[]{:S(2)}) %copy-start.2) | copy-done | bytes 65560
  3.2 0.8 %copy-done.3 = f32[4,4096]{1,0:T(4,128)S(1)} copy-done((f32[4,4096]{1,0:T(4,128)S(1)}, f32[4,4096]{1,0:T(4,128)}, u32[]{:S(2)}) %copy-start.3) | copy-done | bytes 65560
  4.0 0.8 %copy-done.4 = f32[2,4096]{1,0:T(2,128)S(1)} copy-done((f32[2,4096]{1,0:T(2,128)S(1)}, f32[2,4096]{1,0:T(2,128)}, u32[]{:S(2)}) %copy-start.4) | copy-done | bytes 32792
  4.8 0.7 %copy-done.5 = f32[4096]{0:T(1024)S(1)} copy-done((f32[4096]{0:T(1024)S(1)}, f32[4096]{0:T(1024)}, u32[]{:S(2)}) %copy-start.5) | copy-done | bytes 16408
  5.5 0.7 %copy-done.6 = f32[4096]{0:T(1024)S(1)} copy-done((f32[4096]{0:T(1024)S(1)}, f32[4096]{0:T(1024)}, u32[]{:S(2)}) %copy-start.6) | copy-done | bytes 16408
  6.2 0.7 %copy-done.7 = s32[2,16]{1,0:T(2,128)S(1)} copy-done((s32[2,16]{1,0:T(2,128)S(1)}, s32[2,16]{1,0:T(2,128)}, u32[]{:S(2)}) %copy-start.7) | copy-done | bytes 152
  6.9 1.1 %shard_map.112 = (s16[16,3200]{1,0:T(8,128)(2,1)S(1)}, s16[16,1152]{1,0:T(8,128)(2,1)S(1)}, f32[32,128]{1,0:T(8,128)S(1)}, f32[32,128]{1,0:T(8,128)S(1)}, f32[2,...) custom-call(f32[4,4096]{1,0:T(4,128)S(1)} %copy-done.2, f32[4,4096]{1,0:T(4,128)S(1)} %copy-done.3, ...), custom_call_target="tpu_custom_call" | custom-call | tf_op jit(solution)/shard_map/pallas_call | solution.py:393
  8.0 0.0 copy-start
  8.0 1.9 %copy-done = bf16[32,3,128,128]{3,2,1,0:T(8,128)(2,1)S(1)} copy-done((bf16[32,3,128,128]{3,2,1,0:T(8,128)(2,1)S(1)}, bf16[32,3,128,128]{3,2,1,0:T(8,128)(2,1)}, u32[]{:S(2)}) %copy-start) | copy-done | bytes 3145752
  9.9 2.2 %shard_map.114 = (bf16[32,384,128]{2,1,0:T(8,128)(2,1)S(1)}, bf16[1552,128]{1,0:T(8,128)(2,1)S(1)}, bf16[1552,128]{1,0:T(8,128)(2,1)S(1)}) custom-call(s16[16,3200]{1,0:T(8,128)(2,1)S(1)} %get-tuple-element.34.refs_0_.after, bf16[32,3,128,128]{3,2,1,0:T(8,128)(2,1)S(1)} %copy-done, s32[32,3]{1,0:T(8,128)S(1)} %copy.12.ids.refs_9_), custom_call_target="tpu_custom_call" | custom-call | tf_op jit(solution)/shard_map/pallas_call | solution.py:421
  12.1 0.0 copy-start.8
  12.1 0.5 %collective-permute-start.5 = (bf16[1552,128]{1,0:T(8,128)(2,1)S(1)}, bf16[1552,128]{1,0:T(8,128)(2,1)S(1)}, u32[]{:S(2)}, u32[]{:S(2)}) collective-permute-start(bf16[1552,128]{1,0:T(8,128)(2,1)S(1)} %get-tuple-element.45), channel_id=1, source_target_pairs={{0,1},{1,0},{2,3},{3,2},{4,5},{5,4},{6,7},{7,6},{8,9},{9,8},{10,11... | collective-permute-start | bytes 1191944 | tf_op jit(solution)/shard_map/ppermute | solution.py:427
  12.6 3.6 %collective-permute-start.6 = (bf16[1552,128]{1,0:T(8,128)(2,1)S(1)}, bf16[1552,128]{1,0:T(8,128)(2,1)S(1)}, u32[]{:S(2)}, u32[]{:S(2)}) collective-permute-start(bf16[1552,128]{1,0:T(8,128)(2,1)S(1)} %get-tuple-element.46), channel_id=1, source_target_pairs={{0,7},{1,2},{2,1},{3,4},{4,3},{5,6},{6,5},{7,0},{8,15},{9,10},{10,... | collective-permute-start | bytes 1191944 | tf_op jit(solution)/shard_map/ppermute | solution.py:428
  16.2 1.6 %collective-permute-start = (s16[16,3200]{1,0:T(8,128)(2,1)S(1)}, s16[16,3200]{1,0:T(8,128)(2,1)S(1)}, u32[]{:S(2)}, u32[]{:S(2)}) collective-permute-start(s16[16,3200]{1,0:T(8,128)(2,1)S(1)} %get-tuple-element.34.refs_0_.after), channel_id=1, source_target_pairs={{0,8},{8,0},{16,24},{24,16},{1,9},{9,1},{17,25},{25,17},{2,10},{10... | collective-permute-start | bytes 307208 | tf_op jit(solution)/shard_map/ppermute | solution.py:415
  17.8 2.6 %collective-permute-start.1 = (s16[16,3200]{1,0:T(8,128)(2,1)S(1)}, s16[16,3200]{1,0:T(8,128)(2,1)S(1)}, u32[]{:S(2)}, u32[]{:S(2)}) collective-permute-start(s16[16,3200]{1,0:T(8,128)(2,1)S(1)} %get-tuple-element.34.refs_0_.after), channel_id=1, source_target_pairs={{0,16},{8,24},{16,0},{24,8},{1,17},{9,25},{17,1},{25,9},{2,18},{10... | collective-permute-start | bytes 307208 | tf_op jit(solution)/shard_map/ppermute | solution.py:415
  20.4 0.2 collective-permute-start.2
  20.6 1.3 %collective-permute-done.refs_1_ = s16[16,3200]{1,0:T(8,128)(2,1)S(1)} collective-permute-done((s16[16,3200]{1,0:T(8,128)(2,1)S(1)}, s16[16,3200]{1,0:T(8,128)(2,1)S(1)}, u32[]{:S(2)}, u32[]{:S(2)}) %collective-permute-start) | collective-permute-done | bytes 102432 | tf_op jit(solution)/shard_map/ppermute | solution.py:415
  21.9 5.9 %collective-permute-done.1.refs_2_ = s16[16,3200]{1,0:T(8,128)(2,1)S(1)} collective-permute-done((s16[16,3200]{1,0:T(8,128)(2,1)S(1)}, s16[16,3200]{1,0:T(8,128)(2,1)S(1)}, u32[]{:S(2)}, u32[]{:S(2)}) %collective-permute-start.1) | collective-permute-done | bytes 102432 | tf_op jit(solution)/shard_map/ppermute | solution.py:415
  27.8 0.0 collective-permute-done.2.refs_3_
  27.8 0.5 %shard_map.113 = (bf16[32,16,128]{2,1,0:T(8,128)(2,1)S(1)}, f32[32,16,128]{2,1,0:T(8,128)S(1)}, f32[32,16,128]{2,1,0:T(8,128)S(1)}, f32[32,16,128]{2,1,0:T(8,128...) custom-call(s16[16,3200]{1,0:T(8,128)(2,1)S(1)} %get-tuple-element.3, ...), custom_call_target="tpu_custom_call" | custom-call | tf_op jit(solution)/shard_map/pallas_call | solution.py:431
  28.3 0.1 collective-permute-start.3
  28.4 1.6 %collective-permute-start.4 = (bf16[16,16,128]{2,1,0:T(8,128)(2,1)S(1)}, bf16[16,16,128]{2,1,0:T(8,128)(2,1)S(1)}, u32[]{:S(2)}, u32[]{:S(2)}) collective-permute-start(bf16[16,16,128]{2,1,0:T(8,128)(2,1)S(1)} %get-tuple-element.43), channel_id=1, source_target_pairs={{0,7},{1,2},{2,1},{3,4},{4,3},{5,6},{6,5},{7,0},{8,15},{9,10},{10,... | collective-permute-start | bytes 196616 | tf_op jit(solution)/shard_map/ppermute | solution.py:442
  30.0 1.7 %collective-permute-start.11 = (s16[16,1152]{1,0:T(8,128)(2,1)S(1)}, s16[16,1152]{1,0:T(8,128)(2,1)S(1)}, u32[]{:S(2)}, u32[]{:S(2)}) collective-permute-start(s16[16,1152]{1,0:T(8,128)(2,1)S(1)} %get-tuple-element.52.refs_0_), channel_id=1, source_target_pairs={{0,8},{8,0},{16,24},{24,16},{1,9},{9,1},{17,25},{25,17},{2,10},{10... | collective-permute-start | bytes 110600 | tf_op jit(solution)/shard_map/ppermute | solution.py:415
  31.7 0.0 collective-permute-done.3.got_a
  31.7 1.4 %collective-permute-start.12 = (s16[16,1152]{1,0:T(8,128)(2,1)S(1)}, s16[16,1152]{1,0:T(8,128)(2,1)S(1)}, u32[]{:S(2)}, u32[]{:S(2)}) collective-permute-start(s16[16,1152]{1,0:T(8,128)(2,1)S(1)} %get-tuple-element.52.refs_0_), channel_id=1, source_target_pairs={{0,16},{8,24},{16,0},{24,8},{1,17},{9,25},{17,1},{25,9},{2,18},{10... | collective-permute-start | bytes 110600 | tf_op jit(solution)/shard_map/ppermute | solution.py:415
  33.0 0.3 collective-permute-done.4.got_b
  33.3 2.3 %collective-permute-start.13 = (s16[16,1152]{1,0:T(8,128)(2,1)S(1)}, s16[16,1152]{1,0:T(8,128)(2,1)S(1)}, u32[]{:S(2)}, u32[]{:S(2)}) collective-permute-start(s16[16,1152]{1,0:T(8,128)(2,1)S(1)} %get-tuple-element.52.refs_0_), channel_id=1, source_target_pairs={{0,24},{8,16},{16,8},{24,0},{1,25},{9,17},{17,9},{25,1},{2,26},{10... | collective-permute-start | bytes 110600 | tf_op jit(solution)/shard_map/ppermute | solution.py:415
  35.6 0.0 collective-permute-done.5.flow_a
  35.6 1.6 %shard_map.115 = (bf16[40,16,128]{2,1,0:T(8,128)(2,1)S(1)}, f32[32,16,128]{2,1,0:T(8,128)S(1)}, f32[32,16,128]{2,1,0:T(8,128)S(1)}, f32[32,128]{1,0:T(8,128)S(1)}) custom-call(bf16[32,16,128]{2,1,0:T(8,128)(2,1)S(1)} %get-tuple-element.39.wb, f32[32,16,128]{2,1,0:T(8,128)S(1)} %get-tuple-element.40.v0, f32[32,16,128]{2,1,0:T(8,128)S(1)} %get-tuple-element.41.b1, ...), custom_call_target="tpu_custom_call" | custom-call | tf_op jit(solution)/shard_map/pallas_call | solution.py:443
  37.3 0.1 collective-permute-start.7
  37.3 0.0 collective-permute-done.11.refs_1_
  37.4 1.7 %collective-permute-done.13.refs_3_ = s16[16,1152]{1,0:T(8,128)(2,1)S(1)} collective-permute-done((s16[16,1152]{1,0:T(8,128)(2,1)S(1)}, s16[16,1152]{1,0:T(8,128)(2,1)S(1)}, u32[]{:S(2)}, u32[]{:S(2)}) %collective-permute-start.13) | collective-permute-done | bytes 36896 | tf_op jit(solution)/shard_map/ppermute | solution.py:415
  39.0 1.7 %shard_map.116 = (f32[32,16,128]{2,1,0:T(8,128)S(1)}, f32[32,4,128]{2,1,0:T(4,128)S(1)}, f32[32,4,128]{2,1,0:T(4,128)S(1)}, f32[32,4,128]{2,1,0:T(4,128)S(1)}, f...) custom-call(s16[16,1152]{1,0:T(8,128)(2,1)S(1)} %get-tuple-element.52.refs_0_, ...), custom_call_target="tpu_custom_call" | custom-call | tf_op jit(solution)/shard_map/pallas_call | solution.py:450
  40.7 0.1 collective-permute-start.14
  40.8 1.4 %collective-permute-start.15 = (f32[12,4,128]{2,1,0:T(4,128)S(1)}, f32[12,4,128]{2,1,0:T(4,128)S(1)}, u32[]{:S(2)}, u32[]{:S(2)}) collective-permute-start(f32[12,4,128]{2,1,0:T(4,128)S(1)} %get-tuple-element.62), channel_id=1, source_target_pairs={{0,7},{1,2},{2,1},{3,4},{4,3},{5,6},{6,5},{7,0},{8,15},{9,10},{10,... | collective-permute-start | bytes 73736 | tf_op jit(solution)/shard_map/ppermute | solution.py:456
  42.2 0.0 collective-permute-done.7
  42.2 1.9 %collective-permute-start.10 = (f32[32,128]{1,0:T(8,128)S(1)}, f32[32,128]{1,0:T(8,128)S(1)}, u32[]{:S(2)}, u32[]{:S(2)}) collective-permute-start(f32[32,128]{1,0:T(8,128)S(1)} %add.3.refs_0_), channel_id=1, source_target_pairs={{0,6},{1,7},{2,4},{3,5},{4,2},{5,3},{6,0},{7,1},{8,14},{9,15},{10,... | collective-permute-start | bytes 49160 | tf_op jit(solution)/shard_map/ppermute | solution.py:459
  44.1 0.4 collective-permute-start.8
  44.5 1.2 %collective-permute-start.9 = (f32[32,128]{1,0:T(8,128)S(1)}, f32[32,128]{1,0:T(8,128)S(1)}, u32[]{:S(2)}, u32[]{:S(2)}) collective-permute-start(f32[32,128]{1,0:T(8,128)S(1)} %add.3.refs_0_), channel_id=1, source_target_pairs={{0,4},{1,5},{2,6},{3,7},{4,0},{5,1},{6,2},{7,3},{8,12},{9,13},{10,... | collective-permute-start | bytes 49160 | tf_op jit(solution)/shard_map/ppermute | solution.py:459
  45.8 0.0 collective-permute-done.14.got_a
  45.8 0.0 collective-permute-done.15.got_b
  45.8 2.9 %shard_map.118 = (f32[4,4096]{1,0:T(4,128)}, f32[4,4096]{1,0:T(4,128)}) custom-call(f32[32,4,128]{2,1,0:T(4,128)S(1)} %get-tuple-element.58.ws, f32[32,4,128]{2,1,0:T(4,128)S(1)} %get-tuple-element.59.bs, f32[32,4,128]{2,1,0:T(4,128)S(1)} %get-tuple-element.60.v2, f32[12,4,128]{2,1,0:T(4,128)S(1)} %collective-permute-done.14.got_a, ...), custom_call_target="tpu_custom_call" | custom-call | tf_op jit(solution)/shard_map/pallas_call | solution.py:468
  48.7 0.0 collective-permute-done.10.refs_3_
  48.7 0.0 collective-permute-done.8.refs_1_
  48.7 0.0 collective-permute-done.9.refs_2_
  48.7 0.9 %shard_map.117 = f32[2,2,4096]{2,1,0:T(2,128)} custom-call(f32[32,128]{1,0:T(8,128)S(1)} %add.3.refs_0_, f32[32,128]{1,0:T(8,128)S(1)} %collective-permute-done.8.refs_1_, f32[32,128]{1,0:T(8,128)S(1)} %collective-permute-done.9.refs_2_, f32[32,128]{1,0:T(8,128)S(1)} %collective-permute-done.10.refs_3_, f32[32,16,128]{2,1,0:T(8,128)S(1)} %get-tuple-element.49.refs_4_, ...), custom_call_target="tpu_custom_call" | custom-call | tf_op jit(solution)/shard_map/pallas_call | solution.py:474
  (11 shorter events, 0.0 us)
Async XLA Ops:
  1.4 0.9 %copy-start.1 = (f32[4,4,4096]{2,1,0:T(4,128)S(1)}, f32[4,4,4096]{2,1,0:T(4,128)}, u32[]{:S(2)}) copy-start(f32[4,4,4096]{2,1,0:T(4,128)} %rain.1) | copy-start | bytes 786436
  2.3 0.8 %copy-start.2 = (f32[4,4096]{1,0:T(4,128)S(1)}, f32[4,4096]{1,0:T(4,128)}, u32[]{:S(2)}) copy-start(f32[4,4096]{1,0:T(4,128)} %bio.1) | copy-start | bytes 196612
  3.2 0.8 %copy-start.3 = (f32[4,4096]{1,0:T(4,128)S(1)}, f32[4,4096]{1,0:T(4,128)}, u32[]{:S(2)}) copy-start(f32[4,4096]{1,0:T(4,128)} %wat.1) | copy-start | bytes 196612
  4.0 0.8 %copy-start.4 = (f32[2,4096]{1,0:T(2,128)S(1)}, f32[2,4096]{1,0:T(2,128)}, u32[]{:S(2)}) copy-start(f32[2,4096]{1,0:T(2,128)} %obs.1) | copy-start | bytes 98308
  4.8 0.7 %copy-start.5 = (f32[4096]{0:T(1024)S(1)}, f32[4096]{0:T(1024)}, u32[]{:S(2)}) copy-start(f32[4096]{0:T(1024)} %param.14) | copy-start | bytes 49156
  5.5 0.7 %copy-start.6 = (f32[4096]{0:T(1024)S(1)}, f32[4096]{0:T(1024)}, u32[]{:S(2)}) copy-start(f32[4096]{0:T(1024)} %param.16) | copy-start | bytes 49156
  6.2 0.7 %copy-start.7 = (s32[2,16]{1,0:T(2,128)S(1)}, s32[2,16]{1,0:T(2,128)}, u32[]{:S(2)}) copy-start(s32[2,16]{1,0:T(2,128)} %refs_10_.1) | copy-start | bytes 388
  8.0 1.9 %copy-start = (bf16[32,3,128,128]{3,2,1,0:T(8,128)(2,1)S(1)}, bf16[32,3,128,128]{3,2,1,0:T(8,128)(2,1)}, u32[]{:S(2)}) copy-start(bf16[32,3,128,128]{3,2,1,0:T(8,128)(2,1)} %flow.1) | copy-start | bytes 9437188
  12.1 26.9 %copy-start.8 = (s32[2,16]{1,0:T(2,128)S(1)}, s32[2,16]{1,0:T(2,128)}, u32[]{:S(2)}) copy-start(s32[2,16]{1,0:T(2,128)} %refs_10_.1) | copy-start | bytes 388
  12.1 23.5 %collective-permute-start.5 = (bf16[1552,128]{1,0:T(8,128)(2,1)S(1)}, bf16[1552,128]{1,0:T(8,128)(2,1)S(1)}, u32[]{:S(2)}, u32[]{:S(2)}) collective-permute-start(bf16[1552,128]{1,0:T(8,128)(2,1)S(1)} %get-tuple-element.45), channel_id=1, source_target_pairs={{0,1},{1,0},{2,3},{3,2},{4,5},{5,4},{6,7},{7,6},{8,9},{9,8},{10,11... | collective-permute-start | bytes 1191944 | tf_op jit(solution)/shard_map/ppermute | solution.py:427
  12.6 23.0 %collective-permute-start.6 = (bf16[1552,128]{1,0:T(8,128)(2,1)S(1)}, bf16[1552,128]{1,0:T(8,128)(2,1)S(1)}, u32[]{:S(2)}, u32[]{:S(2)}) collective-permute-start(bf16[1552,128]{1,0:T(8,128)(2,1)S(1)} %get-tuple-element.46), channel_id=1, source_target_pairs={{0,7},{1,2},{2,1},{3,4},{4,3},{5,6},{6,5},{7,0},{8,15},{9,10},{10,... | collective-permute-start | bytes 1191944 | tf_op jit(solution)/shard_map/ppermute | solution.py:428
  16.2 5.7 %collective-permute-start = (s16[16,3200]{1,0:T(8,128)(2,1)S(1)}, s16[16,3200]{1,0:T(8,128)(2,1)S(1)}, u32[]{:S(2)}, u32[]{:S(2)}) collective-permute-start(s16[16,3200]{1,0:T(8,128)(2,1)S(1)} %get-tuple-element.34.refs_0_.after), channel_id=1, source_target_pairs={{0,8},{8,0},{16,24},{24,16},{1,9},{9,1},{17,25},{25,17},{2,10},{10... | collective-permute-start | bytes 307208 | tf_op jit(solution)/shard_map/ppermute | solution.py:415
  17.8 10.0 %collective-permute-start.1 = (s16[16,3200]{1,0:T(8,128)(2,1)S(1)}, s16[16,3200]{1,0:T(8,128)(2,1)S(1)}, u32[]{:S(2)}, u32[]{:S(2)}) collective-permute-start(s16[16,3200]{1,0:T(8,128)(2,1)S(1)} %get-tuple-element.34.refs_0_.after), channel_id=1, source_target_pairs={{0,16},{8,24},{16,0},{24,8},{1,17},{9,25},{17,1},{25,9},{2,18},{10... | collective-permute-start | bytes 307208 | tf_op jit(solution)/shard_map/ppermute | solution.py:415
  20.4 7.4 %collective-permute-start.2 = (s16[16,3200]{1,0:T(8,128)(2,1)S(1)}, s16[16,3200]{1,0:T(8,128)(2,1)S(1)}, u32[]{:S(2)}, u32[]{:S(2)}) collective-permute-start(s16[16,3200]{1,0:T(8,128)(2,1)S(1)} %get-tuple-element.34.refs_0_.after), channel_id=1, source_target_pairs={{0,24},{8,16},{16,8},{24,0},{1,25},{9,17},{17,9},{25,1},{2,26},{10... | collective-permute-start | bytes 307208 | tf_op jit(solution)/shard_map/ppermute | solution.py:415
  28.3 3.3 %collective-permute-start.3 = (bf16[16,16,128]{2,1,0:T(8,128)(2,1)S(1)}, bf16[16,16,128]{2,1,0:T(8,128)(2,1)S(1)}, u32[]{:S(2)}, u32[]{:S(2)}) collective-permute-start(bf16[16,16,128]{2,1,0:T(8,128)(2,1)S(1)} %get-tuple-element.42), channel_id=1, source_target_pairs={{0,1},{1,0},{2,3},{3,2},{4,5},{5,4},{6,7},{7,6},{8,9},{9,8},{10,11... | collective-permute-start | bytes 196616 | tf_op jit(solution)/shard_map/ppermute | solution.py:441
  28.4 4.9 %collective-permute-start.4 = (bf16[16,16,128]{2,1,0:T(8,128)(2,1)S(1)}, bf16[16,16,128]{2,1,0:T(8,128)(2,1)S(1)}, u32[]{:S(2)}, u32[]{:S(2)}) collective-permute-start(bf16[16,16,128]{2,1,0:T(8,128)(2,1)S(1)} %get-tuple-element.43), channel_id=1, source_target_pairs={{0,7},{1,2},{2,1},{3,4},{4,3},{5,6},{6,5},{7,0},{8,15},{9,10},{10,... | collective-permute-start | bytes 196616 | tf_op jit(solution)/shard_map/ppermute | solution.py:442
  30.0 7.4 %collective-permute-start.11 = (s16[16,1152]{1,0:T(8,128)(2,1)S(1)}, s16[16,1152]{1,0:T(8,128)(2,1)S(1)}, u32[]{:S(2)}, u32[]{:S(2)}) collective-permute-start(s16[16,1152]{1,0:T(8,128)(2,1)S(1)} %get-tuple-element.52.refs_0_), channel_id=1, source_target_pairs={{0,8},{8,0},{16,24},{24,16},{1,9},{9,1},{17,25},{25,17},{2,10},{10... | collective-permute-start | bytes 110600 | tf_op jit(solution)/shard_map/ppermute | solution.py:415
  31.7 5.7 %collective-permute-start.12 = (s16[16,1152]{1,0:T(8,128)(2,1)S(1)}, s16[16,1152]{1,0:T(8,128)(2,1)S(1)}, u32[]{:S(2)}, u32[]{:S(2)}) collective-permute-start(s16[16,1152]{1,0:T(8,128)(2,1)S(1)} %get-tuple-element.52.refs_0_), channel_id=1, source_target_pairs={{0,16},{8,24},{16,0},{24,8},{1,17},{9,25},{17,1},{25,9},{2,18},{10... | collective-permute-start | bytes 110600 | tf_op jit(solution)/shard_map/ppermute | solution.py:415
  33.3 5.8 %collective-permute-start.13 = (s16[16,1152]{1,0:T(8,128)(2,1)S(1)}, s16[16,1152]{1,0:T(8,128)(2,1)S(1)}, u32[]{:S(2)}, u32[]{:S(2)}) collective-permute-start(s16[16,1152]{1,0:T(8,128)(2,1)S(1)} %get-tuple-element.52.refs_0_), channel_id=1, source_target_pairs={{0,24},{8,16},{16,8},{24,0},{1,25},{9,17},{17,9},{25,1},{2,26},{10... | collective-permute-start | bytes 110600 | tf_op jit(solution)/shard_map/ppermute | solution.py:415
  37.3 5.0 %collective-permute-start.7 = (f32[32,128]{1,0:T(8,128)S(1)}, f32[32,128]{1,0:T(8,128)S(1)}, u32[]{:S(2)}, u32[]{:S(2)}) collective-permute-start(f32[32,128]{1,0:T(8,128)S(1)} %get-tuple-element.48), channel_id=1, source_target_pairs={{0,1},{1,0},{2,3},{3,2},{4,5},{5,4},{6,7},{7,6},{8,9},{9,8},{10,11... | collective-permute-start | bytes 49160 | tf_op jit(solution)/shard_map/ppermute | solution.py:459
  40.7 5.0 %collective-permute-start.14 = (f32[12,4,128]{2,1,0:T(4,128)S(1)}, f32[12,4,128]{2,1,0:T(4,128)S(1)}, u32[]{:S(2)}, u32[]{:S(2)}) collective-permute-start(f32[12,4,128]{2,1,0:T(4,128)S(1)} %get-tuple-element.61), channel_id=1, source_target_pairs={{0,1},{1,0},{2,3},{3,2},{4,5},{5,4},{6,7},{7,6},{8,9},{9,8},{10,11... | collective-permute-start | bytes 73736 | tf_op jit(solution)/shard_map/ppermute | solution.py:455
  40.8 5.0 %collective-permute-start.15 = (f32[12,4,128]{2,1,0:T(4,128)S(1)}, f32[12,4,128]{2,1,0:T(4,128)S(1)}, u32[]{:S(2)}, u32[]{:S(2)}) collective-permute-start(f32[12,4,128]{2,1,0:T(4,128)S(1)} %get-tuple-element.62), channel_id=1, source_target_pairs={{0,7},{1,2},{2,1},{3,4},{4,3},{5,6},{6,5},{7,0},{8,15},{9,10},{10,... | collective-permute-start | bytes 73736 | tf_op jit(solution)/shard_map/ppermute | solution.py:456
  42.2 6.5 %collective-permute-start.10 = (f32[32,128]{1,0:T(8,128)S(1)}, f32[32,128]{1,0:T(8,128)S(1)}, u32[]{:S(2)}, u32[]{:S(2)}) collective-permute-start(f32[32,128]{1,0:T(8,128)S(1)} %add.3.refs_0_), channel_id=1, source_target_pairs={{0,6},{1,7},{2,4},{3,5},{4,2},{5,3},{6,0},{7,1},{8,14},{9,15},{10,... | collective-permute-start | bytes 49160 | tf_op jit(solution)/shard_map/ppermute | solution.py:459
  44.1 4.6 %collective-permute-start.8 = (f32[32,128]{1,0:T(8,128)S(1)}, f32[32,128]{1,0:T(8,128)S(1)}, u32[]{:S(2)}, u32[]{:S(2)}) collective-permute-start(f32[32,128]{1,0:T(8,128)S(1)} %add.3.refs_0_), channel_id=1, source_target_pairs={{0,2},{1,3},{2,0},{3,1},{4,6},{5,7},{6,4},{7,5},{8,10},{9,11},{10,... | collective-permute-start | bytes 49160 | tf_op jit(solution)/shard_map/ppermute | solution.py:459
  44.5 4.2 %collective-permute-start.9 = (f32[32,128]{1,0:T(8,128)S(1)}, f32[32,128]{1,0:T(8,128)S(1)}, u32[]{:S(2)}, u32[]{:S(2)}) collective-permute-start(f32[32,128]{1,0:T(8,128)S(1)} %add.3.refs_0_), channel_id=1, source_target_pairs={{0,4},{1,5},{2,6},{3,7},{4,0},{5,1},{6,2},{7,3},{8,12},{9,13},{10,... | collective-permute-start | bytes 49160 | tf_op jit(solution)/shard_map/ppermute | solution.py:459

commit v3 on v2

--- a/solution.py
+++ b/solution.py
@@ -48,37 +48,16 @@
 
 
 def pack_kernel(
-    bio, wat, rain, growth, prec, obs, anc,
-    wire, later, growth_out, prec_out, obs_out, anc_out, rain_out,
-    fields, held, held1, factor, sems,
+    bio, wat, rain, left, right, ids, wire, pay_a, pay_b, held, factor
 ):
     part, cells = bio.shape
     nb = cells // BLK
-    copies = [
-        pltpu.make_async_copy(src, dst, sems.at[i])
-        for i, (src, dst) in enumerate(
-            (
-                (bio, fields.at[0]),
-                (wat, fields.at[1]),
-                (rain.at[0], fields.at[2]),
-                (rain.at[1], fields.at[3]),
-                (growth, growth_out),
-                (prec, prec_out),
-                (obs, obs_out),
-                (anc, anc_out),
-                (rain.at[pl.ds(2, 2)], rain_out),
-            )
-        )
-    ]
-    for c in copies:
-        c.start()
     half, quarter = cells // 2, cells // 4
     codes = []
-    for f in range(4):
-        copies[f].wait()
-        big = jnp.abs(fields[f, :, 0:BLK])
+    for f, field in enumerate((bio, wat, rain.at[0], rain.at[1])):
+        big = jnp.abs(field[:, 0:BLK])
         for n in range(1, nb):
-            big = jnp.maximum(big, jnp.abs(fields[f, :, lanes(n)]))
+            big = jnp.maximum(big, jnp.abs(field[:, lanes(n)]))
         unit = BOUNDS[min(f, 2)] / SCALE_STEPS
         code = jnp.floor(jnp.max(big, axis=1, keepdims=True) / unit) + 1.0
         inv = jnp.broadcast_to(STEPS / (code * unit), (part, BLK))
@@ -86,60 +65,57 @@
         if f < 2:
             for h in range(2):
                 row = (2 * h + f) * part
-                held[row : row + part, 0:half] = fields[f, :, h * half : (h + 1) * half]
+                held[row : row + part, 0:half] = field[:, h * half : (h + 1) * half]
                 factor[0, row : row + part, :] = inv
         else:
-            ref, at = (held, half) if f == 2 else (held1, 0)
+            at = f * quarter
             for q in range(4):
-                ref[q * part : (q + 1) * part, at : at + quarter] = fields[f, :, q * quarter : (q + 1) * quarter]
+                held[q * part : (q + 1) * part, at : at + quarter] = field[:, q * quarter : (q + 1) * quarter]
                 factor[f - 1, q * part : (q + 1) * part, :] = inv
-    factor[3] = jnp.zeros(factor.shape[1:], jnp.float32)
-    factor[4] = jnp.zeros(factor.shape[1:], jnp.float32)
-    for f in range(3):
+    for f in range(4):
         factor[3, f * part : (f + 1) * part, :] = codes[f]
-    factor[4, 0:part, :] = codes[3]
 
     def coded(x):
         return jnp.round(x).astype(jnp.int32).astype(jnp.int16)
 
     pairs, quads = nb // 2, nb // 4
-    for n in range(pairs + quads):
-        wire[:, lanes(n)] = coded(held[:, lanes(n)] * factor[0 if n < pairs else 1])
-    wire[:, lanes(pairs + quads)] = coded(factor[3])
-    for n in range(quads):
-        later[:, lanes(n)] = coded(held1[:, lanes(n)] * factor[2])
-    later[:, lanes(quads)] = coded(factor[4])
-    for c in copies[4:]:
-        c.wait()
-
-
-def flow_kernel(after, flow, ids, turned, pay_a, pay_b, raw, sems):
-    nb = flow.shape[0]
-    chunk = nb // 4
-    copies = [
-        pltpu.make_async_copy(flow.at[pl.ds(c * chunk, chunk)], raw.at[pl.ds(c * chunk, chunk)], sems.at[c])
-        for c in range(4)
-    ]
-    for c in copies:
-        c.start()
+    for n in range(nb):
+        wire[:, lanes(n)] = coded(held[:, lanes(n)] * factor[0 if n < pairs else 1 if n < pairs + quads else 2])
+    wire[:, lanes(nb)] = coded(factor[3])
+    even = right_first()
     pos = lax.axis_index("tile")
-    even = right_first()
-    depth = NBR * BLK
-    for c in range(4):
-        copies[c].wait()
-        for n in range(c * chunk, (c + 1) * chunk):
-            for k in range(NBR):
-                turned[n, k * BLK : (k + 1) * BLK, :] = raw[n, k].T
     line = lax.broadcasted_iota(jnp.int32, (16, BLK), 0)
-    for pay, right in ((pay_a, even), (pay_b, jnp.logical_not(even))):
-        start = jnp.where(right, nb - HALO, 0)
+
+    def edge(pay, block, start):
         away = jnp.zeros((16, BLK), jnp.float32)
         for m in range(HALO):
-            pay[m * depth : (m + 1) * depth, :] = turned[start + m]
             n = start + m + pos * nb
-            for k, gap in enumerate((n - ids[start + m, 1], ids[start + m, 2] - n)):
+            for k in range(NBR):
+                at = (m * NBR + k) * BLK
+                pay[at : at + BLK, :] = block[m, k]
+            for k, gap in enumerate((n - ids[1, start + m], ids[2, start + m] - n)):
                 away = jnp.where(line == 2 * m + k, gap.astype(jnp.float32), away)
-        pay[HALO * depth : HALO * depth + 16, :] = away.astype(jnp.bfloat16)
+        at = HALO * NBR * BLK
+        pay[at : at + 16, :] = away.astype(jnp.bfloat16)
+
+    @pl.when(even)
+    def _():
+        edge(pay_a, right, nb - HALO)
+        edge(pay_b, left, 0)
+
+    @pl.when(jnp.logical_not(even))
+    def _():
+        edge(pay_a, left, 0)
+        edge(pay_b, right, nb - HALO)
+
+
+def stage_kernel(after, flow, wire, growth, prec, obs, anc, rain, turned, *held):
+    for src, dst in zip((wire, growth, prec, obs, anc), held):
+        dst[...] = src[...]
+    held[-1][...] = rain[2:4]
+    for n in range(flow.shape[0]):
+        for k in range(NBR):
+            turned[n, k * BLK : (k + 1) * BLK, :] = flow[n, k].T
 
 
 def halo_flux(ext, pay, right, nb, m):
@@ -153,7 +129,13 @@
         for d in range(HALO + 1):
             x = jnp.where(gap == d, ext[at + sign * d].astype(jnp.float32), x)
         xs.append(x.astype(jnp.bfloat16))
-    return flux_of(xs, pay[m * depth : (m + 1) * depth, :])
+    total = jnp.zeros(ext.shape[1:], jnp.float32)
+    for k, x in enumerate(xs):
+        at = m * depth + k * BLK
+        total += lax.dot_general(
+            x, pay[at : at + BLK, :], (((1,), (1,)), ((), ())), preferred_element_type=jnp.float32
+        )
+    return total
 
 
 def decode(sel, pieces, cols):
@@ -168,7 +150,7 @@
 def open_kernel(members, unroll, *refs):
     pieces = refs[:members]
     anc, growth, prec, obs = refs[members : members + 4]
-    wb, v0, b1, bq, wq, miss, quad, pay_a, pay_b = refs[members + 4 : members + 13]
+    wb, v0, b1, bq, wq, miss, quad, unit1, pay_a, pay_b = refs[members + 4 : members + 14]
     pair, scaler = refs[-2:]
     nb = growth.shape[0]
     slots = anc.shape[1]
@@ -195,14 +177,15 @@
             pair[at : at + slots, :] = hits(2 * h + i % 2, want)
     for g in range(4):
         quad[g * slots : (g + 1) * slots, :] = hits(g, own)
-    for i, (g, want) in enumerate(((0, chosen), (1, chosen), (0, own), (1, own), (2, own))):
+    for i, (g, want) in enumerate(((0, chosen), (1, chosen), (0, own), (1, own), (2, own), (3, own))):
         scaler[i * slots : (i + 1) * slots, :] = hits(g, want)
 
     pairs, quads = nb // 2, nb // 4
-    codes = decode(scaler[...], pieces, lanes(pairs + quads))
+    codes = decode(scaler[...], pieces, lanes(nb))
     scale = [
-        codes[i * slots : (i + 1) * slots] * (BOUNDS[f] / SCALE_STEPS / STEPS) for i, f in enumerate((0, 1, 0, 1, 2))
+        codes[i * slots : (i + 1) * slots] * (BOUNDS[f] / SCALE_STEPS / STEPS) for i, f in enumerate((0, 1, 0, 1, 2, 2))
     ]
+    unit1[...] = scale[5]
 
     def step(m, acc):
         wet = decode(quad[...], pieces, lanes(m, pairs * BLK))
@@ -249,7 +232,7 @@
     base = WIDE - pos * nb
 
     def step(n, acc):
-        w = v0[n] + flux_of((ext[n + WIDE], ext[ids[n, 1] + base], ext[ids[n, 2] + base]), flow[n])
+        w = v0[n] + flux_of((ext[n + WIDE], ext[ids[1, n] + base], ext[ids[2, n] + base]), flow[n])
         wb1[n + HALO] = w.astype(jnp.bfloat16)
         s = wetness(w)
         row = pl.ds(n, 1)
@@ -271,7 +254,7 @@
 
 def day1_kernel(members, unroll, *refs):
     pieces = refs[:members]
-    wb1, v1, b2, quad, flow, ids, anc, rain, w2, ws, bs, v2, pay_a, pay_b = refs[members:]
+    wb1, v1, b2, quad, unit1, flow, ids, anc, rain, w2, ws, bs, v2, pay_a, pay_b = refs[members:]
     nb, slots = v1.shape[:2]
     part = rain.shape[1]
     pos = lax.axis_index("tile")
@@ -280,13 +263,13 @@
     base = HALO - pos * nb
     picks = [anc[1, me * part + i] for i in range(part)]
     quads = nb // 4
-    scale = decode(quad[0:slots, :], pieces, lanes(quads)) * (BOUNDS[2] / SCALE_STEPS / STEPS)
+    scale = unit1[...]
 
     def step(m, carry):
-        wet = decode(quad[...], pieces, lanes(m))
+        wet = decode(quad[...], pieces, lanes(m, 3 * quads * BLK))
         for q in range(4):
             n = m + q * quads
-            flux = flux_of((wb1[n + HALO], wb1[ids[n, 1] + base], wb1[ids[n, 2] + base]), flow[n])
+            flux = flux_of((wb1[n + HALO], wb1[ids[1, n] + base], wb1[ids[2, n] + base]), flow[n])
             w2[n] = v1[n] + flux + wet[q * slots : (q + 1) * slots] * scale
         return carry
 
@@ -324,7 +307,7 @@
 
     def near(ref, n, at):
         base = at - pos * nb
-        return [ref[i].astype(half) for i in (n + at, ids[n, 1] + base, ids[n, 2] + base)]
+        return [ref[i].astype(half) for i in (n + at, ids[1, n] + base, ids[2, n] + base)]
 
     def step2(n, carry):
         ext3[n + HALO] = v2[n] + flux_of(near(ext, n, WIDE), flow[n])
@@ -367,14 +350,19 @@
     run(nb, unroll, step, 0)
 
 
-def call(kernel, out, specs, scratch=(), mib=32):
+def weigh(flops):
+    return pl.CostEstimate(flops=flops, bytes_accessed=1, transcendentals=0)
+
+
+def call(kernel, out, specs, scratch=(), cost=1):
     return pl.pallas_call(
         kernel,
         out_shape=tuple(jax.ShapeDtypeStruct(s, d) for s, d in out),
         in_specs=specs,
         out_specs=tuple(VMEM for _ in out),
         scratch_shapes=list(scratch),
-        compiler_params=pltpu.CompilerParams(vmem_limit_bytes=mib * 2**20),
+        compiler_params=pltpu.CompilerParams(vmem_limit_bytes=32 * 2**20),
+        cost_estimate=weigh(cost),
     )
 
 
@@ -387,56 +375,53 @@
     f32, bf16, i16 = jnp.float32, jnp.bfloat16, jnp.int16
     swap_a = [(i, i ^ 1) for i in range(tiles)]
     swap_b = [(i, (i - 1) % tiles if i % 2 == 0 else (i + 1) % tiles) for i in range(tiles)]
-    pairs, quads = nb // 2, nb // 4
     rows = 4 * part
-
-    wire, later, growth, prec, obs, anc, rain23 = call(
-        pack_kernel,
-        [
-            ((rows, (pairs + quads + 1) * BLK), i16),
-            ((rows, (quads + 1) * BLK), i16),
-            ((nb, BLK), f32),
-            ((nb, BLK), f32),
-            (observations.shape, f32),
-            (ancestors.shape, jnp.int32),
-            ((2, part, cells), f32),
-        ],
-        [HBM] * 7,
-        [
-            pltpu.VMEM((4, part, cells), f32),
-            pltpu.VMEM((rows, (pairs + quads) * BLK), f32),
-            pltpu.VMEM((rows, quads * BLK), f32),
-            pltpu.VMEM((5, rows, BLK), f32),
-            pltpu.SemaphoreType.DMA((9,)),
-        ],
-    )(biomass, water, rain, growth_rate.reshape(nb, BLK), obs_precision.reshape(nb, BLK), observations, ancestors)
-
-    def gathered(x):
-        return [x] + [lax.ppermute(x, "particle", [(i, i ^ j) for i in range(members)]) for j in range(1, members)]
-
-    pieces = gathered(wire)
-    pieces1 = gathered(later)
+    neighbours = neighbours.T
+
     depth = NBR * BLK
     edge = ((HALO * depth + 16, BLK), bf16)
-    flow, flow_a, flow_b = call(
-        flow_kernel,
-        [((nb, depth, BLK), bf16), edge, edge],
-        [HBM, HBM, SMEM],
-        [pltpu.VMEM((nb, NBR, BLK, BLK), bf16), pltpu.SemaphoreType.DMA((4,))],
-    )(wire, flow_blocks, neighbours)
+    tile = (HALO, NBR, BLK, BLK)
+
+    out = [((rows, (nb + 1) * BLK), i16), edge, edge]
+    wire, flow_a, flow_b = pl.pallas_call(
+        pack_kernel,
+        grid=(1,),
+        out_shape=tuple(jax.ShapeDtypeStruct(s, d) for s, d in out),
+        in_specs=[pl.BlockSpec((part, cells), lambda i: (0, 0))] * 2
+        + [pl.BlockSpec((2, part, cells), lambda i: (0, 0, 0))]
+        + [pl.BlockSpec(tile, lambda i: (0, 0, 0, 0)), pl.BlockSpec(tile, lambda i: (nb // HALO - 1, 0, 0, 0)), SMEM],
+        out_specs=tuple(VMEM for _ in out),
+        scratch_shapes=[
+            pltpu.VMEM((rows, cells), f32),
+            pltpu.VMEM((4, rows, BLK), f32),
+        ],
+        compiler_params=pltpu.CompilerParams(vmem_limit_bytes=60 * 2**20),
+        cost_estimate=weigh(1),
+    )(biomass, water, rain, flow_blocks, flow_blocks, neighbours)
+
+    pieces = [wire] + [
+        lax.ppermute(wire, "particle", [(i, i ^ j) for i in range(members)]) for j in range(1, members)
+    ]
+    small = (wire, growth_rate.reshape(nb, BLK), obs_precision.reshape(nb, BLK), observations, ancestors)
+    flow, pieces[0], growth, prec, obs, anc, rain23 = call(
+        stage_kernel,
+        [((nb, depth, BLK), bf16)] + [(x.shape, x.dtype) for x in small] + [((2, part, cells), f32)],
+        [HBM] + [VMEM] * 7,
+    )(pieces[1], flow_blocks, *small, rain)
     flow_a = lax.ppermute(flow_a, "tile", swap_a)
     flow_b = lax.ppermute(flow_b, "tile", swap_b)
 
     field = ((nb, slots, BLK), f32)
-    wb, v0, b1, bq, wq, miss, quad, pay_a, pay_b = call(
+    wb, v0, b1, bq, wq, miss, quad, unit1, pay_a, pay_b = call(
         functools.partial(open_kernel, members, unroll),
-        [((nb, slots, BLK), bf16), field, field, field, field, ((slots, BLK), f32), ((4 * slots, members * rows * 2), bf16)]
+        [((nb, slots, BLK), bf16), field, field, field, field, ((slots, BLK), f32), ((4 * slots, members * rows * 2), bf16), ((slots, BLK), f32)]
         + [((WIDE + 2 * HALO, slots, BLK), bf16)] * 2,
         [VMEM] * (members + 4),
         [
             pltpu.VMEM((8 * slots, members * rows * 2), bf16),
-            pltpu.VMEM((5 * slots, members * rows * 2), bf16),
+            pltpu.VMEM((6 * slots, members * rows * 2), bf16),
         ],
+        cost=10**10,
     )(*pieces, anc, growth, prec, obs)
     got_a = lax.ppermute(pay_a, "tile", swap_a)
     got_b = lax.ppermute(pay_b, "tile", swap_b)
@@ -450,8 +435,8 @@
     w2, ws, bs, v2, end_a, end_b = call(
         functools.partial(day1_kernel, members, unroll),
         [field, few, few, few] + [((WIDE + HALO, part, BLK), f32)] * 2,
-        [VMEM] * (members + 5) + [SMEM] * 2 + [VMEM],
-    )(*pieces1, wb1, v1, b2, quad, flow, neighbours, ancestors, rain23)
+        [VMEM] * (members + 6) + [SMEM] * 2 + [VMEM],
+    )(*pieces, wb1, v1, b2, quad, unit1, flow, neighbours, ancestors, rain23)
     last_a = lax.ppermute(end_a, "tile", swap_a)
     last_b = lax.ppermute(end_b, "tile", swap_b)
 

time: 50.1 us -> 40.1 us (0.80)
  local copies, waits for them, and re-layouts: 8.15 us -> 0.93 us
  starting transfers between devices: 20.5 us -> 17.4 us
  waiting for transfers between devices: 9.2 us -> 10 us
    unnamed x19 -> x16, local copies, waits for them, and re-layouts: 8.15 us -> 0.93 us
    ppermute x6 -> x3, starting transfers between devices: 9.76 us -> 5.62 us  [body(): lax.ppermute(wire, 'particle', [(i, i ^ j) for i in range(members)])]
    ppermute x1, waiting for transfers between devices: 0.27 us -> 2.18 us  [body(): got_b = lax.ppermute(pay_b, 'tile', swap_b)]
    ppermute x6 -> x3, waiting for transfers between devices: 8.9 us -> 7.84 us  [body(): lax.ppermute(wire, 'particle', [(i, i ^ j) for i in range(members)])]
    ppermute x1, starting transfers between devices: 1.39 us -> 2.41 us  [body(): last_b = lax.ppermute(end_b, 'tile', swap_b)]
    ppermute x1, starting transfers between devices: 3.56 us -> 2.56 us  [body(): flow_b = lax.ppermute(flow_b, 'tile', swap_b)]
    ppermute x1, starting transfers between devices: 1.56 us -> 2.55 us  [body(): got_b = lax.ppermute(pay_b, 'tile', swap_b)]
    ppermute x1, starting transfers between devices: 0.52 us -> 0.01 us  [body(): flow_a = lax.ppermute(flow_a, 'tile', swap_a)]
  transfers between devices with their start and end apart: 16 -> 13, of which waited for: 4 -> 3; matrix products, arithmetic and copies ran while one was open for 0% -> 0% of each run, Pallas kernels for 14% -> 14%
where the time goes in v3:
time: 40.1 us; the launch traced here: 40 us
  starting transfers between devices  17.4 us (43%)
  Pallas kernels  10.8 us (27%)
  waiting for transfers between devices  10 us (25%)
  local copies, waits for them, and re-layouts  0.93 us (2%)
  between operations  0.78 us (2%)
    ppermute x3, waiting for transfers between devices, body(): lax.ppermute(wire, 'particle', [(i, i ^ j) for i in range(members)])  7.84 us
    ppermute x3, starting transfers between devices, body(): lax.ppermute(wire, 'particle', [(i, i ^ j) for i in range(members)])  5.62 us
    ppermute x4, starting transfers between devices, shared(): lax.ppermute(x, 'tile', [(i, i ^ m) for i in range(tiles)])  3.72 us
    pallas_call x1, Pallas kernels, body(): call(functools.partial(close_kernel, unroll), [((part, cells), f32)] * 2,...  2.98 us
    ppermute x1, starting transfers between devices, body(): flow_b = lax.ppermute(flow_b, 'tile', swap_b)  2.56 us
    ppermute x1, starting transfers between devices, body(): got_b = lax.ppermute(pay_b, 'tile', swap_b)  2.55 us
    pallas_call x1, Pallas kernels, body(): pl.pallas_call(pack_kernel, grid=(1,), out_shape=tuple((jax.ShapeDtypeStr...  2.52 us
    ppermute x1, starting transfers between devices, body(): last_b = lax.ppermute(end_b, 'tile', swap_b)  2.41 us
  transfers between devices with their start and end apart: 13, of which 3 were waited for; matrix products, arithmetic and copies ran while one was open for 0% of the time, Pallas kernels for 14%

profile of v3, /device:TPU:0, one launch (start us, length us, event | category | flops | bytes accessed | tf_op | source)
XLA Modules:
  0.0 40.0 jit_solution(13915194028430821848)
XLA Ops:
  0.6 0.0 copy-start
  0.6 0.0 copy-start.1
  0.7 0.0 copy-start.3
  0.7 0.0 copy-start.5
  0.7 0.0 copy-start.6
  0.7 0.0 copy-start.7
  0.7 2.5 %shard_map.112 = (s16[16,4224]{1,0:T(8,128)(2,1)}, bf16[1552,128]{1,0:T(8,128)(2,1)}, bf16[1552,128]{1,0:T(8,128)(2,1)}) custom-call(f32[4,4096]{1,0:T(4,128)} %bio.1, f32[4,4096]{1,0:T(4,128)} %wat.1, f32[4,4,4096]{2,1,0:T(4,128)} %rain.3, bf16[32,3,128,128]{3,2,1,0:T(8,128)(2,1)} %flow.1, bf16[32,3,128,128]{3,2,1,0:T(8,128)(2,1)} %flow.1, s32[3,32]{1,0:T(4,128)} %bitcast.3), custom_call_target="tpu_custom_call" | custom-call | flops 1 | bytes 1 | tf_op jit(solution)/shard_map/pallas_call | solution.py:386
  3.2 3.0 %collective-permute-start = (s16[16,4224]{1,0:T(8,128)(2,1)}, s16[16,4224]{1,0:T(8,128)(2,1)S(1)}, u32[]{:S(2)}, u32[]{:S(2)}) collective-permute-start(s16[16,4224]{1,0:T(8,128)(2,1)} %get-tuple-element.35.wire), channel_id=1, source_target_pairs={{0,8},{8,0},{16,24},{24,16},{1,9},{9,1},{17,25},{25,17},{2,10},{10... | collective-permute-start | bytes 405512 | tf_op jit(solution)/shard_map/ppermute | solution.py:403
  6.2 2.5 %collective-permute-start.2 = (s16[16,4224]{1,0:T(8,128)(2,1)}, s16[16,4224]{1,0:T(8,128)(2,1)S(1)}, u32[]{:S(2)}, u32[]{:S(2)}) collective-permute-start(s16[16,4224]{1,0:T(8,128)(2,1)} %get-tuple-element.35.wire), channel_id=1, source_target_pairs={{0,24},{8,16},{16,8},{24,0},{1,25},{9,17},{17,9},{25,1},{2,26},{10... | collective-permute-start | bytes 405512 | tf_op jit(solution)/shard_map/ppermute | solution.py:403
  8.7 0.1 collective-permute-start.1
  8.8 0.0 collective-permute-start.5
  8.8 2.6 %collective-permute-start.6 = (bf16[1552,128]{1,0:T(8,128)(2,1)}, bf16[1552,128]{1,0:T(8,128)(2,1)S(1)}, u32[]{:S(2)}, u32[]{:S(2)}) collective-permute-start(bf16[1552,128]{1,0:T(8,128)(2,1)} %get-tuple-element.48), channel_id=1, source_target_pairs={{0,7},{1,2},{2,1},{3,4},{4,3},{5,6},{6,5},{7,0},{8,15},{9,10},{10,... | collective-permute-start | bytes 1191944 | tf_op jit(solution)/shard_map/ppermute | solution.py:412
  11.4 0.0 collective-permute-done.after.refs_1_
  11.4 0.0 copy-done
  11.4 0.0 copy-done.1
  11.4 0.0 copy-done.3
  11.4 0.0 copy-done.5
  11.4 0.0 copy-done.6
  11.4 0.0 copy-done.7
  11.4 0.0 copy-start.2
  11.5 0.9 %copy-done.2 = s16[16,4224]{1,0:T(8,128)(2,1)S(1)} copy-done((s16[16,4224]{1,0:T(8,128)(2,1)S(1)}, s16[16,4224]{1,0:T(8,128)(2,1)}, u32[]{:S(2)}) %copy-start.2) | copy-done | bytes 135192
  12.4 0.9 %shard_map.113 = (bf16[32,384,128]{2,1,0:T(8,128)(2,1)S(1)}, s16[16,4224]{1,0:T(8,128)(2,1)S(1)}, f32[32,128]{1,0:T(8,128)S(1)}, f32[32,128]{1,0:T(8,128)S(1)}, ...) custom-call(s16[16,4224]{1,0:T(8,128)(2,1)S(1)} %collective-permute-done.after.refs_1_, ...), custom_call_target="tpu_custom_call" | custom-call | flops 1 | bytes 1 | tf_op jit(solution)/shard_map/pallas_call | solution.py:406
  13.2 3.1 %collective-permute-done.2.refs_3_ = s16[16,4224]{1,0:T(8,128)(2,1)S(1)} collective-permute-done((s16[16,4224]{1,0:T(8,128)(2,1)}, s16[16,4224]{1,0:T(8,128)(2,1)S(1)}, u32[]{:S(2)}, u32[]{:S(2)}) %collective-permute-start.2) | collective-permute-done | bytes 135200 | tf_op jit(solution)/shard_map/ppermute | solution.py:403
  16.4 4.7 %collective-permute-done.1.refs_2_ = s16[16,4224]{1,0:T(8,128)(2,1)S(1)} collective-permute-done((s16[16,4224]{1,0:T(8,128)(2,1)}, s16[16,4224]{1,0:T(8,128)(2,1)S(1)}, u32[]{:S(2)}, u32[]{:S(2)}) %collective-permute-start.1) | collective-permute-done | bytes 135200 | tf_op jit(solution)/shard_map/ppermute | solution.py:403
  21.1 0.5 %shard_map.114 = (bf16[32,16,128]{2,1,0:T(8,128)(2,1)S(1)}, f32[32,16,128]{2,1,0:T(8,128)S(1)}, f32[32,16,128]{2,1,0:T(8,128)S(1)}, f32[32,16,128]{2,1,0:T(8,128...) custom-call(s16[16,4224]{1,0:T(8,128)(2,1)S(1)} %get-tuple-element.3, ...), custom_call_target="tpu_custom_call" | custom-call | flops 10000000000 | bytes 1 | tf_op jit(solution)/shard_map/pallas_call | solution.py:415
  21.6 0.1 collective-permute-start.3
  21.7 2.6 %collective-permute-start.4 = (bf16[16,16,128]{2,1,0:T(8,128)(2,1)S(1)}, bf16[16,16,128]{2,1,0:T(8,128)(2,1)S(1)}, u32[]{:S(2)}, u32[]{:S(2)}) collective-permute-start(bf16[16,16,128]{2,1,0:T(8,128)(2,1)S(1)} %get-tuple-element.45), channel_id=1, source_target_pairs={{0,7},{1,2},{2,1},{3,4},{4,3},{5,6},{6,5},{7,0},{8,15},{9,10},{10,... | collective-permute-start | bytes 196616 | tf_op jit(solution)/shard_map/ppermute | solution.py:427
  24.2 0.0 collective-permute-done.3.got_a
  24.2 2.2 %collective-permute-done.4.got_b = bf16[16,16,128]{2,1,0:T(8,128)(2,1)S(1)} collective-permute-done((bf16[16,16,128]{2,1,0:T(8,128)(2,1)S(1)}, bf16[16,16,128]{2,1,0:T(8,128)(2,1)S(1)}, u32[]{:S(2)}, u32[]{:S(2)}) %collective-permute-start.4) | collective-permute-done | bytes 65568 | tf_op jit(solution)/shard_map/ppermute | solution.py:427
  26.4 0.0 collective-permute-done.5.flow_a
  26.4 0.0 collective-permute-done.6.flow_b
  26.4 0.0 copy-done.4
  26.4 1.6 %shard_map.115 = (bf16[40,16,128]{2,1,0:T(8,128)(2,1)S(1)}, f32[32,16,128]{2,1,0:T(8,128)S(1)}, f32[32,16,128]{2,1,0:T(8,128)S(1)}, f32[32,128]{1,0:T(8,128)S(1)}) custom-call(bf16[32,16,128]{2,1,0:T(8,128)(2,1)S(1)} %get-tuple-element.41.wb, f32[32,16,128]{2,1,0:T(8,128)S(1)} %get-tuple-element.42.v0, f32[32,16,128]{2,1,0:T(8,128)S(1)} %get-tuple-element.43.b1, ...), custom_call_target="tpu_custom_call" | custom-call | flops 1 | bytes 1 | tf_op jit(solution)/shard_map/pallas_call | solution.py:428
  28.1 0.2 collective-permute-start.7
  28.2 1.4 %shard_map.116 = (f32[32,16,128]{2,1,0:T(8,128)S(1)}, f32[32,4,128]{2,1,0:T(4,128)S(1)}, f32[32,4,128]{2,1,0:T(4,128)S(1)}, f32[32,4,128]{2,1,0:T(4,128)S(1)}, f...) custom-call(s16[16,4224]{1,0:T(8,128)(2,1)S(1)} %get-tuple-element.36.refs_0_, ...), custom_call_target="tpu_custom_call" | custom-call | flops 1 | bytes 1 | tf_op jit(solution)/shard_map/pallas_call | solution.py:435
  29.6 0.5 %collective-permute-start.11 = (f32[12,4,128]{2,1,0:T(4,128)S(1)}, f32[12,4,128]{2,1,0:T(4,128)S(1)}, u32[]{:S(2)}, u32[]{:S(2)}) collective-permute-start(f32[12,4,128]{2,1,0:T(4,128)S(1)} %get-tuple-element.63), channel_id=1, source_target_pairs={{0,1},{1,0},{2,3},{3,2},{4,5},{5,4},{6,7},{7,6},{8,9},{9,8},{10,11... | collective-permute-start | bytes 73736 | tf_op jit(solution)/shard_map/ppermute | solution.py:440
  30.1 2.4 %collective-permute-start.12 = (f32[12,4,128]{2,1,0:T(4,128)S(1)}, f32[12,4,128]{2,1,0:T(4,128)S(1)}, u32[]{:S(2)}, u32[]{:S(2)}) collective-permute-start(f32[12,4,128]{2,1,0:T(4,128)S(1)} %get-tuple-element.64), channel_id=1, source_target_pairs={{0,7},{1,2},{2,1},{3,4},{4,3},{5,6},{6,5},{7,0},{8,15},{9,10},{10,... | collective-permute-start | bytes 73736 | tf_op jit(solution)/shard_map/ppermute | solution.py:441
  32.5 0.0 collective-permute-done.7
  32.5 0.6 %collective-permute-start.10 = (f32[32,128]{1,0:T(8,128)S(1)}, f32[32,128]{1,0:T(8,128)S(1)}, u32[]{:S(2)}, u32[]{:S(2)}) collective-permute-start(f32[32,128]{1,0:T(8,128)S(1)} %add.3.refs_0_), channel_id=1, source_target_pairs={{0,6},{1,7},{2,4},{3,5},{4,2},{5,3},{6,0},{7,1},{8,14},{9,15},{10,... | collective-permute-start | bytes 49160 | tf_op jit(solution)/shard_map/ppermute | solution.py:444
  33.1 0.3 collective-permute-start.9
  33.4 2.7 %collective-permute-start.8 = (f32[32,128]{1,0:T(8,128)S(1)}, f32[32,128]{1,0:T(8,128)S(1)}, u32[]{:S(2)}, u32[]{:S(2)}) collective-permute-start(f32[32,128]{1,0:T(8,128)S(1)} %add.3.refs_0_), channel_id=1, source_target_pairs={{0,2},{1,3},{2,0},{3,1},{4,6},{5,7},{6,4},{7,5},{8,10},{9,11},{10,... | collective-permute-start | bytes 49160 | tf_op jit(solution)/shard_map/ppermute | solution.py:444
  36.1 0.0 collective-permute-done.11.got_a
  36.1 0.0 collective-permute-done.12.got_b
  36.1 3.0 %shard_map.118 = (f32[4,4096]{1,0:T(4,128)}, f32[4,4096]{1,0:T(4,128)}) custom-call(f32[32,4,128]{2,1,0:T(4,128)S(1)} %get-tuple-element.60.ws, f32[32,4,128]{2,1,0:T(4,128)S(1)} %get-tuple-element.61.bs, f32[32,4,128]{2,1,0:T(4,128)S(1)} %get-tuple-element.62.v2, f32[12,4,128]{2,1,0:T(4,128)S(1)} %collective-permute-done.11.got_a, ...), custom_call_target="tpu_custom_call" | custom-call | flops 1 | bytes 1 | tf_op jit(solution)/shard_map/pallas_call | solution.py:453
  39.1 0.0 collective-permute-done.10.refs_3_
  39.1 0.0 collective-permute-done.9.refs_2_
  39.1 0.0 collective-permute-done.8.refs_1_
  39.1 0.9 %shard_map.117 = f32[2,2,4096]{2,1,0:T(2,128)} custom-call(f32[32,128]{1,0:T(8,128)S(1)} %add.3.refs_0_, f32[32,128]{1,0:T(8,128)S(1)} %collective-permute-done.8.refs_1_, f32[32,128]{1,0:T(8,128)S(1)} %collective-permute-done.9.refs_2_, f32[32,128]{1,0:T(8,128)S(1)} %collective-permute-done.10.refs_3_, f32[32,16,128]{2,1,0:T(8,128)S(1)} %get-tuple-element.51.refs_4_, ...), custom_call_target="tpu_custom_call" | custom-call | flops 1 | bytes 1 | tf_op jit(solution)/shard_map/pallas_call | solution.py:459
  (2 shorter events, 0.0 us)
Async XLA Ops:
  0.6 10.8 %copy-start = (bf16[32,3,128,128]{3,2,1,0:T(8,128)(2,1)S(1)}, bf16[32,3,128,128]{3,2,1,0:T(8,128)(2,1)}, u32[]{:S(2)}) copy-start(bf16[32,3,128,128]{3,2,1,0:T(8,128)(2,1)} %flow.1) | copy-start | bytes 9437188
  0.6 10.8 %copy-start.1 = (f32[4,4,4096]{2,1,0:T(4,128)S(1)}, f32[4,4,4096]{2,1,0:T(4,128)}, u32[]{:S(2)}) copy-start(f32[4,4,4096]{2,1,0:T(4,128)} %rain.3) | copy-start | bytes 786436
  0.7 10.8 %copy-start.3 = (f32[2,4096]{1,0:T(2,128)S(1)}, f32[2,4096]{1,0:T(2,128)}, u32[]{:S(2)}) copy-start(f32[2,4096]{1,0:T(2,128)} %obs.1) | copy-start | bytes 98308
  0.7 10.8 %copy-start.5 = (f32[4096]{0:T(1024)S(1)}, f32[4096]{0:T(1024)}, u32[]{:S(2)}) copy-start(f32[4096]{0:T(1024)} %param.14) | copy-start | bytes 49156
  0.7 10.8 %copy-start.6 = (f32[4096]{0:T(1024)S(1)}, f32[4096]{0:T(1024)}, u32[]{:S(2)}) copy-start(f32[4096]{0:T(1024)} %param.16) | copy-start | bytes 49156
  0.7 10.8 %copy-start.7 = (s32[2,16]{1,0:T(2,128)S(1)}, s32[2,16]{1,0:T(2,128)}, u32[]{:S(2)}) copy-start(s32[2,16]{1,0:T(2,128)} %refs_11_.1) | copy-start | bytes 388
  3.2 8.2 %collective-permute-start = (s16[16,4224]{1,0:T(8,128)(2,1)}, s16[16,4224]{1,0:T(8,128)(2,1)S(1)}, u32[]{:S(2)}, u32[]{:S(2)}) collective-permute-start(s16[16,4224]{1,0:T(8,128)(2,1)} %get-tuple-element.35.wire), channel_id=1, source_target_pairs={{0,8},{8,0},{16,24},{24,16},{1,9},{9,1},{17,25},{25,17},{2,10},{10... | collective-permute-start | bytes 405512 | tf_op jit(solution)/shard_map/ppermute | solution.py:403
  6.2 10.1 %collective-permute-start.2 = (s16[16,4224]{1,0:T(8,128)(2,1)}, s16[16,4224]{1,0:T(8,128)(2,1)S(1)}, u32[]{:S(2)}, u32[]{:S(2)}) collective-permute-start(s16[16,4224]{1,0:T(8,128)(2,1)} %get-tuple-element.35.wire), channel_id=1, source_target_pairs={{0,24},{8,16},{16,8},{24,0},{1,25},{9,17},{17,9},{25,1},{2,26},{10... | collective-permute-start | bytes 405512 | tf_op jit(solution)/shard_map/ppermute | solution.py:403
  8.7 12.3 %collective-permute-start.1 = (s16[16,4224]{1,0:T(8,128)(2,1)}, s16[16,4224]{1,0:T(8,128)(2,1)S(1)}, u32[]{:S(2)}, u32[]{:S(2)}) collective-permute-start(s16[16,4224]{1,0:T(8,128)(2,1)} %get-tuple-element.35.wire), channel_id=1, source_target_pairs={{0,16},{8,24},{16,0},{24,8},{1,17},{9,25},{17,1},{25,9},{2,18},{10... | collective-permute-start | bytes 405512 | tf_op jit(solution)/shard_map/ppermute | solution.py:403
  8.8 17.6 %collective-permute-start.5 = (bf16[1552,128]{1,0:T(8,128)(2,1)}, bf16[1552,128]{1,0:T(8,128)(2,1)S(1)}, u32[]{:S(2)}, u32[]{:S(2)}) collective-permute-start(bf16[1552,128]{1,0:T(8,128)(2,1)} %get-tuple-element.47), channel_id=1, source_target_pairs={{0,1},{1,0},{2,3},{3,2},{4,5},{5,4},{6,7},{7,6},{8,9},{9,8},{10,11... | collective-permute-start | bytes 1191944 | tf_op jit(solution)/shard_map/ppermute | solution.py:411
  8.8 17.6 %collective-permute-start.6 = (bf16[1552,128]{1,0:T(8,128)(2,1)}, bf16[1552,128]{1,0:T(8,128)(2,1)S(1)}, u32[]{:S(2)}, u32[]{:S(2)}) collective-permute-start(bf16[1552,128]{1,0:T(8,128)(2,1)} %get-tuple-element.48), channel_id=1, source_target_pairs={{0,7},{1,2},{2,1},{3,4},{4,3},{5,6},{6,5},{7,0},{8,15},{9,10},{10,... | collective-permute-start | bytes 1191944 | tf_op jit(solution)/shard_map/ppermute | solution.py:412
  11.4 0.9 %copy-start.2 = (s16[16,4224]{1,0:T(8,128)(2,1)S(1)}, s16[16,4224]{1,0:T(8,128)(2,1)}, u32[]{:S(2)}) copy-start(s16[16,4224]{1,0:T(8,128)(2,1)} %get-tuple-element.35.wire) | copy-start | bytes 405508
  21.1 5.4 %copy-start.4 = (s32[32,3]{0,1:T(4,128)S(1)}, s32[32,3]{0,1:T(4,128)}, u32[]{:S(2)}) copy-start(s32[32,3]{0,1:T(4,128)} %param.12) | copy-start | bytes 1156
  21.6 2.6 %collective-permute-start.3 = (bf16[16,16,128]{2,1,0:T(8,128)(2,1)S(1)}, bf16[16,16,128]{2,1,0:T(8,128)(2,1)S(1)}, u32[]{:S(2)}, u32[]{:S(2)}) collective-permute-start(bf16[16,16,128]{2,1,0:T(8,128)(2,1)S(1)} %get-tuple-element.44), channel_id=1, source_target_pairs={{0,1},{1,0},{2,3},{3,2},{4,5},{5,4},{6,7},{7,6},{8,9},{9,8},{10,11... | collective-permute-start | bytes 196616 | tf_op jit(solution)/shard_map/ppermute | solution.py:426
  21.7 4.7 %collective-permute-start.4 = (bf16[16,16,128]{2,1,0:T(8,128)(2,1)S(1)}, bf16[16,16,128]{2,1,0:T(8,128)(2,1)S(1)}, u32[]{:S(2)}, u32[]{:S(2)}) collective-permute-start(bf16[16,16,128]{2,1,0:T(8,128)(2,1)S(1)} %get-tuple-element.45), channel_id=1, source_target_pairs={{0,7},{1,2},{2,1},{3,4},{4,3},{5,6},{6,5},{7,0},{8,15},{9,10},{10,... | collective-permute-start | bytes 196616 | tf_op jit(solution)/shard_map/ppermute | solution.py:427
  28.1 4.5 %collective-permute-start.7 = (f32[32,128]{1,0:T(8,128)S(1)}, f32[32,128]{1,0:T(8,128)S(1)}, u32[]{:S(2)}, u32[]{:S(2)}) collective-permute-start(f32[32,128]{1,0:T(8,128)S(1)} %get-tuple-element.50), channel_id=1, source_target_pairs={{0,1},{1,0},{2,3},{3,2},{4,5},{5,4},{6,7},{7,6},{8,9},{9,8},{10,11... | collective-permute-start | bytes 49160 | tf_op jit(solution)/shard_map/ppermute | solution.py:444
  29.6 6.4 %collective-permute-start.11 = (f32[12,4,128]{2,1,0:T(4,128)S(1)}, f32[12,4,128]{2,1,0:T(4,128)S(1)}, u32[]{:S(2)}, u32[]{:S(2)}) collective-permute-start(f32[12,4,128]{2,1,0:T(4,128)S(1)} %get-tuple-element.63), channel_id=1, source_target_pairs={{0,1},{1,0},{2,3},{3,2},{4,5},{5,4},{6,7},{7,6},{8,9},{9,8},{10,11... | collective-permute-start | bytes 73736 | tf_op jit(solution)/shard_map/ppermute | solution.py:440
  30.1 6.0 %collective-permute-start.12 = (f32[12,4,128]{2,1,0:T(4,128)S(1)}, f32[12,4,128]{2,1,0:T(4,128)S(1)}, u32[]{:S(2)}, u32[]{:S(2)}) collective-permute-start(f32[12,4,128]{2,1,0:T(4,128)S(1)} %get-tuple-element.64), channel_id=1, source_target_pairs={{0,7},{1,2},{2,1},{3,4},{4,3},{5,6},{6,5},{7,0},{8,15},{9,10},{10,... | collective-permute-start | bytes 73736 | tf_op jit(solution)/shard_map/ppermute | solution.py:441
  32.5 6.5 %collective-permute-start.10 = (f32[32,128]{1,0:T(8,128)S(1)}, f32[32,128]{1,0:T(8,128)S(1)}, u32[]{:S(2)}, u32[]{:S(2)}) collective-permute-start(f32[32,128]{1,0:T(8,128)S(1)} %add.3.refs_0_), channel_id=1, source_target_pairs={{0,6},{1,7},{2,4},{3,5},{4,2},{5,3},{6,0},{7,1},{8,14},{9,15},{10,... | collective-permute-start | bytes 49160 | tf_op jit(solution)/shard_map/ppermute | solution.py:444
  33.1 6.0 %collective-permute-start.9 = (f32[32,128]{1,0:T(8,128)S(1)}, f32[32,128]{1,0:T(8,128)S(1)}, u32[]{:S(2)}, u32[]{:S(2)}) collective-permute-start(f32[32,128]{1,0:T(8,128)S(1)} %add.3.refs_0_), channel_id=1, source_target_pairs={{0,4},{1,5},{2,6},{3,7},{4,0},{5,1},{6,2},{7,3},{8,12},{9,13},{10,... | collective-permute-start | bytes 49160 | tf_op jit(solution)/shard_map/ppermute | solution.py:444
  33.4 5.7 %collective-permute-start.8 = (f32[32,128]{1,0:T(8,128)S(1)}, f32[32,128]{1,0:T(8,128)S(1)}, u32[]{:S(2)}, u32[]{:S(2)}) collective-permute-start(f32[32,128]{1,0:T(8,128)S(1)} %add.3.refs_0_), channel_id=1, source_target_pairs={{0,2},{1,3},{2,0},{3,1},{4,6},{5,7},{6,4},{7,5},{8,10},{9,11},{10,... | collective-permute-start | bytes 49160 | tf_op jit(solution)/shard_map/ppermute | solution.py:444

commit v4 on v3

--- a/solution.py
+++ b/solution.py
@@ -20,12 +20,12 @@
 HBM = pl.BlockSpec(memory_space=pltpu.HBM)
 
 
-def run(count, unroll, step, carry):
+def run(first, last, unroll, step, carry):
     if unroll:
-        for n in range(count):
+        for n in range(first, last):
             carry = step(n, carry)
         return carry
-    return lax.fori_loop(0, count, step, carry)
+    return lax.fori_loop(first, last, step, carry)
 
 
 def lanes(n, at=0):
@@ -47,9 +47,7 @@
     return lax.rem(lax.axis_index("tile"), 2) == 0
 
 
-def pack_kernel(
-    bio, wat, rain, left, right, ids, wire, pay_a, pay_b, held, factor
-):
+def pack_kernel(bio, wat, rain, wire, held, factor):
     part, cells = bio.shape
     nb = cells // BLK
     half, quarter = cells // 2, cells // 4
@@ -82,6 +80,10 @@
     for n in range(nb):
         wire[:, lanes(n)] = coded(held[:, lanes(n)] * factor[0 if n < pairs else 1 if n < pairs + quads else 2])
     wire[:, lanes(nb)] = coded(factor[3])
+
+
+def edge_kernel(after, left, right, ids, pay_a, pay_b):
+    nb = ids.shape[1]
     even = right_first()
     pos = lax.axis_index("tile")
     line = lax.broadcasted_iota(jnp.int32, (16, BLK), 0)
@@ -207,7 +209,7 @@
                 acc = acc + prec[row, :] * (off * off)
         return acc
 
-    miss[...] = run(quads, unroll, step, jnp.zeros((slots, BLK), jnp.float32))
+    miss[...] = run(0, quads, unroll, step, jnp.zeros((slots, BLK), jnp.float32))
     even = right_first()
     for pay, right in ((pay_a, even), (pay_b, jnp.logical_not(even))):
         pay[0:WIDE] = wb[pl.ds(jnp.where(right, nb - WIDE, 0), WIDE)]
@@ -217,119 +219,198 @@
         pay[WIDE + HALO : WIDE + 2 * HALO] = (edge - top.astype(jnp.float32)).astype(jnp.bfloat16)
 
 
-def day0_kernel(
-    unroll, wb, v0, b1, got_a, got_b, flow, flow_a, flow_b, ids, growth, prec, obs, miss,
-    wb1, v1, b2, total, ext,
+def inner01_kernel(members, unroll, *refs):
+    pieces = refs[:members]
+    wb, v0, b1, quad, unit1, flow, ids, growth, prec, obs, anc, rain = refs[members : members + 12]
+    r1, wb1, v1, b2, w2, ws, bs, v2, miss = refs[members + 12 :]
+    nb, slots = wb.shape[:2]
+    part = rain.shape[1]
+    quads = nb // 4
+    scale = unit1[...]
+    base = lax.axis_index("tile") * nb
+
+    def wet_day(m, carry):
+        got = decode(quad[...], pieces, lanes(m, 3 * quads * BLK))
+        for q in range(4):
+            r1[m + q * quads] = got[q * slots : (q + 1) * slots] * scale
+        return carry
+
+    run(0, quads, unroll, wet_day, 0)
+
+    def day0(n, acc):
+        w = v0[n] + flux_of((wb[n], wb[ids[1, n] - base], wb[ids[2, n] - base]), flow[n])
+        wb1[n - HALO] = w.astype(jnp.bfloat16)
+        b, v, acc = settle(n, w, b1, r1, growth, prec, obs, acc)
+        b2[n - HALO] = b
+        v1[n - HALO] = v
+        return acc
+
+    miss[...] = run(HALO, nb - HALO, unroll, day0, jnp.zeros((slots, BLK), jnp.float32))
+    base = base + HALO
+
+    def day1(n, carry):
+        w2[n - WIDE] = v1[n - HALO] + flux_of((wb1[n - HALO], wb1[ids[1, n] - base], wb1[ids[2, n] - base]), flow[n])
+        return carry
+
+    run(WIDE, nb - WIDE, unroll, day1, 0)
+    picks = ancestors_of(anc, part)
+
+    def pick(n, carry):
+        m = n - WIDE
+        choose(picks, w2.at[m], b2.at[n - HALO], rain[0, :, lanes(n)], ws.at[m], bs.at[m], v2.at[m])
+        return carry
+
+    run(WIDE, nb - WIDE, unroll, pick, 0)
+
+
+def settle(n, w, b1, r1, growth, prec, obs, acc):
+    s = wetness(w)
+    row = pl.ds(n, 1)
+    b = b1[n]
+    v = w + r1[n] - 0.2 * b * s
+    b = b + growth[row, :] * b * (s - 0.4 * b)
+    off = b - obs[1:2, lanes(n)]
+    return b, v, acc + prec[row, :] * (off * off)
+
+
+def ancestors_of(anc, part):
+    return [anc[1, lax.axis_index("particle") * part + i] for i in range(part)]
+
+
+def choose(picks, w2, b2, rain, ws, bs, v2):
+    for i, p in enumerate(picks):
+        ws[i : i + 1, :] = w2[pl.ds(p, 1), :]
+        bs[i : i + 1, :] = b2[pl.ds(p, 1), :]
+    w = ws[...]
+    v2[...] = w + rain - 0.2 * bs[...] * wetness(w)
+
+
+def outer01_kernel(
+    unroll, wb, v0, b1, r1, wb1, v1, b2, wi, bi, vi, miss0, miss1, got_a, got_b, flow, flow_a, flow_b, ids,
+    growth, prec, obs, anc, rain, b2_out, w2_out, ws, bs, v2, total, pay_a, pay_b, ext, ext1, v1_out,
 ):
-    nb = growth.shape[0]
-    slots = wb.shape[1]
+    nb, slots = wb.shape[:2]
+    part = rain.shape[1]
     pos = lax.axis_index("tile")
     even = right_first()
-    ext[WIDE : WIDE + nb] = wb[...]
+    lows, highs = (0, WIDE + HALO), (nb - WIDE - HALO, nb)
+    for lo, hi in (lows, highs):
+        ext[WIDE + lo : WIDE + hi] = wb[lo:hi]
+    ext1[WIDE : 2 * WIDE] = wb1[0:WIDE]
+    ext1[nb - WIDE : nb] = wb1[nb - 2 * HALO - WIDE : nb - 2 * HALO]
     sides = ((got_a, flow_a, even), (got_b, flow_b, jnp.logical_not(even)))
     for got, _, right in sides:
         ext[pl.ds(jnp.where(right, nb + WIDE, 0), WIDE)] = got[0:WIDE]
     base = WIDE - pos * nb
 
-    def step(n, acc):
+    def day0(n, acc):
         w = v0[n] + flux_of((ext[n + WIDE], ext[ids[1, n] + base], ext[ids[2, n] + base]), flow[n])
-        wb1[n + HALO] = w.astype(jnp.bfloat16)
-        s = wetness(w)
-        row = pl.ds(n, 1)
-        b = b1[n]
-        v1[n] = w - 0.2 * b * s
-        b = b + growth[row, :] * b * (s - 0.4 * b)
-        b2[n] = b
-        off = b - obs[1:2, lanes(n)]
-        return acc + prec[row, :] * (off * off)
-
-    total[0:slots, :] = miss[...]
-    total[slots : 2 * slots, :] = run(nb, unroll, step, jnp.zeros((slots, BLK), jnp.float32))
+        ext1[n + HALO] = w.astype(jnp.bfloat16)
+        b, v, acc = settle(n, w, b1, r1, growth, prec, obs, acc)
+        m = n if n < HALO else n - (nb - 2 * HALO)
+        b2_out[m] = b
+        v1_out[m] = v
+        return acc
+
+    acc = miss1[...]
+    for n in (*range(HALO), *range(nb - HALO, nb)):
+        acc = day0(n, acc)
+    total[0:slots, :] = miss0[...]
+    total[slots : 2 * slots, :] = acc
     for got, pay, right in sides:
         spot = jnp.where(right, nb + HALO, 0)
         for m in range(HALO):
             edge = got[WIDE + m].astype(jnp.float32) + got[WIDE + HALO + m].astype(jnp.float32)
-            wb1[spot + m] = (edge + halo_flux(ext, pay, right, nb, m)).astype(jnp.bfloat16)
-
-
-def day1_kernel(members, unroll, *refs):
-    pieces = refs[:members]
-    wb1, v1, b2, quad, unit1, flow, ids, anc, rain, w2, ws, bs, v2, pay_a, pay_b = refs[members:]
-    nb, slots = v1.shape[:2]
-    part = rain.shape[1]
-    pos = lax.axis_index("tile")
-    me = lax.axis_index("particle")
-    even = right_first()
+            ext1[spot + m] = (edge + halo_flux(ext, pay, right, nb, m)).astype(jnp.bfloat16)
     base = HALO - pos * nb
-    picks = [anc[1, me * part + i] for i in range(part)]
-    quads = nb // 4
-    scale = unit1[...]
-
-    def step(m, carry):
-        wet = decode(quad[...], pieces, lanes(m, 3 * quads * BLK))
-        for q in range(4):
-            n = m + q * quads
-            flux = flux_of((wb1[n + HALO], wb1[ids[1, n] + base], wb1[ids[2, n] + base]), flow[n])
-            w2[n] = v1[n] + flux + wet[q * slots : (q + 1) * slots] * scale
+    picks = ancestors_of(anc, part)
+    ws[WIDE : nb - WIDE] = wi[...]
+    bs[WIDE : nb - WIDE] = bi[...]
+    v2[WIDE : nb - WIDE] = vi[...]
+    for n in (*range(WIDE), *range(nb - WIDE, nb)):
+        m = n if n < WIDE else n - (nb - 2 * WIDE)
+        if n < HALO or n >= nb - HALO:
+            at = n if n < HALO else n - (nb - 2 * HALO)
+            v, b = v1_out[at], b2_out.at[at]
+        else:
+            v, b = v1[n - HALO], b2.at[n - HALO]
+        w2_out[m] = v + flux_of((ext1[n + HALO], ext1[ids[1, n] + base], ext1[ids[2, n] + base]), flow[n])
+        choose(picks, w2_out.at[m], b, rain[0, :, lanes(n)], ws.at[n], bs.at[n], v2.at[n])
+    for pay, right in ((pay_a, even), (pay_b, jnp.logical_not(even))):
+        for m in range(WIDE):
+            pay[m * part : (m + 1) * part, :] = ws[jnp.where(right, nb - WIDE, 0) + m]
+        for m in range(HALO):
+            pay[(WIDE + m) * part : (WIDE + m + 1) * part, :] = v2[jnp.where(right, nb - HALO, 0) + m]
+    at = (WIDE + HALO) * part
+    pay_a[at : at + 2 * slots, :] = total[...]
+
+
+def inner23_kernel(unroll, ws, bs, v2, flow, ids, growth, rain, w3, wat, bio):
+    nb = ws.shape[0]
+    base = lax.axis_index("tile") * nb
+    half = jnp.bfloat16
+
+    def day2(n, carry):
+        xs = [ws[i].astype(half) for i in (n, ids[1, n] - base, ids[2, n] - base)]
+        w3[n - HALO] = v2[n] + flux_of(xs, flow[n])
         return carry
 
-    run(quads, unroll, step, 0)
-
-    def pick(n, carry):
-        for i in range(part):
-            ws[n, i : i + 1, :] = w2[n, pl.ds(picks[i], 1), :]
-            bs[n, i : i + 1, :] = b2[n, pl.ds(picks[i], 1), :]
-        w = ws[n]
-        v2[n] = w + rain[0, :, lanes(n)] - 0.2 * bs[n] * wetness(w)
+    run(HALO, nb - HALO, unroll, day2, 0)
+
+    def day3(n, carry):
+        xs = [w3[i - HALO].astype(half) for i in (n, ids[1, n] - base, ids[2, n] - base)]
+        m = n - WIDE
+        wat[m], bio[m] = final(n, w3[n - HALO], flux_of(xs, flow[n]), ws[n], bs[n], growth, rain)
         return carry
 
-    run(nb, unroll, pick, 0)
-    for pay, right in ((pay_a, even), (pay_b, jnp.logical_not(even))):
-        pay[0:WIDE] = ws[pl.ds(jnp.where(right, nb - WIDE, 0), WIDE)]
-        pay[WIDE : WIDE + HALO] = v2[pl.ds(jnp.where(right, nb - HALO, 0), HALO)]
-
-
-def close_kernel(
-    unroll, ws, bs, v2, got_a, got_b, flow, flow_a, flow_b, ids, growth, rain, bio_out, wat_out, ext, ext3
+    run(WIDE, nb - WIDE, unroll, day3, 0)
+
+
+def final(n, w3, flux, w, b, growth, rain):
+    g = growth[pl.ds(n, 1), :]
+    b = b + g * b * (wetness(w) - 0.4 * b)
+    s = wetness(w3)
+    return w3 + flux + rain[1, :, lanes(n)] - 0.2 * b * s, b + g * b * (s - 0.4 * b)
+
+
+def outer23_kernel(
+    ws, bs, v2, w3, wat, bio, got_a, got_b, flow, flow_a, flow_b, ids, growth, rain,
+    bio_out, wat_out, ext, ext3,
 ):
-    nb = growth.shape[0]
+    nb, part = ws.shape[:2]
     pos = lax.axis_index("tile")
     even = right_first()
     half = jnp.bfloat16
-    ext[WIDE : WIDE + nb] = ws[...]
+    for n in range(WIDE, nb - WIDE):
+        wat_out[:, lanes(n)] = wat[n - WIDE]
+        bio_out[:, lanes(n)] = bio[n - WIDE]
+    for lo, hi in ((0, WIDE + HALO), (nb - WIDE - HALO, nb)):
+        ext[WIDE + lo : WIDE + hi] = ws[lo:hi]
+    ext3[WIDE : 2 * WIDE] = w3[0:WIDE]
+    ext3[nb - WIDE : nb] = w3[nb - 2 * HALO - WIDE : nb - 2 * HALO]
     sides = ((got_a, flow_a, even), (got_b, flow_b, jnp.logical_not(even)))
     for got, _, right in sides:
-        ext[pl.ds(jnp.where(right, nb + WIDE, 0), WIDE)] = got[0:WIDE]
+        for m in range(WIDE):
+            ext[jnp.where(right, nb + WIDE, 0) + m] = got[m * part : (m + 1) * part, :]
+    base = WIDE - pos * nb
+    for n in (*range(HALO), *range(nb - HALO, nb)):
+        xs = [ext[i].astype(half) for i in (n + WIDE, ids[1, n] + base, ids[2, n] + base)]
+        ext3[n + HALO] = v2[n] + flux_of(xs, flow[n])
     for got, pay, right in sides:
         spot = jnp.where(right, nb + HALO, 0)
         for m in range(HALO):
-            ext3[spot + m] = got[WIDE + m] + halo_flux(ext, pay, right, nb, m)
-
-    def near(ref, n, at):
-        base = at - pos * nb
-        return [ref[i].astype(half) for i in (n + at, ids[1, n] + base, ids[2, n] + base)]
-
-    def step2(n, carry):
-        ext3[n + HALO] = v2[n] + flux_of(near(ext, n, WIDE), flow[n])
-        return carry
-
-    run(nb, unroll, step2, 0)
-
-    def step3(n, carry):
-        g = growth[pl.ds(n, 1), :]
-        b = bs[n]
-        b = b + g * b * (wetness(ws[n]) - 0.4 * b)
-        w = ext3[n + HALO]
-        s = wetness(w)
-        wat_out[:, lanes(n)] = w + flux_of(near(ext3, n, HALO), flow[n]) + rain[1, :, lanes(n)] - 0.2 * b * s
-        bio_out[:, lanes(n)] = b + g * b * (s - 0.4 * b)
-        return carry
-
-    run(nb, unroll, step3, 0)
+            edge = got[(WIDE + m) * part : (WIDE + m + 1) * part, :]
+            ext3[spot + m] = edge + halo_flux(ext, pay, right, nb, m)
+    base = HALO - pos * nb
+    for n in (*range(WIDE), *range(nb - WIDE, nb)):
+        xs = [ext3[i].astype(half) for i in (n + HALO, ids[1, n] + base, ids[2, n] + base)]
+        w, b = final(n, ext3[n + HALO], flux_of(xs, flow[n]), ws[n], bs[n], growth, rain)
+        wat_out[:, lanes(n)] = w
+        bio_out[:, lanes(n)] = b
 
 
 def means_kernel(unroll, count, *refs):
-    bq, wq, b2, w2, means = refs[count:]
+    bq, wq, b2, w2, b2_edge, w2_edge, means = refs[count:]
     nb, slots = bq.shape[:2]
     level = [ref[...] for ref in refs[:count]]
     while len(level) > 1:
@@ -341,13 +422,22 @@
         e = jnp.exp(x - jnp.max(x, axis=0, keepdims=True))
         weights.append(jnp.broadcast_to(e / jnp.sum(e, axis=0, keepdims=True), (slots, BLK)))
 
-    def step(n, carry):
-        for c, fields in enumerate(((bq, wq), (b2, w2))):
-            for f, ref in enumerate(fields):
-                means[c, f : f + 1, lanes(n)] = jnp.sum(weights[c] * ref[n], axis=0, keepdims=True)
-        return carry
-
-    run(nb, unroll, step, 0)
+    def mean(c, f, n, x):
+        means[c, f : f + 1, lanes(n)] = jnp.sum(weights[c] * x, axis=0, keepdims=True)
+
+    def fill(c, f, ref, first, last, shift):
+        def step(n, carry):
+            mean(c, f, n, ref[n - shift])
+            return carry
+
+        run(first, last, unroll, step, 0)
+
+    fill(0, 0, bq, 0, nb, 0)
+    fill(0, 1, wq, 0, nb, 0)
+    for f, ref, edge, width in ((0, b2, b2_edge, HALO), (1, w2, w2_edge, WIDE)):
+        fill(1, f, ref, width, nb - width, width)
+        fill(1, f, edge, 0, width, 0)
+        fill(1, f, edge, nb - width, nb, nb - 2 * width)
 
 
 def weigh(flops):
@@ -382,22 +472,31 @@
     edge = ((HALO * depth + 16, BLK), bf16)
     tile = (HALO, NBR, BLK, BLK)
 
-    out = [((rows, (nb + 1) * BLK), i16), edge, edge]
-    wire, flow_a, flow_b = pl.pallas_call(
+    wire = pl.pallas_call(
         pack_kernel,
         grid=(1,),
-        out_shape=tuple(jax.ShapeDtypeStruct(s, d) for s, d in out),
+        out_shape=jax.ShapeDtypeStruct((rows, (nb + 1) * BLK), i16),
         in_specs=[pl.BlockSpec((part, cells), lambda i: (0, 0))] * 2
-        + [pl.BlockSpec((2, part, cells), lambda i: (0, 0, 0))]
-        + [pl.BlockSpec(tile, lambda i: (0, 0, 0, 0)), pl.BlockSpec(tile, lambda i: (nb // HALO - 1, 0, 0, 0)), SMEM],
-        out_specs=tuple(VMEM for _ in out),
-        scratch_shapes=[
-            pltpu.VMEM((rows, cells), f32),
-            pltpu.VMEM((4, rows, BLK), f32),
-        ],
+        + [pl.BlockSpec((2, part, cells), lambda i: (0, 0, 0))],
+        out_specs=VMEM,
+        scratch_shapes=[pltpu.VMEM((rows, cells), f32), pltpu.VMEM((4, rows, BLK), f32)],
         compiler_params=pltpu.CompilerParams(vmem_limit_bytes=60 * 2**20),
         cost_estimate=weigh(1),
-    )(biomass, water, rain, flow_blocks, flow_blocks, neighbours)
+    )(biomass, water, rain)
+    flow_a, flow_b = pl.pallas_call(
+        edge_kernel,
+        grid=(1,),
+        out_shape=tuple(jax.ShapeDtypeStruct(*edge) for _ in range(2)),
+        in_specs=[
+            HBM,
+            pl.BlockSpec(tile, lambda i: (0, 0, 0, 0)),
+            pl.BlockSpec(tile, lambda i: (nb // HALO - 1, 0, 0, 0)),
+            SMEM,
+        ],
+        out_specs=(VMEM, VMEM),
+        compiler_params=pltpu.CompilerParams(vmem_limit_bytes=60 * 2**20),
+        cost_estimate=weigh(1),
+    )(wire, flow_blocks, flow_blocks, neighbours)
 
     pieces = [wire] + [
         lax.ppermute(wire, "particle", [(i, i ^ j) for i in range(members)]) for j in range(1, members)
@@ -425,40 +524,58 @@
     )(*pieces, anc, growth, prec, obs)
     got_a = lax.ppermute(pay_a, "tile", swap_a)
     got_b = lax.ppermute(pay_b, "tile", swap_b)
-    wb1, v1, b2, total = call(
-        functools.partial(day0_kernel, unroll),
-        [((nb + WIDE, slots, BLK), bf16), field, field, ((2 * slots, BLK), f32)],
-        [VMEM] * 8 + [SMEM] + [VMEM] * 4,
-        [pltpu.VMEM((nb + 2 * WIDE, slots, BLK), bf16)],
-    )(wb, v0, b1, got_a, got_b, flow, flow_a, flow_b, neighbours, growth, prec, obs, miss)
-    few = ((nb, part, BLK), f32)
-    w2, ws, bs, v2, end_a, end_b = call(
-        functools.partial(day1_kernel, members, unroll),
-        [field, few, few, few] + [((WIDE + HALO, part, BLK), f32)] * 2,
-        [VMEM] * (members + 6) + [SMEM] * 2 + [VMEM],
-    )(*pieces, wb1, v1, b2, quad, unit1, flow, neighbours, ancestors, rain23)
+    inner, core = nb - 2 * HALO, nb - 2 * WIDE
+
+    def blocks(count, height=slots, kind=f32):
+        return ((count, height, BLK), kind)
+
+    r1, wb1, v1, b2, w2, wi, bi, vi, miss1 = call(
+        functools.partial(inner01_kernel, members, unroll),
+        [blocks(nb), blocks(inner, kind=bf16), blocks(inner), blocks(inner), blocks(core)]
+        + [blocks(core, part)] * 3
+        + [((slots, BLK), f32)],
+        [VMEM] * (members + 6) + [SMEM] + [VMEM] * 3 + [SMEM, VMEM],
+    )(*pieces, wb, v0, b1, quad, unit1, flow, neighbours, growth, prec, obs, ancestors, rain23)
+    swap_rows = (WIDE + HALO) * part
+    b2_edge, w2_edge, ws, bs, v2, total, end_a, end_b = call(
+        functools.partial(outer01_kernel, unroll),
+        [blocks(2 * HALO), blocks(2 * WIDE)]
+        + [blocks(nb, part)] * 3
+        + [((2 * slots, BLK), f32), ((swap_rows + 2 * slots, BLK), f32), ((swap_rows, BLK), f32)],
+        [VMEM] * 17 + [SMEM] + [VMEM] * 3 + [SMEM, VMEM],
+        [
+            pltpu.VMEM((nb + 2 * WIDE, slots, BLK), bf16),
+            pltpu.VMEM((nb + WIDE, slots, BLK), bf16),
+            pltpu.VMEM((2 * HALO, slots, BLK), f32),
+        ],
+    )(
+        wb, v0, b1, r1, wb1, v1, b2, wi, bi, vi, miss, miss1, got_a, got_b, flow, flow_a, flow_b, neighbours,
+        growth, prec, obs, ancestors, rain23,
+    )
     last_a = lax.ppermute(end_a, "tile", swap_a)
     last_b = lax.ppermute(end_b, "tile", swap_b)
 
-    def shared(x, masks):
-        return [x] + [lax.ppermute(x, "tile", [(i, i ^ m) for i in range(tiles)]) for m in masks]
-
-    terms = shared(total, [1])
+    terms = [total, last_a[swap_rows:]]
     span = 2
     while span < tiles:
         total = sum(terms[1:], terms[0])
         masks = [span] if span * 2 >= tiles else [span, 2 * span, 3 * span]
-        terms = shared(total, masks)
+        terms = [total] + [lax.ppermute(total, "tile", [(i, i ^ m) for i in range(tiles)]) for m in masks]
         span *= 2 ** (len(masks) // 2 + 1)
+    w3, wat, bio = call(
+        functools.partial(inner23_kernel, unroll),
+        [blocks(inner, part), blocks(core, part), blocks(core, part)],
+        [VMEM] * 4 + [SMEM] + [VMEM] * 2,
+    )(ws, bs, v2, flow, neighbours, growth, rain23)
     bio_out, wat_out = call(
-        functools.partial(close_kernel, unroll),
+        outer23_kernel,
         [((part, cells), f32)] * 2,
-        [VMEM] * 8 + [SMEM] + [VMEM] * 2,
+        [VMEM] * 11 + [SMEM] + [VMEM] * 2,
         [pltpu.VMEM((nb + 2 * WIDE, part, BLK), f32), pltpu.VMEM((nb + WIDE, part, BLK), f32)],
-    )(ws, bs, v2, last_a, last_b, flow, flow_a, flow_b, neighbours, growth, rain23)
+    )(ws, bs, v2, w3, wat, bio, last_a, last_b, flow, flow_a, flow_b, neighbours, growth, rain23)
     (means,) = call(
-        functools.partial(means_kernel, unroll, len(terms)), [((CYCLES, 2, cells), f32)], [VMEM] * (len(terms) + 4)
-    )(*terms, bq, wq, b2, w2)
+        functools.partial(means_kernel, unroll, len(terms)), [((CYCLES, 2, cells), f32)], [VMEM] * (len(terms) + 6)
+    )(*terms, bq, wq, b2, w2, b2_edge, w2_edge)
     return means, bio_out, wat_out
 
 

time: 40.1 us -> 36.7 us (0.915)
  waiting for transfers between devices: 10 us -> 5.34 us
  Pallas kernels: 10.8 us -> 13.3 us
  local copies, waits for them, and re-layouts: 0.93 us -> 0.04 us
    ppermute x3, waiting for transfers between devices: 7.84 us -> 4.83 us  [body(): lax.ppermute(wire, 'particle', [(i, i ^ j) for i in range(members)])]
    pallas_call x4 -> x6, Pallas kernels: 8.54 us -> 11.1 us  [the longest x1 2.25 us: body(): call(outer23_kernel, [((part, cells), f32)] * 2, [VMEM] * 11 + [SMEM] + [...]
    ppermute x1, waiting for transfers between devices: 2.18 us -> 0.49 us  [body(): got_b = lax.ppermute(pay_b, 'tile', swap_b)]
    unnamed x16, local copies, waits for them, and re-layouts: 0.93 us -> 0.04 us
    ppermute x4 -> x3, starting transfers between devices: 3.72 us -> 3.49 us  [body(): lax.ppermute(total, 'tile', [(i, i ^ m) for i in range(tiles)])]
  transfers between devices with their start and end apart: 13 -> 12, of which waited for: 3 -> 2; matrix products, arithmetic and copies ran while one was open for 0% -> 0% of each run, Pallas kernels for 14% -> 25%
where the time goes in v4:
time: 36.7 us; the launch traced here: 36.6 us
  starting transfers between devices  17.1 us (47%)
  Pallas kernels  13.3 us (36%)
  waiting for transfers between devices  5.34 us (15%)
  between operations  0.78 us (2%)
    ppermute x3, starting transfers between devices, body(): lax.ppermute(wire, 'particle', [(i, i ^ j) for i in range(members)])  5.62 us
    ppermute x3, waiting for transfers between devices, body(): lax.ppermute(wire, 'particle', [(i, i ^ j) for i in range(members)])  4.83 us
    ppermute x3, starting transfers between devices, body(): lax.ppermute(total, 'tile', [(i, i ^ m) for i in range(tiles)])  3.49 us
    ppermute x1, starting transfers between devices, body(): flow_b = lax.ppermute(flow_b, 'tile', swap_b)  2.77 us
    ppermute x1, starting transfers between devices, body(): got_b = lax.ppermute(pay_b, 'tile', swap_b)  2.55 us
    ppermute x1, starting transfers between devices, body(): last_b = lax.ppermute(end_b, 'tile', swap_b)  2.39 us
    pallas_call x1, Pallas kernels, body(): call(outer23_kernel, [((part, cells), f32)] * 2, [VMEM] * 11 + [SMEM] + [...  2.25 us
    pallas_call x1, Pallas kernels, body(): pl.pallas_call(edge_kernel, grid=(1,), out_shape=tuple((jax.ShapeDtypeStr...  2.23 us
  transfers between devices with their start and end apart: 12, of which 2 were waited for; matrix products, arithmetic and copies ran while one was open for 0% of the time, Pallas kernels for 25%

profile of v4, /device:TPU:0, one launch (start us, length us, event | category | flops | bytes accessed | tf_op | source)
XLA Modules:
  0.0 36.6 jit_solution(3199935899766938392)
XLA Ops:
  0.6 1.8 %shard_map.112.wire.after = s16[16,4224]{1,0:T(8,128)(2,1)} custom-call(f32[4,4096]{1,0:T(4,128)} %bio.1, f32[4,4096]{1,0:T(4,128)} %wat.1, f32[4,4,4096]{2,1,0:T(4,128)} %rain.3), custom_call_target="tpu_custom_call" | custom-call | flops 1 | bytes 1 | tf_op jit(solution)/shard_map/pallas_call | solution.py:475
  2.4 3.0 %collective-permute-start = (s16[16,4224]{1,0:T(8,128)(2,1)}, s16[16,4224]{1,0:T(8,128)(2,1)S(1)}, u32[]{:S(2)}, u32[]{:S(2)}) collective-permute-start(s16[16,4224]{1,0:T(8,128)(2,1)} %shard_map.112.wire.after), channel_id=1, source_target_pairs={{0,8},{8,0},{16,24},{24,16},{1,9},{9,1},{17,25},{25,17},{2,10},{10... | collective-permute-start | bytes 405512 | tf_op jit(solution)/shard_map/ppermute | solution.py:502
  5.4 2.6 %collective-permute-start.1 = (s16[16,4224]{1,0:T(8,128)(2,1)}, s16[16,4224]{1,0:T(8,128)(2,1)S(1)}, u32[]{:S(2)}, u32[]{:S(2)}) collective-permute-start(s16[16,4224]{1,0:T(8,128)(2,1)} %shard_map.112.wire.after), channel_id=1, source_target_pairs={{0,16},{8,24},{16,0},{24,8},{1,17},{9,25},{17,1},{25,9},{2,18},{10... | collective-permute-start | bytes 405512 | tf_op jit(solution)/shard_map/ppermute | solution.py:502
  8.0 0.0 collective-permute-start.2
  8.0 0.0 copy-start
  8.0 0.0 copy-start.1
  8.0 0.0 copy-start.2
  8.0 0.0 copy-start.4
  8.0 0.0 copy-start.5
  8.0 0.0 copy-start.6
  8.1 0.0 copy-start.7
  8.1 2.2 %shard_map.116 = (bf16[1552,128]{1,0:T(8,128)(2,1)}, bf16[1552,128]{1,0:T(8,128)(2,1)}) custom-call(s16[16,4224]{1,0:T(8,128)(2,1)} %shard_map.112.wire.after, bf16[32,3,128,128]{3,2,1,0:T(8,128)(2,1)} %right.1, bf16[32,3,128,128]{3,2,1,0:T(8,128)(2,1)} %right.1, s32[3,32]{1,0:T(4,128)} %bitcast.3), custom_call_target="tpu_custom_call" | custom-call | flops 1 | bytes 1 | tf_op jit(solution)/shard_map/pallas_call | solution.py:486
  10.3 0.0 collective-permute-start.5
  10.3 2.8 %collective-permute-start.6 = (bf16[1552,128]{1,0:T(8,128)(2,1)}, bf16[1552,128]{1,0:T(8,128)(2,1)S(1)}, u32[]{:S(2)}, u32[]{:S(2)}) collective-permute-start(bf16[1552,128]{1,0:T(8,128)(2,1)} %get-tuple-element.68), channel_id=1, source_target_pairs={{0,7},{1,2},{2,1},{3,4},{4,3},{5,6},{6,5},{7,0},{8,15},{9,10},{10,... | collective-permute-start | bytes 1191944 | tf_op jit(solution)/shard_map/ppermute | solution.py:511
  13.1 0.0 collective-permute-done.after.refs_1_
  13.1 0.0 copy-done
  13.1 0.0 copy-done.1
  13.1 0.0 copy-done.2
  13.1 0.0 copy-done.4
  13.1 0.0 copy-done.5
  13.1 0.0 copy-done.6
  13.1 0.0 copy-done.7
  13.1 0.9 %shard_map.113 = (bf16[32,384,128]{2,1,0:T(8,128)(2,1)S(1)}, s16[16,4224]{1,0:T(8,128)(2,1)S(1)}, f32[32,128]{1,0:T(8,128)S(1)}, f32[32,128]{1,0:T(8,128)S(1)}, ...) custom-call(s16[16,4224]{1,0:T(8,128)(2,1)S(1)} %collective-permute-done.after.refs_1_, ...), custom_call_target="tpu_custom_call" | custom-call | flops 1 | bytes 1 | tf_op jit(solution)/shard_map/pallas_call | solution.py:505
  14.0 4.8 %collective-permute-done.1.refs_2_ = s16[16,4224]{1,0:T(8,128)(2,1)S(1)} collective-permute-done((s16[16,4224]{1,0:T(8,128)(2,1)}, s16[16,4224]{1,0:T(8,128)(2,1)S(1)}, u32[]{:S(2)}, u32[]{:S(2)}) %collective-permute-start.1) | collective-permute-done | bytes 135200 | tf_op jit(solution)/shard_map/ppermute | solution.py:502
  18.8 0.0 collective-permute-done.2.refs_3_
  18.8 0.5 %shard_map.114 = (bf16[32,16,128]{2,1,0:T(8,128)(2,1)S(1)}, f32[32,16,128]{2,1,0:T(8,128)S(1)}, f32[32,16,128]{2,1,0:T(8,128)S(1)}, f32[32,16,128]{2,1,0:T(8,128...) custom-call(s16[16,4224]{1,0:T(8,128)(2,1)S(1)} %get-tuple-element.4, ...), custom_call_target="tpu_custom_call" | custom-call | flops 10000000000 | bytes 1 | tf_op jit(solution)/shard_map/pallas_call | solution.py:514
  19.4 0.1 collective-permute-start.3
  19.5 2.5 %collective-permute-start.4 = (bf16[16,16,128]{2,1,0:T(8,128)(2,1)S(1)}, bf16[16,16,128]{2,1,0:T(8,128)(2,1)S(1)}, u32[]{:S(2)}, u32[]{:S(2)}) collective-permute-start(bf16[16,16,128]{2,1,0:T(8,128)(2,1)S(1)} %get-tuple-element.66), channel_id=1, source_target_pairs={{0,7},{1,2},{2,1},{3,4},{4,3},{5,6},{6,5},{7,0},{8,15},{9,10},{10,... | collective-permute-start | bytes 196616 | tf_op jit(solution)/shard_map/ppermute | solution.py:526
  22.0 0.0 copy-done.3
  22.0 1.7 %shard_map.115 = (f32[32,16,128]{2,1,0:T(8,128)S(1)}, bf16[24,16,128]{2,1,0:T(8,128)(2,1)S(1)}, f32[24,16,128]{2,1,0:T(8,128)S(1)}, f32[24,16,128]{2,1,0:T(8,128...) custom-call(s16[16,4224]{1,0:T(8,128)(2,1)S(1)} %get-tuple-element.4, ...), custom_call_target="tpu_custom_call" | custom-call | flops 1 | bytes 1 | tf_op jit(solution)/shard_map/pallas_call | solution.py:532
  23.7 0.0 collective-permute-done.3.got_a
  23.7 0.5 %collective-permute-done.4.got_b = bf16[16,16,128]{2,1,0:T(8,128)(2,1)S(1)} collective-permute-done((bf16[16,16,128]{2,1,0:T(8,128)(2,1)S(1)}, bf16[16,16,128]{2,1,0:T(8,128)(2,1)S(1)}, u32[]{:S(2)}, u32[]{:S(2)}) %collective-permute-start.4) | collective-permute-done | bytes 65568 | tf_op jit(solution)/shard_map/ppermute | solution.py:526
  24.2 0.0 collective-permute-done.5.flow_a
  24.2 0.0 collective-permute-done.6.flow_b
  24.2 1.7 %shard_map.117 = (f32[8,16,128]{2,1,0:T(8,128)S(1)}, f32[16,16,128]{2,1,0:T(8,128)S(1)}, f32[32,4,128]{2,1,0:T(4,128)S(1)}, f32[32,4,128]{2,1,0:T(4,128)S(1)}, f...) custom-call(bf16[32,16,128]{2,1,0:T(8,128)(2,1)S(1)} %get-tuple-element.49.refs, ...), custom_call_target="tpu_custom_call" | custom-call | flops 1 | bytes 1 | tf_op jit(solution)/shard_map/pallas_call | solution.py:540
  25.9 0.2 collective-permute-start.7
  26.0 2.4 %collective-permute-start.11 = (f32[48,128]{1,0:T(8,128)S(1)}, f32[48,128]{1,0:T(8,128)S(1)}, u32[]{:S(2)}, u32[]{:S(2)}) collective-permute-start(f32[48,128]{1,0:T(8,128)S(1)} %get-tuple-element.82), channel_id=1, source_target_pairs={{0,7},{1,2},{2,1},{3,4},{4,3},{5,6},{6,5},{7,0},{8,15},{9,10},{10,... | collective-permute-start | bytes 73736 | tf_op jit(solution)/shard_map/ppermute | solution.py:556
  28.4 0.0 collective-permute-done.7.got_a
  28.4 1.2 %collective-permute-start.10 = (f32[32,128]{1,0:T(8,128)S(1)}, f32[32,128]{1,0:T(8,128)S(1)}, u32[]{:S(2)}, u32[]{:S(2)}) collective-permute-start(f32[32,128]{1,0:T(8,128)S(1)} %slice_add_fusion.refs_0_), channel_id=1, source_target_pairs={{0,6},{1,7},{2,4},{3,5},{4,2},{5,3},{6,0},{7,1},{8,14},{9,15},{10,... | collective-permute-start | bytes 49160 | tf_op jit(solution)/shard_map/ppermute | solution.py:563
  29.6 0.9 %collective-permute-start.8 = (f32[32,128]{1,0:T(8,128)S(1)}, f32[32,128]{1,0:T(8,128)S(1)}, u32[]{:S(2)}, u32[]{:S(2)}) collective-permute-start(f32[32,128]{1,0:T(8,128)S(1)} %slice_add_fusion.refs_0_), channel_id=1, source_target_pairs={{0,2},{1,3},{2,0},{3,1},{4,6},{5,7},{6,4},{7,5},{8,10},{9,11},{10,... | collective-permute-start | bytes 49160 | tf_op jit(solution)/shard_map/ppermute | solution.py:563
  30.6 1.4 %collective-permute-start.9 = (f32[32,128]{1,0:T(8,128)S(1)}, f32[32,128]{1,0:T(8,128)S(1)}, u32[]{:S(2)}, u32[]{:S(2)}) collective-permute-start(f32[32,128]{1,0:T(8,128)S(1)} %slice_add_fusion.refs_0_), channel_id=1, source_target_pairs={{0,4},{1,5},{2,6},{3,7},{4,0},{5,1},{6,2},{7,3},{8,12},{9,13},{10,... | collective-permute-start | bytes 49160 | tf_op jit(solution)/shard_map/ppermute | solution.py:563
  31.9 1.5 %shard_map.119 = (f32[24,4,128]{2,1,0:T(4,128)S(1)}, f32[16,4,128]{2,1,0:T(4,128)S(1)}, f32[16,4,128]{2,1,0:T(4,128)S(1)}) custom-call(f32[32,4,128]{2,1,0:T(4,128)S(1)} %get-tuple-element.76.ws, f32[32,4,128]{2,1,0:T(4,128)S(1)} %get-tuple-element.77.bs, f32[32,4,128]{2,1,0:T(4,128)S(1)} %get-tuple-element.78.v2, ...), custom_call_target="tpu_custom_call" | custom-call | flops 1 | bytes 1 | tf_op jit(solution)/shard_map/pallas_call | solution.py:565
  33.4 0.0 collective-permute-done.11.got_b
  33.4 2.3 %shard_map.120 = (f32[4,4096]{1,0:T(4,128)}, f32[4,4096]{1,0:T(4,128)}) custom-call(f32[32,4,128]{2,1,0:T(4,128)S(1)} %get-tuple-element.76.ws, f32[32,4,128]{2,1,0:T(4,128)S(1)} %get-tuple-element.77.bs, f32[32,4,128]{2,1,0:T(4,128)S(1)} %get-tuple-element.78.v2, f32[24,4,128]{2,1,0:T(4,128)S(1)} %get-tuple-element.79.w3, ...), custom_call_target="tpu_custom_call" | custom-call | flops 1 | bytes 1 | tf_op jit(solution)/shard_map/pallas_call | solution.py:570
  35.7 0.0 collective-permute-done.10.refs_3_
  35.7 0.0 collective-permute-done.8.refs_1_
  35.7 0.0 collective-permute-done.9.refs_2_
  35.7 0.9 %shard_map.118 = f32[2,2,4096]{2,1,0:T(2,128)} custom-call(f32[32,128]{1,0:T(8,128)S(1)} %slice_add_fusion.refs_0_, f32[32,128]{1,0:T(8,128)S(1)} %collective-permute-done.8.refs_1_, f32[32,128]{1,0:T(8,128)S(1)} %collective-permute-done.9.refs_2_, f32[32,128]{1,0:T(8,128)S(1)} %collective-permute-done.10.refs_3_, ...), custom_call_target="tpu_custom_call" | custom-call | flops 1 | bytes 1 | tf_op jit(solution)/shard_map/pallas_call | solution.py:576
  (2 shorter events, 0.0 us)
Async XLA Ops:
  2.4 10.7 %collective-permute-start = (s16[16,4224]{1,0:T(8,128)(2,1)}, s16[16,4224]{1,0:T(8,128)(2,1)S(1)}, u32[]{:S(2)}, u32[]{:S(2)}) collective-permute-start(s16[16,4224]{1,0:T(8,128)(2,1)} %shard_map.112.wire.after), channel_id=1, source_target_pairs={{0,8},{8,0},{16,24},{24,16},{1,9},{9,1},{17,25},{25,17},{2,10},{10... | collective-permute-start | bytes 405512 | tf_op jit(solution)/shard_map/ppermute | solution.py:502
  5.4 13.4 %collective-permute-start.1 = (s16[16,4224]{1,0:T(8,128)(2,1)}, s16[16,4224]{1,0:T(8,128)(2,1)S(1)}, u32[]{:S(2)}, u32[]{:S(2)}) collective-permute-start(s16[16,4224]{1,0:T(8,128)(2,1)} %shard_map.112.wire.after), channel_id=1, source_target_pairs={{0,16},{8,24},{16,0},{24,8},{1,17},{9,25},{17,1},{25,9},{2,18},{10... | collective-permute-start | bytes 405512 | tf_op jit(solution)/shard_map/ppermute | solution.py:502
  8.0 10.8 %collective-permute-start.2 = (s16[16,4224]{1,0:T(8,128)(2,1)}, s16[16,4224]{1,0:T(8,128)(2,1)S(1)}, u32[]{:S(2)}, u32[]{:S(2)}) collective-permute-start(s16[16,4224]{1,0:T(8,128)(2,1)} %shard_map.112.wire.after), channel_id=1, source_target_pairs={{0,24},{8,16},{16,8},{24,0},{1,25},{9,17},{17,9},{25,1},{2,26},{10... | collective-permute-start | bytes 405512 | tf_op jit(solution)/shard_map/ppermute | solution.py:502
  8.0 5.1 %copy-start = (bf16[32,3,128,128]{3,2,1,0:T(8,128)(2,1)S(1)}, bf16[32,3,128,128]{3,2,1,0:T(8,128)(2,1)}, u32[]{:S(2)}) copy-start(bf16[32,3,128,128]{3,2,1,0:T(8,128)(2,1)} %right.1) | copy-start | bytes 9437188
  8.0 5.1 %copy-start.1 = (s16[16,4224]{1,0:T(8,128)(2,1)S(1)}, s16[16,4224]{1,0:T(8,128)(2,1)}, u32[]{:S(2)}) copy-start(s16[16,4224]{1,0:T(8,128)(2,1)} %shard_map.112.wire.after) | copy-start | bytes 405508
  8.0 5.1 %copy-start.2 = (f32[4,4,4096]{2,1,0:T(4,128)S(1)}, f32[4,4,4096]{2,1,0:T(4,128)}, u32[]{:S(2)}) copy-start(f32[4,4,4096]{2,1,0:T(4,128)} %rain.3) | copy-start | bytes 786436
  8.0 5.1 %copy-start.4 = (f32[2,4096]{1,0:T(2,128)S(1)}, f32[2,4096]{1,0:T(2,128)}, u32[]{:S(2)}) copy-start(f32[2,4096]{1,0:T(2,128)} %obs.1) | copy-start | bytes 98308
  8.0 5.1 %copy-start.5 = (f32[4096]{0:T(1024)S(1)}, f32[4096]{0:T(1024)}, u32[]{:S(2)}) copy-start(f32[4096]{0:T(1024)} %param.14) | copy-start | bytes 49156
  8.0 5.1 %copy-start.6 = (f32[4096]{0:T(1024)S(1)}, f32[4096]{0:T(1024)}, u32[]{:S(2)}) copy-start(f32[4096]{0:T(1024)} %param.16) | copy-start | bytes 49156
  8.1 5.1 %copy-start.7 = (s32[2,16]{1,0:T(2,128)S(1)}, s32[2,16]{1,0:T(2,128)}, u32[]{:S(2)}) copy-start(s32[2,16]{1,0:T(2,128)} %anc.3) | copy-start | bytes 388
  10.3 13.9 %collective-permute-start.5 = (bf16[1552,128]{1,0:T(8,128)(2,1)}, bf16[1552,128]{1,0:T(8,128)(2,1)S(1)}, u32[]{:S(2)}, u32[]{:S(2)}) collective-permute-start(bf16[1552,128]{1,0:T(8,128)(2,1)} %get-tuple-element.67), channel_id=1, source_target_pairs={{0,1},{1,0},{2,3},{3,2},{4,5},{5,4},{6,7},{7,6},{8,9},{9,8},{10,11... | collective-permute-start | bytes 1191944 | tf_op jit(solution)/shard_map/ppermute | solution.py:510
  10.3 13.9 %collective-permute-start.6 = (bf16[1552,128]{1,0:T(8,128)(2,1)}, bf16[1552,128]{1,0:T(8,128)(2,1)S(1)}, u32[]{:S(2)}, u32[]{:S(2)}) collective-permute-start(bf16[1552,128]{1,0:T(8,128)(2,1)} %get-tuple-element.68), channel_id=1, source_target_pairs={{0,7},{1,2},{2,1},{3,4},{4,3},{5,6},{6,5},{7,0},{8,15},{9,10},{10,... | collective-permute-start | bytes 1191944 | tf_op jit(solution)/shard_map/ppermute | solution.py:511
  18.8 3.2 %copy-start.3 = (s32[32,3]{0,1:T(4,128)S(1)}, s32[32,3]{0,1:T(4,128)}, u32[]{:S(2)}) copy-start(s32[32,3]{0,1:T(4,128)} %param.12) | copy-start | bytes 1156
  19.4 4.3 %collective-permute-start.3 = (bf16[16,16,128]{2,1,0:T(8,128)(2,1)S(1)}, bf16[16,16,128]{2,1,0:T(8,128)(2,1)S(1)}, u32[]{:S(2)}, u32[]{:S(2)}) collective-permute-start(bf16[16,16,128]{2,1,0:T(8,128)(2,1)S(1)} %get-tuple-element.65), channel_id=1, source_target_pairs={{0,1},{1,0},{2,3},{3,2},{4,5},{5,4},{6,7},{7,6},{8,9},{9,8},{10,11... | collective-permute-start | bytes 196616 | tf_op jit(solution)/shard_map/ppermute | solution.py:525
  19.5 4.7 %collective-permute-start.4 = (bf16[16,16,128]{2,1,0:T(8,128)(2,1)S(1)}, bf16[16,16,128]{2,1,0:T(8,128)(2,1)S(1)}, u32[]{:S(2)}, u32[]{:S(2)}) collective-permute-start(bf16[16,16,128]{2,1,0:T(8,128)(2,1)S(1)} %get-tuple-element.66), channel_id=1, source_target_pairs={{0,7},{1,2},{2,1},{3,4},{4,3},{5,6},{6,5},{7,0},{8,15},{9,10},{10,... | collective-permute-start | bytes 196616 | tf_op jit(solution)/shard_map/ppermute | solution.py:526
  25.9 2.6 %collective-permute-start.7 = (f32[80,128]{1,0:T(8,128)S(1)}, f32[80,128]{1,0:T(8,128)S(1)}, u32[]{:S(2)}, u32[]{:S(2)}) collective-permute-start(f32[80,128]{1,0:T(8,128)S(1)} %get-tuple-element.70), channel_id=1, source_target_pairs={{0,1},{1,0},{2,3},{3,2},{4,5},{5,4},{6,7},{7,6},{8,9},{9,8},{10,11... | collective-permute-start | bytes 122888 | tf_op jit(solution)/shard_map/ppermute | solution.py:555
  26.0 7.4 %collective-permute-start.11 = (f32[48,128]{1,0:T(8,128)S(1)}, f32[48,128]{1,0:T(8,128)S(1)}, u32[]{:S(2)}, u32[]{:S(2)}) collective-permute-start(f32[48,128]{1,0:T(8,128)S(1)} %get-tuple-element.82), channel_id=1, source_target_pairs={{0,7},{1,2},{2,1},{3,4},{4,3},{5,6},{6,5},{7,0},{8,15},{9,10},{10,... | collective-permute-start | bytes 73736 | tf_op jit(solution)/shard_map/ppermute | solution.py:556
  28.4 7.2 %collective-permute-start.10 = (f32[32,128]{1,0:T(8,128)S(1)}, f32[32,128]{1,0:T(8,128)S(1)}, u32[]{:S(2)}, u32[]{:S(2)}) collective-permute-start(f32[32,128]{1,0:T(8,128)S(1)} %slice_add_fusion.refs_0_), channel_id=1, source_target_pairs={{0,6},{1,7},{2,4},{3,5},{4,2},{5,3},{6,0},{7,1},{8,14},{9,15},{10,... | collective-permute-start | bytes 49160 | tf_op jit(solution)/shard_map/ppermute | solution.py:563
  29.6 6.0 %collective-permute-start.8 = (f32[32,128]{1,0:T(8,128)S(1)}, f32[32,128]{1,0:T(8,128)S(1)}, u32[]{:S(2)}, u32[]{:S(2)}) collective-permute-start(f32[32,128]{1,0:T(8,128)S(1)} %slice_add_fusion.refs_0_), channel_id=1, source_target_pairs={{0,2},{1,3},{2,0},{3,1},{4,6},{5,7},{6,4},{7,5},{8,10},{9,11},{10,... | collective-permute-start | bytes 49160 | tf_op jit(solution)/shard_map/ppermute | solution.py:563
  30.6 5.1 %collective-permute-start.9 = (f32[32,128]{1,0:T(8,128)S(1)}, f32[32,128]{1,0:T(8,128)S(1)}, u32[]{:S(2)}, u32[]{:S(2)}) collective-permute-start(f32[32,128]{1,0:T(8,128)S(1)} %slice_add_fusion.refs_0_), channel_id=1, source_target_pairs={{0,4},{1,5},{2,6},{3,7},{4,0},{5,1},{6,2},{7,3},{8,12},{9,13},{10,... | collective-permute-start | bytes 49160 | tf_op jit(solution)/shard_map/ppermute | solution.py:563

commit v5 on v4

--- a/solution.py
+++ b/solution.py
@@ -47,7 +47,7 @@
     return lax.rem(lax.axis_index("tile"), 2) == 0
 
 
-def pack_kernel(bio, wat, rain, wire, held, factor):
+def pack_kernel(bio, wat, rain, wire, fields, rains, held, factor):
     part, cells = bio.shape
     nb = cells // BLK
     half, quarter = cells // 2, cells // 4
@@ -78,8 +78,16 @@
 
     pairs, quads = nb // 2, nb // 4
     for n in range(nb):
-        wire[:, lanes(n)] = coded(held[:, lanes(n)] * factor[0 if n < pairs else 1 if n < pairs + quads else 2])
-    wire[:, lanes(nb)] = coded(factor[3])
+        x = coded(held[:, lanes(n)] * factor[0 if n < pairs else 1 if n < pairs + quads else 2])
+        if n < pairs:
+            wire[:, lanes(n)] = x
+            fields[:, lanes(n)] = x
+        else:
+            wire[:, lanes(n + 1)] = x
+            rains[:, lanes(n - pairs)] = x
+    x = coded(factor[3])
+    wire[:, lanes(pairs)] = x
+    fields[:, lanes(pairs)] = x
 
 
 def edge_kernel(after, left, right, ids, pay_a, pay_b):
@@ -140,23 +148,27 @@
     return total
 
 
-def decode(sel, pieces, cols):
+def decode(sel, pieces, n):
     parts = []
-    for ref in pieces:
-        q = ref[:, cols].astype(jnp.int32)
+    for ref, first in pieces:
+        q = ref[:, lanes(n + first)].astype(jnp.int32)
         parts.append((q >> 8).astype(jnp.float32).astype(jnp.bfloat16))
         parts.append((q & 255).astype(jnp.float32).astype(jnp.bfloat16))
     return jnp.dot(sel, jnp.concatenate(parts, axis=0), preferred_element_type=jnp.float32)
 
 
-def open_kernel(members, unroll, *refs):
-    pieces = refs[:members]
-    anc, growth, prec, obs = refs[members : members + 4]
-    wb, v0, b1, bq, wq, miss, quad, unit1, pay_a, pay_b = refs[members + 4 : members + 14]
-    pair, scaler = refs[-2:]
-    nb = growth.shape[0]
+def split(members, nb, refs):
+    both = refs[:2]
+    fields = [(r, 0) for r in (*both, *refs[2:members])]
+    rains = [(r, nb // 2 + 1) for r in both] + [(r, 0) for r in refs[members : 2 * members - 2]]
+    return fields, rains, refs[2 * members - 2 :]
+
+
+def open_kernel(members, unroll, nb, *refs):
+    pieces, rains, refs = split(members, nb, refs)
+    anc, growth, prec, obs, wb, v0, b1, bq, wq, miss, quad, unit1, pay_a, pay_b, pair, scaler = refs
     slots = anc.shape[1]
-    rows = pieces[0].shape[0]
+    rows = pieces[0][0].shape[0]
     part = rows // 4
     depth = members * rows * 2
     me = lax.axis_index("particle")
@@ -183,16 +195,16 @@
         scaler[i * slots : (i + 1) * slots, :] = hits(g, want)
 
     pairs, quads = nb // 2, nb // 4
-    codes = decode(scaler[...], pieces, lanes(nb))
+    codes = decode(scaler[...], pieces, pairs)
     scale = [
         codes[i * slots : (i + 1) * slots] * (BOUNDS[f] / SCALE_STEPS / STEPS) for i, f in enumerate((0, 1, 0, 1, 2, 2))
     ]
     unit1[...] = scale[5]
 
     def step(m, acc):
-        wet = decode(quad[...], pieces, lanes(m, pairs * BLK))
+        wet = decode(quad[...], rains, m)
         for p in range(2):
-            got = decode(pair[...], pieces, lanes(m + p * quads))
+            got = decode(pair[...], pieces, m + p * quads)
             for h in range(2):
                 q = 2 * h + p
                 n = m + q * quads
@@ -220,17 +232,17 @@
 
 
 def inner01_kernel(members, unroll, *refs):
-    pieces = refs[:members]
-    wb, v0, b1, quad, unit1, flow, ids, growth, prec, obs, anc, rain = refs[members : members + 12]
-    r1, wb1, v1, b2, w2, ws, bs, v2, miss = refs[members + 12 :]
+    (wb, v0, b1, quad, unit1, flow, ids, growth, prec, obs, anc, rain), rains = refs[:12], refs[12 : 12 + members]
+    r1, wb1, v1, b2, w2, ws, bs, v2, miss = refs[12 + members :]
     nb, slots = wb.shape[:2]
+    rains = [(r, nb // 2 + 1) for r in rains[:2]] + [(r, 0) for r in rains[2:]]
     part = rain.shape[1]
     quads = nb // 4
     scale = unit1[...]
     base = lax.axis_index("tile") * nb
 
     def wet_day(m, carry):
-        got = decode(quad[...], pieces, lanes(m, 3 * quads * BLK))
+        got = decode(quad[...], rains, m + quads)
         for q in range(4):
             r1[m + q * quads] = got[q * slots : (q + 1) * slots] * scale
         return carry
@@ -472,17 +484,22 @@
     edge = ((HALO * depth + 16, BLK), bf16)
     tile = (HALO, NBR, BLK, BLK)
 
-    wire = pl.pallas_call(
+    wire, fields, rains = pl.pallas_call(
         pack_kernel,
         grid=(1,),
-        out_shape=jax.ShapeDtypeStruct((rows, (nb + 1) * BLK), i16),
+        out_shape=tuple(
+            jax.ShapeDtypeStruct((rows, n * BLK), i16) for n in (nb + 1, nb // 2 + 1, nb // 2)
+        ),
         in_specs=[pl.BlockSpec((part, cells), lambda i: (0, 0))] * 2
         + [pl.BlockSpec((2, part, cells), lambda i: (0, 0, 0))],
-        out_specs=VMEM,
+        out_specs=(VMEM, VMEM, VMEM),
         scratch_shapes=[pltpu.VMEM((rows, cells), f32), pltpu.VMEM((4, rows, BLK), f32)],
         compiler_params=pltpu.CompilerParams(vmem_limit_bytes=60 * 2**20),
         cost_estimate=weigh(1),
     )(biomass, water, rain)
+    def over(x, j):
+        return lax.ppermute(x, "particle", [(i, i ^ j) for i in range(members)])
+
     flow_a, flow_b = pl.pallas_call(
         edge_kernel,
         grid=(1,),
@@ -498,30 +515,36 @@
         cost_estimate=weigh(1),
     )(wire, flow_blocks, flow_blocks, neighbours)
 
-    pieces = [wire] + [
-        lax.ppermute(wire, "particle", [(i, i ^ j) for i in range(members)]) for j in range(1, members)
-    ]
+    beside = over(wire, 1)
+    far_rains = []
+    for j in range(2, members):
+        if j % 2 == 0:
+            far_rains.append(over(rains, j))
+        else:
+            got, flow_a = lax.optimization_barrier((far_rains[-1], flow_a))
+            far_rains.append(over(got, 1))
+    far_fields = [over(fields, j) for j in range(2, members)]
     small = (wire, growth_rate.reshape(nb, BLK), obs_precision.reshape(nb, BLK), observations, ancestors)
-    flow, pieces[0], growth, prec, obs, anc, rain23 = call(
+    flow, wire, growth, prec, obs, anc, rain23 = call(
         stage_kernel,
         [((nb, depth, BLK), bf16)] + [(x.shape, x.dtype) for x in small] + [((2, part, cells), f32)],
         [HBM] + [VMEM] * 7,
-    )(pieces[1], flow_blocks, *small, rain)
+    )(beside, flow_blocks, *small, rain)
     flow_a = lax.ppermute(flow_a, "tile", swap_a)
     flow_b = lax.ppermute(flow_b, "tile", swap_b)
 
     field = ((nb, slots, BLK), f32)
     wb, v0, b1, bq, wq, miss, quad, unit1, pay_a, pay_b = call(
-        functools.partial(open_kernel, members, unroll),
+        functools.partial(open_kernel, members, unroll, nb),
         [((nb, slots, BLK), bf16), field, field, field, field, ((slots, BLK), f32), ((4 * slots, members * rows * 2), bf16), ((slots, BLK), f32)]
         + [((WIDE + 2 * HALO, slots, BLK), bf16)] * 2,
-        [VMEM] * (members + 4),
+        [VMEM] * (2 * members + 2),
         [
             pltpu.VMEM((8 * slots, members * rows * 2), bf16),
             pltpu.VMEM((6 * slots, members * rows * 2), bf16),
         ],
         cost=10**10,
-    )(*pieces, anc, growth, prec, obs)
+    )(wire, beside, *far_fields, *far_rains, anc, growth, prec, obs)
     got_a = lax.ppermute(pay_a, "tile", swap_a)
     got_b = lax.ppermute(pay_b, "tile", swap_b)
     inner, core = nb - 2 * HALO, nb - 2 * WIDE
@@ -534,8 +557,10 @@
         [blocks(nb), blocks(inner, kind=bf16), blocks(inner), blocks(inner), blocks(core)]
         + [blocks(core, part)] * 3
         + [((slots, BLK), f32)],
-        [VMEM] * (members + 6) + [SMEM] + [VMEM] * 3 + [SMEM, VMEM],
-    )(*pieces, wb, v0, b1, quad, unit1, flow, neighbours, growth, prec, obs, ancestors, rain23)
+        [VMEM] * 6 + [SMEM] + [VMEM] * 3 + [SMEM] + [VMEM] * (1 + members),
+    )(
+        wb, v0, b1, quad, unit1, flow, neighbours, growth, prec, obs, ancestors, rain23, wire, beside, *far_rains
+    )
     swap_rows = (WIDE + HALO) * part
     b2_edge, w2_edge, ws, bs, v2, total, end_a, end_b = call(
         functools.partial(outer01_kernel, unroll),

time: 36.7 us -> 40.7 us (1.11)
  starting transfers between devices: 17.1 us -> 19.2 us
  waiting for transfers between devices: 5.34 us -> 7.04 us
    ppermute x1, waiting for transfers between devices: 0.49 us -> 5.94 us  [body(): got_b = lax.ppermute(pay_b, 'tile', swap_b)]
    ppermute x3 -> x5, starting transfers between devices: 5.62 us -> 10.6 us  [over(): return lax.ppermute(x, 'particle', [(i, i ^ j) for i in range(members)])]
    ppermute x3 -> x5, waiting for transfers between devices: 4.83 us -> 0.72 us  [over(): return lax.ppermute(x, 'particle', [(i, i ^ j) for i in range(members)])]
    ppermute x1, starting transfers between devices: 2.77 us -> 0.01 us  [body(): flow_b = lax.ppermute(flow_b, 'tile', swap_b)]
    ppermute x1, starting transfers between devices: 0.01 us -> 1.6 us  [body(): flow_a = lax.ppermute(flow_a, 'tile', swap_a)]
    ppermute x1, starting transfers between devices: 2.39 us -> 0.84 us  [body(): last_b = lax.ppermute(end_b, 'tile', swap_b)]
  transfers between devices with their start and end apart: 12 -> 14, of which waited for: 2 -> 5; matrix products, arithmetic and copies ran while one was open for 0% -> 0% of each run, Pallas kernels for 25% -> 22%
where the time goes in v5:
time: 40.7 us; the launch traced here: 40.5 us
  starting transfers between devices  19.2 us (47%)
  Pallas kernels  13.4 us (33%)
  waiting for transfers between devices  7.04 us (17%)
  between operations  0.78 us (2%)
    ppermute x5, starting transfers between devices, over(): return lax.ppermute(x, 'particle', [(i, i ^ j) for i in range(members)])  10.6 us
    ppermute x1, waiting for transfers between devices, body(): got_b = lax.ppermute(pay_b, 'tile', swap_b)  5.94 us
    ppermute x3, starting transfers between devices, body(): lax.ppermute(total, 'tile', [(i, i ^ m) for i in range(tiles)])  3.49 us
    ppermute x1, starting transfers between devices, body(): got_b = lax.ppermute(pay_b, 'tile', swap_b)  2.57 us
    pallas_call x1, Pallas kernels, body(): pl.pallas_call(edge_kernel, grid=(1,), out_shape=tuple((jax.ShapeDtypeStr...  2.26 us
    pallas_call x1, Pallas kernels, body(): call(outer23_kernel, [((part, cells), f32)] * 2, [VMEM] * 11 + [SMEM] + [...  2.25 us
    pallas_call x1, Pallas kernels, body(): pl.pallas_call(pack_kernel, grid=(1,), out_shape=tuple((jax.ShapeDtypeStr...  1.83 us
    pallas_call x1, Pallas kernels, body(): call(functools.partial(outer01_kernel, unroll), [blocks(2 * HALO), blocks...  1.7 us
  transfers between devices with their start and end apart: 14, of which 5 were waited for; matrix products, arithmetic and copies ran while one was open for 0% of the time, Pallas kernels for 22%

profile of v5, /device:TPU:0, one launch (start us, length us, event | category | flops | bytes accessed | tf_op | source)
XLA Modules:
  0.0 40.5 jit_solution(441107612791088621)
XLA Ops:
  0.6 1.8 %shard_map.112 = (s16[16,4224]{1,0:T(8,128)(2,1)}, s16[16,2176]{1,0:T(8,128)(2,1)}, s16[16,2048]{1,0:T(8,128)(2,1)}) custom-call(f32[4,4096]{1,0:T(4,128)} %bio.1, f32[4,4096]{1,0:T(4,128)} %wat.1, f32[4,4,4096]{2,1,0:T(4,128)} %rain.3), custom_call_target="tpu_custom_call" | custom-call | flops 1 | bytes 1 | tf_op jit(solution)/shard_map/pallas_call | solution.py:487
  2.5 3.0 %collective-permute-start = (s16[16,4224]{1,0:T(8,128)(2,1)}, s16[16,4224]{1,0:T(8,128)(2,1)S(1)}, u32[]{:S(2)}, u32[]{:S(2)}) collective-permute-start(s16[16,4224]{1,0:T(8,128)(2,1)} %get-tuple-element.49.wire.after), channel_id=1, source_target_pairs={{0,8},{8,0},{16,24},{24,16},{1,9},{9,1},{17,25},{25,17},{2,10},{10... | collective-permute-start | bytes 405512 | tf_op jit(solution)/shard_map/ppermute | solution.py:501
  5.5 2.6 %collective-permute-start.3 = (s16[16,2048]{1,0:T(8,128)(2,1)}, s16[16,2048]{1,0:T(8,128)(2,1)S(1)}, u32[]{:S(2)}, u32[]{:S(2)}) collective-permute-start(s16[16,2048]{1,0:T(8,128)(2,1)} %get-tuple-element.52), channel_id=1, source_target_pairs={{0,16},{8,24},{16,0},{24,8},{1,17},{9,25},{17,1},{25,9},{2,18},{10... | collective-permute-start | bytes 196616 | tf_op jit(solution)/shard_map/ppermute | solution.py:501
  8.1 0.0 collective-permute-start.2
  8.1 1.9 %collective-permute-start.1 = (s16[16,2176]{1,0:T(8,128)(2,1)}, s16[16,2176]{1,0:T(8,128)(2,1)S(1)}, u32[]{:S(2)}, u32[]{:S(2)}) collective-permute-start(s16[16,2176]{1,0:T(8,128)(2,1)} %get-tuple-element.51), channel_id=1, source_target_pairs={{0,16},{8,24},{16,0},{24,8},{1,17},{9,25},{17,1},{25,9},{2,18},{10... | collective-permute-start | bytes 208904 | tf_op jit(solution)/shard_map/ppermute | solution.py:501
  10.0 0.0 copy-start.5
  10.0 0.0 copy-start.6
  10.0 0.0 copy-start.7
  10.0 2.3 %shard_map.114 = (bf16[1552,128]{1,0:T(8,128)(2,1)}, bf16[1552,128]{1,0:T(8,128)(2,1)}) custom-call(s16[16,4224]{1,0:T(8,128)(2,1)} %get-tuple-element.49.wire.after, bf16[32,3,128,128]{3,2,1,0:T(8,128)(2,1)} %right.1, bf16[32,3,128,128]{3,2,1,0:T(8,128)(2,1)} %right.1, s32[3,32]{1,0:T(4,128)} %bitcast.3), custom_call_target="tpu_custom_call" | custom-call | flops 1 | bytes 1 | tf_op jit(solution)/shard_map/pallas_call | solution.py:503
  12.3 0.1 collective-permute-done.3.refs_4_.refs_14_
  12.4 3.1 %collective-permute-start.4 = (s16[16,2048]{1,0:T(8,128)(2,1)S(1)}, s16[16,2048]{1,0:T(8,128)(2,1)S(1)}, u32[]{:S(2)}, u32[]{:S(2)}) collective-permute-start(s16[16,2048]{1,0:T(8,128)(2,1)S(1)} %collective-permute-done.3.refs_4_.refs_14_), channel_id=1, source_target_pairs={{0,8},{8,0},{16,24},{24,16},{1,9},{9,1},{17,25},{25,17},{2,10},{10... | collective-permute-start | bytes 196616 | tf_op jit(solution)/shard_map/ppermute | solution.py:501
  15.5 0.0 collective-permute-start.8
  15.5 0.0 collective-permute-done.after.refs_1_.refs_13_
  15.5 1.6 %collective-permute-start.7 = (bf16[1552,128]{1,0:T(8,128)(2,1)}, bf16[1552,128]{1,0:T(8,128)(2,1)S(1)}, u32[]{:S(2)}, u32[]{:S(2)}) collective-permute-start(bf16[1552,128]{1,0:T(8,128)(2,1)} %get-tuple-element.77), channel_id=1, source_target_pairs={{0,1},{1,0},{2,3},{3,2},{4,5},{5,4},{6,7},{7,6},{8,9},{9,8},{10,11... | collective-permute-start | bytes 1191944 | tf_op jit(solution)/shard_map/ppermute | solution.py:533
  17.1 0.0 copy-done
  17.1 0.0 copy-done.1
  17.1 0.0 copy-done.2
  17.1 0.0 copy-done.4
  17.1 0.0 copy-done.5
  17.1 0.0 copy-done.6
  17.1 0.0 copy-done.7
  17.1 0.9 %shard_map.113 = (bf16[32,384,128]{2,1,0:T(8,128)(2,1)S(1)}, s16[16,4224]{1,0:T(8,128)(2,1)S(1)}, f32[32,128]{1,0:T(8,128)S(1)}, f32[32,128]{1,0:T(8,128)S(1)}, ...) custom-call(s16[16,4224]{1,0:T(8,128)(2,1)S(1)} %collective-permute-done.after.refs_1_.refs_13_, ...), custom_call_target="tpu_custom_call" | custom-call | flops 1 | bytes 1 | tf_op jit(solution)/shard_map/pallas_call | solution.py:528
  18.0 0.0 collective-permute-done.2.refs_3_
  18.0 0.1 collective-permute-done.1.refs_2_
  18.2 0.4 %collective-permute-done.4.refs_5_.refs_15_ = s16[16,2048]{1,0:T(8,128)(2,1)S(1)} collective-permute-done((s16[16,2048]{1,0:T(8,128)(2,1)S(1)}, s16[16,2048]{1,0:T(8,128)(2,1)S(1)}, u32[]{:S(2)}, u32[]{:S(2)}) %collective-permute-start.4) | collective-permute-done | bytes 65568 | tf_op jit(solution)/shard_map/ppermute | solution.py:501
  18.6 0.5 %shard_map.115 = (bf16[32,16,128]{2,1,0:T(8,128)(2,1)S(1)}, f32[32,16,128]{2,1,0:T(8,128)S(1)}, f32[32,16,128]{2,1,0:T(8,128)S(1)}, f32[32,16,128]{2,1,0:T(8,128...) custom-call(s16[16,4224]{1,0:T(8,128)(2,1)S(1)} %get-tuple-element.5, ...), custom_call_target="tpu_custom_call" | custom-call | flops 10000000000 | bytes 1 | tf_op jit(solution)/shard_map/pallas_call | solution.py:537
  19.1 0.1 collective-permute-start.5
  19.2 2.6 %collective-permute-start.6 = (bf16[16,16,128]{2,1,0:T(8,128)(2,1)S(1)}, bf16[16,16,128]{2,1,0:T(8,128)(2,1)S(1)}, u32[]{:S(2)}, u32[]{:S(2)}) collective-permute-start(bf16[16,16,128]{2,1,0:T(8,128)(2,1)S(1)} %get-tuple-element.76), channel_id=1, source_target_pairs={{0,7},{1,2},{2,1},{3,4},{4,3},{5,6},{6,5},{7,0},{8,15},{9,10},{10,... | collective-permute-start | bytes 196616 | tf_op jit(solution)/shard_map/ppermute | solution.py:549
  21.8 0.0 copy-done.3
  21.8 1.7 %shard_map.116 = (f32[32,16,128]{2,1,0:T(8,128)S(1)}, bf16[24,16,128]{2,1,0:T(8,128)(2,1)S(1)}, f32[24,16,128]{2,1,0:T(8,128)S(1)}, f32[24,16,128]{2,1,0:T(8,128...) custom-call(bf16[32,16,128]{2,1,0:T(8,128)(2,1)S(1)} %get-tuple-elem, ...), custom_call_target="tpu_custom_call" | custom-call | flops 1 | bytes 1 | tf_op jit(solution)/shard_map/pallas_call | solution.py:555
  23.5 0.0 collective-permute-done.5.got_a
  23.5 5.9 %collective-permute-done.6.got_b = bf16[16,16,128]{2,1,0:T(8,128)(2,1)S(1)} collective-permute-done((bf16[16,16,128]{2,1,0:T(8,128)(2,1)S(1)}, bf16[16,16,128]{2,1,0:T(8,128)(2,1)S(1)}, u32[]{:S(2)}, u32[]{:S(2)}) %collective-permute-start.6) | collective-permute-done | bytes 65568 | tf_op jit(solution)/shard_map/ppermute | solution.py:549
  29.4 0.0 collective-permute-done.8.flow_b
  29.4 0.0 collective-permute-done.7.flow_a
  29.4 1.7 %shard_map.117 = (f32[8,16,128]{2,1,0:T(8,128)S(1)}, f32[16,16,128]{2,1,0:T(8,128)S(1)}, f32[32,4,128]{2,1,0:T(4,128)S(1)}, f32[32,4,128]{2,1,0:T(4,128)S(1)}, f...) custom-call(bf16[32,16,128]{2,1,0:T(8,128)(2,1)S(1)} %get-tuple-element.59.refs, ...), custom_call_target="tpu_custom_call" | custom-call | flops 1 | bytes 1 | tf_op jit(solution)/shard_map/pallas_call | solution.py:565
  31.1 0.1 collective-permute-start.9
  31.2 0.8 %collective-permute-start.13 = (f32[48,128]{1,0:T(8,128)S(1)}, f32[48,128]{1,0:T(8,128)S(1)}, u32[]{:S(2)}, u32[]{:S(2)}) collective-permute-start(f32[48,128]{1,0:T(8,128)S(1)} %get-tuple-element.92), channel_id=1, source_target_pairs={{0,7},{1,2},{2,1},{3,4},{4,3},{5,6},{6,5},{7,0},{8,15},{9,10},{10,... | collective-permute-start | bytes 73736 | tf_op jit(solution)/shard_map/ppermute | solution.py:581
  32.0 0.4 collective-permute-done.9.got_a
  32.4 1.1 %collective-permute-start.12 = (f32[32,128]{1,0:T(8,128)S(1)}, f32[32,128]{1,0:T(8,128)S(1)}, u32[]{:S(2)}, u32[]{:S(2)}) collective-permute-start(f32[32,128]{1,0:T(8,128)S(1)} %slice_add_fusion.refs_0_), channel_id=1, source_target_pairs={{0,6},{1,7},{2,4},{3,5},{4,2},{5,3},{6,0},{7,1},{8,14},{9,15},{10,... | collective-permute-start | bytes 49160 | tf_op jit(solution)/shard_map/ppermute | solution.py:588
  33.5 1.3 %collective-permute-start.11 = (f32[32,128]{1,0:T(8,128)S(1)}, f32[32,128]{1,0:T(8,128)S(1)}, u32[]{:S(2)}, u32[]{:S(2)}) collective-permute-start(f32[32,128]{1,0:T(8,128)S(1)} %slice_add_fusion.refs_0_), channel_id=1, source_target_pairs={{0,4},{1,5},{2,6},{3,7},{4,0},{5,1},{6,2},{7,3},{8,12},{9,13},{10,... | collective-permute-start | bytes 49160 | tf_op jit(solution)/shard_map/ppermute | solution.py:588
  34.8 1.1 %collective-permute-start.10 = (f32[32,128]{1,0:T(8,128)S(1)}, f32[32,128]{1,0:T(8,128)S(1)}, u32[]{:S(2)}, u32[]{:S(2)}) collective-permute-start(f32[32,128]{1,0:T(8,128)S(1)} %slice_add_fusion.refs_0_), channel_id=1, source_target_pairs={{0,2},{1,3},{2,0},{3,1},{4,6},{5,7},{6,4},{7,5},{8,10},{9,11},{10,... | collective-permute-start | bytes 49160 | tf_op jit(solution)/shard_map/ppermute | solution.py:588
  35.9 1.5 %shard_map.119 = (f32[24,4,128]{2,1,0:T(4,128)S(1)}, f32[16,4,128]{2,1,0:T(4,128)S(1)}, f32[16,4,128]{2,1,0:T(4,128)S(1)}) custom-call(f32[32,4,128]{2,1,0:T(4,128)S(1)} %get-tuple-element.86.ws, f32[32,4,128]{2,1,0:T(4,128)S(1)} %get-tuple-element.87.bs, f32[32,4,128]{2,1,0:T(4,128)S(1)} %get-tuple-element.88.v2, ...), custom_call_target="tpu_custom_call" | custom-call | flops 1 | bytes 1 | tf_op jit(solution)/shard_map/pallas_call | solution.py:590
  37.4 0.0 collective-permute-done.13.got_b
  37.4 2.3 %shard_map.120 = (f32[4,4096]{1,0:T(4,128)}, f32[4,4096]{1,0:T(4,128)}) custom-call(f32[32,4,128]{2,1,0:T(4,128)S(1)} %get-tuple-element.86.ws, f32[32,4,128]{2,1,0:T(4,128)S(1)} %get-tuple-element.87.bs, f32[32,4,128]{2,1,0:T(4,128)S(1)} %get-tuple-element.88.v2, f32[24,4,128]{2,1,0:T(4,128)S(1)} %get-tuple-element.89.w3, ...), custom_call_target="tpu_custom_call" | custom-call | flops 1 | bytes 1 | tf_op jit(solution)/shard_map/pallas_call | solution.py:595
  39.6 0.0 collective-permute-done.12.refs_3_
  39.6 0.0 collective-permute-done.11.refs_2_
  39.6 0.0 collective-permute-done.10.refs_1_
  39.6 0.9 %shard_map.118 = f32[2,2,4096]{2,1,0:T(2,128)} custom-call(f32[32,128]{1,0:T(8,128)S(1)} %slice_add_fusion.refs_0_, f32[32,128]{1,0:T(8,128)S(1)} %collective-permute-done.10.refs_1_, f32[32,128]{1,0:T(8,128)S(1)} %collective-permute-done.11.refs_2_, f32[32,128]{1,0:T(8,128)S(1)} %collective-permute-done.12.refs_3_, ...), custom_call_target="tpu_custom_call" | custom-call | flops 1 | bytes 1 | tf_op jit(solution)/shard_map/pallas_call | solution.py:601
  (6 shorter events, 0.0 us)
Async XLA Ops:
  2.5 13.0 %collective-permute-start = (s16[16,4224]{1,0:T(8,128)(2,1)}, s16[16,4224]{1,0:T(8,128)(2,1)S(1)}, u32[]{:S(2)}, u32[]{:S(2)}) collective-permute-start(s16[16,4224]{1,0:T(8,128)(2,1)} %get-tuple-element.49.wire.after), channel_id=1, source_target_pairs={{0,8},{8,0},{16,24},{24,16},{1,9},{9,1},{17,25},{25,17},{2,10},{10... | collective-permute-start | bytes 405512 | tf_op jit(solution)/shard_map/ppermute | solution.py:501
  5.5 6.9 %collective-permute-start.3 = (s16[16,2048]{1,0:T(8,128)(2,1)}, s16[16,2048]{1,0:T(8,128)(2,1)S(1)}, u32[]{:S(2)}, u32[]{:S(2)}) collective-permute-start(s16[16,2048]{1,0:T(8,128)(2,1)} %get-tuple-element.52), channel_id=1, source_target_pairs={{0,16},{8,24},{16,0},{24,8},{1,17},{9,25},{17,1},{25,9},{2,18},{10... | collective-permute-start | bytes 196616 | tf_op jit(solution)/shard_map/ppermute | solution.py:501
  8.1 10.0 %collective-permute-start.2 = (s16[16,2176]{1,0:T(8,128)(2,1)}, s16[16,2176]{1,0:T(8,128)(2,1)S(1)}, u32[]{:S(2)}, u32[]{:S(2)}) collective-permute-start(s16[16,2176]{1,0:T(8,128)(2,1)} %get-tuple-element.51), channel_id=1, source_target_pairs={{0,24},{8,16},{16,8},{24,0},{1,25},{9,17},{17,9},{25,1},{2,26},{10... | collective-permute-start | bytes 208904 | tf_op jit(solution)/shard_map/ppermute | solution.py:501
  8.1 10.1 %collective-permute-start.1 = (s16[16,2176]{1,0:T(8,128)(2,1)}, s16[16,2176]{1,0:T(8,128)(2,1)S(1)}, u32[]{:S(2)}, u32[]{:S(2)}) collective-permute-start(s16[16,2176]{1,0:T(8,128)(2,1)} %get-tuple-element.51), channel_id=1, source_target_pairs={{0,16},{8,24},{16,0},{24,8},{1,17},{9,25},{17,1},{25,9},{2,18},{10... | collective-permute-start | bytes 208904 | tf_op jit(solution)/shard_map/ppermute | solution.py:501
  10.0 7.1 %copy-start = (bf16[32,3,128,128]{3,2,1,0:T(8,128)(2,1)S(1)}, bf16[32,3,128,128]{3,2,1,0:T(8,128)(2,1)}, u32[]{:S(2)}) copy-start(bf16[32,3,128,128]{3,2,1,0:T(8,128)(2,1)} %right.1) | copy-start | bytes 9437188
  10.0 7.1 %copy-start.1 = (f32[4,4,4096]{2,1,0:T(4,128)S(1)}, f32[4,4,4096]{2,1,0:T(4,128)}, u32[]{:S(2)}) copy-start(f32[4,4,4096]{2,1,0:T(4,128)} %rain.3) | copy-start | bytes 786436
  10.0 7.1 %copy-start.2 = (s16[16,4224]{1,0:T(8,128)(2,1)S(1)}, s16[16,4224]{1,0:T(8,128)(2,1)}, u32[]{:S(2)}) copy-start(s16[16,4224]{1,0:T(8,128)(2,1)} %get-tuple-element.49.wire.after) | copy-start | bytes 405508
  10.0 7.1 %copy-start.4 = (f32[2,4096]{1,0:T(2,128)S(1)}, f32[2,4096]{1,0:T(2,128)}, u32[]{:S(2)}) copy-start(f32[2,4096]{1,0:T(2,128)} %obs.1) | copy-start | bytes 98308
  10.0 7.1 %copy-start.5 = (f32[4096]{0:T(1024)S(1)}, f32[4096]{0:T(1024)}, u32[]{:S(2)}) copy-start(f32[4096]{0:T(1024)} %param.14) | copy-start | bytes 49156
  10.0 7.1 %copy-start.6 = (f32[4096]{0:T(1024)S(1)}, f32[4096]{0:T(1024)}, u32[]{:S(2)}) copy-start(f32[4096]{0:T(1024)} %param.16) | copy-start | bytes 49156
  10.0 7.1 %copy-start.7 = (s32[2,16]{1,0:T(2,128)S(1)}, s32[2,16]{1,0:T(2,128)}, u32[]{:S(2)}) copy-start(s32[2,16]{1,0:T(2,128)} %anc.3) | copy-start | bytes 388
  12.4 6.2 %collective-permute-start.4 = (s16[16,2048]{1,0:T(8,128)(2,1)S(1)}, s16[16,2048]{1,0:T(8,128)(2,1)S(1)}, u32[]{:S(2)}, u32[]{:S(2)}) collective-permute-start(s16[16,2048]{1,0:T(8,128)(2,1)S(1)} %collective-permute-done.3.refs_4_.refs_14_), channel_id=1, source_target_pairs={{0,8},{8,0},{16,24},{24,16},{1,9},{9,1},{17,25},{25,17},{2,10},{10... | collective-permute-start | bytes 196616 | tf_op jit(solution)/shard_map/ppermute | solution.py:501
  15.5 13.9 %collective-permute-start.8 = (bf16[1552,128]{1,0:T(8,128)(2,1)}, bf16[1552,128]{1,0:T(8,128)(2,1)S(1)}, u32[]{:S(2)}, u32[]{:S(2)}) collective-permute-start(bf16[1552,128]{1,0:T(8,128)(2,1)} %get-tuple-element.78), channel_id=1, source_target_pairs={{0,7},{1,2},{2,1},{3,4},{4,3},{5,6},{6,5},{7,0},{8,15},{9,10},{10,... | collective-permute-start | bytes 1191944 | tf_op jit(solution)/shard_map/ppermute | solution.py:534
  15.5 13.9 %collective-permute-start.7 = (bf16[1552,128]{1,0:T(8,128)(2,1)}, bf16[1552,128]{1,0:T(8,128)(2,1)S(1)}, u32[]{:S(2)}, u32[]{:S(2)}) collective-permute-start(bf16[1552,128]{1,0:T(8,128)(2,1)} %get-tuple-element.77), channel_id=1, source_target_pairs={{0,1},{1,0},{2,3},{3,2},{4,5},{5,4},{6,7},{7,6},{8,9},{9,8},{10,11... | collective-permute-start | bytes 1191944 | tf_op jit(solution)/shard_map/ppermute | solution.py:533
  18.6 3.2 %copy-start.3 = (s32[32,3]{0,1:T(4,128)S(1)}, s32[32,3]{0,1:T(4,128)}, u32[]{:S(2)}) copy-start(s32[32,3]{0,1:T(4,128)} %param.12) | copy-start | bytes 1156
  19.1 4.3 %collective-permute-start.5 = (bf16[16,16,128]{2,1,0:T(8,128)(2,1)S(1)}, bf16[16,16,128]{2,1,0:T(8,128)(2,1)S(1)}, u32[]{:S(2)}, u32[]{:S(2)}) collective-permute-start(bf16[16,16,128]{2,1,0:T(8,128)(2,1)S(1)} %get-tuple-element.75), channel_id=1, source_target_pairs={{0,1},{1,0},{2,3},{3,2},{4,5},{5,4},{6,7},{7,6},{8,9},{9,8},{10,11... | collective-permute-start | bytes 196616 | tf_op jit(solution)/shard_map/ppermute | solution.py:548
  19.2 10.2 %collective-permute-start.6 = (bf16[16,16,128]{2,1,0:T(8,128)(2,1)S(1)}, bf16[16,16,128]{2,1,0:T(8,128)(2,1)S(1)}, u32[]{:S(2)}, u32[]{:S(2)}) collective-permute-start(bf16[16,16,128]{2,1,0:T(8,128)(2,1)S(1)} %get-tuple-element.76), channel_id=1, source_target_pairs={{0,7},{1,2},{2,1},{3,4},{4,3},{5,6},{6,5},{7,0},{8,15},{9,10},{10,... | collective-permute-start | bytes 196616 | tf_op jit(solution)/shard_map/ppermute | solution.py:549
  31.1 1.3 %collective-permute-start.9 = (f32[80,128]{1,0:T(8,128)S(1)}, f32[80,128]{1,0:T(8,128)S(1)}, u32[]{:S(2)}, u32[]{:S(2)}) collective-permute-start(f32[80,128]{1,0:T(8,128)S(1)} %get-tuple-element.80), channel_id=1, source_target_pairs={{0,1},{1,0},{2,3},{3,2},{4,5},{5,4},{6,7},{7,6},{8,9},{9,8},{10,11... | collective-permute-start | bytes 122888 | tf_op jit(solution)/shard_map/ppermute | solution.py:580
  31.2 6.2 %collective-permute-start.13 = (f32[48,128]{1,0:T(8,128)S(1)}, f32[48,128]{1,0:T(8,128)S(1)}, u32[]{:S(2)}, u32[]{:S(2)}) collective-permute-start(f32[48,128]{1,0:T(8,128)S(1)} %get-tuple-element.92), channel_id=1, source_target_pairs={{0,7},{1,2},{2,1},{3,4},{4,3},{5,6},{6,5},{7,0},{8,15},{9,10},{10,... | collective-permute-start | bytes 73736 | tf_op jit(solution)/shard_map/ppermute | solution.py:581
  32.4 7.2 %collective-permute-start.12 = (f32[32,128]{1,0:T(8,128)S(1)}, f32[32,128]{1,0:T(8,128)S(1)}, u32[]{:S(2)}, u32[]{:S(2)}) collective-permute-start(f32[32,128]{1,0:T(8,128)S(1)} %slice_add_fusion.refs_0_), channel_id=1, source_target_pairs={{0,6},{1,7},{2,4},{3,5},{4,2},{5,3},{6,0},{7,1},{8,14},{9,15},{10,... | collective-permute-start | bytes 49160 | tf_op jit(solution)/shard_map/ppermute | solution.py:588
  33.5 6.2 %collective-permute-start.11 = (f32[32,128]{1,0:T(8,128)S(1)}, f32[32,128]{1,0:T(8,128)S(1)}, u32[]{:S(2)}, u32[]{:S(2)}) collective-permute-start(f32[32,128]{1,0:T(8,128)S(1)} %slice_add_fusion.refs_0_), channel_id=1, source_target_pairs={{0,4},{1,5},{2,6},{3,7},{4,0},{5,1},{6,2},{7,3},{8,12},{9,13},{10,... | collective-permute-start | bytes 49160 | tf_op jit(solution)/shard_map/ppermute | solution.py:588
  34.8 4.8 %collective-permute-start.10 = (f32[32,128]{1,0:T(8,128)S(1)}, f32[32,128]{1,0:T(8,128)S(1)}, u32[]{:S(2)}, u32[]{:S(2)}) collective-permute-start(f32[32,128]{1,0:T(8,128)S(1)} %slice_add_fusion.refs_0_), channel_id=1, source_target_pairs={{0,2},{1,3},{2,0},{3,1},{4,6},{5,7},{6,4},{7,5},{8,10},{9,11},{10,... | collective-permute-start | bytes 49160 | tf_op jit(solution)/shard_map/ppermute | solution.py:588

commit v6 on v4

--- a/solution.py
+++ b/solution.py
@@ -47,7 +47,27 @@
     return lax.rem(lax.axis_index("tile"), 2) == 0
 
 
-def pack_kernel(bio, wat, rain, wire, held, factor):
+def pack_kernel(bio, wat, rain, flow, ids, wire, pay_a, pay_b, held, factor, gaps, sems):
+    nb = ids.shape[1]
+    depth = NBR * BLK
+    span = HALO * depth
+    even = right_first()
+    pos = lax.axis_index("tile")
+    line = lax.broadcasted_iota(jnp.int32, (16, BLK), 0)
+    copies = []
+    for i, (pay, right) in enumerate(((pay_a, even), (pay_b, jnp.logical_not(even)))):
+        start = jnp.where(right, nb - HALO, 0)
+        away = jnp.zeros((16, BLK), jnp.float32)
+        for m in range(HALO):
+            n = start + m + pos * nb
+            for k, gap in enumerate((n - ids[1, start + m], ids[2, start + m] - n)):
+                away = jnp.where(line == 2 * m + k, gap.astype(jnp.float32), away)
+        gaps[i] = away.astype(jnp.bfloat16)
+        at = pl.multiple_of(start * depth, depth)
+        copies.append(pltpu.make_async_copy(flow.at[pl.ds(at, span)], pay.at[pl.ds(0, span)], sems.at[2 * i]))
+        copies.append(pltpu.make_async_copy(gaps.at[i], pay.at[pl.ds(span, 16)], sems.at[2 * i + 1]))
+    for c in copies:
+        c.start()
     part, cells = bio.shape
     nb = cells // BLK
     half, quarter = cells // 2, cells // 4
@@ -80,35 +100,8 @@
     for n in range(nb):
         wire[:, lanes(n)] = coded(held[:, lanes(n)] * factor[0 if n < pairs else 1 if n < pairs + quads else 2])
     wire[:, lanes(nb)] = coded(factor[3])
-
-
-def edge_kernel(after, left, right, ids, pay_a, pay_b):
-    nb = ids.shape[1]
-    even = right_first()
-    pos = lax.axis_index("tile")
-    line = lax.broadcasted_iota(jnp.int32, (16, BLK), 0)
-
-    def edge(pay, block, start):
-        away = jnp.zeros((16, BLK), jnp.float32)
-        for m in range(HALO):
-            n = start + m + pos * nb
-            for k in range(NBR):
-                at = (m * NBR + k) * BLK
-                pay[at : at + BLK, :] = block[m, k]
-            for k, gap in enumerate((n - ids[1, start + m], ids[2, start + m] - n)):
-                away = jnp.where(line == 2 * m + k, gap.astype(jnp.float32), away)
-        at = HALO * NBR * BLK
-        pay[at : at + 16, :] = away.astype(jnp.bfloat16)
-
-    @pl.when(even)
-    def _():
-        edge(pay_a, right, nb - HALO)
-        edge(pay_b, left, 0)
-
-    @pl.when(jnp.logical_not(even))
-    def _():
-        edge(pay_a, left, 0)
-        edge(pay_b, right, nb - HALO)
+    for c in copies:
+        c.wait()
 
 
 def stage_kernel(after, flow, wire, growth, prec, obs, anc, rain, turned, *held):
@@ -131,13 +124,7 @@
         for d in range(HALO + 1):
             x = jnp.where(gap == d, ext[at + sign * d].astype(jnp.float32), x)
         xs.append(x.astype(jnp.bfloat16))
-    total = jnp.zeros(ext.shape[1:], jnp.float32)
-    for k, x in enumerate(xs):
-        at = m * depth + k * BLK
-        total += lax.dot_general(
-            x, pay[at : at + BLK, :], (((1,), (1,)), ((), ())), preferred_element_type=jnp.float32
-        )
-    return total
+    return flux_of(xs, pay[m * depth : (m + 1) * depth, :])
 
 
 def decode(sel, pieces, cols):
@@ -221,8 +208,8 @@
 
 def inner01_kernel(members, unroll, *refs):
     pieces = refs[:members]
-    wb, v0, b1, quad, unit1, flow, ids, growth, prec, obs, anc, rain = refs[members : members + 12]
-    r1, wb1, v1, b2, w2, ws, bs, v2, miss = refs[members + 12 :]
+    wb, v0, b1, quad, unit1, flow, ids, growth, prec, obs, anc, rain, flow_a, flow_b = refs[members : members + 14]
+    r1, wb1, v1, b2, w2, ws, bs, v2, miss, turn_a, turn_b = refs[members + 14 :]
     nb, slots = wb.shape[:2]
     part = rain.shape[1]
     quads = nb // 4
@@ -261,6 +248,10 @@
         return carry
 
     run(WIDE, nb - WIDE, unroll, pick, 0)
+    for raw, turned in ((flow_a, turn_a), (flow_b, turn_b)):
+        for at in range(0, HALO * NBR * BLK, BLK):
+            turned[at : at + BLK, :] = raw[at : at + BLK, :].T
+        turned[HALO * NBR * BLK :, :] = raw[HALO * NBR * BLK :, :]
 
 
 def settle(n, w, b1, r1, growth, prec, obs, acc):
@@ -470,33 +461,22 @@
 
     depth = NBR * BLK
     edge = ((HALO * depth + 16, BLK), bf16)
-    tile = (HALO, NBR, BLK, BLK)
-
-    wire = pl.pallas_call(
+    wire, flow_a, flow_b = pl.pallas_call(
         pack_kernel,
         grid=(1,),
-        out_shape=jax.ShapeDtypeStruct((rows, (nb + 1) * BLK), i16),
+        out_shape=(jax.ShapeDtypeStruct((rows, (nb + 1) * BLK), i16), *(jax.ShapeDtypeStruct(*edge) for _ in range(2))),
         in_specs=[pl.BlockSpec((part, cells), lambda i: (0, 0))] * 2
-        + [pl.BlockSpec((2, part, cells), lambda i: (0, 0, 0))],
-        out_specs=VMEM,
-        scratch_shapes=[pltpu.VMEM((rows, cells), f32), pltpu.VMEM((4, rows, BLK), f32)],
+        + [pl.BlockSpec((2, part, cells), lambda i: (0, 0, 0)), HBM, SMEM],
+        out_specs=(VMEM, HBM, HBM),
+        scratch_shapes=[
+            pltpu.VMEM((rows, cells), f32),
+            pltpu.VMEM((4, rows, BLK), f32),
+            pltpu.VMEM((2, 16, BLK), bf16),
+            pltpu.SemaphoreType.DMA((4,)),
+        ],
         compiler_params=pltpu.CompilerParams(vmem_limit_bytes=60 * 2**20),
         cost_estimate=weigh(1),
-    )(biomass, water, rain)
-    flow_a, flow_b = pl.pallas_call(
-        edge_kernel,
-        grid=(1,),
-        out_shape=tuple(jax.ShapeDtypeStruct(*edge) for _ in range(2)),
-        in_specs=[
-            HBM,
-            pl.BlockSpec(tile, lambda i: (0, 0, 0, 0)),
-            pl.BlockSpec(tile, lambda i: (nb // HALO - 1, 0, 0, 0)),
-            SMEM,
-        ],
-        out_specs=(VMEM, VMEM),
-        compiler_params=pltpu.CompilerParams(vmem_limit_bytes=60 * 2**20),
-        cost_estimate=weigh(1),
-    )(wire, flow_blocks, flow_blocks, neighbours)
+    )(biomass, water, rain, flow_blocks.reshape(nb * depth, BLK), neighbours)
 
     pieces = [wire] + [
         lax.ppermute(wire, "particle", [(i, i ^ j) for i in range(members)]) for j in range(1, members)
@@ -529,13 +509,15 @@
     def blocks(count, height=slots, kind=f32):
         return ((count, height, BLK), kind)
 
-    r1, wb1, v1, b2, w2, wi, bi, vi, miss1 = call(
+    r1, wb1, v1, b2, w2, wi, bi, vi, miss1, turn_a, turn_b = call(
         functools.partial(inner01_kernel, members, unroll),
         [blocks(nb), blocks(inner, kind=bf16), blocks(inner), blocks(inner), blocks(core)]
         + [blocks(core, part)] * 3
-        + [((slots, BLK), f32)],
-        [VMEM] * (members + 6) + [SMEM] + [VMEM] * 3 + [SMEM, VMEM],
-    )(*pieces, wb, v0, b1, quad, unit1, flow, neighbours, growth, prec, obs, ancestors, rain23)
+        + [((slots, BLK), f32), edge, edge],
+        [VMEM] * (members + 6) + [SMEM] + [VMEM] * 3 + [SMEM] + [VMEM] * 3,
+    )(
+        *pieces, wb, v0, b1, quad, unit1, flow, neighbours, growth, prec, obs, ancestors, rain23, flow_a, flow_b
+    )
     swap_rows = (WIDE + HALO) * part
     b2_edge, w2_edge, ws, bs, v2, total, end_a, end_b = call(
         functools.partial(outer01_kernel, unroll),
@@ -549,7 +531,7 @@
             pltpu.VMEM((2 * HALO, slots, BLK), f32),
         ],
     )(
-        wb, v0, b1, r1, wb1, v1, b2, wi, bi, vi, miss, miss1, got_a, got_b, flow, flow_a, flow_b, neighbours,
+        wb, v0, b1, r1, wb1, v1, b2, wi, bi, vi, miss, miss1, got_a, got_b, flow, turn_a, turn_b, neighbours,
         growth, prec, obs, ancestors, rain23,
     )
     last_a = lax.ppermute(end_a, "tile", swap_a)
@@ -572,7 +554,7 @@
         [((part, cells), f32)] * 2,
         [VMEM] * 11 + [SMEM] + [VMEM] * 2,
         [pltpu.VMEM((nb + 2 * WIDE, part, BLK), f32), pltpu.VMEM((nb + WIDE, part, BLK), f32)],
-    )(ws, bs, v2, w3, wat, bio, last_a, last_b, flow, flow_a, flow_b, neighbours, growth, rain23)
+    )(ws, bs, v2, w3, wat, bio, last_a, last_b, flow, turn_a, turn_b, neighbours, growth, rain23)
     (means,) = call(
         functools.partial(means_kernel, unroll, len(terms)), [((CYCLES, 2, cells), f32)], [VMEM] * (len(terms) + 6)
     )(*terms, bq, wq, b2, w2, b2_edge, w2_edge)

time: 36.7 us -> 62.8 us (1.71)
  Pallas kernels: 13.3 us -> 35.6 us
  waiting for transfers between devices: 5.34 us -> 8.31 us
  local copies, waits for them, and re-layouts: 0.04 us -> 0.93 us
    pallas_call x2 -> x1, Pallas kernels: 4 us -> 26.8 us  [body(): pl.pallas_call(pack_kernel, grid=(1,), out_shape=(jax.ShapeDtypeStruct((r...]
    ppermute x3, waiting for transfers between devices: 4.83 us -> 7.84 us  [body(): lax.ppermute(wire, 'particle', [(i, i ^ j) for i in range(members)])]
    unnamed x16, local copies, waits for them, and re-layouts: 0.04 us -> 0.93 us
  transfers between devices with their start and end apart: 12 -> 12, of which waited for: 2 -> 3; matrix products, arithmetic and copies ran while one was open for 0% -> 0% of each run, Pallas kernels for 25% -> 10%
where the time goes in v6:
time: 62.8 us; the launch traced here: 62.6 us
  Pallas kernels  35.6 us (57%)
  starting transfers between devices  16.9 us (27%)
  waiting for transfers between devices  8.31 us (13%)
  local copies, waits for them, and re-layouts  0.93 us (1%)
  between operations  0.81 us (1%)
    pallas_call x1, Pallas kernels, body(): pl.pallas_call(pack_kernel, grid=(1,), out_shape=(jax.ShapeDtypeStruct((r...  26.8 us
    ppermute x3, waiting for transfers between devices, body(): lax.ppermute(wire, 'particle', [(i, i ^ j) for i in range(members)])  7.84 us
    ppermute x3, starting transfers between devices, body(): lax.ppermute(wire, 'particle', [(i, i ^ j) for i in range(members)])  5.68 us
    ppermute x3, starting transfers between devices, body(): lax.ppermute(total, 'tile', [(i, i ^ m) for i in range(tiles)])  3.49 us
    ppermute x1, starting transfers between devices, body(): got_b = lax.ppermute(pay_b, 'tile', swap_b)  2.57 us
    ppermute x1, starting transfers between devices, body(): flow_b = lax.ppermute(flow_b, 'tile', swap_b)  2.56 us
    ppermute x1, starting transfers between devices, body(): last_b = lax.ppermute(end_b, 'tile', swap_b)  2.4 us
    pallas_call x1, Pallas kernels, body(): call(outer23_kernel, [((part, cells), f32)] * 2, [VMEM] * 11 + [SMEM] + [...  1.98 us
  transfers between devices with their start and end apart: 12, of which 3 were waited for; matrix products, arithmetic and copies ran while one was open for 0% of the time, Pallas kernels for 10%

profile of v6, /device:TPU:0, one launch (start us, length us, event | category | flops | bytes accessed | tf_op | source)
XLA Modules:
  0.0 62.6 jit_solution(6032770421526187525)
XLA Ops:
  0.6 0.0 copy-start.1
  0.6 0.0 copy-start
  0.7 0.0 copy-start.7
  0.7 0.0 copy-start.6
  0.7 0.0 copy-start.4
  0.7 0.0 copy-start.5
  0.7 26.8 %shard_map.112 = (s16[16,4224]{1,0:T(8,128)(2,1)}, bf16[1552,128]{1,0:T(8,128)(2,1)}, bf16[1552,128]{1,0:T(8,128)(2,1)}) custom-call(f32[4,4096]{1,0:T(4,128)} %bio.1, f32[4,4096]{1,0:T(4,128)} %wat.1, f32[4,4,4096]{2,1,0:T(4,128)} %rain.3, bf16[12288,128]{1,0:T(8,128)(2,1)} %bitcast.4, s32[3,32]{1,0:T(4,128)} %bitcast.5), custom_call_target="tpu_custom_call" | custom-call | flops 1 | bytes 1 | tf_op jit(solution)/shard_map/pallas_call | solution.py:464
  27.5 3.1 %collective-permute-start = (s16[16,4224]{1,0:T(8,128)(2,1)}, s16[16,4224]{1,0:T(8,128)(2,1)S(1)}, u32[]{:S(2)}, u32[]{:S(2)}) collective-permute-start(s16[16,4224]{1,0:T(8,128)(2,1)} %get-tuple-element.47.wire), channel_id=1, source_target_pairs={{0,8},{8,0},{16,24},{24,16},{1,9},{9,1},{17,25},{25,17},{2,10},{10... | collective-permute-start | bytes 405512 | tf_op jit(solution)/shard_map/ppermute | solution.py:482
  30.6 2.5 %collective-permute-start.2 = (s16[16,4224]{1,0:T(8,128)(2,1)}, s16[16,4224]{1,0:T(8,128)(2,1)S(1)}, u32[]{:S(2)}, u32[]{:S(2)}) collective-permute-start(s16[16,4224]{1,0:T(8,128)(2,1)} %get-tuple-element.47.wire), channel_id=1, source_target_pairs={{0,24},{8,16},{16,8},{24,0},{1,25},{9,17},{17,9},{25,1},{2,26},{10... | collective-permute-start | bytes 405512 | tf_op jit(solution)/shard_map/ppermute | solution.py:482
  33.0 0.1 collective-permute-start.1
  33.2 0.0 collective-permute-start.3
  33.2 2.6 %collective-permute-start.4 = (bf16[1552,128]{1,0:T(8,128)(2,1)}, bf16[1552,128]{1,0:T(8,128)(2,1)S(1)}, u32[]{:S(2)}, u32[]{:S(2)}) collective-permute-start(bf16[1552,128]{1,0:T(8,128)(2,1)} %get-tuple-element.61), channel_id=1, source_target_pairs={{0,7},{1,2},{2,1},{3,4},{4,3},{5,6},{6,5},{7,0},{8,15},{9,10},{10,... | collective-permute-start | bytes 1191944 | tf_op jit(solution)/shard_map/ppermute | solution.py:491
  35.7 0.0 collective-permute-done.after.refs_1_
  35.7 0.0 copy-done.1
  35.7 0.0 copy-done
  35.7 0.0 copy-done.7
  35.7 0.0 copy-done.6
  35.8 0.0 copy-done.4
  35.8 0.0 copy-done.5
  35.8 0.0 copy-start.2
  35.8 0.9 %copy-done.2 = s16[16,4224]{1,0:T(8,128)(2,1)S(1)} copy-done((s16[16,4224]{1,0:T(8,128)(2,1)S(1)}, s16[16,4224]{1,0:T(8,128)(2,1)}, u32[]{:S(2)}) %copy-start.2) | copy-done | bytes 135192
  36.7 0.9 %shard_map.113 = (bf16[32,384,128]{2,1,0:T(8,128)(2,1)S(1)}, s16[16,4224]{1,0:T(8,128)(2,1)S(1)}, f32[32,128]{1,0:T(8,128)S(1)}, f32[32,128]{1,0:T(8,128)S(1)}, ...) custom-call(s16[16,4224]{1,0:T(8,128)(2,1)S(1)} %collective-permute-done.after.refs_1_, ...), custom_call_target="tpu_custom_call" | custom-call | flops 1 | bytes 1 | tf_op jit(solution)/shard_map/pallas_call | solution.py:485
  37.6 3.1 %collective-permute-done.2.refs_3_ = s16[16,4224]{1,0:T(8,128)(2,1)S(1)} collective-permute-done((s16[16,4224]{1,0:T(8,128)(2,1)}, s16[16,4224]{1,0:T(8,128)(2,1)S(1)}, u32[]{:S(2)}, u32[]{:S(2)}) %collective-permute-start.2) | collective-permute-done | bytes 135200 | tf_op jit(solution)/shard_map/ppermute | solution.py:482
  40.7 4.7 %collective-permute-done.1.refs_2_ = s16[16,4224]{1,0:T(8,128)(2,1)S(1)} collective-permute-done((s16[16,4224]{1,0:T(8,128)(2,1)}, s16[16,4224]{1,0:T(8,128)(2,1)S(1)}, u32[]{:S(2)}, u32[]{:S(2)}) %collective-permute-start.1) | collective-permute-done | bytes 135200 | tf_op jit(solution)/shard_map/ppermute | solution.py:482
  45.4 0.0 copy-start.3
  45.4 0.5 shard_map.114
  45.9 0.1 collective-permute-start.5
  46.0 2.6 %collective-permute-start.6 = (bf16[16,16,128]{2,1,0:T(8,128)(2,1)S(1)}, bf16[16,16,128]{2,1,0:T(8,128)(2,1)S(1)}, u32[]{:S(2)}, u32[]{:S(2)}) collective-permute-start(bf16[16,16,128]{2,1,0:T(8,128)(2,1)S(1)} %get-tuple-element.72), channel_id=1, source_target_pairs={{0,7},{1,2},{2,1},{3,4},{4,3},{5,6},{6,5},{7,0},{8,15},{9,10},{10,... | collective-permute-start | bytes 196616 | tf_op jit(solution)/shard_map/ppermute | solution.py:506
  48.6 0.0 collective-permute-done.3.refs_16_
  48.6 0.0 collective-permute-done.4.refs_17_
  48.6 0.0 copy-done.3
  48.6 1.7 %shard_map.115 = (f32[32,16,128]{2,1,0:T(8,128)S(1)}, bf16[24,16,128]{2,1,0:T(8,128)(2,1)S(1)}, f32[24,16,128]{2,1,0:T(8,128)S(1)}, f32[24,16,128]{2,1,0:T(8,128...) custom-call(s16[16,4224]{1,0:T(8,128)(2,1)S(1)} %get-tuple-element.4, ...), custom_call_target="tpu_custom_call" | custom-call | flops 1 | bytes 1 | tf_op jit(solution)/shard_map/pallas_call | solution.py:512
  50.3 0.0 collective-permute-done.5.got_a
  50.3 0.4 collective-permute-done.6.got_b
  50.7 1.4 %shard_map.116 = (f32[8,16,128]{2,1,0:T(8,128)S(1)}, f32[16,16,128]{2,1,0:T(8,128)S(1)}, f32[32,4,128]{2,1,0:T(4,128)S(1)}, f32[32,4,128]{2,1,0:T(4,128)S(1)}, f...) custom-call(bf16[32,16,128]{2,1,0:T(8,128)(2,1)S(1)} %get-tuple-element.53.refs, ...), custom_call_target="tpu_custom_call" | custom-call | flops 1 | bytes 1 | tf_op jit(solution)/shard_map/pallas_call | solution.py:522
  52.2 0.2 collective-permute-start.7
  52.3 2.4 %collective-permute-start.11 = (f32[48,128]{1,0:T(8,128)S(1)}, f32[48,128]{1,0:T(8,128)S(1)}, u32[]{:S(2)}, u32[]{:S(2)}) collective-permute-start(f32[48,128]{1,0:T(8,128)S(1)} %get-tuple-element.88), channel_id=1, source_target_pairs={{0,7},{1,2},{2,1},{3,4},{4,3},{5,6},{6,5},{7,0},{8,15},{9,10},{10,... | collective-permute-start | bytes 73736 | tf_op jit(solution)/shard_map/ppermute | solution.py:538
  54.7 0.0 collective-permute-done.7.got_a
  54.7 1.2 %collective-permute-start.10 = (f32[32,128]{1,0:T(8,128)S(1)}, f32[32,128]{1,0:T(8,128)S(1)}, u32[]{:S(2)}, u32[]{:S(2)}) collective-permute-start(f32[32,128]{1,0:T(8,128)S(1)} %slice_add_fusion.refs_0_), channel_id=1, source_target_pairs={{0,6},{1,7},{2,4},{3,5},{4,2},{5,3},{6,0},{7,1},{8,14},{9,15},{10,... | collective-permute-start | bytes 49160 | tf_op jit(solution)/shard_map/ppermute | solution.py:545
  55.9 0.7 %collective-permute-start.9 = (f32[32,128]{1,0:T(8,128)S(1)}, f32[32,128]{1,0:T(8,128)S(1)}, u32[]{:S(2)}, u32[]{:S(2)}) collective-permute-start(f32[32,128]{1,0:T(8,128)S(1)} %slice_add_fusion.refs_0_), channel_id=1, source_target_pairs={{0,4},{1,5},{2,6},{3,7},{4,0},{5,1},{6,2},{7,3},{8,12},{9,13},{10,... | collective-permute-start | bytes 49160 | tf_op jit(solution)/shard_map/ppermute | solution.py:545
  56.6 1.7 %collective-permute-start.8 = (f32[32,128]{1,0:T(8,128)S(1)}, f32[32,128]{1,0:T(8,128)S(1)}, u32[]{:S(2)}, u32[]{:S(2)}) collective-permute-start(f32[32,128]{1,0:T(8,128)S(1)} %slice_add_fusion.refs_0_), channel_id=1, source_target_pairs={{0,2},{1,3},{2,0},{3,1},{4,6},{5,7},{6,4},{7,5},{8,10},{9,11},{10,... | collective-permute-start | bytes 49160 | tf_op jit(solution)/shard_map/ppermute | solution.py:545
  58.2 1.5 %shard_map.118 = (f32[24,4,128]{2,1,0:T(4,128)S(1)}, f32[16,4,128]{2,1,0:T(4,128)S(1)}, f32[16,4,128]{2,1,0:T(4,128)S(1)}) custom-call(f32[32,4,128]{2,1,0:T(4,128)S(1)} %get-tuple-element.82.ws, f32[32,4,128]{2,1,0:T(4,128)S(1)} %get-tuple-element.83.bs, f32[32,4,128]{2,1,0:T(4,128)S(1)} %get-tuple-element.84.v2, ...), custom_call_target="tpu_custom_call" | custom-call | flops 1 | bytes 1 | tf_op jit(solution)/shard_map/pallas_call | solution.py:547
  59.7 0.0 collective-permute-done.11.got_b
  59.7 2.0 %shard_map.119 = (f32[4,4096]{1,0:T(4,128)}, f32[4,4096]{1,0:T(4,128)}) custom-call(f32[32,4,128]{2,1,0:T(4,128)S(1)} %get-tuple-element.82.ws, f32[32,4,128]{2,1,0:T(4,128)S(1)} %get-tuple-element.83.bs, f32[32,4,128]{2,1,0:T(4,128)S(1)} %get-tuple-element.84.v2, f32[24,4,128]{2,1,0:T(4,128)S(1)} %get-tuple-element.85.w3, ...), custom_call_target="tpu_custom_call" | custom-call | flops 1 | bytes 1 | tf_op jit(solution)/shard_map/pallas_call | solution.py:552
  61.7 0.0 collective-permute-done.10.refs_3_
  61.7 0.0 collective-permute-done.9.refs_2_
  61.7 0.0 collective-permute-done.8.refs_1_
  61.7 0.9 %shard_map.117 = f32[2,2,4096]{2,1,0:T(2,128)} custom-call(f32[32,128]{1,0:T(8,128)S(1)} %slice_add_fusion.refs_0_, f32[32,128]{1,0:T(8,128)S(1)} %collective-permute-done.8.refs_1_, f32[32,128]{1,0:T(8,128)S(1)} %collective-permute-done.9.refs_2_, f32[32,128]{1,0:T(8,128)S(1)} %collective-permute-done.10.refs_3_, ...), custom_call_target="tpu_custom_call" | custom-call | flops 1 | bytes 1 | tf_op jit(solution)/shard_map/pallas_call | solution.py:558
  (1 shorter events, 0.0 us)
Async XLA Ops:
  0.6 35.1 %copy-start.1 = (f32[4,4,4096]{2,1,0:T(4,128)S(1)}, f32[4,4,4096]{2,1,0:T(4,128)}, u32[]{:S(2)}) copy-start(f32[4,4,4096]{2,1,0:T(4,128)} %rain.3) | copy-start | bytes 786436
  0.6 35.1 %copy-start = (bf16[32,3,128,128]{3,2,1,0:T(8,128)(2,1)S(1)}, bf16[32,3,128,128]{3,2,1,0:T(8,128)(2,1)}, u32[]{:S(2)}) copy-start(bf16[32,3,128,128]{3,2,1,0:T(8,128)(2,1)} %flow.1) | copy-start | bytes 9437188
  0.7 35.1 %copy-start.7 = (s32[2,16]{1,0:T(2,128)S(1)}, s32[2,16]{1,0:T(2,128)}, u32[]{:S(2)}) copy-start(s32[2,16]{1,0:T(2,128)} %anc.3) | copy-start | bytes 388
  0.7 35.1 %copy-start.6 = (f32[4096]{0:T(1024)S(1)}, f32[4096]{0:T(1024)}, u32[]{:S(2)}) copy-start(f32[4096]{0:T(1024)} %param.16) | copy-start | bytes 49156
  0.7 35.1 %copy-start.4 = (f32[2,4096]{1,0:T(2,128)S(1)}, f32[2,4096]{1,0:T(2,128)}, u32[]{:S(2)}) copy-start(f32[2,4096]{1,0:T(2,128)} %obs.1) | copy-start | bytes 98308
  0.7 35.1 %copy-start.5 = (f32[4096]{0:T(1024)S(1)}, f32[4096]{0:T(1024)}, u32[]{:S(2)}) copy-start(f32[4096]{0:T(1024)} %param.14) | copy-start | bytes 49156
  27.5 8.2 %collective-permute-start = (s16[16,4224]{1,0:T(8,128)(2,1)}, s16[16,4224]{1,0:T(8,128)(2,1)S(1)}, u32[]{:S(2)}, u32[]{:S(2)}) collective-permute-start(s16[16,4224]{1,0:T(8,128)(2,1)} %get-tuple-element.47.wire), channel_id=1, source_target_pairs={{0,8},{8,0},{16,24},{24,16},{1,9},{9,1},{17,25},{25,17},{2,10},{10... | collective-permute-start | bytes 405512 | tf_op jit(solution)/shard_map/ppermute | solution.py:482
  30.6 10.1 %collective-permute-start.2 = (s16[16,4224]{1,0:T(8,128)(2,1)}, s16[16,4224]{1,0:T(8,128)(2,1)S(1)}, u32[]{:S(2)}, u32[]{:S(2)}) collective-permute-start(s16[16,4224]{1,0:T(8,128)(2,1)} %get-tuple-element.47.wire), channel_id=1, source_target_pairs={{0,24},{8,16},{16,8},{24,0},{1,25},{9,17},{17,9},{25,1},{2,26},{10... | collective-permute-start | bytes 405512 | tf_op jit(solution)/shard_map/ppermute | solution.py:482
  33.0 12.3 %collective-permute-start.1 = (s16[16,4224]{1,0:T(8,128)(2,1)}, s16[16,4224]{1,0:T(8,128)(2,1)S(1)}, u32[]{:S(2)}, u32[]{:S(2)}) collective-permute-start(s16[16,4224]{1,0:T(8,128)(2,1)} %get-tuple-element.47.wire), channel_id=1, source_target_pairs={{0,16},{8,24},{16,0},{24,8},{1,17},{9,25},{17,1},{25,9},{2,18},{10... | collective-permute-start | bytes 405512 | tf_op jit(solution)/shard_map/ppermute | solution.py:482
  33.2 15.4 %collective-permute-start.3 = (bf16[1552,128]{1,0:T(8,128)(2,1)}, bf16[1552,128]{1,0:T(8,128)(2,1)S(1)}, u32[]{:S(2)}, u32[]{:S(2)}) collective-permute-start(bf16[1552,128]{1,0:T(8,128)(2,1)} %get-tuple-element.60), channel_id=1, source_target_pairs={{0,1},{1,0},{2,3},{3,2},{4,5},{5,4},{6,7},{7,6},{8,9},{9,8},{10,11... | collective-permute-start | bytes 1191944 | tf_op jit(solution)/shard_map/ppermute | solution.py:490
  33.2 15.4 %collective-permute-start.4 = (bf16[1552,128]{1,0:T(8,128)(2,1)}, bf16[1552,128]{1,0:T(8,128)(2,1)S(1)}, u32[]{:S(2)}, u32[]{:S(2)}) collective-permute-start(bf16[1552,128]{1,0:T(8,128)(2,1)} %get-tuple-element.61), channel_id=1, source_target_pairs={{0,7},{1,2},{2,1},{3,4},{4,3},{5,6},{6,5},{7,0},{8,15},{9,10},{10,... | collective-permute-start | bytes 1191944 | tf_op jit(solution)/shard_map/ppermute | solution.py:491
  35.8 0.9 %copy-start.2 = (s16[16,4224]{1,0:T(8,128)(2,1)S(1)}, s16[16,4224]{1,0:T(8,128)(2,1)}, u32[]{:S(2)}) copy-start(s16[16,4224]{1,0:T(8,128)(2,1)} %get-tuple-element.47.wire) | copy-start | bytes 405508
  45.4 3.2 %copy-start.3 = (s32[32,3]{0,1:T(4,128)S(1)}, s32[32,3]{0,1:T(4,128)}, u32[]{:S(2)}) copy-start(s32[32,3]{0,1:T(4,128)} %param.12) | copy-start | bytes 1156
  45.9 4.4 %collective-permute-start.5 = (bf16[16,16,128]{2,1,0:T(8,128)(2,1)S(1)}, bf16[16,16,128]{2,1,0:T(8,128)(2,1)S(1)}, u32[]{:S(2)}, u32[]{:S(2)}) collective-permute-start(bf16[16,16,128]{2,1,0:T(8,128)(2,1)S(1)} %get-tuple-element.71), channel_id=1, source_target_pairs={{0,1},{1,0},{2,3},{3,2},{4,5},{5,4},{6,7},{7,6},{8,9},{9,8},{10,11... | collective-permute-start | bytes 196616 | tf_op jit(solution)/shard_map/ppermute | solution.py:505
  46.0 4.7 %collective-permute-start.6 = (bf16[16,16,128]{2,1,0:T(8,128)(2,1)S(1)}, bf16[16,16,128]{2,1,0:T(8,128)(2,1)S(1)}, u32[]{:S(2)}, u32[]{:S(2)}) collective-permute-start(bf16[16,16,128]{2,1,0:T(8,128)(2,1)S(1)} %get-tuple-element.72), channel_id=1, source_target_pairs={{0,7},{1,2},{2,1},{3,4},{4,3},{5,6},{6,5},{7,0},{8,15},{9,10},{10,... | collective-permute-start | bytes 196616 | tf_op jit(solution)/shard_map/ppermute | solution.py:506
  52.2 2.6 %collective-permute-start.7 = (f32[80,128]{1,0:T(8,128)S(1)}, f32[80,128]{1,0:T(8,128)S(1)}, u32[]{:S(2)}, u32[]{:S(2)}) collective-permute-start(f32[80,128]{1,0:T(8,128)S(1)} %get-tuple-element.76), channel_id=1, source_target_pairs={{0,1},{1,0},{2,3},{3,2},{4,5},{5,4},{6,7},{7,6},{8,9},{9,8},{10,11... | collective-permute-start | bytes 122888 | tf_op jit(solution)/shard_map/ppermute | solution.py:537
  52.3 7.4 %collective-permute-start.11 = (f32[48,128]{1,0:T(8,128)S(1)}, f32[48,128]{1,0:T(8,128)S(1)}, u32[]{:S(2)}, u32[]{:S(2)}) collective-permute-start(f32[48,128]{1,0:T(8,128)S(1)} %get-tuple-element.88), channel_id=1, source_target_pairs={{0,7},{1,2},{2,1},{3,4},{4,3},{5,6},{6,5},{7,0},{8,15},{9,10},{10,... | collective-permute-start | bytes 73736 | tf_op jit(solution)/shard_map/ppermute | solution.py:538
  54.7 7.0 %collective-permute-start.10 = (f32[32,128]{1,0:T(8,128)S(1)}, f32[32,128]{1,0:T(8,128)S(1)}, u32[]{:S(2)}, u32[]{:S(2)}) collective-permute-start(f32[32,128]{1,0:T(8,128)S(1)} %slice_add_fusion.refs_0_), channel_id=1, source_target_pairs={{0,6},{1,7},{2,4},{3,5},{4,2},{5,3},{6,0},{7,1},{8,14},{9,15},{10,... | collective-permute-start | bytes 49160 | tf_op jit(solution)/shard_map/ppermute | solution.py:545
  55.9 5.8 %collective-permute-start.9 = (f32[32,128]{1,0:T(8,128)S(1)}, f32[32,128]{1,0:T(8,128)S(1)}, u32[]{:S(2)}, u32[]{:S(2)}) collective-permute-start(f32[32,128]{1,0:T(8,128)S(1)} %slice_add_fusion.refs_0_), channel_id=1, source_target_pairs={{0,4},{1,5},{2,6},{3,7},{4,0},{5,1},{6,2},{7,3},{8,12},{9,13},{10,... | collective-permute-start | bytes 49160 | tf_op jit(solution)/shard_map/ppermute | solution.py:545
  56.6 5.1 %collective-permute-start.8 = (f32[32,128]{1,0:T(8,128)S(1)}, f32[32,128]{1,0:T(8,128)S(1)}, u32[]{:S(2)}, u32[]{:S(2)}) collective-permute-start(f32[32,128]{1,0:T(8,128)S(1)} %slice_add_fusion.refs_0_), channel_id=1, source_target_pairs={{0,2},{1,3},{2,0},{3,1},{4,6},{5,7},{6,4},{7,5},{8,10},{9,11},{10,... | collective-permute-start | bytes 49160 | tf_op jit(solution)/shard_map/ppermute | solution.py:545

commit v7 on v4

--- a/solution.py
+++ b/solution.py
@@ -131,13 +131,7 @@
         for d in range(HALO + 1):
             x = jnp.where(gap == d, ext[at + sign * d].astype(jnp.float32), x)
         xs.append(x.astype(jnp.bfloat16))
-    total = jnp.zeros(ext.shape[1:], jnp.float32)
-    for k, x in enumerate(xs):
-        at = m * depth + k * BLK
-        total += lax.dot_general(
-            x, pay[at : at + BLK, :], (((1,), (1,)), ((), ())), preferred_element_type=jnp.float32
-        )
-    return total
+    return flux_of(xs, pay[m * depth : (m + 1) * depth, :])
 
 
 def decode(sel, pieces, cols):
@@ -221,8 +215,8 @@
 
 def inner01_kernel(members, unroll, *refs):
     pieces = refs[:members]
-    wb, v0, b1, quad, unit1, flow, ids, growth, prec, obs, anc, rain = refs[members : members + 12]
-    r1, wb1, v1, b2, w2, ws, bs, v2, miss = refs[members + 12 :]
+    wb, v0, b1, quad, unit1, flow, ids, growth, prec, obs, anc, rain, flow_a, flow_b = refs[members : members + 14]
+    r1, wb1, v1, b2, w2, ws, bs, v2, miss, turn_a, turn_b = refs[members + 14 :]
     nb, slots = wb.shape[:2]
     part = rain.shape[1]
     quads = nb // 4
@@ -261,6 +255,10 @@
         return carry
 
     run(WIDE, nb - WIDE, unroll, pick, 0)
+    for raw, turned in ((flow_a, turn_a), (flow_b, turn_b)):
+        for at in range(0, HALO * NBR * BLK, BLK):
+            turned[at : at + BLK, :] = raw[at : at + BLK, :].T
+        turned[HALO * NBR * BLK :, :] = raw[HALO * NBR * BLK :, :]
 
 
 def settle(n, w, b1, r1, growth, prec, obs, acc):
@@ -345,27 +343,6 @@
     pay_a[at : at + 2 * slots, :] = total[...]
 
 
-def inner23_kernel(unroll, ws, bs, v2, flow, ids, growth, rain, w3, wat, bio):
-    nb = ws.shape[0]
-    base = lax.axis_index("tile") * nb
-    half = jnp.bfloat16
-
-    def day2(n, carry):
-        xs = [ws[i].astype(half) for i in (n, ids[1, n] - base, ids[2, n] - base)]
-        w3[n - HALO] = v2[n] + flux_of(xs, flow[n])
-        return carry
-
-    run(HALO, nb - HALO, unroll, day2, 0)
-
-    def day3(n, carry):
-        xs = [w3[i - HALO].astype(half) for i in (n, ids[1, n] - base, ids[2, n] - base)]
-        m = n - WIDE
-        wat[m], bio[m] = final(n, w3[n - HALO], flux_of(xs, flow[n]), ws[n], bs[n], growth, rain)
-        return carry
-
-    run(WIDE, nb - WIDE, unroll, day3, 0)
-
-
 def final(n, w3, flux, w, b, growth, rain):
     g = growth[pl.ds(n, 1), :]
     b = b + g * b * (wetness(w) - 0.4 * b)
@@ -373,40 +350,40 @@
     return w3 + flux + rain[1, :, lanes(n)] - 0.2 * b * s, b + g * b * (s - 0.4 * b)
 
 
-def outer23_kernel(
-    ws, bs, v2, w3, wat, bio, got_a, got_b, flow, flow_a, flow_b, ids, growth, rain,
-    bio_out, wat_out, ext, ext3,
+def close_kernel(
+    unroll, ws, bs, v2, got_a, got_b, flow, flow_a, flow_b, ids, growth, rain, bio_out, wat_out, ext, ext3
 ):
     nb, part = ws.shape[:2]
     pos = lax.axis_index("tile")
     even = right_first()
     half = jnp.bfloat16
-    for n in range(WIDE, nb - WIDE):
-        wat_out[:, lanes(n)] = wat[n - WIDE]
-        bio_out[:, lanes(n)] = bio[n - WIDE]
-    for lo, hi in ((0, WIDE + HALO), (nb - WIDE - HALO, nb)):
-        ext[WIDE + lo : WIDE + hi] = ws[lo:hi]
-    ext3[WIDE : 2 * WIDE] = w3[0:WIDE]
-    ext3[nb - WIDE : nb] = w3[nb - 2 * HALO - WIDE : nb - 2 * HALO]
+    ext[WIDE : WIDE + nb] = ws[...]
     sides = ((got_a, flow_a, even), (got_b, flow_b, jnp.logical_not(even)))
     for got, _, right in sides:
         for m in range(WIDE):
             ext[jnp.where(right, nb + WIDE, 0) + m] = got[m * part : (m + 1) * part, :]
-    base = WIDE - pos * nb
-    for n in (*range(HALO), *range(nb - HALO, nb)):
-        xs = [ext[i].astype(half) for i in (n + WIDE, ids[1, n] + base, ids[2, n] + base)]
-        ext3[n + HALO] = v2[n] + flux_of(xs, flow[n])
     for got, pay, right in sides:
         spot = jnp.where(right, nb + HALO, 0)
         for m in range(HALO):
             edge = got[(WIDE + m) * part : (WIDE + m + 1) * part, :]
             ext3[spot + m] = edge + halo_flux(ext, pay, right, nb, m)
-    base = HALO - pos * nb
-    for n in (*range(WIDE), *range(nb - WIDE, nb)):
-        xs = [ext3[i].astype(half) for i in (n + HALO, ids[1, n] + base, ids[2, n] + base)]
-        w, b = final(n, ext3[n + HALO], flux_of(xs, flow[n]), ws[n], bs[n], growth, rain)
-        wat_out[:, lanes(n)] = w
-        bio_out[:, lanes(n)] = b
+
+    def near(ref, n, at):
+        base = at - pos * nb
+        return [ref[i].astype(half) for i in (n + at, ids[1, n] + base, ids[2, n] + base)]
+
+    def day2(n, carry):
+        ext3[n + HALO] = v2[n] + flux_of(near(ext, n, WIDE), flow[n])
+        return carry
+
+    run(0, nb, unroll, day2, 0)
+
+    def day3(n, carry):
+        flux = flux_of(near(ext3, n, HALO), flow[n])
+        wat_out[:, lanes(n)], bio_out[:, lanes(n)] = final(n, ext3[n + HALO], flux, ws[n], bs[n], growth, rain)
+        return carry
+
+    run(0, nb, unroll, day3, 0)
 
 
 def means_kernel(unroll, count, *refs):
@@ -471,7 +448,6 @@
     depth = NBR * BLK
     edge = ((HALO * depth + 16, BLK), bf16)
     tile = (HALO, NBR, BLK, BLK)
-
     wire = pl.pallas_call(
         pack_kernel,
         grid=(1,),
@@ -498,15 +474,16 @@
         cost_estimate=weigh(1),
     )(wire, flow_blocks, flow_blocks, neighbours)
 
-    pieces = [wire] + [
-        lax.ppermute(wire, "particle", [(i, i ^ j) for i in range(members)]) for j in range(1, members)
-    ]
+    pieces = {0: wire}
+    for j in reversed(range(1, members)):
+        pieces[j] = lax.ppermute(wire, "particle", [(i, i ^ j) for i in range(members)])
     small = (wire, growth_rate.reshape(nb, BLK), obs_precision.reshape(nb, BLK), observations, ancestors)
     flow, pieces[0], growth, prec, obs, anc, rain23 = call(
         stage_kernel,
         [((nb, depth, BLK), bf16)] + [(x.shape, x.dtype) for x in small] + [((2, part, cells), f32)],
         [HBM] + [VMEM] * 7,
-    )(pieces[1], flow_blocks, *small, rain)
+    )(wire, flow_blocks, *small, rain)
+    pieces = [pieces[j] for j in range(members)]
     flow_a = lax.ppermute(flow_a, "tile", swap_a)
     flow_b = lax.ppermute(flow_b, "tile", swap_b)
 
@@ -529,13 +506,15 @@
     def blocks(count, height=slots, kind=f32):
         return ((count, height, BLK), kind)
 
-    r1, wb1, v1, b2, w2, wi, bi, vi, miss1 = call(
+    r1, wb1, v1, b2, w2, wi, bi, vi, miss1, turn_a, turn_b = call(
         functools.partial(inner01_kernel, members, unroll),
         [blocks(nb), blocks(inner, kind=bf16), blocks(inner), blocks(inner), blocks(core)]
         + [blocks(core, part)] * 3
-        + [((slots, BLK), f32)],
-        [VMEM] * (members + 6) + [SMEM] + [VMEM] * 3 + [SMEM, VMEM],
-    )(*pieces, wb, v0, b1, quad, unit1, flow, neighbours, growth, prec, obs, ancestors, rain23)
+        + [((slots, BLK), f32), edge, edge],
+        [VMEM] * (members + 6) + [SMEM] + [VMEM] * 3 + [SMEM] + [VMEM] * 3,
+    )(
+        *pieces, wb, v0, b1, quad, unit1, flow, neighbours, growth, prec, obs, ancestors, rain23, flow_a, flow_b
+    )
     swap_rows = (WIDE + HALO) * part
     b2_edge, w2_edge, ws, bs, v2, total, end_a, end_b = call(
         functools.partial(outer01_kernel, unroll),
@@ -549,7 +528,7 @@
             pltpu.VMEM((2 * HALO, slots, BLK), f32),
         ],
     )(
-        wb, v0, b1, r1, wb1, v1, b2, wi, bi, vi, miss, miss1, got_a, got_b, flow, flow_a, flow_b, neighbours,
+        wb, v0, b1, r1, wb1, v1, b2, wi, bi, vi, miss, miss1, got_a, got_b, flow, turn_a, turn_b, neighbours,
         growth, prec, obs, ancestors, rain23,
     )
     last_a = lax.ppermute(end_a, "tile", swap_a)
@@ -562,17 +541,12 @@
         masks = [span] if span * 2 >= tiles else [span, 2 * span, 3 * span]
         terms = [total] + [lax.ppermute(total, "tile", [(i, i ^ m) for i in range(tiles)]) for m in masks]
         span *= 2 ** (len(masks) // 2 + 1)
-    w3, wat, bio = call(
-        functools.partial(inner23_kernel, unroll),
-        [blocks(inner, part), blocks(core, part), blocks(core, part)],
-        [VMEM] * 4 + [SMEM] + [VMEM] * 2,
-    )(ws, bs, v2, flow, neighbours, growth, rain23)
     bio_out, wat_out = call(
-        outer23_kernel,
+        functools.partial(close_kernel, unroll),
         [((part, cells), f32)] * 2,
-        [VMEM] * 11 + [SMEM] + [VMEM] * 2,
+        [VMEM] * 8 + [SMEM] + [VMEM] * 2,
         [pltpu.VMEM((nb + 2 * WIDE, part, BLK), f32), pltpu.VMEM((nb + WIDE, part, BLK), f32)],
-    )(ws, bs, v2, w3, wat, bio, last_a, last_b, flow, flow_a, flow_b, neighbours, growth, rain23)
+    )(ws, bs, v2, last_a, last_b, flow, turn_a, turn_b, neighbours, growth, rain23)
     (means,) = call(
         functools.partial(means_kernel, unroll, len(terms)), [((CYCLES, 2, cells), f32)], [VMEM] * (len(terms) + 6)
     )(*terms, bq, wq, b2, w2, b2_edge, w2_edge)

time: 36.7 us -> 35.7 us (0.973)
  Pallas kernels: 13.3 us -> 12.1 us
    pallas_call x2 -> x1, Pallas kernels: 3.71 us -> 2.67 us  [body(): call(functools.partial(close_kernel, unroll), [((part, cells), f32)] * 2,...]
  transfers between devices with their start and end apart: 12 -> 12, of which waited for: 2 -> 2; matrix products, arithmetic and copies ran while one was open for 0% -> 0% of each run, Pallas kernels for 25% -> 23%
where the time goes in v7:
time: 35.7 us; the launch traced here: 35.5 us
  starting transfers between devices  17 us (48%)
  Pallas kernels  12.1 us (34%)
  waiting for transfers between devices  5.58 us (16%)
  between operations  0.75 us (2%)
    ppermute x3, starting transfers between devices, body(): lax.ppermute(wire, 'particle', [(i, i ^ j) for i in range(members)])  5.62 us
    ppermute x3, waiting for transfers between devices, body(): lax.ppermute(wire, 'particle', [(i, i ^ j) for i in range(members)])  5.08 us
    ppermute x3, starting transfers between devices, body(): lax.ppermute(total, 'tile', [(i, i ^ m) for i in range(tiles)])  3.49 us
    ppermute x1, starting transfers between devices, body(): flow_b = lax.ppermute(flow_b, 'tile', swap_b)  2.78 us
    pallas_call x1, Pallas kernels, body(): call(functools.partial(close_kernel, unroll), [((part, cells), f32)] * 2,...  2.67 us
    ppermute x1, starting transfers between devices, body(): got_b = lax.ppermute(pay_b, 'tile', swap_b)  2.54 us
    ppermute x1, starting transfers between devices, body(): last_b = lax.ppermute(end_b, 'tile', swap_b)  2.37 us
    pallas_call x1, Pallas kernels, body(): pl.pallas_call(edge_kernel, grid=(1,), out_shape=tuple((jax.ShapeDtypeStr...  2.24 us
  transfers between devices with their start and end apart: 12, of which 2 were waited for; matrix products, arithmetic and copies ran while one was open for 0% of the time, Pallas kernels for 23%

profile of v7, /device:TPU:0, one launch (start us, length us, event | category | flops | bytes accessed | tf_op | source)
XLA Modules:
  0.0 35.5 jit_solution(14456721822911044297)
XLA Ops:
  0.6 1.8 %shard_map.112.after.wire = s16[16,4224]{1,0:T(8,128)(2,1)} custom-call(f32[4,4096]{1,0:T(4,128)} %bio.1, f32[4,4096]{1,0:T(4,128)} %wat.1, f32[4,4,4096]{2,1,0:T(4,128)} %rain.3), custom_call_target="tpu_custom_call" | custom-call | flops 1 | bytes 1 | tf_op jit(solution)/shard_map/pallas_call | solution.py:451
  2.4 5.0 %collective-permute-start.2 = (s16[16,4224]{1,0:T(8,128)(2,1)}, s16[16,4224]{1,0:T(8,128)(2,1)S(1)}, u32[]{:S(2)}, u32[]{:S(2)}) collective-permute-start(s16[16,4224]{1,0:T(8,128)(2,1)} %shard_map.112.after.wire), channel_id=1, source_target_pairs={{0,24},{8,16},{16,8},{24,0},{1,25},{9,17},{17,9},{25,1},{2,26},{10... | collective-permute-start | bytes 405512 | tf_op jit(solution)/shard_map/ppermute | solution.py:479
  7.4 0.0 collective-permute-start.1
  7.4 0.6 %collective-permute-start = (s16[16,4224]{1,0:T(8,128)(2,1)}, s16[16,4224]{1,0:T(8,128)(2,1)S(1)}, u32[]{:S(2)}, u32[]{:S(2)}) collective-permute-start(s16[16,4224]{1,0:T(8,128)(2,1)} %shard_map.112.after.wire), channel_id=1, source_target_pairs={{0,8},{8,0},{16,24},{24,16},{1,9},{9,1},{17,25},{25,17},{2,10},{10... | collective-permute-start | bytes 405512 | tf_op jit(solution)/shard_map/ppermute | solution.py:479
  8.0 0.0 copy-start
  8.0 0.0 copy-start.1
  8.0 0.0 copy-start.2
  8.0 0.0 copy-start.4
  8.0 0.0 copy-start.5
  8.0 0.0 copy-start.6
  8.0 0.0 copy-start.7
  8.0 2.2 %shard_map.115 = (bf16[1552,128]{1,0:T(8,128)(2,1)}, bf16[1552,128]{1,0:T(8,128)(2,1)}) custom-call(s16[16,4224]{1,0:T(8,128)(2,1)} %shard_map.112.after.wire, bf16[32,3,128,128]{3,2,1,0:T(8,128)(2,1)} %right.1, bf16[32,3,128,128]{3,2,1,0:T(8,128)(2,1)} %right.1, s32[3,32]{1,0:T(4,128)} %bitcast.3), custom_call_target="tpu_custom_call" | custom-call | flops 1 | bytes 1 | tf_op jit(solution)/shard_map/pallas_call | solution.py:462
  10.3 0.0 collective-permute-start.3
  10.3 2.8 %collective-permute-start.4 = (bf16[1552,128]{1,0:T(8,128)(2,1)}, bf16[1552,128]{1,0:T(8,128)(2,1)S(1)}, u32[]{:S(2)}, u32[]{:S(2)}) collective-permute-start(bf16[1552,128]{1,0:T(8,128)(2,1)} %get-tuple-element.56), channel_id=1, source_target_pairs={{0,7},{1,2},{2,1},{3,4},{4,3},{5,6},{6,5},{7,0},{8,15},{9,10},{10,... | collective-permute-start | bytes 1191944 | tf_op jit(solution)/shard_map/ppermute | solution.py:488
  13.1 0.0 copy-done
  13.1 0.0 copy-done.1
  13.1 0.0 copy-done.2
  13.1 0.0 copy-done.4
  13.1 0.0 copy-done.5
  13.1 0.0 copy-done.6
  13.1 0.0 copy-done.7
  13.1 0.9 %shard_map.113 = (bf16[32,384,128]{2,1,0:T(8,128)(2,1)S(1)}, s16[16,4224]{1,0:T(8,128)(2,1)S(1)}, f32[32,128]{1,0:T(8,128)S(1)}, f32[32,128]{1,0:T(8,128)S(1)}, ...) custom-call(s16[16,4224]{1,0:T(8,128)(2,1)S(1)} %copy-done.1, ...), custom_call_target="tpu_custom_call" | custom-call | flops 1 | bytes 1 | tf_op jit(solution)/shard_map/pallas_call | solution.py:481
  14.0 0.0 collective-permute-done.2.refs_3_
  14.0 5.1 %collective-permute-done.1.refs_2_ = s16[16,4224]{1,0:T(8,128)(2,1)S(1)} collective-permute-done((s16[16,4224]{1,0:T(8,128)(2,1)}, s16[16,4224]{1,0:T(8,128)(2,1)S(1)}, u32[]{:S(2)}, u32[]{:S(2)}) %collective-permute-start.1) | collective-permute-done | bytes 135200 | tf_op jit(solution)/shard_map/ppermute | solution.py:479
  19.1 0.0 collective-permute-done.refs_1_
  19.1 0.0 copy-start.3
  19.1 0.5 %shard_map.114 = (bf16[32,16,128]{2,1,0:T(8,128)(2,1)S(1)}, f32[32,16,128]{2,1,0:T(8,128)S(1)}, f32[32,16,128]{2,1,0:T(8,128)S(1)}, f32[32,16,128]{2,1,0:T(8,128...) custom-call(s16[16,4224]{1,0:T(8,128)(2,1)S(1)} %get-tuple-element.4, ...), custom_call_target="tpu_custom_call" | custom-call | flops 10000000000 | bytes 1 | tf_op jit(solution)/shard_map/pallas_call | solution.py:491
  19.6 0.1 collective-permute-start.5
  19.7 2.5 %collective-permute-start.6 = (bf16[16,16,128]{2,1,0:T(8,128)(2,1)S(1)}, bf16[16,16,128]{2,1,0:T(8,128)(2,1)S(1)}, u32[]{:S(2)}, u32[]{:S(2)}) collective-permute-start(bf16[16,16,128]{2,1,0:T(8,128)(2,1)S(1)} %get-tuple-element.67), channel_id=1, source_target_pairs={{0,7},{1,2},{2,1},{3,4},{4,3},{5,6},{6,5},{7,0},{8,15},{9,10},{10,... | collective-permute-start | bytes 196616 | tf_op jit(solution)/shard_map/ppermute | solution.py:503
  22.2 0.0 collective-permute-done.3.refs_16_
  22.2 0.0 collective-permute-done.4.refs_17_
  22.3 0.0 copy-done.3
  22.3 1.7 %shard_map.116 = (f32[32,16,128]{2,1,0:T(8,128)S(1)}, bf16[24,16,128]{2,1,0:T(8,128)(2,1)S(1)}, f32[24,16,128]{2,1,0:T(8,128)S(1)}, f32[24,16,128]{2,1,0:T(8,128...) custom-call(s16[16,4224]{1,0:T(8,128)(2,1)S(1)} %get-tuple-element.4, ...), custom_call_target="tpu_custom_call" | custom-call | flops 1 | bytes 1 | tf_op jit(solution)/shard_map/pallas_call | solution.py:509
  23.9 0.0 collective-permute-done.5.got_a
  24.0 0.5 %collective-permute-done.6.got_b = bf16[16,16,128]{2,1,0:T(8,128)(2,1)S(1)} collective-permute-done((bf16[16,16,128]{2,1,0:T(8,128)(2,1)S(1)}, bf16[16,16,128]{2,1,0:T(8,128)(2,1)S(1)}, u32[]{:S(2)}, u32[]{:S(2)}) %collective-permute-start.6) | collective-permute-done | bytes 65568 | tf_op jit(solution)/shard_map/ppermute | solution.py:503
  24.4 1.4 %shard_map.117 = (f32[8,16,128]{2,1,0:T(8,128)S(1)}, f32[16,16,128]{2,1,0:T(8,128)S(1)}, f32[32,4,128]{2,1,0:T(4,128)S(1)}, f32[32,4,128]{2,1,0:T(4,128)S(1)}, f...) custom-call(bf16[32,16,128]{2,1,0:T(8,128)(2,1)S(1)} %get-tuple-element.48.refs, ...), custom_call_target="tpu_custom_call" | custom-call | flops 1 | bytes 1 | tf_op jit(solution)/shard_map/pallas_call | solution.py:519
  25.9 0.2 collective-permute-start.7
  26.0 2.4 %collective-permute-start.11 = (f32[48,128]{1,0:T(8,128)S(1)}, f32[48,128]{1,0:T(8,128)S(1)}, u32[]{:S(2)}, u32[]{:S(2)}) collective-permute-start(f32[48,128]{1,0:T(8,128)S(1)} %get-tuple-element.80), channel_id=1, source_target_pairs={{0,7},{1,2},{2,1},{3,4},{4,3},{5,6},{6,5},{7,0},{8,15},{9,10},{10,... | collective-permute-start | bytes 73736 | tf_op jit(solution)/shard_map/ppermute | solution.py:535
  28.4 0.0 collective-permute-done.7.got_a
  28.4 1.2 %collective-permute-start.10 = (f32[32,128]{1,0:T(8,128)S(1)}, f32[32,128]{1,0:T(8,128)S(1)}, u32[]{:S(2)}, u32[]{:S(2)}) collective-permute-start(f32[32,128]{1,0:T(8,128)S(1)} %slice_add_fusion.refs_0_), channel_id=1, source_target_pairs={{0,6},{1,7},{2,4},{3,5},{4,2},{5,3},{6,0},{7,1},{8,14},{9,15},{10,... | collective-permute-start | bytes 49160 | tf_op jit(solution)/shard_map/ppermute | solution.py:542
  29.6 0.7 %collective-permute-start.9 = (f32[32,128]{1,0:T(8,128)S(1)}, f32[32,128]{1,0:T(8,128)S(1)}, u32[]{:S(2)}, u32[]{:S(2)}) collective-permute-start(f32[32,128]{1,0:T(8,128)S(1)} %slice_add_fusion.refs_0_), channel_id=1, source_target_pairs={{0,4},{1,5},{2,6},{3,7},{4,0},{5,1},{6,2},{7,3},{8,12},{9,13},{10,... | collective-permute-start | bytes 49160 | tf_op jit(solution)/shard_map/ppermute | solution.py:542
  30.3 1.7 %collective-permute-start.8 = (f32[32,128]{1,0:T(8,128)S(1)}, f32[32,128]{1,0:T(8,128)S(1)}, u32[]{:S(2)}, u32[]{:S(2)}) collective-permute-start(f32[32,128]{1,0:T(8,128)S(1)} %slice_add_fusion.refs_0_), channel_id=1, source_target_pairs={{0,2},{1,3},{2,0},{3,1},{4,6},{5,7},{6,4},{7,5},{8,10},{9,11},{10,... | collective-permute-start | bytes 49160 | tf_op jit(solution)/shard_map/ppermute | solution.py:542
  31.9 0.0 collective-permute-done.11.got_b
  31.9 2.7 %shard_map.119 = (f32[4,4096]{1,0:T(4,128)}, f32[4,4096]{1,0:T(4,128)}) custom-call(f32[32,4,128]{2,1,0:T(4,128)S(1)} %get-tuple-element.77.ws, f32[32,4,128]{2,1,0:T(4,128)S(1)} %get-tuple-element.78.bs, f32[32,4,128]{2,1,0:T(4,128)S(1)} %get-tuple-element.79.v2, f32[80,128]{1,0:T(8,128)S(1)} %collective-permute-done.7.got_a, ...), custom_call_target="tpu_custom_call" | custom-call | flops 1 | bytes 1 | tf_op jit(solution)/shard_map/pallas_call | solution.py:544
  34.6 0.0 collective-permute-done.10.refs_3_
  34.6 0.0 collective-permute-done.9.refs_2_
  34.6 0.0 collective-permute-done.8.refs_1_
  34.6 0.9 %shard_map.118 = f32[2,2,4096]{2,1,0:T(2,128)} custom-call(f32[32,128]{1,0:T(8,128)S(1)} %slice_add_fusion.refs_0_, f32[32,128]{1,0:T(8,128)S(1)} %collective-permute-done.8.refs_1_, f32[32,128]{1,0:T(8,128)S(1)} %collective-permute-done.9.refs_2_, f32[32,128]{1,0:T(8,128)S(1)} %collective-permute-done.10.refs_3_, ...), custom_call_target="tpu_custom_call" | custom-call | flops 1 | bytes 1 | tf_op jit(solution)/shard_map/pallas_call | solution.py:550
  (1 shorter events, 0.0 us)
Async XLA Ops:
  2.4 11.6 %collective-permute-start.2 = (s16[16,4224]{1,0:T(8,128)(2,1)}, s16[16,4224]{1,0:T(8,128)(2,1)S(1)}, u32[]{:S(2)}, u32[]{:S(2)}) collective-permute-start(s16[16,4224]{1,0:T(8,128)(2,1)} %shard_map.112.after.wire), channel_id=1, source_target_pairs={{0,24},{8,16},{16,8},{24,0},{1,25},{9,17},{17,9},{25,1},{2,26},{10... | collective-permute-start | bytes 405512 | tf_op jit(solution)/shard_map/ppermute | solution.py:479
  7.4 11.6 %collective-permute-start.1 = (s16[16,4224]{1,0:T(8,128)(2,1)}, s16[16,4224]{1,0:T(8,128)(2,1)S(1)}, u32[]{:S(2)}, u32[]{:S(2)}) collective-permute-start(s16[16,4224]{1,0:T(8,128)(2,1)} %shard_map.112.after.wire), channel_id=1, source_target_pairs={{0,16},{8,24},{16,0},{24,8},{1,17},{9,25},{17,1},{25,9},{2,18},{10... | collective-permute-start | bytes 405512 | tf_op jit(solution)/shard_map/ppermute | solution.py:479
  7.4 11.6 %collective-permute-start = (s16[16,4224]{1,0:T(8,128)(2,1)}, s16[16,4224]{1,0:T(8,128)(2,1)S(1)}, u32[]{:S(2)}, u32[]{:S(2)}) collective-permute-start(s16[16,4224]{1,0:T(8,128)(2,1)} %shard_map.112.after.wire), channel_id=1, source_target_pairs={{0,8},{8,0},{16,24},{24,16},{1,9},{9,1},{17,25},{25,17},{2,10},{10... | collective-permute-start | bytes 405512 | tf_op jit(solution)/shard_map/ppermute | solution.py:479
  8.0 5.1 %copy-start = (bf16[32,3,128,128]{3,2,1,0:T(8,128)(2,1)S(1)}, bf16[32,3,128,128]{3,2,1,0:T(8,128)(2,1)}, u32[]{:S(2)}) copy-start(bf16[32,3,128,128]{3,2,1,0:T(8,128)(2,1)} %right.1) | copy-start | bytes 9437188
  8.0 5.1 %copy-start.1 = (s16[16,4224]{1,0:T(8,128)(2,1)S(1)}, s16[16,4224]{1,0:T(8,128)(2,1)}, u32[]{:S(2)}) copy-start(s16[16,4224]{1,0:T(8,128)(2,1)} %shard_map.112.after.wire) | copy-start | bytes 405508
  8.0 5.1 %copy-start.2 = (f32[4,4,4096]{2,1,0:T(4,128)S(1)}, f32[4,4,4096]{2,1,0:T(4,128)}, u32[]{:S(2)}) copy-start(f32[4,4,4096]{2,1,0:T(4,128)} %rain.3) | copy-start | bytes 786436
  8.0 5.1 %copy-start.4 = (f32[2,4096]{1,0:T(2,128)S(1)}, f32[2,4096]{1,0:T(2,128)}, u32[]{:S(2)}) copy-start(f32[2,4096]{1,0:T(2,128)} %obs.1) | copy-start | bytes 98308
  8.0 5.1 %copy-start.5 = (f32[4096]{0:T(1024)S(1)}, f32[4096]{0:T(1024)}, u32[]{:S(2)}) copy-start(f32[4096]{0:T(1024)} %param.14) | copy-start | bytes 49156
  8.0 5.1 %copy-start.6 = (f32[4096]{0:T(1024)S(1)}, f32[4096]{0:T(1024)}, u32[]{:S(2)}) copy-start(f32[4096]{0:T(1024)} %param.16) | copy-start | bytes 49156
  8.0 5.1 %copy-start.7 = (s32[2,16]{1,0:T(2,128)S(1)}, s32[2,16]{1,0:T(2,128)}, u32[]{:S(2)}) copy-start(s32[2,16]{1,0:T(2,128)} %anc.3) | copy-start | bytes 388
  10.3 12.0 %collective-permute-start.3 = (bf16[1552,128]{1,0:T(8,128)(2,1)}, bf16[1552,128]{1,0:T(8,128)(2,1)S(1)}, u32[]{:S(2)}, u32[]{:S(2)}) collective-permute-start(bf16[1552,128]{1,0:T(8,128)(2,1)} %get-tuple-element.55), channel_id=1, source_target_pairs={{0,1},{1,0},{2,3},{3,2},{4,5},{5,4},{6,7},{7,6},{8,9},{9,8},{10,11... | collective-permute-start | bytes 1191944 | tf_op jit(solution)/shard_map/ppermute | solution.py:487
  10.3 12.0 %collective-permute-start.4 = (bf16[1552,128]{1,0:T(8,128)(2,1)}, bf16[1552,128]{1,0:T(8,128)(2,1)S(1)}, u32[]{:S(2)}, u32[]{:S(2)}) collective-permute-start(bf16[1552,128]{1,0:T(8,128)(2,1)} %get-tuple-element.56), channel_id=1, source_target_pairs={{0,7},{1,2},{2,1},{3,4},{4,3},{5,6},{6,5},{7,0},{8,15},{9,10},{10,... | collective-permute-start | bytes 1191944 | tf_op jit(solution)/shard_map/ppermute | solution.py:488
  19.1 3.2 %copy-start.3 = (s32[32,3]{0,1:T(4,128)S(1)}, s32[32,3]{0,1:T(4,128)}, u32[]{:S(2)}) copy-start(s32[32,3]{0,1:T(4,128)} %param.12) | copy-start | bytes 1156
  19.6 4.3 %collective-permute-start.5 = (bf16[16,16,128]{2,1,0:T(8,128)(2,1)S(1)}, bf16[16,16,128]{2,1,0:T(8,128)(2,1)S(1)}, u32[]{:S(2)}, u32[]{:S(2)}) collective-permute-start(bf16[16,16,128]{2,1,0:T(8,128)(2,1)S(1)} %get-tuple-element.66), channel_id=1, source_target_pairs={{0,1},{1,0},{2,3},{3,2},{4,5},{5,4},{6,7},{7,6},{8,9},{9,8},{10,11... | collective-permute-start | bytes 196616 | tf_op jit(solution)/shard_map/ppermute | solution.py:502
  19.7 4.7 %collective-permute-start.6 = (bf16[16,16,128]{2,1,0:T(8,128)(2,1)S(1)}, bf16[16,16,128]{2,1,0:T(8,128)(2,1)S(1)}, u32[]{:S(2)}, u32[]{:S(2)}) collective-permute-start(bf16[16,16,128]{2,1,0:T(8,128)(2,1)S(1)} %get-tuple-element.67), channel_id=1, source_target_pairs={{0,7},{1,2},{2,1},{3,4},{4,3},{5,6},{6,5},{7,0},{8,15},{9,10},{10,... | collective-permute-start | bytes 196616 | tf_op jit(solution)/shard_map/ppermute | solution.py:503
  25.9 2.5 %collective-permute-start.7 = (f32[80,128]{1,0:T(8,128)S(1)}, f32[80,128]{1,0:T(8,128)S(1)}, u32[]{:S(2)}, u32[]{:S(2)}) collective-permute-start(f32[80,128]{1,0:T(8,128)S(1)} %get-tuple-element.71), channel_id=1, source_target_pairs={{0,1},{1,0},{2,3},{3,2},{4,5},{5,4},{6,7},{7,6},{8,9},{9,8},{10,11... | collective-permute-start | bytes 122888 | tf_op jit(solution)/shard_map/ppermute | solution.py:534
  26.0 5.9 %collective-permute-start.11 = (f32[48,128]{1,0:T(8,128)S(1)}, f32[48,128]{1,0:T(8,128)S(1)}, u32[]{:S(2)}, u32[]{:S(2)}) collective-permute-start(f32[48,128]{1,0:T(8,128)S(1)} %get-tuple-element.80), channel_id=1, source_target_pairs={{0,7},{1,2},{2,1},{3,4},{4,3},{5,6},{6,5},{7,0},{8,15},{9,10},{10,... | collective-permute-start | bytes 73736 | tf_op jit(solution)/shard_map/ppermute | solution.py:535
  28.4 6.2 %collective-permute-start.10 = (f32[32,128]{1,0:T(8,128)S(1)}, f32[32,128]{1,0:T(8,128)S(1)}, u32[]{:S(2)}, u32[]{:S(2)}) collective-permute-start(f32[32,128]{1,0:T(8,128)S(1)} %slice_add_fusion.refs_0_), channel_id=1, source_target_pairs={{0,6},{1,7},{2,4},{3,5},{4,2},{5,3},{6,0},{7,1},{8,14},{9,15},{10,... | collective-permute-start | bytes 49160 | tf_op jit(solution)/shard_map/ppermute | solution.py:542
  29.6 5.0 %collective-permute-start.9 = (f32[32,128]{1,0:T(8,128)S(1)}, f32[32,128]{1,0:T(8,128)S(1)}, u32[]{:S(2)}, u32[]{:S(2)}) collective-permute-start(f32[32,128]{1,0:T(8,128)S(1)} %slice_add_fusion.refs_0_), channel_id=1, source_target_pairs={{0,4},{1,5},{2,6},{3,7},{4,0},{5,1},{6,2},{7,3},{8,12},{9,13},{10,... | collective-permute-start | bytes 49160 | tf_op jit(solution)/shard_map/ppermute | solution.py:542
  30.3 4.3 %collective-permute-start.8 = (f32[32,128]{1,0:T(8,128)S(1)}, f32[32,128]{1,0:T(8,128)S(1)}, u32[]{:S(2)}, u32[]{:S(2)}) collective-permute-start(f32[32,128]{1,0:T(8,128)S(1)} %slice_add_fusion.refs_0_), channel_id=1, source_target_pairs={{0,2},{1,3},{2,0},{3,1},{4,6},{5,7},{6,4},{7,5},{8,10},{9,11},{10,... | collective-permute-start | bytes 49160 | tf_op jit(solution)/shard_map/ppermute | solution.py:542

commit v8 on v7

--- a/solution.py
+++ b/solution.py
@@ -88,30 +88,38 @@
     pos = lax.axis_index("tile")
     line = lax.broadcasted_iota(jnp.int32, (16, BLK), 0)
 
-    def edge(pay, block, start):
+    def edge(pay, block, start, k):
         away = jnp.zeros((16, BLK), jnp.float32)
         for m in range(HALO):
-            n = start + m + pos * nb
-            for k in range(NBR):
-                at = (m * NBR + k) * BLK
-                pay[at : at + BLK, :] = block[m, k]
-            for k, gap in enumerate((n - ids[1, start + m], ids[2, start + m] - n)):
-                away = jnp.where(line == 2 * m + k, gap.astype(jnp.float32), away)
-        at = HALO * NBR * BLK
-        pay[at : at + 16, :] = away.astype(jnp.bfloat16)
+            pay[m * BLK : (m + 1) * BLK, :] = block[m, 0]
+            gap = jnp.abs(ids[k, start + m] - (start + m + pos * nb))
+            away = jnp.where(line == m, gap.astype(jnp.float32), away)
+        pay[HALO * BLK : HALO * BLK + 16, :] = away.astype(jnp.bfloat16)
 
     @pl.when(even)
     def _():
-        edge(pay_a, right, nb - HALO)
-        edge(pay_b, left, 0)
+        edge(pay_a, right, nb - HALO, 2)
+        edge(pay_b, left, 0, 1)
 
     @pl.when(jnp.logical_not(even))
     def _():
-        edge(pay_a, left, 0)
-        edge(pay_b, right, nb - HALO)
-
-
-def stage_kernel(after, flow, wire, growth, prec, obs, anc, rain, turned, *held):
+        edge(pay_a, left, 0, 1)
+        edge(pay_b, right, nb - HALO, 2)
+
+
+def stage_kernel(after, flow, wire, growth, prec, obs, anc, rain, ids, turned, *held):
+    held, gaps, few_gaps = held[:-2], held[-2], held[-1]
+    nb = ids.shape[1]
+    pos = lax.axis_index("tile")
+
+    def measure(n, carry):
+        for k in range(2):
+            gap = jnp.abs(ids[k + 1, n] - (n + pos * nb)).astype(jnp.float32)
+            gaps[2 * n + k] = jnp.full(gaps.shape[1:], gap, jnp.float32).astype(jnp.bfloat16)
+            few_gaps[2 * n + k] = jnp.full(few_gaps.shape[1:], gap, jnp.float32)
+        return carry
+
+    run(0, nb, True, measure, 0)
     for src, dst in zip((wire, growth, prec, obs, anc), held):
         dst[...] = src[...]
     held[-1][...] = rain[2:4]
@@ -120,18 +128,30 @@
             turned[n, k * BLK : (k + 1) * BLK, :] = flow[n, k].T
 
 
-def halo_flux(ext, pay, right, nb, m):
-    depth = NBR * BLK
-    away = pay[HALO * depth : HALO * depth + 16, :].astype(jnp.float32)
-    at = jnp.where(right, nb + WIDE + m, HALO + m)
-    xs = [ext[at].astype(jnp.bfloat16)]
+def halo_flux(inside, pay, right, nb, m):
+    away = pay[HALO * BLK : HALO * BLK + 16, :].astype(jnp.float32)
+    gap = jnp.broadcast_to(away[m : m + 1, :], inside.shape[1:])
+    at = jnp.where(right, nb + HALO + m, m)
+    x = jnp.zeros(inside.shape[1:], jnp.float32)
+    for d in range(1, HALO + 1):
+        x = jnp.where(gap == d, inside[at + jnp.where(right, -d, d)].astype(jnp.float32), x)
+    return flux_of([x.astype(jnp.bfloat16)], pay[m * BLK : (m + 1) * BLK, :])
+
+
+def nearby(cells, at, n, gaps):
+    xs = [cells[at]]
     for k, sign in enumerate((-1, 1)):
-        gap = jnp.broadcast_to(away[2 * m + k : 2 * m + k + 1, :], ext.shape[1:])
-        x = jnp.zeros(ext.shape[1:], jnp.float32)
-        for d in range(HALO + 1):
-            x = jnp.where(gap == d, ext[at + sign * d].astype(jnp.float32), x)
-        xs.append(x.astype(jnp.bfloat16))
-    return flux_of(xs, pay[m * depth : (m + 1) * depth, :])
+        gap = gaps[2 * n + k]
+        x = xs[0]
+        for d in range(1, HALO + 1):
+            x = jnp.where(gap == d, cells[at + sign * d], x)
+        xs.append(x)
+    return [x.astype(jnp.bfloat16) for x in xs]
+
+
+def clear_ends(ref):
+    for m in (*range(HALO), *range(ref.shape[0] - HALO, ref.shape[0])):
+        ref[m] = jnp.zeros(ref.shape[1:], ref.dtype)
 
 
 def decode(sel, pieces, cols):
@@ -145,9 +165,9 @@
 
 def open_kernel(members, unroll, *refs):
     pieces = refs[:members]
-    anc, growth, prec, obs = refs[members : members + 4]
-    wb, v0, b1, bq, wq, miss, quad, unit1, pay_a, pay_b = refs[members + 4 : members + 14]
-    pair, scaler = refs[-2:]
+    anc, growth, prec, obs, flow, gaps = refs[members : members + 6]
+    wb, v0, b1, bq, wq, miss, quad, unit1, pay_a, pay_b = refs[members + 6 : members + 16]
+    pair, scaler, parts = refs[-3:]
     nb = growth.shape[0]
     slots = anc.shape[1]
     rows = pieces[0].shape[0]
@@ -194,7 +214,7 @@
                 rain0 = wet[q * slots : (q + 1) * slots] * scale[4]
                 s = wetness(w)
                 row = pl.ds(n, 1)
-                wb[n] = w.astype(jnp.bfloat16)
+                wb[n + HALO] = w.astype(jnp.bfloat16)
                 v0[n] = w + rain0 - 0.2 * b * s
                 b1[n] = b + growth[row, :] * b * (s - 0.4 * b)
                 bq[n] = bi
@@ -203,25 +223,30 @@
                 acc = acc + prec[row, :] * (off * off)
         return acc
 
+    clear_ends(wb)
     miss[...] = run(0, quads, unroll, step, jnp.zeros((slots, BLK), jnp.float32))
+    for m, n in enumerate((*range(HALO), *range(nb - HALO, nb))):
+        edge = v0[n] + flux_of(nearby(wb, n + HALO, n, gaps), flow[n])
+        top = edge.astype(jnp.bfloat16)
+        parts[0, m] = top
+        parts[1, m] = (edge - top.astype(jnp.float32)).astype(jnp.bfloat16)
     even = right_first()
     for pay, right in ((pay_a, even), (pay_b, jnp.logical_not(even))):
-        pay[0:WIDE] = wb[pl.ds(jnp.where(right, nb - WIDE, 0), WIDE)]
-        edge = v0[pl.ds(jnp.where(right, nb - HALO, 0), HALO)]
-        top = edge.astype(jnp.bfloat16)
-        pay[WIDE : WIDE + HALO] = top
-        pay[WIDE + HALO : WIDE + 2 * HALO] = (edge - top.astype(jnp.float32)).astype(jnp.bfloat16)
+        pay[0:HALO] = wb[pl.ds(jnp.where(right, nb, HALO), HALO)]
+        for i in range(2):
+            pay[(i + 1) * HALO : (i + 2) * HALO] = parts[i, pl.ds(jnp.where(right, HALO, 0), HALO)]
 
 
 def inner01_kernel(members, unroll, *refs):
     pieces = refs[:members]
-    wb, v0, b1, quad, unit1, flow, ids, growth, prec, obs, anc, rain, flow_a, flow_b = refs[members : members + 14]
-    r1, wb1, v1, b2, w2, ws, bs, v2, miss, turn_a, turn_b = refs[members + 14 :]
-    nb, slots = wb.shape[:2]
+    wb, v0, b1, quad, unit1, flow, gaps, growth, prec, obs, heirs, rain, flow_a, flow_b = refs[members : members + 14]
+    r1, wb1, v1, b2, w2, ws, bs, v2, miss, turn_a, turn_b, anc, sem = refs[members + 14 :]
+    early = pltpu.make_async_copy(heirs, anc, sem)
+    early.start()
+    nb, slots = v0.shape[:2]
     part = rain.shape[1]
     quads = nb // 4
     scale = unit1[...]
-    base = lax.axis_index("tile") * nb
 
     def wet_day(m, carry):
         got = decode(quad[...], pieces, lanes(m, 3 * quads * BLK))
@@ -230,9 +255,10 @@
         return carry
 
     run(0, quads, unroll, wet_day, 0)
+    early.wait()
 
     def day0(n, acc):
-        w = v0[n] + flux_of((wb[n], wb[ids[1, n] - base], wb[ids[2, n] - base]), flow[n])
+        w = v0[n] + flux_of(nearby(wb, n + HALO, n, gaps), flow[n])
         wb1[n - HALO] = w.astype(jnp.bfloat16)
         b, v, acc = settle(n, w, b1, r1, growth, prec, obs, acc)
         b2[n - HALO] = b
@@ -240,10 +266,8 @@
         return acc
 
     miss[...] = run(HALO, nb - HALO, unroll, day0, jnp.zeros((slots, BLK), jnp.float32))
-    base = base + HALO
-
     def day1(n, carry):
-        w2[n - WIDE] = v1[n - HALO] + flux_of((wb1[n - HALO], wb1[ids[1, n] - base], wb1[ids[2, n] - base]), flow[n])
+        w2[n - WIDE] = v1[n - HALO] + flux_of(nearby(wb1, n - HALO, n, gaps), flow[n])
         return carry
 
     run(WIDE, nb - WIDE, unroll, day1, 0)
@@ -256,9 +280,9 @@
 
     run(WIDE, nb - WIDE, unroll, pick, 0)
     for raw, turned in ((flow_a, turn_a), (flow_b, turn_b)):
-        for at in range(0, HALO * NBR * BLK, BLK):
+        for at in range(0, HALO * BLK, BLK):
             turned[at : at + BLK, :] = raw[at : at + BLK, :].T
-        turned[HALO * NBR * BLK :, :] = raw[HALO * NBR * BLK :, :]
+        turned[HALO * BLK :, :] = raw[HALO * BLK :, :]
 
 
 def settle(n, w, b1, r1, growth, prec, obs, acc):
@@ -284,25 +308,29 @@
 
 
 def outer01_kernel(
-    unroll, wb, v0, b1, r1, wb1, v1, b2, wi, bi, vi, miss0, miss1, got_a, got_b, flow, flow_a, flow_b, ids,
-    growth, prec, obs, anc, rain, b2_out, w2_out, ws, bs, v2, total, pay_a, pay_b, ext, ext1, v1_out,
+    unroll, wb, v0, b1, r1, wb1, v1, b2, wi, bi, vi, miss0, miss1, got_a, got_b, flow, flow_a, flow_b, gaps, few_gaps,
+    growth, prec, obs, heirs, rain, b2_out, w2_out, ws, bs, v2, total, pay_a, pay_b, ext, ext1, v1_out, anc, sem, parts,
 ):
-    nb, slots = wb.shape[:2]
+    early = pltpu.make_async_copy(heirs, anc, sem)
+    early.start()
+    nb, slots = v0.shape[:2]
     part = rain.shape[1]
-    pos = lax.axis_index("tile")
     even = right_first()
-    lows, highs = (0, WIDE + HALO), (nb - WIDE - HALO, nb)
-    for lo, hi in (lows, highs):
-        ext[WIDE + lo : WIDE + hi] = wb[lo:hi]
+    for lo, hi in ((0, WIDE), (nb - WIDE, nb)):
+        ext[HALO + lo : HALO + hi] = wb[HALO + lo : HALO + hi]
     ext1[WIDE : 2 * WIDE] = wb1[0:WIDE]
     ext1[nb - WIDE : nb] = wb1[nb - 2 * HALO - WIDE : nb - 2 * HALO]
     sides = ((got_a, flow_a, even), (got_b, flow_b, jnp.logical_not(even)))
     for got, _, right in sides:
-        ext[pl.ds(jnp.where(right, nb + WIDE, 0), WIDE)] = got[0:WIDE]
-    base = WIDE - pos * nb
-
+        ext[pl.ds(jnp.where(right, nb + HALO, 0), HALO)] = got[0:HALO]
+    for got, pay, right in sides:
+        spot = jnp.where(right, nb + HALO, 0)
+        for m in range(HALO):
+            edge = got[HALO + m].astype(jnp.float32) + got[2 * HALO + m].astype(jnp.float32)
+            ext1[spot + m] = (edge + halo_flux(wb, pay, right, nb, m)).astype(jnp.bfloat16)
+    early.wait()
     def day0(n, acc):
-        w = v0[n] + flux_of((ext[n + WIDE], ext[ids[1, n] + base], ext[ids[2, n] + base]), flow[n])
+        w = v0[n] + flux_of(nearby(ext, n + HALO, n, gaps), flow[n])
         ext1[n + HALO] = w.astype(jnp.bfloat16)
         b, v, acc = settle(n, w, b1, r1, growth, prec, obs, acc)
         m = n if n < HALO else n - (nb - 2 * HALO)
@@ -315,14 +343,9 @@
         acc = day0(n, acc)
     total[0:slots, :] = miss0[...]
     total[slots : 2 * slots, :] = acc
-    for got, pay, right in sides:
-        spot = jnp.where(right, nb + HALO, 0)
-        for m in range(HALO):
-            edge = got[WIDE + m].astype(jnp.float32) + got[WIDE + HALO + m].astype(jnp.float32)
-            ext1[spot + m] = (edge + halo_flux(ext, pay, right, nb, m)).astype(jnp.bfloat16)
-    base = HALO - pos * nb
     picks = ancestors_of(anc, part)
-    ws[WIDE : nb - WIDE] = wi[...]
+    clear_ends(ws)
+    ws[HALO + WIDE : HALO + nb - WIDE] = wi[...]
     bs[WIDE : nb - WIDE] = bi[...]
     v2[WIDE : nb - WIDE] = vi[...]
     for n in (*range(WIDE), *range(nb - WIDE, nb)):
@@ -332,14 +355,15 @@
             v, b = v1_out[at], b2_out.at[at]
         else:
             v, b = v1[n - HALO], b2.at[n - HALO]
-        w2_out[m] = v + flux_of((ext1[n + HALO], ext1[ids[1, n] + base], ext1[ids[2, n] + base]), flow[n])
-        choose(picks, w2_out.at[m], b, rain[0, :, lanes(n)], ws.at[n], bs.at[n], v2.at[n])
+        w2_out[m] = v + flux_of(nearby(ext1, n + HALO, n, gaps), flow[n])
+        choose(picks, w2_out.at[m], b, rain[0, :, lanes(n)], ws.at[n + HALO], bs.at[n], v2.at[n])
+    for m, n in enumerate((*range(HALO), *range(nb - HALO, nb))):
+        parts[m] = v2[n] + flux_of(nearby(ws, n + HALO, n, few_gaps), flow[n])
     for pay, right in ((pay_a, even), (pay_b, jnp.logical_not(even))):
-        for m in range(WIDE):
-            pay[m * part : (m + 1) * part, :] = ws[jnp.where(right, nb - WIDE, 0) + m]
         for m in range(HALO):
-            pay[(WIDE + m) * part : (WIDE + m + 1) * part, :] = v2[jnp.where(right, nb - HALO, 0) + m]
-    at = (WIDE + HALO) * part
+            pay[m * part : (m + 1) * part, :] = ws[jnp.where(right, nb, HALO) + m]
+            pay[(HALO + m) * part : (HALO + m + 1) * part, :] = parts[jnp.where(right, HALO, 0) + m]
+    at = 2 * HALO * part
     pay_a[at : at + 2 * slots, :] = total[...]
 
 
@@ -351,36 +375,30 @@
 
 
 def close_kernel(
-    unroll, ws, bs, v2, got_a, got_b, flow, flow_a, flow_b, ids, growth, rain, bio_out, wat_out, ext, ext3
+    unroll, ws, bs, v2, got_a, got_b, flow, flow_a, flow_b, gaps, growth, rain, bio_out, wat_out, ext, ext3
 ):
-    nb, part = ws.shape[:2]
-    pos = lax.axis_index("tile")
+    nb, part = bs.shape[:2]
     even = right_first()
-    half = jnp.bfloat16
-    ext[WIDE : WIDE + nb] = ws[...]
+    ext[HALO : HALO + nb] = ws[HALO : HALO + nb]
     sides = ((got_a, flow_a, even), (got_b, flow_b, jnp.logical_not(even)))
     for got, _, right in sides:
-        for m in range(WIDE):
-            ext[jnp.where(right, nb + WIDE, 0) + m] = got[m * part : (m + 1) * part, :]
+        for m in range(HALO):
+            ext[jnp.where(right, nb + HALO, 0) + m] = got[m * part : (m + 1) * part, :]
     for got, pay, right in sides:
         spot = jnp.where(right, nb + HALO, 0)
         for m in range(HALO):
-            edge = got[(WIDE + m) * part : (WIDE + m + 1) * part, :]
-            ext3[spot + m] = edge + halo_flux(ext, pay, right, nb, m)
-
-    def near(ref, n, at):
-        base = at - pos * nb
-        return [ref[i].astype(half) for i in (n + at, ids[1, n] + base, ids[2, n] + base)]
+            edge = got[(HALO + m) * part : (HALO + m + 1) * part, :]
+            ext3[spot + m] = edge + halo_flux(ws, pay, right, nb, m)
 
     def day2(n, carry):
-        ext3[n + HALO] = v2[n] + flux_of(near(ext, n, WIDE), flow[n])
+        ext3[n + HALO] = v2[n] + flux_of(nearby(ext, n + HALO, n, gaps), flow[n])
         return carry
 
     run(0, nb, unroll, day2, 0)
 
     def day3(n, carry):
-        flux = flux_of(near(ext3, n, HALO), flow[n])
-        wat_out[:, lanes(n)], bio_out[:, lanes(n)] = final(n, ext3[n + HALO], flux, ws[n], bs[n], growth, rain)
+        flux = flux_of(nearby(ext3, n + HALO, n, gaps), flow[n])
+        wat_out[:, lanes(n)], bio_out[:, lanes(n)] = final(n, ext3[n + HALO], flux, ws[n + HALO], bs[n], growth, rain)
         return carry
 
     run(0, nb, unroll, day3, 0)
@@ -446,8 +464,8 @@
     neighbours = neighbours.T
 
     depth = NBR * BLK
-    edge = ((HALO * depth + 16, BLK), bf16)
-    tile = (HALO, NBR, BLK, BLK)
+    edge = ((HALO * BLK + 16, BLK), bf16)
+    tile = (HALO, 1, BLK, BLK)
     wire = pl.pallas_call(
         pack_kernel,
         grid=(1,),
@@ -465,8 +483,8 @@
         out_shape=tuple(jax.ShapeDtypeStruct(*edge) for _ in range(2)),
         in_specs=[
             HBM,
-            pl.BlockSpec(tile, lambda i: (0, 0, 0, 0)),
-            pl.BlockSpec(tile, lambda i: (nb // HALO - 1, 0, 0, 0)),
+            pl.BlockSpec(tile, lambda i: (0, 1, 0, 0)),
+            pl.BlockSpec(tile, lambda i: (nb // HALO - 1, 2, 0, 0)),
             SMEM,
         ],
         out_specs=(VMEM, VMEM),
@@ -474,15 +492,23 @@
         cost_estimate=weigh(1),
     )(wire, flow_blocks, flow_blocks, neighbours)
 
-    pieces = {0: wire}
-    for j in reversed(range(1, members)):
-        pieces[j] = lax.ppermute(wire, "particle", [(i, i ^ j) for i in range(members)])
+    def over(x, j):
+        return lax.ppermute(x, "particle", [(i, i ^ j) for i in range(members)])
+
+    pieces = {j: over(wire, j) for j in range(members - 2, 0, -2)}
+    pieces[1] = over(wire, 1)
+    pieces[0] = wire
+    for j in range(3, members, 2):
+        got, flow_a = lax.optimization_barrier((pieces[j - 1], flow_a))
+        pieces[j] = over(got, 1)
     small = (wire, growth_rate.reshape(nb, BLK), obs_precision.reshape(nb, BLK), observations, ancestors)
-    flow, pieces[0], growth, prec, obs, anc, rain23 = call(
+    flow, pieces[0], growth, prec, obs, anc, rain23, gaps, few_gaps = call(
         stage_kernel,
-        [((nb, depth, BLK), bf16)] + [(x.shape, x.dtype) for x in small] + [((2, part, cells), f32)],
-        [HBM] + [VMEM] * 7,
-    )(wire, flow_blocks, *small, rain)
+        [((nb, depth, BLK), bf16)]
+        + [(x.shape, x.dtype) for x in small]
+        + [((2, part, cells), f32), ((2 * nb, slots, BLK), bf16), ((2 * nb, part, BLK), f32)],
+        [HBM] + [VMEM] * 7 + [SMEM],
+    )(wire, flow_blocks, *small, rain, neighbours)
     pieces = [pieces[j] for j in range(members)]
     flow_a = lax.ppermute(flow_a, "tile", swap_a)
     flow_b = lax.ppermute(flow_b, "tile", swap_b)
@@ -490,18 +516,23 @@
     field = ((nb, slots, BLK), f32)
     wb, v0, b1, bq, wq, miss, quad, unit1, pay_a, pay_b = call(
         functools.partial(open_kernel, members, unroll),
-        [((nb, slots, BLK), bf16), field, field, field, field, ((slots, BLK), f32), ((4 * slots, members * rows * 2), bf16), ((slots, BLK), f32)]
-        + [((WIDE + 2 * HALO, slots, BLK), bf16)] * 2,
-        [VMEM] * (members + 4),
+        [((nb + 2 * HALO, slots, BLK), bf16), field, field, field, field, ((slots, BLK), f32), ((4 * slots, members * rows * 2), bf16), ((slots, BLK), f32)]
+        + [((3 * HALO, slots, BLK), bf16)] * 2,
+        [VMEM] * (members + 6),
         [
             pltpu.VMEM((8 * slots, members * rows * 2), bf16),
             pltpu.VMEM((6 * slots, members * rows * 2), bf16),
+            pltpu.VMEM((2, 2 * HALO, slots, BLK), bf16),
         ],
         cost=10**10,
-    )(*pieces, anc, growth, prec, obs)
+    )(*pieces, anc, growth, prec, obs, flow, gaps)
     got_a = lax.ppermute(pay_a, "tile", swap_a)
     got_b = lax.ppermute(pay_b, "tile", swap_b)
     inner, core = nb - 2 * HALO, nb - 2 * WIDE
+    indices = [
+        pltpu.SMEM(ancestors.shape, jnp.int32),
+        pltpu.SemaphoreType.DMA,
+    ]
 
     def blocks(count, height=slots, kind=f32):
         return ((count, height, BLK), kind)
@@ -511,25 +542,28 @@
         [blocks(nb), blocks(inner, kind=bf16), blocks(inner), blocks(inner), blocks(core)]
         + [blocks(core, part)] * 3
         + [((slots, BLK), f32), edge, edge],
-        [VMEM] * (members + 6) + [SMEM] + [VMEM] * 3 + [SMEM] + [VMEM] * 3,
+        [VMEM] * (members + 14),
+        indices,
     )(
-        *pieces, wb, v0, b1, quad, unit1, flow, neighbours, growth, prec, obs, ancestors, rain23, flow_a, flow_b
+        *pieces, wb, v0, b1, quad, unit1, flow, gaps, growth, prec, obs, anc, rain23, flow_a, flow_b
     )
-    swap_rows = (WIDE + HALO) * part
+    swap_rows = 2 * HALO * part
     b2_edge, w2_edge, ws, bs, v2, total, end_a, end_b = call(
         functools.partial(outer01_kernel, unroll),
         [blocks(2 * HALO), blocks(2 * WIDE)]
-        + [blocks(nb, part)] * 3
+        + [blocks(nb + 2 * HALO, part), blocks(nb, part), blocks(nb, part)]
         + [((2 * slots, BLK), f32), ((swap_rows + 2 * slots, BLK), f32), ((swap_rows, BLK), f32)],
-        [VMEM] * 17 + [SMEM] + [VMEM] * 3 + [SMEM, VMEM],
+        [VMEM] * 24,
         [
-            pltpu.VMEM((nb + 2 * WIDE, slots, BLK), bf16),
-            pltpu.VMEM((nb + WIDE, slots, BLK), bf16),
+            pltpu.VMEM((nb + 2 * HALO, slots, BLK), bf16),
+            pltpu.VMEM((nb + 2 * HALO, slots, BLK), bf16),
             pltpu.VMEM((2 * HALO, slots, BLK), f32),
-        ],
+        ]
+        + indices
+        + [pltpu.VMEM((2 * HALO, part, BLK), f32)],
     )(
-        wb, v0, b1, r1, wb1, v1, b2, wi, bi, vi, miss, miss1, got_a, got_b, flow, turn_a, turn_b, neighbours,
-        growth, prec, obs, ancestors, rain23,
+        wb, v0, b1, r1, wb1, v1, b2, wi, bi, vi, miss, miss1, got_a, got_b, flow, turn_a, turn_b, gaps, few_gaps,
+        growth, prec, obs, anc, rain23,
     )
     last_a = lax.ppermute(end_a, "tile", swap_a)
     last_b = lax.ppermute(end_b, "tile", swap_b)
@@ -544,9 +578,9 @@
     bio_out, wat_out = call(
         functools.partial(close_kernel, unroll),
         [((part, cells), f32)] * 2,
-        [VMEM] * 8 + [SMEM] + [VMEM] * 2,
-        [pltpu.VMEM((nb + 2 * WIDE, part, BLK), f32), pltpu.VMEM((nb + WIDE, part, BLK), f32)],
-    )(ws, bs, v2, last_a, last_b, flow, turn_a, turn_b, neighbours, growth, rain23)
+        [VMEM] * 11,
+        [pltpu.VMEM((nb + 2 * HALO, part, BLK), f32)] * 2,
+    )(ws, bs, v2, last_a, last_b, flow, turn_a, turn_b, few_gaps, growth, rain23)
     (means,) = call(
         functools.partial(means_kernel, unroll, len(terms)), [((CYCLES, 2, cells), f32)], [VMEM] * (len(terms) + 6)
     )(*terms, bq, wq, b2, w2, b2_edge, w2_edge)

time: 35.7 us -> 34.2 us (0.958)
  waiting for transfers between devices: 5.58 us -> 4.48 us
  Pallas kernels: 12.1 us -> 11.7 us
    ppermute x1, starting transfers between devices: 2.78 us -> 1.79 us  [body(): flow_b = lax.ppermute(flow_b, 'tile', swap_b)]
    ppermute x3, waiting for transfers between devices: 5.08 us -> 4.14 us  [over(): return lax.ppermute(x, 'particle', [(i, i ^ j) for i in range(members)])]
    pallas_call x1, Pallas kernels: 2.67 us -> 1.93 us  [body(): call(functools.partial(close_kernel, unroll), [((part, cells), f32)] * 2,...]
    ppermute x3, starting transfers between devices: 5.62 us -> 6.33 us  [over(): return lax.ppermute(x, 'particle', [(i, i ^ j) for i in range(members)])]
    pallas_call x1, Pallas kernels: 0.87 us -> 1.48 us  [body(): call(stage_kernel, [((nb, depth, BLK), bf16)] + [(x.shape, x.dtype) for x...]
    pallas_call x1, Pallas kernels: 2.24 us -> 1.88 us  [body(): pl.pallas_call(edge_kernel, grid=(1,), out_shape=tuple((jax.ShapeDtypeStr...]
  transfers between devices with their start and end apart: 12 -> 12, of which waited for: 2 -> 3; matrix products, arithmetic and copies ran while one was open for 0% -> 0% of each run, Pallas kernels for 23% -> 22%
where the time goes in v8:
time: 34.2 us; the launch traced here: 34.1 us
  starting transfers between devices  17.1 us (50%)
  Pallas kernels  11.7 us (34%)
  waiting for transfers between devices  4.48 us (13%)
  between operations  0.79 us (2%)
    ppermute x3, starting transfers between devices, over(): return lax.ppermute(x, 'particle', [(i, i ^ j) for i in range(members)])  6.33 us
    ppermute x3, waiting for transfers between devices, over(): return lax.ppermute(x, 'particle', [(i, i ^ j) for i in range(members)])  4.14 us
    ppermute x3, starting transfers between devices, body(): lax.ppermute(total, 'tile', [(i, i ^ m) for i in range(tiles)])  3.55 us
    ppermute x1, starting transfers between devices, body(): got_b = lax.ppermute(pay_b, 'tile', swap_b)  2.6 us
    ppermute x1, starting transfers between devices, body(): last_b = lax.ppermute(end_b, 'tile', swap_b)  2.56 us
    pallas_call x1, Pallas kernels, body(): call(functools.partial(close_kernel, unroll), [((part, cells), f32)] * 2,...  1.93 us
    pallas_call x1, Pallas kernels, body(): pl.pallas_call(edge_kernel, grid=(1,), out_shape=tuple((jax.ShapeDtypeStr...  1.88 us
    ppermute x1, starting transfers between devices, body(): flow_b = lax.ppermute(flow_b, 'tile', swap_b)  1.79 us
  transfers between devices with their start and end apart: 12, of which 3 were waited for; matrix products, arithmetic and copies ran while one was open for 0% of the time, Pallas kernels for 22%

profile of v8, /device:TPU:0, one launch (start us, length us, event | category | flops | bytes accessed | tf_op | source)
XLA Modules:
  0.0 34.1 jit_solution(15585397908758133388)
XLA Ops:
  0.6 1.8 %shard_map.112.after.wire = s16[16,4224]{1,0:T(8,128)(2,1)} custom-call(f32[4,4096]{1,0:T(4,128)} %bio.1, f32[4,4096]{1,0:T(4,128)} %wat.1, f32[4,4,4096]{2,1,0:T(4,128)} %rain.3), custom_call_target="tpu_custom_call" | custom-call | flops 1 | bytes 1 | tf_op jit(solution)/shard_map/pallas_call | solution.py:469
  2.4 4.0 %collective-permute-start.1 = (s16[16,4224]{1,0:T(8,128)(2,1)}, s16[16,4224]{1,0:T(8,128)(2,1)S(1)}, u32[]{:S(2)}, u32[]{:S(2)}) collective-permute-start(s16[16,4224]{1,0:T(8,128)(2,1)} %shard_map.112.after.wire), channel_id=1, source_target_pairs={{0,16},{8,24},{16,0},{24,8},{1,17},{9,25},{17,1},{25,9},{2,18},{10... | collective-permute-start | bytes 405512 | tf_op jit(solution)/shard_map/ppermute | solution.py:496
  6.4 1.6 %collective-permute-start = (s16[16,4224]{1,0:T(8,128)(2,1)}, s16[16,4224]{1,0:T(8,128)(2,1)S(1)}, u32[]{:S(2)}, u32[]{:S(2)}) collective-permute-start(s16[16,4224]{1,0:T(8,128)(2,1)} %shard_map.112.after.wire), channel_id=1, source_target_pairs={{0,8},{8,0},{16,24},{24,16},{1,9},{9,1},{17,25},{25,17},{2,10},{10... | collective-permute-start | bytes 405512 | tf_op jit(solution)/shard_map/ppermute | solution.py:496
  8.0 0.0 copy-start
  8.0 0.0 copy-start.1
  8.0 0.0 copy-start.2
  8.0 0.0 copy-start.4
  8.0 0.0 copy-start.5
  8.1 0.0 copy-start.6
  8.1 0.0 copy-start.7
  8.1 1.9 %shard_map.114 = (bf16[528,128]{1,0:T(8,128)(2,1)}, bf16[528,128]{1,0:T(8,128)(2,1)}) custom-call(s16[16,4224]{1,0:T(8,128)(2,1)} %shard_map.112.after.wire, bf16[32,3,128,128]{3,2,1,0:T(8,128)(2,1)} %right.1, bf16[32,3,128,128]{3,2,1,0:T(8,128)(2,1)} %right.1, s32[3,32]{1,0:T(4,128)} %bitcast.5), custom_call_target="tpu_custom_call" | custom-call | flops 1 | bytes 1 | tf_op jit(solution)/shard_map/pallas_call | solution.py:480
  10.0 3.3 %collective-permute-done.1.refs_2_ = s16[16,4224]{1,0:T(8,128)(2,1)S(1)} collective-permute-done((s16[16,4224]{1,0:T(8,128)(2,1)}, s16[16,4224]{1,0:T(8,128)(2,1)S(1)}, u32[]{:S(2)}, u32[]{:S(2)}) %collective-permute-start.1) | collective-permute-done | bytes 135200 | tf_op jit(solution)/shard_map/ppermute | solution.py:496
  13.2 0.7 %collective-permute-start.2 = (s16[16,4224]{1,0:T(8,128)(2,1)S(1)}, s16[16,4224]{1,0:T(8,128)(2,1)S(1)}, u32[]{:S(2)}, u32[]{:S(2)}) collective-permute-start(s16[16,4224]{1,0:T(8,128)(2,1)S(1)} %collective-permute-done.1.refs_2_), channel_id=1, source_target_pairs={{0,8},{8,0},{16,24},{24,16},{1,9},{9,1},{17,25},{25,17},{2,10},{10... | collective-permute-start | bytes 405512 | tf_op jit(solution)/shard_map/ppermute | solution.py:496
  14.0 1.8 %collective-permute-start.4 = (bf16[528,128]{1,0:T(8,128)(2,1)}, bf16[528,128]{1,0:T(8,128)(2,1)S(1)}, u32[]{:S(2)}, u32[]{:S(2)}) collective-permute-start(bf16[528,128]{1,0:T(8,128)(2,1)} %get-tuple-element.63), channel_id=1, source_target_pairs={{0,7},{1,2},{2,1},{3,4},{4,3},{5,6},{6,5},{7,0},{8,15},{9,10},{10,... | collective-permute-start | bytes 405512 | tf_op jit(solution)/shard_map/ppermute | solution.py:514
  15.7 0.0 copy-done
  15.8 0.0 copy-done.1
  15.8 0.0 copy-done.2
  15.8 0.0 copy-done.3
  15.8 0.0 copy-done.4
  15.8 0.0 copy-done.5
  15.8 0.0 copy-done.6
  15.8 0.0 copy-done.7
  15.8 1.5 %shard_map.113 = (bf16[32,384,128]{2,1,0:T(8,128)(2,1)S(1)}, s16[16,4224]{1,0:T(8,128)(2,1)S(1)}, f32[32,128]{1,0:T(8,128)S(1)}, f32[32,128]{1,0:T(8,128)S(1)}, ...) custom-call(s16[16,4224]{1,0:T(8,128)(2,1)S(1)} %copy-done.1, ...), custom_call_target="tpu_custom_call" | custom-call | flops 1 | bytes 1 | tf_op jit(solution)/shard_map/pallas_call | solution.py:505
  17.3 0.0 copy-done.8
  17.3 0.1 collective-permute-start.3
  17.4 0.0 collective-permute-done.refs_1_
  17.4 0.9 %collective-permute-done.2.refs_3_ = s16[16,4224]{1,0:T(8,128)(2,1)S(1)} collective-permute-done((s16[16,4224]{1,0:T(8,128)(2,1)S(1)}, s16[16,4224]{1,0:T(8,128)(2,1)S(1)}, u32[]{:S(2)}, u32[]{:S(2)}) %collective-permute-start.2) | collective-permute-done | bytes 135200 | tf_op jit(solution)/shard_map/ppermute | solution.py:496
  18.2 0.7 %shard_map.115 = (bf16[40,16,128]{2,1,0:T(8,128)(2,1)S(1)}, f32[32,16,128]{2,1,0:T(8,128)S(1)}, f32[32,16,128]{2,1,0:T(8,128)S(1)}, f32[32,16,128]{2,1,0:T(8,128...) custom-call(s16[16,4224]{1,0:T(8,128)(2,1)S(1)} %get-tuple-element.4, ...), custom_call_target="tpu_custom_call" | custom-call | flops 10000000000 | bytes 1 | tf_op jit(solution)/shard_map/pallas_call | solution.py:517
  19.0 0.1 collective-permute-start.5
  19.1 2.6 %collective-permute-start.6 = (bf16[12,16,128]{2,1,0:T(8,128)(2,1)S(1)}, bf16[12,16,128]{2,1,0:T(8,128)(2,1)S(1)}, u32[]{:S(2)}, u32[]{:S(2)}) collective-permute-start(bf16[12,16,128]{2,1,0:T(8,128)(2,1)S(1)} %get-tuple-element.74), channel_id=1, source_target_pairs={{0,7},{1,2},{2,1},{3,4},{4,3},{5,6},{6,5},{7,0},{8,15},{9,10},{10,... | collective-permute-start | bytes 147464 | tf_op jit(solution)/shard_map/ppermute | solution.py:530
  21.7 0.0 collective-permute-done.4.refs_17_
  21.7 0.0 collective-permute-done.3.refs_16_
  21.7 1.5 %shard_map.116 = (f32[32,16,128]{2,1,0:T(8,128)S(1)}, bf16[24,16,128]{2,1,0:T(8,128)(2,1)S(1)}, f32[24,16,128]{2,1,0:T(8,128)S(1)}, f32[24,16,128]{2,1,0:T(8,128...) custom-call(s16[16,4224]{1,0:T(8,128)(2,1)S(1)} %get-tuple-element.4, ...), custom_call_target="tpu_custom_call" | custom-call | flops 1 | bytes 1 | tf_op jit(solution)/shard_map/pallas_call | solution.py:540
  23.2 0.0 collective-permute-done.5.got_a
  23.2 0.3 collective-permute-done.6.got_b
  23.6 1.4 %shard_map.117 = (f32[8,16,128]{2,1,0:T(8,128)S(1)}, f32[16,16,128]{2,1,0:T(8,128)S(1)}, f32[40,4,128]{2,1,0:T(4,128)S(1)}, f32[32,4,128]{2,1,0:T(4,128)S(1)}, f...) custom-call(bf16[40,16,128]{2,1,0:T(8,128)(2,1)S(1)} %get-tuple-element.56.refs, ...), custom_call_target="tpu_custom_call" | custom-call | flops 1 | bytes 1 | tf_op jit(solution)/shard_map/pallas_call | solution.py:551
  25.0 0.1 collective-permute-start.7
  25.1 2.6 %collective-permute-start.11 = (f32[32,128]{1,0:T(8,128)S(1)}, f32[32,128]{1,0:T(8,128)S(1)}, u32[]{:S(2)}, u32[]{:S(2)}) collective-permute-start(f32[32,128]{1,0:T(8,128)S(1)} %get-tuple-element.88), channel_id=1, source_target_pairs={{0,7},{1,2},{2,1},{3,4},{4,3},{5,6},{6,5},{7,0},{8,15},{9,10},{10,... | collective-permute-start | bytes 49160 | tf_op jit(solution)/shard_map/ppermute | solution.py:569
  27.7 0.0 collective-permute-done.7.got_a
  27.7 1.2 %collective-permute-start.10 = (f32[32,128]{1,0:T(8,128)S(1)}, f32[32,128]{1,0:T(8,128)S(1)}, u32[]{:S(2)}, u32[]{:S(2)}) collective-permute-start(f32[32,128]{1,0:T(8,128)S(1)} %slice_add_fusion.refs_0_), channel_id=1, source_target_pairs={{0,6},{1,7},{2,4},{3,5},{4,2},{5,3},{6,0},{7,1},{8,14},{9,15},{10,... | collective-permute-start | bytes 49160 | tf_op jit(solution)/shard_map/ppermute | solution.py:576
  28.9 0.5 %collective-permute-start.9 = (f32[32,128]{1,0:T(8,128)S(1)}, f32[32,128]{1,0:T(8,128)S(1)}, u32[]{:S(2)}, u32[]{:S(2)}) collective-permute-start(f32[32,128]{1,0:T(8,128)S(1)} %slice_add_fusion.refs_0_), channel_id=1, source_target_pairs={{0,4},{1,5},{2,6},{3,7},{4,0},{5,1},{6,2},{7,3},{8,12},{9,13},{10,... | collective-permute-start | bytes 49160 | tf_op jit(solution)/shard_map/ppermute | solution.py:576
  29.4 1.9 %collective-permute-start.8 = (f32[32,128]{1,0:T(8,128)S(1)}, f32[32,128]{1,0:T(8,128)S(1)}, u32[]{:S(2)}, u32[]{:S(2)}) collective-permute-start(f32[32,128]{1,0:T(8,128)S(1)} %slice_add_fusion.refs_0_), channel_id=1, source_target_pairs={{0,2},{1,3},{2,0},{3,1},{4,6},{5,7},{6,4},{7,5},{8,10},{9,11},{10,... | collective-permute-start | bytes 49160 | tf_op jit(solution)/shard_map/ppermute | solution.py:576
  31.2 0.0 collective-permute-done.11.got_b
  31.2 1.9 %shard_map.119 = (f32[4,4096]{1,0:T(4,128)}, f32[4,4096]{1,0:T(4,128)}) custom-call(f32[40,4,128]{2,1,0:T(4,128)S(1)} %get-tuple-element.85.ws, f32[32,4,128]{2,1,0:T(4,128)S(1)} %get-tuple-element.86.bs, f32[32,4,128]{2,1,0:T(4,128)S(1)} %get-tuple-element.87.v2, f32[64,128]{1,0:T(8,128)S(1)} %collective-permute-done.7.got_a, ...), custom_call_target="tpu_custom_call" | custom-call | flops 1 | bytes 1 | tf_op jit(solution)/shard_map/pallas_call | solution.py:578
  33.2 0.0 collective-permute-done.10.refs_3_
  33.2 0.0 collective-permute-done.9.refs_2_
  33.2 0.0 collective-permute-done.8.refs_1_
  33.2 0.9 %shard_map.118 = f32[2,2,4096]{2,1,0:T(2,128)} custom-call(f32[32,128]{1,0:T(8,128)S(1)} %slice_add_fusion.refs_0_, f32[32,128]{1,0:T(8,128)S(1)} %collective-permute-done.8.refs_1_, f32[32,128]{1,0:T(8,128)S(1)} %collective-permute-done.9.refs_2_, f32[32,128]{1,0:T(8,128)S(1)} %collective-permute-done.10.refs_3_, ...), custom_call_target="tpu_custom_call" | custom-call | flops 1 | bytes 1 | tf_op jit(solution)/shard_map/pallas_call | solution.py:584
  (3 shorter events, 0.0 us)
Async XLA Ops:
  2.4 10.8 %collective-permute-start.1 = (s16[16,4224]{1,0:T(8,128)(2,1)}, s16[16,4224]{1,0:T(8,128)(2,1)S(1)}, u32[]{:S(2)}, u32[]{:S(2)}) collective-permute-start(s16[16,4224]{1,0:T(8,128)(2,1)} %shard_map.112.after.wire), channel_id=1, source_target_pairs={{0,16},{8,24},{16,0},{24,8},{1,17},{9,25},{17,1},{25,9},{2,18},{10... | collective-permute-start | bytes 405512 | tf_op jit(solution)/shard_map/ppermute | solution.py:496
  6.4 10.9 %collective-permute-start = (s16[16,4224]{1,0:T(8,128)(2,1)}, s16[16,4224]{1,0:T(8,128)(2,1)S(1)}, u32[]{:S(2)}, u32[]{:S(2)}) collective-permute-start(s16[16,4224]{1,0:T(8,128)(2,1)} %shard_map.112.after.wire), channel_id=1, source_target_pairs={{0,8},{8,0},{16,24},{24,16},{1,9},{9,1},{17,25},{25,17},{2,10},{10... | collective-permute-start | bytes 405512 | tf_op jit(solution)/shard_map/ppermute | solution.py:496
  8.0 7.7 %copy-start = (bf16[32,3,128,128]{3,2,1,0:T(8,128)(2,1)S(1)}, bf16[32,3,128,128]{3,2,1,0:T(8,128)(2,1)}, u32[]{:S(2)}) copy-start(bf16[32,3,128,128]{3,2,1,0:T(8,128)(2,1)} %right.1) | copy-start | bytes 9437188
  8.0 7.7 %copy-start.1 = (s16[16,4224]{1,0:T(8,128)(2,1)S(1)}, s16[16,4224]{1,0:T(8,128)(2,1)}, u32[]{:S(2)}) copy-start(s16[16,4224]{1,0:T(8,128)(2,1)} %shard_map.112.after.wire) | copy-start | bytes 405508
  8.0 7.7 %copy-start.2 = (f32[4,4,4096]{2,1,0:T(4,128)S(1)}, f32[4,4,4096]{2,1,0:T(4,128)}, u32[]{:S(2)}) copy-start(f32[4,4,4096]{2,1,0:T(4,128)} %rain.3) | copy-start | bytes 786436
  8.0 7.7 %copy-start.3 = (f32[2,4096]{1,0:T(2,128)S(1)}, f32[2,4096]{1,0:T(2,128)}, u32[]{:S(2)}) copy-start(f32[2,4096]{1,0:T(2,128)} %obs.1) | copy-start | bytes 98308
  8.0 7.7 %copy-start.4 = (f32[4096]{0:T(1024)S(1)}, f32[4096]{0:T(1024)}, u32[]{:S(2)}) copy-start(f32[4096]{0:T(1024)} %param.14) | copy-start | bytes 49156
  8.0 7.7 %copy-start.5 = (f32[4096]{0:T(1024)S(1)}, f32[4096]{0:T(1024)}, u32[]{:S(2)}) copy-start(f32[4096]{0:T(1024)} %param.16) | copy-start | bytes 49156
  8.1 7.7 %copy-start.6 = (s32[32,3]{0,1:T(4,128)S(1)}, s32[32,3]{0,1:T(4,128)}, u32[]{:S(2)}) copy-start(s32[32,3]{0,1:T(4,128)} %param.12) | copy-start | bytes 1156
  8.1 7.7 %copy-start.7 = (s32[2,16]{1,0:T(2,128)S(1)}, s32[2,16]{1,0:T(2,128)}, u32[]{:S(2)}) copy-start(s32[2,16]{1,0:T(2,128)} %anc.1) | copy-start | bytes 388
  10.0 7.3 %copy-start.8 = (bf16[528,128]{1,0:T(8,128)(2,1)S(1)}, bf16[528,128]{1,0:T(8,128)(2,1)}, u32[]{:S(2)}) copy-start(bf16[528,128]{1,0:T(8,128)(2,1)} %get-tuple-element.62) | copy-start | bytes 405508
  13.2 5.0 %collective-permute-start.2 = (s16[16,4224]{1,0:T(8,128)(2,1)S(1)}, s16[16,4224]{1,0:T(8,128)(2,1)S(1)}, u32[]{:S(2)}, u32[]{:S(2)}) collective-permute-start(s16[16,4224]{1,0:T(8,128)(2,1)S(1)} %collective-permute-done.1.refs_2_), channel_id=1, source_target_pairs={{0,8},{8,0},{16,24},{24,16},{1,9},{9,1},{17,25},{25,17},{2,10},{10... | collective-permute-start | bytes 405512 | tf_op jit(solution)/shard_map/ppermute | solution.py:496
  14.0 7.7 %collective-permute-start.4 = (bf16[528,128]{1,0:T(8,128)(2,1)}, bf16[528,128]{1,0:T(8,128)(2,1)S(1)}, u32[]{:S(2)}, u32[]{:S(2)}) collective-permute-start(bf16[528,128]{1,0:T(8,128)(2,1)} %get-tuple-element.63), channel_id=1, source_target_pairs={{0,7},{1,2},{2,1},{3,4},{4,3},{5,6},{6,5},{7,0},{8,15},{9,10},{10,... | collective-permute-start | bytes 405512 | tf_op jit(solution)/shard_map/ppermute | solution.py:514
  17.3 4.4 %collective-permute-start.3 = (bf16[528,128]{1,0:T(8,128)(2,1)S(1)}, bf16[528,128]{1,0:T(8,128)(2,1)S(1)}, u32[]{:S(2)}, u32[]{:S(2)}) collective-permute-start(bf16[528,128]{1,0:T(8,128)(2,1)S(1)} %copy-done.8), channel_id=1, source_target_pairs={{0,1},{1,0},{2,3},{3,2},{4,5},{5,4},{6,7},{7,6},{8,9},{9,8},{10,11... | collective-permute-start | bytes 405512 | tf_op jit(solution)/shard_map/ppermute | solution.py:513
  19.0 4.2 %collective-permute-start.5 = (bf16[12,16,128]{2,1,0:T(8,128)(2,1)S(1)}, bf16[12,16,128]{2,1,0:T(8,128)(2,1)S(1)}, u32[]{:S(2)}, u32[]{:S(2)}) collective-permute-start(bf16[12,16,128]{2,1,0:T(8,128)(2,1)S(1)} %get-tuple-element.73), channel_id=1, source_target_pairs={{0,1},{1,0},{2,3},{3,2},{4,5},{5,4},{6,7},{7,6},{8,9},{9,8},{10,11... | collective-permute-start | bytes 147464 | tf_op jit(solution)/shard_map/ppermute | solution.py:529
  19.1 4.5 %collective-permute-start.6 = (bf16[12,16,128]{2,1,0:T(8,128)(2,1)S(1)}, bf16[12,16,128]{2,1,0:T(8,128)(2,1)S(1)}, u32[]{:S(2)}, u32[]{:S(2)}) collective-permute-start(bf16[12,16,128]{2,1,0:T(8,128)(2,1)S(1)} %get-tuple-element.74), channel_id=1, source_target_pairs={{0,7},{1,2},{2,1},{3,4},{4,3},{5,6},{6,5},{7,0},{8,15},{9,10},{10,... | collective-permute-start | bytes 147464 | tf_op jit(solution)/shard_map/ppermute | solution.py:530
  25.0 2.7 %collective-permute-start.7 = (f32[64,128]{1,0:T(8,128)S(1)}, f32[64,128]{1,0:T(8,128)S(1)}, u32[]{:S(2)}, u32[]{:S(2)}) collective-permute-start(f32[64,128]{1,0:T(8,128)S(1)} %get-tuple-element.79), channel_id=1, source_target_pairs={{0,1},{1,0},{2,3},{3,2},{4,5},{5,4},{6,7},{7,6},{8,9},{9,8},{10,11... | collective-permute-start | bytes 98312 | tf_op jit(solution)/shard_map/ppermute | solution.py:568
  25.1 6.1 %collective-permute-start.11 = (f32[32,128]{1,0:T(8,128)S(1)}, f32[32,128]{1,0:T(8,128)S(1)}, u32[]{:S(2)}, u32[]{:S(2)}) collective-permute-start(f32[32,128]{1,0:T(8,128)S(1)} %get-tuple-element.88), channel_id=1, source_target_pairs={{0,7},{1,2},{2,1},{3,4},{4,3},{5,6},{6,5},{7,0},{8,15},{9,10},{10,... | collective-permute-start | bytes 49160 | tf_op jit(solution)/shard_map/ppermute | solution.py:569
  27.7 5.5 %collective-permute-start.10 = (f32[32,128]{1,0:T(8,128)S(1)}, f32[32,128]{1,0:T(8,128)S(1)}, u32[]{:S(2)}, u32[]{:S(2)}) collective-permute-start(f32[32,128]{1,0:T(8,128)S(1)} %slice_add_fusion.refs_0_), channel_id=1, source_target_pairs={{0,6},{1,7},{2,4},{3,5},{4,2},{5,3},{6,0},{7,1},{8,14},{9,15},{10,... | collective-permute-start | bytes 49160 | tf_op jit(solution)/shard_map/ppermute | solution.py:576
  28.9 4.3 %collective-permute-start.9 = (f32[32,128]{1,0:T(8,128)S(1)}, f32[32,128]{1,0:T(8,128)S(1)}, u32[]{:S(2)}, u32[]{:S(2)}) collective-permute-start(f32[32,128]{1,0:T(8,128)S(1)} %slice_add_fusion.refs_0_), channel_id=1, source_target_pairs={{0,4},{1,5},{2,6},{3,7},{4,0},{5,1},{6,2},{7,3},{8,12},{9,13},{10,... | collective-permute-start | bytes 49160 | tf_op jit(solution)/shard_map/ppermute | solution.py:576
  29.4 3.8 %collective-permute-start.8 = (f32[32,128]{1,0:T(8,128)S(1)}, f32[32,128]{1,0:T(8,128)S(1)}, u32[]{:S(2)}, u32[]{:S(2)}) collective-permute-start(f32[32,128]{1,0:T(8,128)S(1)} %slice_add_fusion.refs_0_), channel_id=1, source_target_pairs={{0,2},{1,3},{2,0},{3,1},{4,6},{5,7},{6,4},{7,5},{8,10},{9,11},{10,... | collective-permute-start | bytes 49160 | tf_op jit(solution)/shard_map/ppermute | solution.py:576

commit v9 on v8

--- a/solution.py
+++ b/solution.py
@@ -47,7 +47,7 @@
     return lax.rem(lax.axis_index("tile"), 2) == 0
 
 
-def pack_kernel(bio, wat, rain, wire, held, factor):
+def pack_kernel(bio, wat, rain, wire, early, late, held, factor):
     part, cells = bio.shape
     nb = cells // BLK
     half, quarter = cells // 2, cells // 4
@@ -77,9 +77,14 @@
         return jnp.round(x).astype(jnp.int32).astype(jnp.int16)
 
     pairs, quads = nb // 2, nb // 4
-    for n in range(nb):
-        wire[:, lanes(n)] = coded(held[:, lanes(n)] * factor[0 if n < pairs else 1 if n < pairs + quads else 2])
-    wire[:, lanes(nb)] = coded(factor[3])
+    for n in range(pairs + 1):
+        x = coded(factor[3] if n == pairs else held[:, lanes(n)] * factor[0])
+        wire[:, lanes(n)] = x
+        early[:, lanes(n)] = x
+    for n in range(pairs):
+        x = coded(held[:, lanes(pairs + n)] * factor[1 if n < quads else 2])
+        wire[:, lanes(pairs + 1 + n)] = x
+        late[:, lanes(n)] = x
 
 
 def edge_kernel(after, left, right, ids, pay_a, pay_b):
@@ -154,23 +159,27 @@
         ref[m] = jnp.zeros(ref.shape[1:], ref.dtype)
 
 
-def decode(sel, pieces, cols):
+def decode(sel, pieces, n):
     parts = []
-    for ref in pieces:
-        q = ref[:, cols].astype(jnp.int32)
+    for ref, first in pieces:
+        q = ref[:, lanes(n + first)].astype(jnp.int32)
         parts.append((q >> 8).astype(jnp.float32).astype(jnp.bfloat16))
         parts.append((q & 255).astype(jnp.float32).astype(jnp.bfloat16))
     return jnp.dot(sel, jnp.concatenate(parts, axis=0), preferred_element_type=jnp.float32)
 
 
+def rain_of(both, others):
+    return [(r, (r.shape[1] // BLK + 1) // 2) for r in both] + [(r, 0) for r in others]
+
+
 def open_kernel(members, unroll, *refs):
-    pieces = refs[:members]
+    pieces, rains, refs = [(r, 0) for r in refs[:members]], rain_of(refs[:2], refs[members : 2 * members - 2]), refs[members - 2 :]
     anc, growth, prec, obs, flow, gaps = refs[members : members + 6]
     wb, v0, b1, bq, wq, miss, quad, unit1, pay_a, pay_b = refs[members + 6 : members + 16]
     pair, scaler, parts = refs[-3:]
     nb = growth.shape[0]
     slots = anc.shape[1]
-    rows = pieces[0].shape[0]
+    rows = pieces[0][0].shape[0]
     part = rows // 4
     depth = members * rows * 2
     me = lax.axis_index("particle")
@@ -197,16 +206,16 @@
         scaler[i * slots : (i + 1) * slots, :] = hits(g, want)
 
     pairs, quads = nb // 2, nb // 4
-    codes = decode(scaler[...], pieces, lanes(nb))
+    codes = decode(scaler[...], pieces, pairs)
     scale = [
         codes[i * slots : (i + 1) * slots] * (BOUNDS[f] / SCALE_STEPS / STEPS) for i, f in enumerate((0, 1, 0, 1, 2, 2))
     ]
     unit1[...] = scale[5]
 
     def step(m, acc):
-        wet = decode(quad[...], pieces, lanes(m, pairs * BLK))
+        wet = decode(quad[...], rains, m)
         for p in range(2):
-            got = decode(pair[...], pieces, lanes(m + p * quads))
+            got = decode(pair[...], pieces, m + p * quads)
             for h in range(2):
                 q = 2 * h + p
                 n = m + q * quads
@@ -238,7 +247,7 @@
 
 
 def inner01_kernel(members, unroll, *refs):
-    pieces = refs[:members]
+    pieces = rain_of(refs[:2], refs[2:members])
     wb, v0, b1, quad, unit1, flow, gaps, growth, prec, obs, heirs, rain, flow_a, flow_b = refs[members : members + 14]
     r1, wb1, v1, b2, w2, ws, bs, v2, miss, turn_a, turn_b, anc, sem = refs[members + 14 :]
     early = pltpu.make_async_copy(heirs, anc, sem)
@@ -249,7 +258,7 @@
     scale = unit1[...]
 
     def wet_day(m, carry):
-        got = decode(quad[...], pieces, lanes(m, 3 * quads * BLK))
+        got = decode(quad[...], pieces, m + quads)
         for q in range(4):
             r1[m + q * quads] = got[q * slots : (q + 1) * slots] * scale
         return carry
@@ -466,13 +475,13 @@
     depth = NBR * BLK
     edge = ((HALO * BLK + 16, BLK), bf16)
     tile = (HALO, 1, BLK, BLK)
-    wire = pl.pallas_call(
+    wire, early, late = pl.pallas_call(
         pack_kernel,
         grid=(1,),
-        out_shape=jax.ShapeDtypeStruct((rows, (nb + 1) * BLK), i16),
+        out_shape=tuple(jax.ShapeDtypeStruct((rows, n * BLK), i16) for n in (nb + 1, nb // 2 + 1, nb // 2)),
         in_specs=[pl.BlockSpec((part, cells), lambda i: (0, 0))] * 2
         + [pl.BlockSpec((2, part, cells), lambda i: (0, 0, 0))],
-        out_specs=VMEM,
+        out_specs=(VMEM, VMEM, VMEM),
         scratch_shapes=[pltpu.VMEM((rows, cells), f32), pltpu.VMEM((4, rows, BLK), f32)],
         compiler_params=pltpu.CompilerParams(vmem_limit_bytes=60 * 2**20),
         cost_estimate=weigh(1),
@@ -495,21 +504,27 @@
     def over(x, j):
         return lax.ppermute(x, "particle", [(i, i ^ j) for i in range(members)])
 
-    pieces = {j: over(wire, j) for j in range(members - 2, 0, -2)}
-    pieces[1] = over(wire, 1)
-    pieces[0] = wire
+    far, later = {}, {}
+    for j in range(members - 2, 0, -2):
+        far[j] = over(early, j)
+    beside = over(wire, 1)
+    for j in range(members - 2, 0, -2):
+        later[j] = over(late, j)
     for j in range(3, members, 2):
-        got, flow_a = lax.optimization_barrier((pieces[j - 1], flow_a))
-        pieces[j] = over(got, 1)
+        got, flow_a = lax.optimization_barrier((far[j - 1], flow_a))
+        far[j] = over(got, 1)
     small = (wire, growth_rate.reshape(nb, BLK), obs_precision.reshape(nb, BLK), observations, ancestors)
-    flow, pieces[0], growth, prec, obs, anc, rain23, gaps, few_gaps = call(
+    flow, wire, growth, prec, obs, anc, rain23, gaps, few_gaps = call(
         stage_kernel,
         [((nb, depth, BLK), bf16)]
         + [(x.shape, x.dtype) for x in small]
         + [((2, part, cells), f32), ((2 * nb, slots, BLK), bf16), ((2 * nb, part, BLK), f32)],
         [HBM] + [VMEM] * 7 + [SMEM],
-    )(wire, flow_blocks, *small, rain, neighbours)
-    pieces = [pieces[j] for j in range(members)]
+    )(far[2], flow_blocks, *small, rain, neighbours)
+    for j in range(3, members, 2):
+        got, few_gaps = lax.optimization_barrier((later[j - 1], few_gaps))
+        later[j] = over(got, 1)
+    far, later = ([x[j] for j in range(2, members)] for x in (far, later))
     flow_a = lax.ppermute(flow_a, "tile", swap_a)
     flow_b = lax.ppermute(flow_b, "tile", swap_b)
 
@@ -518,14 +533,14 @@
         functools.partial(open_kernel, members, unroll),
         [((nb + 2 * HALO, slots, BLK), bf16), field, field, field, field, ((slots, BLK), f32), ((4 * slots, members * rows * 2), bf16), ((slots, BLK), f32)]
         + [((3 * HALO, slots, BLK), bf16)] * 2,
-        [VMEM] * (members + 6),
+        [VMEM] * (2 * members + 4),
         [
             pltpu.VMEM((8 * slots, members * rows * 2), bf16),
             pltpu.VMEM((6 * slots, members * rows * 2), bf16),
             pltpu.VMEM((2, 2 * HALO, slots, BLK), bf16),
         ],
         cost=10**10,
-    )(*pieces, anc, growth, prec, obs, flow, gaps)
+    )(wire, beside, *far, *later, anc, growth, prec, obs, flow, gaps)
     got_a = lax.ppermute(pay_a, "tile", swap_a)
     got_b = lax.ppermute(pay_b, "tile", swap_b)
     inner, core = nb - 2 * HALO, nb - 2 * WIDE
@@ -545,7 +560,7 @@
         [VMEM] * (members + 14),
         indices,
     )(
-        *pieces, wb, v0, b1, quad, unit1, flow, gaps, growth, prec, obs, anc, rain23, flow_a, flow_b
+        wire, beside, *later, wb, v0, b1, quad, unit1, flow, gaps, growth, prec, obs, anc, rain23, flow_a, flow_b
     )
     swap_rows = 2 * HALO * part
     b2_edge, w2_edge, ws, bs, v2, total, end_a, end_b = call(

time: 34.2 us -> 34 us (level)
  waiting for transfers between devices: 4.48 us -> 2.42 us
  starting transfers between devices: 17.1 us -> 18.8 us
    ppermute x3 -> x5, waiting for transfers between devices: 4.14 us -> 2.03 us  [over(): return lax.ppermute(x, 'particle', [(i, i ^ j) for i in range(members)])]
    ppermute x3 -> x5, starting transfers between devices: 6.33 us -> 8.4 us  [over(): return lax.ppermute(x, 'particle', [(i, i ^ j) for i in range(members)])]
    ppermute x1, starting transfers between devices: 1.79 us -> 0.36 us  [body(): flow_b = lax.ppermute(flow_b, 'tile', swap_b)]
    ppermute x1, starting transfers between devices: 0.07 us -> 1.24 us  [body(): flow_a = lax.ppermute(flow_a, 'tile', swap_a)]
  transfers between devices with their start and end apart: 12 -> 14, of which waited for: 3 -> 4; matrix products, arithmetic and copies ran while one was open for 0% -> 0% of each run, Pallas kernels for 22% -> 22%
where the time goes in v9:
time: 34 us; the launch traced here: 33.8 us
  starting transfers between devices  18.8 us (55%)
  Pallas kernels  11.8 us (35%)
  waiting for transfers between devices  2.42 us (7%)
  between operations  0.78 us (2%)
    ppermute x5, starting transfers between devices, over(): return lax.ppermute(x, 'particle', [(i, i ^ j) for i in range(members)])  8.4 us
    ppermute x3, starting transfers between devices, body(): lax.ppermute(total, 'tile', [(i, i ^ m) for i in range(tiles)])  3.55 us
    ppermute x1, starting transfers between devices, body(): got_b = lax.ppermute(pay_b, 'tile', swap_b)  2.54 us
    ppermute x1, starting transfers between devices, body(): last_b = lax.ppermute(end_b, 'tile', swap_b)  2.54 us
    ppermute x5, waiting for transfers between devices, over(): return lax.ppermute(x, 'particle', [(i, i ^ j) for i in range(members)])  2.03 us
    pallas_call x1, Pallas kernels, body(): call(functools.partial(close_kernel, unroll), [((part, cells), f32)] * 2,...  1.94 us
    pallas_call x1, Pallas kernels, body(): pl.pallas_call(edge_kernel, grid=(1,), out_shape=tuple((jax.ShapeDtypeStr...  1.88 us
    pallas_call x1, Pallas kernels, body(): pl.pallas_call(pack_kernel, grid=(1,), out_shape=tuple((jax.ShapeDtypeStr...  1.83 us
  transfers between devices with their start and end apart: 14, of which 4 were waited for; matrix products, arithmetic and copies ran while one was open for 0% of the time, Pallas kernels for 22%

profile of v9, /device:TPU:0, one launch (start us, length us, event | category | flops | bytes accessed | tf_op | source)
XLA Modules:
  0.0 33.8 jit_solution(13072702215079994652)
XLA Ops:
  0.6 1.8 %shard_map.112 = (s16[16,4224]{1,0:T(8,128)(2,1)}, s16[16,2176]{1,0:T(8,128)(2,1)}, s16[16,2048]{1,0:T(8,128)(2,1)}) custom-call(f32[4,4096]{1,0:T(4,128)} %bio.1, f32[4,4096]{1,0:T(4,128)} %wat.1, f32[4,4,4096]{2,1,0:T(4,128)} %rain.3), custom_call_target="tpu_custom_call" | custom-call | flops 1 | bytes 1 | tf_op jit(solution)/shard_map/pallas_call | solution.py:478
  2.5 4.0 %collective-permute-start = (s16[16,2176]{1,0:T(8,128)(2,1)}, s16[16,2176]{1,0:T(8,128)(2,1)S(1)}, u32[]{:S(2)}, u32[]{:S(2)}) collective-permute-start(s16[16,2176]{1,0:T(8,128)(2,1)} %get-tuple-element.52), channel_id=1, source_target_pairs={{0,16},{8,24},{16,0},{24,8},{1,17},{9,25},{17,1},{25,9},{2,18},{10... | collective-permute-start | bytes 208904 | tf_op jit(solution)/shard_map/ppermute | solution.py:505
  6.5 1.6 %collective-permute-start.1 = (s16[16,4224]{1,0:T(8,128)(2,1)}, s16[16,4224]{1,0:T(8,128)(2,1)S(1)}, u32[]{:S(2)}, u32[]{:S(2)}) collective-permute-start(s16[16,4224]{1,0:T(8,128)(2,1)} %get-tuple-element.53.wire.after), channel_id=1, source_target_pairs={{0,8},{8,0},{16,24},{24,16},{1,9},{9,1},{17,25},{25,17},{2,10},{10... | collective-permute-start | bytes 405512 | tf_op jit(solution)/shard_map/ppermute | solution.py:505
  8.1 0.3 collective-permute-start.3
  8.4 0.0 copy-start.4
  8.4 0.0 copy-start.5
  8.4 0.0 copy-start.6
  8.5 0.0 copy-start.7
  8.5 1.9 %shard_map.114 = (bf16[528,128]{1,0:T(8,128)(2,1)}, bf16[528,128]{1,0:T(8,128)(2,1)}) custom-call(s16[16,4224]{1,0:T(8,128)(2,1)} %get-tuple-element.53.wire.after, bf16[32,3,128,128]{3,2,1,0:T(8,128)(2,1)} %right.1, bf16[32,3,128,128]{3,2,1,0:T(8,128)(2,1)} %right.1, s32[3,32]{1,0:T(4,128)} %bitcast.5), custom_call_target="tpu_custom_call" | custom-call | flops 1 | bytes 1 | tf_op jit(solution)/shard_map/pallas_call | solution.py:489
  10.4 0.0 collective-permute-done.after.refs_2_
  10.4 1.3 %collective-permute-start.2 = (s16[16,2176]{1,0:T(8,128)(2,1)S(1)}, s16[16,2176]{1,0:T(8,128)(2,1)S(1)}, u32[]{:S(2)}, u32[]{:S(2)}) collective-permute-start(s16[16,2176]{1,0:T(8,128)(2,1)S(1)} %collective-permute-done.after.refs_2_), channel_id=1, source_target_pairs={{0,8},{8,0},{16,24},{24,16},{1,9},{9,1},{17,25},{25,17},{2,10},{10... | collective-permute-start | bytes 208904 | tf_op jit(solution)/shard_map/ppermute | solution.py:505
  11.7 0.0 copy-done
  11.7 0.0 copy-done.1
  11.7 0.0 copy-done.2
  11.7 0.0 copy-done.4
  11.7 0.0 copy-done.5
  11.7 0.0 copy-done.6
  11.7 0.0 copy-done.7
  11.7 1.5 %shard_map.113 = (bf16[32,384,128]{2,1,0:T(8,128)(2,1)S(1)}, s16[16,4224]{1,0:T(8,128)(2,1)S(1)}, f32[32,128]{1,0:T(8,128)S(1)}, f32[32,128]{1,0:T(8,128)S(1)}, ...) custom-call(s16[16,2176]{1,0:T(8,128)(2,1)S(1)} %collective-permute-, ...), custom_call_target="tpu_custom_call" | custom-call | flops 1 | bytes 1 | tf_op jit(solution)/shard_map/pallas_call | solution.py:517
  13.2 0.5 %collective-permute-done.3.refs_4_.refs_2_ = s16[16,2048]{1,0:T(8,128)(2,1)S(1)} collective-permute-done((s16[16,2048]{1,0:T(8,128)(2,1)}, s16[16,2048]{1,0:T(8,128)(2,1)S(1)}, u32[]{:S(2)}, u32[]{:S(2)}) %collective-permute-start.3) | collective-permute-done | bytes 65568 | tf_op jit(solution)/shard_map/ppermute | solution.py:505
  13.7 1.2 %collective-permute-start.4 = (s16[16,2048]{1,0:T(8,128)(2,1)S(1)}, s16[16,2048]{1,0:T(8,128)(2,1)S(1)}, u32[]{:S(2)}, u32[]{:S(2)}) collective-permute-start(s16[16,2048]{1,0:T(8,128)(2,1)S(1)} %collective-permute-done.3.refs_4_.refs_2_), channel_id=1, source_target_pairs={{0,8},{8,0},{16,24},{24,16},{1,9},{9,1},{17,25},{25,17},{2,10},{10... | collective-permute-start | bytes 196616 | tf_op jit(solution)/shard_map/ppermute | solution.py:505
  14.9 0.0 copy-done.9
  14.9 0.4 %collective-permute-start.6 = (bf16[528,128]{1,0:T(8,128)(2,1)S(1)}, bf16[528,128]{1,0:T(8,128)(2,1)S(1)}, u32[]{:S(2)}, u32[]{:S(2)}) collective-permute-start(bf16[528,128]{1,0:T(8,128)(2,1)S(1)} %copy-done.9), channel_id=1, source_target_pairs={{0,7},{1,2},{2,1},{3,4},{4,3},{5,6},{6,5},{7,0},{8,15},{9,10},{10,... | collective-permute-start | bytes 405512 | tf_op jit(solution)/shard_map/ppermute | solution.py:529
  15.3 1.2 %collective-permute-start.5 = (bf16[528,128]{1,0:T(8,128)(2,1)S(1)}, bf16[528,128]{1,0:T(8,128)(2,1)S(1)}, u32[]{:S(2)}, u32[]{:S(2)}) collective-permute-start(bf16[528,128]{1,0:T(8,128)(2,1)S(1)} %copy-done.8), channel_id=1, source_target_pairs={{0,1},{1,0},{2,3},{3,2},{4,5},{5,4},{6,7},{7,6},{8,9},{9,8},{10,11... | collective-permute-start | bytes 405512 | tf_op jit(solution)/shard_map/ppermute | solution.py:528
  16.5 0.0 collective-permute-done.1.refs_1_
  16.5 1.5 %collective-permute-done.4.refs_5_.refs_3_ = s16[16,2048]{1,0:T(8,128)(2,1)S(1)} collective-permute-done((s16[16,2048]{1,0:T(8,128)(2,1)S(1)}, s16[16,2048]{1,0:T(8,128)(2,1)S(1)}, u32[]{:S(2)}, u32[]{:S(2)}) %collective-permute-start.4) | collective-permute-done | bytes 65568 | tf_op jit(solution)/shard_map/ppermute | solution.py:505
  18.0 0.0 collective-permute-done.2.refs_3_
  18.0 0.8 %shard_map.115 = (bf16[40,16,128]{2,1,0:T(8,128)(2,1)S(1)}, f32[32,16,128]{2,1,0:T(8,128)S(1)}, f32[32,16,128]{2,1,0:T(8,128)S(1)}, f32[32,16,128]{2,1,0:T(8,128...) custom-call(s16[16,4224]{1,0:T(8,128)(2,1)S(1)} %get-tuple-element.5, ...), custom_call_target="tpu_custom_call" | custom-call | flops 10000000000 | bytes 1 | tf_op jit(solution)/shard_map/pallas_call | solution.py:532
  18.8 0.1 collective-permute-start.7
  18.8 2.5 %collective-permute-start.8 = (bf16[12,16,128]{2,1,0:T(8,128)(2,1)S(1)}, bf16[12,16,128]{2,1,0:T(8,128)(2,1)S(1)}, u32[]{:S(2)}, u32[]{:S(2)}) collective-permute-start(bf16[12,16,128]{2,1,0:T(8,128)(2,1)S(1)} %get-tuple-element.84), channel_id=1, source_target_pairs={{0,7},{1,2},{2,1},{3,4},{4,3},{5,6},{6,5},{7,0},{8,15},{9,10},{10,... | collective-permute-start | bytes 147464 | tf_op jit(solution)/shard_map/ppermute | solution.py:545
  21.4 0.2 collective-permute-done.6.refs_17_
  21.6 0.0 collective-permute-done.5.refs_16_
  21.6 1.5 %shard_map.116 = (f32[32,16,128]{2,1,0:T(8,128)S(1)}, bf16[24,16,128]{2,1,0:T(8,128)(2,1)S(1)}, f32[24,16,128]{2,1,0:T(8,128)S(1)}, f32[24,16,128]{2,1,0:T(8,128...) custom-call(s16[16,4224]{1,0:T(8,128)(2,1)S(1)} %get-tuple-element.5, ...), custom_call_target="tpu_custom_call" | custom-call | flops 1 | bytes 1 | tf_op jit(solution)/shard_map/pallas_call | solution.py:555
  23.1 0.0 collective-permute-done.7.got_a
  23.1 0.2 collective-permute-done.8.got_b
  23.3 1.5 %shard_map.117 = (f32[8,16,128]{2,1,0:T(8,128)S(1)}, f32[16,16,128]{2,1,0:T(8,128)S(1)}, f32[40,4,128]{2,1,0:T(4,128)S(1)}, f32[32,4,128]{2,1,0:T(4,128)S(1)}, f...) custom-call(bf16[40,16,128]{2,1,0:T(8,128)(2,1)S(1)} %get-tuple-element.66.refs, ...), custom_call_target="tpu_custom_call" | custom-call | flops 1 | bytes 1 | tf_op jit(solution)/shard_map/pallas_call | solution.py:566
  24.8 0.1 collective-permute-start.9
  24.9 2.5 %collective-permute-start.13 = (f32[32,128]{1,0:T(8,128)S(1)}, f32[32,128]{1,0:T(8,128)S(1)}, u32[]{:S(2)}, u32[]{:S(2)}) collective-permute-start(f32[32,128]{1,0:T(8,128)S(1)} %get-tuple-element.98), channel_id=1, source_target_pairs={{0,7},{1,2},{2,1},{3,4},{4,3},{5,6},{6,5},{7,0},{8,15},{9,10},{10,... | collective-permute-start | bytes 49160 | tf_op jit(solution)/shard_map/ppermute | solution.py:584
  27.4 0.0 collective-permute-done.9.got_a
  27.4 1.2 %collective-permute-start.12 = (f32[32,128]{1,0:T(8,128)S(1)}, f32[32,128]{1,0:T(8,128)S(1)}, u32[]{:S(2)}, u32[]{:S(2)}) collective-permute-start(f32[32,128]{1,0:T(8,128)S(1)} %slice_add_fusion.refs_0_), channel_id=1, source_target_pairs={{0,6},{1,7},{2,4},{3,5},{4,2},{5,3},{6,0},{7,1},{8,14},{9,15},{10,... | collective-permute-start | bytes 49160 | tf_op jit(solution)/shard_map/ppermute | solution.py:591
  28.6 0.5 %collective-permute-start.11 = (f32[32,128]{1,0:T(8,128)S(1)}, f32[32,128]{1,0:T(8,128)S(1)}, u32[]{:S(2)}, u32[]{:S(2)}) collective-permute-start(f32[32,128]{1,0:T(8,128)S(1)} %slice_add_fusion.refs_0_), channel_id=1, source_target_pairs={{0,4},{1,5},{2,6},{3,7},{4,0},{5,1},{6,2},{7,3},{8,12},{9,13},{10,... | collective-permute-start | bytes 49160 | tf_op jit(solution)/shard_map/ppermute | solution.py:591
  29.1 1.9 %collective-permute-start.10 = (f32[32,128]{1,0:T(8,128)S(1)}, f32[32,128]{1,0:T(8,128)S(1)}, u32[]{:S(2)}, u32[]{:S(2)}) collective-permute-start(f32[32,128]{1,0:T(8,128)S(1)} %slice_add_fusion.refs_0_), channel_id=1, source_target_pairs={{0,2},{1,3},{2,0},{3,1},{4,6},{5,7},{6,4},{7,5},{8,10},{9,11},{10,... | collective-permute-start | bytes 49160 | tf_op jit(solution)/shard_map/ppermute | solution.py:591
  31.0 0.0 collective-permute-done.13.got_b
  31.0 1.9 %shard_map.119 = (f32[4,4096]{1,0:T(4,128)}, f32[4,4096]{1,0:T(4,128)}) custom-call(f32[40,4,128]{2,1,0:T(4,128)S(1)} %get-tuple-element.95.ws, f32[32,4,128]{2,1,0:T(4,128)S(1)} %get-tuple-element.96.bs, f32[32,4,128]{2,1,0:T(4,128)S(1)} %get-tuple-element.97.v2, f32[64,128]{1,0:T(8,128)S(1)} %collective-permute-done.9.got_a, ...), custom_call_target="tpu_custom_call" | custom-call | flops 1 | bytes 1 | tf_op jit(solution)/shard_map/pallas_call | solution.py:593
  32.9 0.0 collective-permute-done.12.refs_3_
  32.9 0.0 collective-permute-done.11.refs_2_
  32.9 0.0 collective-permute-done.10.refs_1_
  32.9 0.9 %shard_map.118 = f32[2,2,4096]{2,1,0:T(2,128)} custom-call(f32[32,128]{1,0:T(8,128)S(1)} %slice_add_fusion.refs_0_, f32[32,128]{1,0:T(8,128)S(1)} %collective-permute-done.10.refs_1_, f32[32,128]{1,0:T(8,128)S(1)} %collective-permute-done.11.refs_2_, f32[32,128]{1,0:T(8,128)S(1)} %collective-permute-done.12.refs_3_, ...), custom_call_target="tpu_custom_call" | custom-call | flops 1 | bytes 1 | tf_op jit(solution)/shard_map/pallas_call | solution.py:599
  (9 shorter events, 0.0 us)
Async XLA Ops:
  2.5 7.9 %collective-permute-start = (s16[16,2176]{1,0:T(8,128)(2,1)}, s16[16,2176]{1,0:T(8,128)(2,1)S(1)}, u32[]{:S(2)}, u32[]{:S(2)}) collective-permute-start(s16[16,2176]{1,0:T(8,128)(2,1)} %get-tuple-element.52), channel_id=1, source_target_pairs={{0,16},{8,24},{16,0},{24,8},{1,17},{9,25},{17,1},{25,9},{2,18},{10... | collective-permute-start | bytes 208904 | tf_op jit(solution)/shard_map/ppermute | solution.py:505
  6.5 10.0 %collective-permute-start.1 = (s16[16,4224]{1,0:T(8,128)(2,1)}, s16[16,4224]{1,0:T(8,128)(2,1)S(1)}, u32[]{:S(2)}, u32[]{:S(2)}) collective-permute-start(s16[16,4224]{1,0:T(8,128)(2,1)} %get-tuple-element.53.wire.after), channel_id=1, source_target_pairs={{0,8},{8,0},{16,24},{24,16},{1,9},{9,1},{17,25},{25,17},{2,10},{10... | collective-permute-start | bytes 405512 | tf_op jit(solution)/shard_map/ppermute | solution.py:505
  8.1 5.7 %collective-permute-start.3 = (s16[16,2048]{1,0:T(8,128)(2,1)}, s16[16,2048]{1,0:T(8,128)(2,1)S(1)}, u32[]{:S(2)}, u32[]{:S(2)}) collective-permute-start(s16[16,2048]{1,0:T(8,128)(2,1)} %get-tuple-element.57), channel_id=1, source_target_pairs={{0,16},{8,24},{16,0},{24,8},{1,17},{9,25},{17,1},{25,9},{2,18},{10... | collective-permute-start | bytes 196616 | tf_op jit(solution)/shard_map/ppermute | solution.py:505
  8.4 3.3 %copy-start = (bf16[32,3,128,128]{3,2,1,0:T(8,128)(2,1)S(1)}, bf16[32,3,128,128]{3,2,1,0:T(8,128)(2,1)}, u32[]{:S(2)}) copy-start(bf16[32,3,128,128]{3,2,1,0:T(8,128)(2,1)} %right.1) | copy-start | bytes 9437188
  8.4 3.3 %copy-start.1 = (f32[4,4,4096]{2,1,0:T(4,128)S(1)}, f32[4,4,4096]{2,1,0:T(4,128)}, u32[]{:S(2)}) copy-start(f32[4,4,4096]{2,1,0:T(4,128)} %rain.3) | copy-start | bytes 786436
  8.4 3.3 %copy-start.2 = (s16[16,4224]{1,0:T(8,128)(2,1)S(1)}, s16[16,4224]{1,0:T(8,128)(2,1)}, u32[]{:S(2)}) copy-start(s16[16,4224]{1,0:T(8,128)(2,1)} %get-tuple-element.53.wire.after) | copy-start | bytes 405508
  8.4 3.3 %copy-start.3 = (f32[2,4096]{1,0:T(2,128)S(1)}, f32[2,4096]{1,0:T(2,128)}, u32[]{:S(2)}) copy-start(f32[2,4096]{1,0:T(2,128)} %obs.1) | copy-start | bytes 98308
  8.4 3.3 %copy-start.4 = (f32[4096]{0:T(1024)S(1)}, f32[4096]{0:T(1024)}, u32[]{:S(2)}) copy-start(f32[4096]{0:T(1024)} %param.14) | copy-start | bytes 49156
  8.4 3.3 %copy-start.5 = (f32[4096]{0:T(1024)S(1)}, f32[4096]{0:T(1024)}, u32[]{:S(2)}) copy-start(f32[4096]{0:T(1024)} %param.16) | copy-start | bytes 49156
  8.4 3.3 %copy-start.6 = (s32[32,3]{0,1:T(4,128)S(1)}, s32[32,3]{0,1:T(4,128)}, u32[]{:S(2)}) copy-start(s32[32,3]{0,1:T(4,128)} %param.12) | copy-start | bytes 1156
  8.5 3.2 %copy-start.7 = (s32[2,16]{1,0:T(2,128)S(1)}, s32[2,16]{1,0:T(2,128)}, u32[]{:S(2)}) copy-start(s32[2,16]{1,0:T(2,128)} %anc.1) | copy-start | bytes 388
  10.4 4.5 %copy-start.9 = (bf16[528,128]{1,0:T(8,128)(2,1)S(1)}, bf16[528,128]{1,0:T(8,128)(2,1)}, u32[]{:S(2)}) copy-start(bf16[528,128]{1,0:T(8,128)(2,1)} %get-tuple-element.73) | copy-start | bytes 405508
  10.4 4.9 %copy-start.8 = (bf16[528,128]{1,0:T(8,128)(2,1)S(1)}, bf16[528,128]{1,0:T(8,128)(2,1)}, u32[]{:S(2)}) copy-start(bf16[528,128]{1,0:T(8,128)(2,1)} %get-tuple-element.72) | copy-start | bytes 405508
  10.4 7.6 %collective-permute-start.2 = (s16[16,2176]{1,0:T(8,128)(2,1)S(1)}, s16[16,2176]{1,0:T(8,128)(2,1)S(1)}, u32[]{:S(2)}, u32[]{:S(2)}) collective-permute-start(s16[16,2176]{1,0:T(8,128)(2,1)S(1)} %collective-permute-done.after.refs_2_), channel_id=1, source_target_pairs={{0,8},{8,0},{16,24},{24,16},{1,9},{9,1},{17,25},{25,17},{2,10},{10... | collective-permute-start | bytes 208904 | tf_op jit(solution)/shard_map/ppermute | solution.py:505
  13.7 4.3 %collective-permute-start.4 = (s16[16,2048]{1,0:T(8,128)(2,1)S(1)}, s16[16,2048]{1,0:T(8,128)(2,1)S(1)}, u32[]{:S(2)}, u32[]{:S(2)}) collective-permute-start(s16[16,2048]{1,0:T(8,128)(2,1)S(1)} %collective-permute-done.3.refs_4_.refs_2_), channel_id=1, source_target_pairs={{0,8},{8,0},{16,24},{24,16},{1,9},{9,1},{17,25},{25,17},{2,10},{10... | collective-permute-start | bytes 196616 | tf_op jit(solution)/shard_map/ppermute | solution.py:505
  14.9 6.7 %collective-permute-start.6 = (bf16[528,128]{1,0:T(8,128)(2,1)S(1)}, bf16[528,128]{1,0:T(8,128)(2,1)S(1)}, u32[]{:S(2)}, u32[]{:S(2)}) collective-permute-start(bf16[528,128]{1,0:T(8,128)(2,1)S(1)} %copy-done.9), channel_id=1, source_target_pairs={{0,7},{1,2},{2,1},{3,4},{4,3},{5,6},{6,5},{7,0},{8,15},{9,10},{10,... | collective-permute-start | bytes 405512 | tf_op jit(solution)/shard_map/ppermute | solution.py:529
  15.3 6.3 %collective-permute-start.5 = (bf16[528,128]{1,0:T(8,128)(2,1)S(1)}, bf16[528,128]{1,0:T(8,128)(2,1)S(1)}, u32[]{:S(2)}, u32[]{:S(2)}) collective-permute-start(bf16[528,128]{1,0:T(8,128)(2,1)S(1)} %copy-done.8), channel_id=1, source_target_pairs={{0,1},{1,0},{2,3},{3,2},{4,5},{5,4},{6,7},{7,6},{8,9},{9,8},{10,11... | collective-permute-start | bytes 405512 | tf_op jit(solution)/shard_map/ppermute | solution.py:528
  18.8 4.4 %collective-permute-start.7 = (bf16[12,16,128]{2,1,0:T(8,128)(2,1)S(1)}, bf16[12,16,128]{2,1,0:T(8,128)(2,1)S(1)}, u32[]{:S(2)}, u32[]{:S(2)}) collective-permute-start(bf16[12,16,128]{2,1,0:T(8,128)(2,1)S(1)} %get-tuple-element.83), channel_id=1, source_target_pairs={{0,1},{1,0},{2,3},{3,2},{4,5},{5,4},{6,7},{7,6},{8,9},{9,8},{10,11... | collective-permute-start | bytes 147464 | tf_op jit(solution)/shard_map/ppermute | solution.py:544
  18.8 4.5 %collective-permute-start.8 = (bf16[12,16,128]{2,1,0:T(8,128)(2,1)S(1)}, bf16[12,16,128]{2,1,0:T(8,128)(2,1)S(1)}, u32[]{:S(2)}, u32[]{:S(2)}) collective-permute-start(bf16[12,16,128]{2,1,0:T(8,128)(2,1)S(1)} %get-tuple-element.84), channel_id=1, source_target_pairs={{0,7},{1,2},{2,1},{3,4},{4,3},{5,6},{6,5},{7,0},{8,15},{9,10},{10,... | collective-permute-start | bytes 147464 | tf_op jit(solution)/shard_map/ppermute | solution.py:545
  24.8 2.6 %collective-permute-start.9 = (f32[64,128]{1,0:T(8,128)S(1)}, f32[64,128]{1,0:T(8,128)S(1)}, u32[]{:S(2)}, u32[]{:S(2)}) collective-permute-start(f32[64,128]{1,0:T(8,128)S(1)} %get-tuple-element.89), channel_id=1, source_target_pairs={{0,1},{1,0},{2,3},{3,2},{4,5},{5,4},{6,7},{7,6},{8,9},{9,8},{10,11... | collective-permute-start | bytes 98312 | tf_op jit(solution)/shard_map/ppermute | solution.py:583
  24.9 6.1 %collective-permute-start.13 = (f32[32,128]{1,0:T(8,128)S(1)}, f32[32,128]{1,0:T(8,128)S(1)}, u32[]{:S(2)}, u32[]{:S(2)}) collective-permute-start(f32[32,128]{1,0:T(8,128)S(1)} %get-tuple-element.98), channel_id=1, source_target_pairs={{0,7},{1,2},{2,1},{3,4},{4,3},{5,6},{6,5},{7,0},{8,15},{9,10},{10,... | collective-permute-start | bytes 49160 | tf_op jit(solution)/shard_map/ppermute | solution.py:584
  27.4 5.5 %collective-permute-start.12 = (f32[32,128]{1,0:T(8,128)S(1)}, f32[32,128]{1,0:T(8,128)S(1)}, u32[]{:S(2)}, u32[]{:S(2)}) collective-permute-start(f32[32,128]{1,0:T(8,128)S(1)} %slice_add_fusion.refs_0_), channel_id=1, source_target_pairs={{0,6},{1,7},{2,4},{3,5},{4,2},{5,3},{6,0},{7,1},{8,14},{9,15},{10,... | collective-permute-start | bytes 49160 | tf_op jit(solution)/shard_map/ppermute | solution.py:591
  28.6 4.3 %collective-permute-start.11 = (f32[32,128]{1,0:T(8,128)S(1)}, f32[32,128]{1,0:T(8,128)S(1)}, u32[]{:S(2)}, u32[]{:S(2)}) collective-permute-start(f32[32,128]{1,0:T(8,128)S(1)} %slice_add_fusion.refs_0_), channel_id=1, source_target_pairs={{0,4},{1,5},{2,6},{3,7},{4,0},{5,1},{6,2},{7,3},{8,12},{9,13},{10,... | collective-permute-start | bytes 49160 | tf_op jit(solution)/shard_map/ppermute | solution.py:591
  29.1 3.8 %collective-permute-start.10 = (f32[32,128]{1,0:T(8,128)S(1)}, f32[32,128]{1,0:T(8,128)S(1)}, u32[]{:S(2)}, u32[]{:S(2)}) collective-permute-start(f32[32,128]{1,0:T(8,128)S(1)} %slice_add_fusion.refs_0_), channel_id=1, source_target_pairs={{0,2},{1,3},{2,0},{3,1},{4,6},{5,7},{6,4},{7,5},{8,10},{9,11},{10,... | collective-permute-start | bytes 49160 | tf_op jit(solution)/shard_map/ppermute | solution.py:591
